TPU v7x, 32 devices: a whole 2x2x4 slice. The times are simulated.
32 devices in a mesh: section: 2 (over core), seq: 8 (over z, x), traj: 2 (over y).
Axes of the slice: x: 2, y: 2, z: 4, core: 2. Of those that a mesh axis runs over, the one named last changes fastest.
Arguments:
- tokens: bfloat16 [2048, 2048], P(('traj', 'seq')), parts along dimension 0, may hold values from -6 to 6
- norm_gain: float32 [2, 2048], P('section'), may hold values from 0.25 to 1.75
- w_qkv: bfloat16 [2, 2048, 3072], P('section'), may hold values from -0.125 to 0.125
- w_rate: bfloat16 [2, 2048, 16], P('section'), may hold values from -0.125 to 0.125
- rate_base: float32 [2, 16], P('section'), may hold values from 0.0125 to 0.015625
- init_state: float32 [2, 16, 64, 64], P('section'), may hold values from -6 to 6
- w_out: bfloat16 [2, 1024, 2048], P('section'), may hold values from -0.1875 to 0.1875
Outputs:
- layer_out: bfloat16 [2, 2048, 2048], P('section', ('traj', 'seq')), parts along dimension 1
There are 2 independent parts, one for each index of `traj`. A program takes and returns all parts, laid end to end along the dimension named above; an argument that names none is the same for every part. Nothing has to cross between parts.
All inputs are finite; a program needn't handle non-finite values.
Results may differ from a plain program's by a relative error of at most 0.017.
Values may be sent and summed in bfloat16 or wider, within the bound.
No kernel may reach another device: no remote copies, remote signals or barrier semaphores. Data moves between devices by JAX's collectives and lax.ppermute only.
A program may use at most 128 MiB of HBM per device.

v0:
```python
import jax
import jax.numpy as jnp
from jax import lax
from jax.sharding import PartitionSpec as P

HD = 64
MB = 64


def from_behind(value, axis, steps):
    count = lax.axis_size(axis)
    initial, last = (max(0, -steps), min(count, count - steps))
    return lax.ppermute(value, axis, [(source, source + steps) for source in range(initial, last)])


def inner_block(weight_state, block):
    precise_mode = lax.Precision.HIGHEST
    query_rows, key_input, value_input, rates = block
    predicted_values = jnp.einsum("ylc,yci->yli", key_input, weight_state, precision=precise_mode)
    scaled_gradient = rates[..., None] * (predicted_values - value_input)
    causal_mask = jnp.tril(jnp.ones((query_rows.shape[1], query_rows.shape[1]), query_rows.dtype))
    attention_scores = (
        jnp.einsum("kxw,kqw->kxq", query_rows, key_input, precision=precise_mode) * causal_mask
    )
    inner_output = jnp.einsum(
        "ylc,yci->yli", query_rows, weight_state, precision=precise_mode
    ) - jnp.einsum("ixb,ibt->ixt", attention_scores, scaled_gradient, precision=precise_mode)
    updated_state = weight_state - jnp.einsum(
        "ncz,ncp->nzp", key_input, scaled_gradient, precision=precise_mode
    )
    return (updated_state, inner_output)


def inner_inputs(hidden, gain, w_qkv, w_rate, rate_base):
    wide = hidden.astype(jnp.float32)
    mean_sq = jnp.mean(wide * wide, axis=-1, keepdims=True)
    normed = (wide * lax.rsqrt(mean_sq + 1e-06) * gain).astype(jnp.bfloat16)
    projected = jnp.dot(normed, w_qkv, preferred_element_type=jnp.float32)
    rows = hidden.shape[0]
    heads = rate_base.shape[0]
    width = heads * HD
    query_rows = projected[:, :width].reshape(rows, heads, HD)
    key_input = projected[:, width : 2 * width].reshape(rows, heads, HD)
    value_input = projected[:, 2 * width :].reshape(rows, heads, HD)
    query_rows = query_rows * lax.rsqrt(
        jnp.sum(query_rows * query_rows, axis=-1, keepdims=True) + 1e-06
    )
    key_input = key_input * lax.rsqrt(
        jnp.sum(key_input * key_input, axis=-1, keepdims=True) + 1e-06
    )
    rates = rate_base[None, :] * jax.nn.sigmoid(
        jnp.dot(normed, w_rate, preferred_element_type=jnp.float32)
    )
    blocks = rows // MB

    def to_blocks(array):
        return array.reshape(blocks, MB, heads, HD).transpose(0, 2, 1, 3)

    rate_blocks = rates.reshape(blocks, MB, heads).transpose(0, 2, 1)
    return (to_blocks(query_rows), to_blocks(key_input), to_blocks(value_input), rate_blocks)


def apply_map(linear_output, position_offset, weight_state):
    return (
        jnp.einsum("hde,hef->hdf", linear_output, weight_state, precision=lax.Precision.HIGHEST)
        + position_offset
    )


def compose_maps(earlier, later):
    return (
        jnp.einsum("hde,hef->hdf", later[0], earlier[0], precision=lax.Precision.HIGHEST),
        apply_map(later[0], later[1], earlier[1]),
    )


def block_map(carry, block):
    precise_mode = lax.Precision.HIGHEST
    query_rows, key_input, value_input, rates = block
    weighted_values = rates[..., None] * key_input
    identity_matrix = jnp.broadcast_to(
        jnp.eye(key_input.shape[2], dtype=jnp.float32), carry[0].shape
    )
    linear_output = identity_matrix - jnp.einsum(
        "ncz,ncp->nzp", key_input, weighted_values, precision=precise_mode
    )
    position_offset = jnp.einsum(
        "ncz,ncp->nzp", weighted_values, value_input, precision=precise_mode
    )
    return (compose_maps(carry, (linear_output, position_offset)), None)


def layer_terms(hidden, gain, w_qkv, w_rate, rate_base, init_state, w_out):
    blocks = inner_inputs(hidden, gain, w_qkv, w_rate, rate_base)
    identity_matrix = jnp.broadcast_to(
        jnp.eye(init_state.shape[1], dtype=jnp.float32), init_state.shape
    )
    empty = jnp.zeros_like(init_state)
    slab_map, unused = lax.scan(block_map, (identity_matrix, empty), blocks)
    seq_index = lax.axis_index("seq")

    def relay(turn_index, start_state):
        slab_end = apply_map(slab_map[0], slab_map[1], start_state)
        received = from_behind(slab_end, "seq", 1)
        return jnp.where(seq_index == 0, init_state, received)

    start_state = lax.fori_loop(0, lax.axis_size("seq") - 1, relay, init_state)
    final_state, inner_output = lax.scan(inner_block, start_state, blocks)
    rows = hidden.shape[0]
    inner_bf = inner_output.transpose(0, 2, 1, 3).reshape(rows, -1).astype(jnp.bfloat16)
    return jnp.dot(inner_bf, w_out, preferred_element_type=jnp.float32)


def shards(tokens, norm_gain, w_qkv, w_rate, rate_base, init_state, w_out):
    count = lax.axis_size("section")
    section_index = lax.axis_index("section")
    kept = jnp.zeros_like(tokens)
    current = tokens
    for round_index in range(count):
        mixed = layer_terms(
            current, norm_gain[0], w_qkv[0], w_rate[0], rate_base[0], init_state[0], w_out[0]
        )
        result = (current.astype(jnp.float32) + mixed).astype(jnp.bfloat16)
        kept = jnp.where(section_index == round_index, result, kept)
        if round_index + 1 < count:
            current = from_behind(result, "section", 1)
    return kept[None]


def solution(mesh):
    return jax.shard_map(
        shards,
        mesh=mesh,
        in_specs=(
            P(("traj", "seq"), None),
            P("section", None),
            P("section", None, None),
            P("section", None, None),
            P("section", None),
            P("section", None, None, None),
            P("section", None, None),
        ),
        out_specs=P("section", ("traj", "seq"), None),
        check_vma=False,
    )
```

profile of v0, /device:TPU:8, one launch (start us, length us, event | category | flops | bytes accessed | tf_op | source)
XLA Modules:
  0.0 341.5 jit_solution(8885560117110273975)
XLA Ops:
  1.3 6.7 %fusion.76 = f32[128,3072]{1,0:T(8,128)S(1)} fusion(bf16[1,2048,3072]{2,1,0:T(8,128)(2,1)} %param.21, bf16[128,2048]{1,0:T(8,128)(2,1)} %param.19, f32[2048]{0:T(1024)} %bitcast.276, f32[128]{0:T(128)S(1)} %add_rsqrt_fusion.5), kind=kOutput, calls=%fused_computation.100 | convolution fusion | flops 1611661312 | bytes 14688768 | tf_op jit(solution)/shard_map/dot_general | solution.py:38
  14.7 3.3 fusion.115
  18.1 8.4 %while.78 = (s32[]{:T(128)}, f32[16,64,64]{2,1,0:T(8,128)S(1)}, f32[16,64,64]{2,1,0:T(8,128)S(1)}, f32[2,16,64,64]{2,3,1,0:T(8,128)S(1)}, f32[2,16,64]{2,1,0:T(8...) while((s32[]{:T(128)}, f32[16,64,64]{2,1,0:T(8,128)S(1)}, ...), condition=%wide.region_3.4_spmd.clone, body=%wide.region_2.0_spmd.clone.sunk | while | flops 201662464 | bytes 4773987 | solution.py:99
  26.6 122.1 %while.74 = (s32[]{:T(128)}, f32[16,64,64]{2,1,0:T(8,128)S(1)}, pred[]{:T(512)}, f32[16,64,64]{2,1,0:T(8,128)S(1)}, f32[16,64,64]{2,1,0:T(8,128)S(1)}, /*index=5*/f32[16,64,64]{2,1,0:T(8,128)S(1)}, s32[]{:T(128)}) while((s32[]{:T(128)}, f32[16,64,64]{2,1,0:T(8,128)S(1)}, pred[]{:T(512)}, f32[16,64,64]{2,1,0:T(8,128)S(1)}, ...), condition=%wide.region_5.6_spmd, body=%wide.region_4.5_spmd.sunk | while | flops 50462720 | bytes 3932306 | solution.py:107
  28.1 3.4 collective-permute-start
  31.4 13.3 %collective-permute-done = f32[16,64,64]{2,1,0:T(8,128)S(1)} collective-permute-done((f32[16,64,64]{2,1,0:T(8,128)}, f32[16,64,64]{2,1,0:T(8,128)S(1)}, u32[]{:S(2)}, u32[]{:S(2)}) %collective-permute-start) | collective-permute-done | bytes 262176 | tf_op jit(solution)/shard_map/while/body/eval_jaxpr/ppermute | solution.py:13
  48.1 2.5 collective-permute-start
  50.6 13.3 %collective-permute-done = f32[16,64,64]{2,1,0:T(8,128)S(1)} collective-permute-done((f32[16,64,64]{2,1,0:T(8,128)}, f32[16,64,64]{2,1,0:T(8,128)S(1)}, u32[]{:S(2)}, u32[]{:S(2)}) %collective-permute-start) | collective-permute-done | bytes 262176 | tf_op jit(solution)/shard_map/while/body/eval_jaxpr/ppermute | solution.py:13
  67.2 1.9 collective-permute-start
  69.1 12.9 %collective-permute-done = f32[16,64,64]{2,1,0:T(8,128)S(1)} collective-permute-done((f32[16,64,64]{2,1,0:T(8,128)}, f32[16,64,64]{2,1,0:T(8,128)S(1)}, u32[]{:S(2)}, u32[]{:S(2)}) %collective-permute-start) | collective-permute-done | bytes 262176 | tf_op jit(solution)/shard_map/while/body/eval_jaxpr/ppermute | solution.py:13
  85.4 1.9 collective-permute-start
  87.3 12.0 %collective-permute-done = f32[16,64,64]{2,1,0:T(8,128)S(1)} collective-permute-done((f32[16,64,64]{2,1,0:T(8,128)}, f32[16,64,64]{2,1,0:T(8,128)S(1)}, u32[]{:S(2)}, u32[]{:S(2)}) %collective-permute-start) | collective-permute-done | bytes 262176 | tf_op jit(solution)/shard_map/while/body/eval_jaxpr/ppermute | solution.py:13
  104.6 11.1 %collective-permute-done = f32[16,64,64]{2,1,0:T(8,128)S(1)} collective-permute-done((f32[16,64,64]{2,1,0:T(8,128)}, f32[16,64,64]{2,1,0:T(8,128)S(1)}, u32[]{:S(2)}, u32[]{:S(2)}) %collective-permute-start) | collective-permute-done | bytes 262176 | tf_op jit(solution)/shard_map/while/body/eval_jaxpr/ppermute | solution.py:13
  121.0 10.3 %collective-permute-done = f32[16,64,64]{2,1,0:T(8,128)S(1)} collective-permute-done((f32[16,64,64]{2,1,0:T(8,128)}, f32[16,64,64]{2,1,0:T(8,128)S(1)}, u32[]{:S(2)}, u32[]{:S(2)}) %collective-permute-start) | collective-permute-done | bytes 262176 | tf_op jit(solution)/shard_map/while/body/eval_jaxpr/ppermute | solution.py:13
  136.5 10.3 %collective-permute-done = f32[16,64,64]{2,1,0:T(8,128)S(1)} collective-permute-done((f32[16,64,64]{2,1,0:T(8,128)}, f32[16,64,64]{2,1,0:T(8,128)S(1)}, u32[]{:S(2)}, u32[]{:S(2)}) %collective-permute-start) | collective-permute-done | bytes 262176 | tf_op jit(solution)/shard_map/while/body/eval_jaxpr/ppermute | solution.py:13
  149.6 15.8 %while.75 = (s32[]{:T(128)}, f32[16,64,64]{2,1,0:T(8,128)S(1)}, bf16[2,16,64,64]{3,2,1,0:T(8,128)(2,1)}, f32[2,16,64,64]{2,3,1,0:T(8,128)S(1)}, f32[2,16,64]{2,1...) while((s32[]{:T(128)}, f32[16,64,64]{2,1,0:T(8,128)S(1)}, ...), condition=%wide.region_8.9_spmd, body=%wide.region_7.8_spmd.sunk | while | flops 251994112 | bytes 10029721 | solution.py:108
  149.6 2.2 fusion.213
  157.5 2.2 fusion.213
  167.2 2.9 fusion.91
  173.1 6.5 %fusion.74 = f32[128,3072]{1,0:T(8,128)S(1)} fusion(bf16[1,2048,3072]{2,1,0:T(8,128)(2,1)} %param.21, bf16[128,2048]{1,0:T(8,128)(2,1)S(1)} %collective-permute-done.2, f32[128]{0:T(128)S(1)} %add_rsqrt_fusion.4, f32[2048]{0:T(1024)S(1)} %bitcast.278), kind=kOutput, calls=%fused_computation.98 | convolution fusion | flops 1611661312 | bytes 14688768 | tf_op jit(solution)/shard_map/dot_general | solution.py:38
  188.9 10.9 %while.79 = (s32[]{:T(128)}, f32[16,64,64]{2,1,0:T(8,128)S(1)}, f32[16,64,64]{2,1,0:T(8,128)}, f32[2,16,64,64]{2,3,1,0:T(8,128)S(1)}, f32[2,16,64]{2,1,0:T(8,128...) while((s32[]{:T(128)}, f32[16,64,64]{2,1,0:T(8,128)S(1)}, ...), condition=%wide.region_12.13_spmd.clone, body=%wide.region_11.12_spmd.clone.sunk | while | flops 201662464 | bytes 4773987 | solution.py:99
  190.6 2.5 convolution_add_fusion.11
  196.6 2.5 convolution_add_fusion.11
  199.8 2.7 fusion.114
  202.5 120.0 %while.76 = (s32[]{:T(128)}, f32[16,64,64]{2,1,0:T(8,128)S(1)}, pred[]{:T(512)}, f32[16,64,64]{2,1,0:T(8,128)S(1)}, f32[16,64,64]{2,1,0:T(8,128)}, /*index=5*/f32[16,64,64]{2,1,0:T(8,128)S(1)}, s32[]{:T(128)}) while((s32[]{:T(128)}, f32[16,64,64]{2,1,0:T(8,128)S(1)}, pred[]{:T(512)}, f32[16,64,64]{2,1,0:T(8,128)S(1)}, ...), condition=%wide.region_14.15_spmd, body=%wide.region_13.14_spmd.sunk | while | flops 50462720 | bytes 2883702 | solution.py:107
  202.5 2.5 convolution_add_fusion.9
  205.0 1.9 collective-permute-start.1
  206.9 15.3 %collective-permute-done.1 = f32[16,64,64]{2,1,0:T(8,128)S(1)} collective-permute-done((f32[16,64,64]{2,1,0:T(8,128)}, f32[16,64,64]{2,1,0:T(8,128)S(1)}, u32[]{:S(2)}, u32[]{:S(2)}) %collective-permute-start.1) | collective-permute-done | bytes 262176 | tf_op jit(solution)/shard_map/while/body/eval_jaxpr/ppermute | solution.py:13
  222.2 2.5 convolution_add_fusion.9
  224.7 1.9 collective-permute-start.1
  226.6 14.5 %collective-permute-done.1 = f32[16,64,64]{2,1,0:T(8,128)S(1)} collective-permute-done((f32[16,64,64]{2,1,0:T(8,128)}, f32[16,64,64]{2,1,0:T(8,128)S(1)}, u32[]{:S(2)}, u32[]{:S(2)}) %collective-permute-start.1) | collective-permute-done | bytes 262176 | tf_op jit(solution)/shard_map/while/body/eval_jaxpr/ppermute | solution.py:13
  241.2 2.5 convolution_add_fusion.9
  243.7 1.9 collective-permute-start.1
  245.6 13.5 %collective-permute-done.1 = f32[16,64,64]{2,1,0:T(8,128)S(1)} collective-permute-done((f32[16,64,64]{2,1,0:T(8,128)}, f32[16,64,64]{2,1,0:T(8,128)S(1)}, u32[]{:S(2)}, u32[]{:S(2)}) %collective-permute-start.1) | collective-permute-done | bytes 262176 | tf_op jit(solution)/shard_map/while/body/eval_jaxpr/ppermute | solution.py:13
  259.2 2.5 convolution_add_fusion.9
  261.7 1.9 collective-permute-start.1
  263.6 12.6 %collective-permute-done.1 = f32[16,64,64]{2,1,0:T(8,128)S(1)} collective-permute-done((f32[16,64,64]{2,1,0:T(8,128)}, f32[16,64,64]{2,1,0:T(8,128)S(1)}, u32[]{:S(2)}, u32[]{:S(2)}) %collective-permute-start.1) | collective-permute-done | bytes 262176 | tf_op jit(solution)/shard_map/while/body/eval_jaxpr/ppermute | solution.py:13
  276.3 2.5 convolution_add_fusion.9
  280.7 11.7 %collective-permute-done.1 = f32[16,64,64]{2,1,0:T(8,128)S(1)} collective-permute-done((f32[16,64,64]{2,1,0:T(8,128)}, f32[16,64,64]{2,1,0:T(8,128)S(1)}, u32[]{:S(2)}, u32[]{:S(2)}) %collective-permute-start.1) | collective-permute-done | bytes 262176 | tf_op jit(solution)/shard_map/while/body/eval_jaxpr/ppermute | solution.py:13
  292.5 2.5 convolution_add_fusion.9
  295.0 1.9 collective-permute-start.1
  296.9 10.8 %collective-permute-done.1 = f32[16,64,64]{2,1,0:T(8,128)S(1)} collective-permute-done((f32[16,64,64]{2,1,0:T(8,128)}, f32[16,64,64]{2,1,0:T(8,128)S(1)}, u32[]{:S(2)}, u32[]{:S(2)}) %collective-permute-start.1) | collective-permute-done | bytes 262176 | tf_op jit(solution)/shard_map/while/body/eval_jaxpr/ppermute | solution.py:13
  307.8 2.5 convolution_add_fusion.9
  312.2 10.3 %collective-permute-done.1 = f32[16,64,64]{2,1,0:T(8,128)S(1)} collective-permute-done((f32[16,64,64]{2,1,0:T(8,128)}, f32[16,64,64]{2,1,0:T(8,128)S(1)}, u32[]{:S(2)}, u32[]{:S(2)}) %collective-permute-start.1) | collective-permute-done | bytes 262176 | tf_op jit(solution)/shard_map/while/body/eval_jaxpr/ppermute | solution.py:13
  322.7 14.2 %while.77 = (s32[]{:T(128)}, f32[16,64,64]{2,1,0:T(8,128)S(1)}, bf16[2,16,64,64]{3,2,1,0:T(8,128)(2,1)S(1)}, f32[2,16,64,64]{2,3,1,0:T(8,128)S(1)}, f32[2,16,64]...) while((s32[]{:T(128)}, f32[16,64,64]{2,1,0:T(8,128)S(1)}, ...), condition=%wide.region_17.18_spmd, body=%wide.region_16.17_spmd.sunk | while | flops 251994112 | bytes 7932513 | solution.py:108
  322.7 2.2 fusion.229
  329.8 2.1 fusion.229
  337.5 3.9 %fusion.97 = bf16[1,128,2048]{2,1,0:T(8,128)(2,1)} fusion(bf16[128,1024]{1,0:T(8,128)(2,1)S(1)} %convert_element_type.61, bf16[1,1024,2048]{2,1,0:T(8,128)(2,1)} %param.25, bf16[128,2048]{1,0:T(8,128)(2,1)S(1)} %copy-done.4, bf16[128,2048]{1,0:T(8,128)(2,1)} %copy-done.9, pred[]{:T(512)S(6)} %eq.29, pred[]{:T(512)S(6)} %eq.26), kind=kOutput, calls=%fused_computation.111 | convolution fusion | flops 538181632 | bytes 6029314 | tf_op jit(solution)/shard_map/dot_general | solution.py:111
  (174 shorter events, 91.9 us)
Async XLA Ops:
  0.0 14.1 %copy-start = (bf16[1,2048,16]{1,2,0:T(8,128)(2,1)S(1)}, bf16[1,2048,16]{1,2,0:T(8,128)(2,1)}, u32[]{:S(2)}) copy-start(bf16[1,2048,16]{1,2,0:T(8,128)(2,1)} %param.22) | copy-start | bytes 196612
  10.4 3.7 %copy-start.5 = (bf16[128,2048]{1,0:T(8,128)(2,1)S(1)}, bf16[128,2048]{1,0:T(8,128)(2,1)}, u32[]{:S(2)}) copy-start(bf16[128,2048]{1,0:T(8,128)(2,1)} %param.19) | copy-start | bytes 1572868
  10.4 3.8 %copy-start.10 = (f32[1,2048]{1,0:T(1,128)S(1)}, f32[1,2048]{1,0:T(1,128)}, u32[]{:S(2)}) copy-start(f32[1,2048]{1,0:T(1,128)} %param.20) | copy-start | bytes 24580
  10.4 3.8 %copy-start.11 = (f32[1,16]{1,0:T(1,128)S(1)}, f32[1,16]{1,0:T(1,128)}, u32[]{:S(2)}) copy-start(f32[1,16]{1,0:T(1,128)} %param.23) | copy-start | bytes 196
  18.1 8.4 %copy-start.1 = (f32[1,16,64,64]{3,2,1,0:T(8,128)S(1)}, f32[1,16,64,64]{3,2,1,0:T(8,128)}, u32[]{:S(2)}) copy-start(f32[1,16,64,64]{3,2,1,0:T(8,128)} %param.24) | copy-start | bytes 786436
  28.1 16.7 %collective-permute-start = (f32[16,64,64]{2,1,0:T(8,128)}, f32[16,64,64]{2,1,0:T(8,128)S(1)}, u32[]{:S(2)}, u32[]{:S(2)}) collective-permute-start(f32[16,64,64]{2,1,0:T(8,128)} %convolution_add_fusion.8), channel_id=1, source_target_pairs={{0,2},{2,4},{4,6},{6,8},{8,10},{10,12},{12,14},{1,3},{3,5},{5,7},{... | collective-permute-start | bytes 786440 | tf_op jit(solution)/shard_map/while/body/eval_jaxpr/ppermute | solution.py:13
  44.7 0.8 copy-start.2
  48.1 15.8 %collective-permute-start = (f32[16,64,64]{2,1,0:T(8,128)}, f32[16,64,64]{2,1,0:T(8,128)S(1)}, u32[]{:S(2)}, u32[]{:S(2)}) collective-permute-start(f32[16,64,64]{2,1,0:T(8,128)} %convolution_add_fusion.8), channel_id=1, source_target_pairs={{0,2},{2,4},{4,6},{6,8},{8,10},{10,12},{12,14},{1,3},{3,5},{5,7},{... | collective-permute-start | bytes 786440 | tf_op jit(solution)/shard_map/while/body/eval_jaxpr/ppermute | solution.py:13
  63.8 0.8 copy-start.2
  67.2 14.9 %collective-permute-start = (f32[16,64,64]{2,1,0:T(8,128)}, f32[16,64,64]{2,1,0:T(8,128)S(1)}, u32[]{:S(2)}, u32[]{:S(2)}) collective-permute-start(f32[16,64,64]{2,1,0:T(8,128)} %convolution_add_fusion.8), channel_id=1, source_target_pairs={{0,2},{2,4},{4,6},{6,8},{8,10},{10,12},{12,14},{1,3},{3,5},{5,7},{... | collective-permute-start | bytes 786440 | tf_op jit(solution)/shard_map/while/body/eval_jaxpr/ppermute | solution.py:13
  82.1 0.8 copy-start.2
  85.4 13.9 %collective-permute-start = (f32[16,64,64]{2,1,0:T(8,128)}, f32[16,64,64]{2,1,0:T(8,128)S(1)}, u32[]{:S(2)}, u32[]{:S(2)}) collective-permute-start(f32[16,64,64]{2,1,0:T(8,128)} %convolution_add_fusion.8), channel_id=1, source_target_pairs={{0,2},{2,4},{4,6},{6,8},{8,10},{10,12},{12,14},{1,3},{3,5},{5,7},{... | collective-permute-start | bytes 786440 | tf_op jit(solution)/shard_map/while/body/eval_jaxpr/ppermute | solution.py:13
  99.4 0.8 copy-start.2
  102.7 13.0 %collective-permute-start = (f32[16,64,64]{2,1,0:T(8,128)}, f32[16,64,64]{2,1,0:T(8,128)S(1)}, u32[]{:S(2)}, u32[]{:S(2)}) collective-permute-start(f32[16,64,64]{2,1,0:T(8,128)} %convolution_add_fusion.8), channel_id=1, source_target_pairs={{0,2},{2,4},{4,6},{6,8},{8,10},{10,12},{12,14},{1,3},{3,5},{5,7},{... | collective-permute-start | bytes 786440 | tf_op jit(solution)/shard_map/while/body/eval_jaxpr/ppermute | solution.py:13
  115.7 0.8 copy-start.2
  119.1 12.2 %collective-permute-start = (f32[16,64,64]{2,1,0:T(8,128)}, f32[16,64,64]{2,1,0:T(8,128)S(1)}, u32[]{:S(2)}, u32[]{:S(2)}) collective-permute-start(f32[16,64,64]{2,1,0:T(8,128)} %convolution_add_fusion.8), channel_id=1, source_target_pairs={{0,2},{2,4},{4,6},{6,8},{8,10},{10,12},{12,14},{1,3},{3,5},{5,7},{... | collective-permute-start | bytes 786440 | tf_op jit(solution)/shard_map/while/body/eval_jaxpr/ppermute | solution.py:13
  131.2 0.8 copy-start.2
  134.6 12.2 %collective-permute-start = (f32[16,64,64]{2,1,0:T(8,128)}, f32[16,64,64]{2,1,0:T(8,128)S(1)}, u32[]{:S(2)}, u32[]{:S(2)}) collective-permute-start(f32[16,64,64]{2,1,0:T(8,128)} %convolution_add_fusion.8), channel_id=1, source_target_pairs={{0,2},{2,4},{4,6},{6,8},{8,10},{10,12},{12,14},{1,3},{3,5},{5,7},{... | collective-permute-start | bytes 786440 | tf_op jit(solution)/shard_map/while/body/eval_jaxpr/ppermute | solution.py:13
  146.8 0.8 copy-start.2
  149.6 17.6 %copy-start.6 = (bf16[128,2048]{1,0:T(8,128)(2,1)S(1)}, bf16[128,2048]{1,0:T(8,128)(2,1)}, u32[]{:S(2)}) copy-start(bf16[128,2048]{1,0:T(8,128)(2,1)} %param.19) | copy-start | bytes 1572868
  149.6 5.6 %copy-start.7 = (bf16[2,16,64,64]{3,2,1,0:T(8,128)(2,1)S(1)}, bf16[2,16,64,64]{3,2,1,0:T(8,128)(2,1)}, u32[]{:S(2)}) copy-start(bf16[2,16,64,64]{3,2,1,0:T(8,128)(2,1)} %get-tuple-element.744) | copy-start | bytes 786436 | tf_op jit(solution)/shard_map/while
  155.9 0.8 copy-start.8
  157.5 5.6 %copy-start.7 = (bf16[2,16,64,64]{3,2,1,0:T(8,128)(2,1)S(1)}, bf16[2,16,64,64]{3,2,1,0:T(8,128)(2,1)}, u32[]{:S(2)}) copy-start(bf16[2,16,64,64]{3,2,1,0:T(8,128)(2,1)} %get-tuple-element.744) | copy-start | bytes 786436 | tf_op jit(solution)/shard_map/while
  163.8 0.8 copy-start.8
  170.1 9.5 %copy-start.9 = (bf16[128,2048]{1,0:T(8,128)(2,1)}, bf16[128,2048]{1,0:T(8,128)(2,1)S(1)}, u32[]{:S(2)}) copy-start(bf16[128,2048]{1,0:T(8,128)(2,1)S(1)} %fusion.91) | copy-start | bytes 1572868
  170.1 2.8 collective-permute-start.2
  172.9 10.7 %copy-start.3 = (bf16[128,2048]{1,0:T(8,128)(2,1)}, bf16[128,2048]{1,0:T(8,128)(2,1)S(1)}, u32[]{:S(2)}) copy-start(bf16[128,2048]{1,0:T(8,128)(2,1)S(1)} %collective-permute-done.2) | copy-start | bytes 1572868
  205.0 17.2 %collective-permute-start.1 = (f32[16,64,64]{2,1,0:T(8,128)}, f32[16,64,64]{2,1,0:T(8,128)S(1)}, u32[]{:S(2)}, u32[]{:S(2)}) collective-permute-start(f32[16,64,64]{2,1,0:T(8,128)} %convolution_add_fusion.9), channel_id=1, source_target_pairs={{0,2},{2,4},{4,6},{6,8},{8,10},{10,12},{12,14},{1,3},{3,5},{5,7},{... | collective-permute-start | bytes 786440 | tf_op jit(solution)/shard_map/while/body/eval_jaxpr/ppermute | solution.py:13
  224.7 16.4 %collective-permute-start.1 = (f32[16,64,64]{2,1,0:T(8,128)}, f32[16,64,64]{2,1,0:T(8,128)S(1)}, u32[]{:S(2)}, u32[]{:S(2)}) collective-permute-start(f32[16,64,64]{2,1,0:T(8,128)} %convolution_add_fusion.9), channel_id=1, source_target_pairs={{0,2},{2,4},{4,6},{6,8},{8,10},{10,12},{12,14},{1,3},{3,5},{5,7},{... | collective-permute-start | bytes 786440 | tf_op jit(solution)/shard_map/while/body/eval_jaxpr/ppermute | solution.py:13
  243.7 15.5 %collective-permute-start.1 = (f32[16,64,64]{2,1,0:T(8,128)}, f32[16,64,64]{2,1,0:T(8,128)S(1)}, u32[]{:S(2)}, u32[]{:S(2)}) collective-permute-start(f32[16,64,64]{2,1,0:T(8,128)} %convolution_add_fusion.9), channel_id=1, source_target_pairs={{0,2},{2,4},{4,6},{6,8},{8,10},{10,12},{12,14},{1,3},{3,5},{5,7},{... | collective-permute-start | bytes 786440 | tf_op jit(solution)/shard_map/while/body/eval_jaxpr/ppermute | solution.py:13
  261.7 14.5 %collective-permute-start.1 = (f32[16,64,64]{2,1,0:T(8,128)}, f32[16,64,64]{2,1,0:T(8,128)S(1)}, u32[]{:S(2)}, u32[]{:S(2)}) collective-permute-start(f32[16,64,64]{2,1,0:T(8,128)} %convolution_add_fusion.9), channel_id=1, source_target_pairs={{0,2},{2,4},{4,6},{6,8},{8,10},{10,12},{12,14},{1,3},{3,5},{5,7},{... | collective-permute-start | bytes 786440 | tf_op jit(solution)/shard_map/while/body/eval_jaxpr/ppermute | solution.py:13
  278.8 13.6 %collective-permute-start.1 = (f32[16,64,64]{2,1,0:T(8,128)}, f32[16,64,64]{2,1,0:T(8,128)S(1)}, u32[]{:S(2)}, u32[]{:S(2)}) collective-permute-start(f32[16,64,64]{2,1,0:T(8,128)} %convolution_add_fusion.9), channel_id=1, source_target_pairs={{0,2},{2,4},{4,6},{6,8},{8,10},{10,12},{12,14},{1,3},{3,5},{5,7},{... | collective-permute-start | bytes 786440 | tf_op jit(solution)/shard_map/while/body/eval_jaxpr/ppermute | solution.py:13
  295.0 12.7 %collective-permute-start.1 = (f32[16,64,64]{2,1,0:T(8,128)}, f32[16,64,64]{2,1,0:T(8,128)S(1)}, u32[]{:S(2)}, u32[]{:S(2)}) collective-permute-start(f32[16,64,64]{2,1,0:T(8,128)} %convolution_add_fusion.9), channel_id=1, source_target_pairs={{0,2},{2,4},{4,6},{6,8},{8,10},{10,12},{12,14},{1,3},{3,5},{5,7},{... | collective-permute-start | bytes 786440 | tf_op jit(solution)/shard_map/while/body/eval_jaxpr/ppermute | solution.py:13
  310.3 12.2 %collective-permute-start.1 = (f32[16,64,64]{2,1,0:T(8,128)}, f32[16,64,64]{2,1,0:T(8,128)S(1)}, u32[]{:S(2)}, u32[]{:S(2)}) collective-permute-start(f32[16,64,64]{2,1,0:T(8,128)} %convolution_add_fusion.9), channel_id=1, source_target_pairs={{0,2},{2,4},{4,6},{6,8},{8,10},{10,12},{12,14},{1,3},{3,5},{5,7},{... | collective-permute-start | bytes 786440 | tf_op jit(solution)/shard_map/while/body/eval_jaxpr/ppermute | solution.py:13
  322.6 14.9 %copy-start.4 = (bf16[128,2048]{1,0:T(8,128)(2,1)S(1)}, bf16[128,2048]{1,0:T(8,128)(2,1)}, u32[]{:S(2)}) copy-start(bf16[128,2048]{1,0:T(8,128)(2,1)} %copy-done.3) | copy-start | bytes 1572868
where the time goes:
time: 344 us; the launch traced here: 341 us
  waiting for transfers between devices  173 us (50%)
  matrix products  94.9 us (28%)
  starting transfers between devices  30.3 us (9%)
  local copies, waits for them, and re-layouts  23.3 us (7%)
  other arithmetic  18.5 us (5%)
    ppermute x15, waiting for transfers between devices, from_behind(): lax.ppermute(value, axis, [(source, source + steps) for source in range(i...  173 us
    dot_general x18, matrix products, apply_map(): jnp.einsum('hde,hef->hdf', linear_output, weight_state, precision=lax.Pre...  31.2 us
    ppermute x15, starting transfers between devices, from_behind(): lax.ppermute(value, axis, [(source, source + steps) for source in range(i...  30.3 us
    dot_general x2, matrix products, inner_inputs(): projected = jnp.dot(normed, w_qkv, preferred_element_type=jnp.float32)  13.2 us
    dot_general x4, matrix products, inner_block(): jnp.einsum('ylc,yci->yli', key_input, weight_state, precision=precise_mode)  8.61 us
    dot_general x4, matrix products, block_map(): jnp.einsum('ncz,ncp->nzp', weighted_values, value_input, precision=precis...  8.39 us
    select_n x14, other arithmetic, relay(): return jnp.where(seq_index == 0, init_state, received)  8.1 us
    while x26, local copies, waits for them, and re-layouts  7.3 us
  transfers between devices with their start and end apart: 15, of which 15 were waited for; matrix products, arithmetic and copies ran while one was open for 0% of the time, Pallas kernels for 0%

commit v1 on v0

v1 whole, which is shorter than its diff:
```python
import functools

import jax
import jax.numpy as jnp
from jax import lax
from jax.experimental import pallas as pl
from jax.experimental.pallas import tpu as pltpu
from jax.sharding import PartitionSpec as P

HD = 64
PAIR = 2 * HD
QUAD = 4 * HD
F32 = jnp.float32
BF16 = jnp.bfloat16
EPS = 1e-6
VMEM_LIMIT = 28 * 1024 * 1024


def mm(a, b):
    return jnp.dot(a, b, preferred_element_type=F32)


def mm_nt(a, b):
    return lax.dot_general(a, b, (((1,), (1,)), ((), ())), preferred_element_type=F32)


def mm_tn(a, b):
    return lax.dot_general(a, b, (((0,), (0,)), ((), ())), preferred_element_type=F32)


def head_masks(rows, lanes):
    lane = lax.broadcasted_iota(jnp.int32, (rows, lanes), 1)
    return [lane // HD == index for index in range(lanes // HD)]


def spread(value):
    zero = jnp.zeros_like(value)
    masks = head_masks(*value.shape)
    return jnp.concatenate([jnp.where(mask, value, zero) for mask in masks], axis=0)


def spread_two(left, right):
    return jnp.concatenate([spread(left), spread(right)], axis=1)


def diagonal(product):
    first = lax.broadcasted_iota(jnp.int32, (HD, PAIR), 1) < HD
    return jnp.where(first, product[:HD], product[HD:])


def head_ones():
    row = lax.broadcasted_iota(jnp.int32, (QUAD, QUAD), 0) // HD
    lane = lax.broadcasted_iota(jnp.int32, (QUAD, QUAD), 1) // HD
    return jnp.where(row == lane, 1.0, 0.0).astype(BF16)


def unit_heads(value, ones):
    squares = mm((value * value).astype(BF16), ones)
    return value * lax.rsqrt(squares + EPS)


def norm_rows(hidden, gain):
    wide = hidden.astype(F32)
    mean_sq = jnp.mean(wide * wide, axis=-1, keepdims=True)
    return (wide * lax.rsqrt(mean_sq + EPS) * gain).astype(BF16)


def spread_rates(normed, w_rate, rate_base):
    rates = rate_base * jax.nn.sigmoid(mm(normed, w_rate))
    high = rates.astype(BF16)
    low = (rates - high.astype(F32)).astype(BF16)
    heads = rates.shape[1]
    row = lax.broadcasted_iota(jnp.int32, (heads, heads * HD), 0)
    lane = lax.broadcasted_iota(jnp.int32, (heads, heads * HD), 1) // HD
    pick = jnp.where(row == lane, 1.0, 0.0).astype(BF16)
    return mm(high, pick) + mm(low, pick)


def slab_maps(normed, rates, wkv, wait_group, keys_out, x_out, y_out, maps, lw):
    width = keys_out.shape[1]
    ones = head_ones()
    per_pair = PAIR // lw
    for quad in range(width // QUAD):
        wait_group(quad)
        lanes = slice(quad * QUAD, (quad + 1) * QUAD)
        keys = mm(normed, wkv[:, lanes])
        values = mm(normed, wkv[:, width + quad * QUAD : width + (quad + 1) * QUAD])
        keys = unit_heads(keys, ones)
        keys_bf = keys.astype(BF16)
        rate = rates[:, lanes]
        rated_keys = rate * keys
        rated_values = rate * values
        keys_out[:, lanes] = keys_bf
        for half in range(2):
            pair = quad * 2 + half
            own = slice(half * PAIR, (half + 1) * PAIR)
            first, second = keys_bf[:HD, own], keys_bf[HD:, own]
            x_first = rated_keys[:HD, own]
            y_first = rated_values[:HD, own]
            cross = mm_nt(second, spread(first)).astype(BF16)
            fix = mm(cross, spread_two(x_first.astype(BF16), y_first.astype(BF16)))
            x_second = rated_keys[HD:, own] - rate[HD:, own] * fix[:, :PAIR]
            y_second = rated_values[HD:, own] - rate[HD:, own] * fix[:, PAIR:]
            x_all = jnp.concatenate([x_first, x_second], axis=0).astype(BF16)
            y_all = jnp.concatenate([y_first, y_second], axis=0).astype(BF16)
            place = slice(pair * PAIR, (pair + 1) * PAIR)
            x_out[:, place] = x_all
            y_out[:, place] = y_all
            both = mm_tn(keys_bf[:, own], jnp.concatenate([x_all, y_all], axis=1))
            s_map = diagonal(both[:, :PAIR])
            b_map = diagonal(both[:, PAIR:])
            for part in range(per_pair):
                cut = slice(part * lw, (part + 1) * lw)
                maps[pair * per_pair + part] = jnp.concatenate([s_map[:, cut], b_map[:, cut]], axis=1).astype(BF16)


def place_out(refs, table, count):
    me = lax.axis_index("seq")
    for step, ref in enumerate(refs):
        ref[...] = table[lax.rem(me + step, count)]


def place_in(refs, table, count):
    me = lax.axis_index("seq")
    for step, ref in enumerate(refs):
        table[lax.rem(me + count - step, count)] = ref[...]


def first_front(count, lw, h_ref, gain_ref, w_hbm, w_rate_ref, base_ref, *rest):
    outs = rest[:count]
    wkv, normed_out, keys_out, x_out, y_out, maps, sems = rest[count:]
    width = keys_out.shape[1]
    quads = width // QUAD

    def copies(quad):
        made = []
        for side in range(2):
            made.append(
                pltpu.make_async_copy(
                    w_hbm.at[0, :, pl.ds((side + 1) * width + quad * QUAD, QUAD)],
                    wkv.at[:, pl.ds(side * width + quad * QUAD, QUAD)],
                    sems.at[quad, side],
                )
            )
        return made

    for quad in range(quads):
        for copy in copies(quad):
            copy.start()

    def wait_group(quad):
        for copy in copies(quad):
            copy.wait()

    @pl.when(lax.axis_index("section") == 0)
    def _():
        normed = norm_rows(h_ref[...], gain_ref[...])
        normed_out[...] = normed
        rates = spread_rates(normed, w_rate_ref[0], base_ref[...])
        slab_maps(normed, rates, wkv, wait_group, keys_out, x_out, y_out, maps, lw)
        place_out(outs, maps, count)

    @pl.when(lax.axis_index("section") != 0)
    def _():
        for quad in range(quads):
            wait_group(quad)


def read_out(normed, wq, wait_group, keys_ref, x_ref, y_ref, qo_out):
    rows, width = keys_ref.shape
    ones = head_ones()
    row = lax.broadcasted_iota(jnp.int32, (rows, 2 * rows), 0)
    lane = lax.rem(lax.broadcasted_iota(jnp.int32, (rows, 2 * rows), 1), rows)
    causal = row >= lane
    for quad in range(width // QUAD):
        wait_group(quad)
        queries = unit_heads(mm(normed, wq[:, quad * QUAD : (quad + 1) * QUAD]), ones)
        queries_bf = queries.astype(BF16)
        for half in range(2):
            own = slice(half * PAIR, (half + 1) * PAIR)
            place = slice(quad * QUAD + half * PAIR, quad * QUAD + (half + 1) * PAIR)
            scores = mm_nt(queries_bf[:, own], spread(keys_ref[:, place]))
            scores = jnp.where(causal, scores, 0.0).astype(BF16)
            both = mm(scores, spread_two(x_ref[:, place], y_ref[:, place]))
            qo_out[:, place] = (queries[:, own] - both[:, :PAIR]).astype(BF16)
            qo_out[:, width + place.start : width + place.stop] = both[:, PAIR:].astype(BF16)


def first_reads(normed_ref, keys_ref, x_ref, y_ref, w_hbm, qo_out, wq, sems):
    width = keys_ref.shape[1]
    quads = width // QUAD

    def copy(quad):
        return pltpu.make_async_copy(
            w_hbm.at[0, :, pl.ds(quad * QUAD, QUAD)], wq.at[:, pl.ds(quad * QUAD, QUAD)], sems.at[quad]
        )

    for quad in range(quads):
        copy(quad).start()

    @pl.when(lax.axis_index("section") == 0)
    def _():
        read_out(normed_ref[...], wq, lambda quad: copy(quad).wait(), keys_ref, x_ref, y_ref, qo_out)

    @pl.when(lax.axis_index("section") != 0)
    def _():
        for quad in range(quads):
            copy(quad).wait()


def later_reads(normed_ref, keys_ref, x_ref, y_ref, wq, qo_out):
    @pl.when(lax.axis_index("section") == 1)
    def _():
        read_out(normed_ref[...], wq, lambda quad: None, keys_ref, x_ref, y_ref, qo_out)


def relay(count, lw, active, *refs):
    pieces = refs[:count]
    init_ref = refs[count]
    outs = refs[count + 1 : 2 * count + 1]
    table, states = refs[2 * count + 1 :]

    @pl.when(lax.axis_index("section") == active)
    def _():
        place_in(pieces, table, count)
        heads = lw // HD
        me = lax.axis_index("seq")
        state = jnp.concatenate([init_ref[0, me * heads + index] for index in range(heads)], axis=1)
        states[0] = state.astype(BF16)
        for slab in range(count - 1):
            step = table[slab]
            state = state - mm(step[:, :lw], spread(state.astype(BF16))) + step[:, lw:].astype(F32)
            states[slab + 1] = state.astype(BF16)
        place_out(outs, states, count)


def finish(pieces, table, qo_ref, w_out, h_ref, count, lw):
    place_in(pieces, table, count)
    width = qo_ref.shape[1] // 2
    per_quad = QUAD // lw
    parts = []
    for quad in range(width // QUAD):
        lanes = slice(quad * QUAD, (quad + 1) * QUAD)
        state = jnp.concatenate([table[quad * per_quad + index] for index in range(per_quad)], axis=1)
        inner = mm(qo_ref[:, lanes], spread(state)) + qo_ref[:, width + quad * QUAD : width + (quad + 1) * QUAD].astype(F32)
        parts.append(inner.astype(BF16))
    inner_bf = jnp.concatenate(parts, axis=1)
    return (h_ref[...].astype(F32) + mm(inner_bf, w_out)).astype(BF16)


def later_front(count, lw, *refs):
    pieces = refs[:count]
    qo_ref, w_out_ref, h_ref, gain_ref, wkv, w_rate_ref, base_ref = refs[count : count + 7]
    outs = refs[count + 7 : 2 * count + 7]
    h_out, normed_out, keys_out, x_out, y_out, table, maps = refs[2 * count + 7 :]

    @pl.when(lax.axis_index("section") == 1)
    def _():
        result = finish(pieces, table, qo_ref, w_out_ref[...], h_ref, count, lw)
        h_out[...] = result
        normed = norm_rows(result, gain_ref[...])
        normed_out[...] = normed
        rates = spread_rates(normed, w_rate_ref[0], base_ref[...])
        slab_maps(normed, rates, wkv, lambda quad: None, keys_out, x_out, y_out, maps, lw)
        place_out(outs, maps, count)


def last_finish(count, lw, *refs):
    pieces = refs[:count]
    qo_ref, w_out_ref, h_ref, back_ref, out_ref, table = refs[count:]

    @pl.when(lax.axis_index("section") == 1)
    def _():
        out_ref[0] = finish(pieces, table, qo_ref, w_out_ref[0], h_ref, count, lw)

    @pl.when(lax.axis_index("section") == 0)
    def _():
        out_ref[0] = back_ref[...]


def call(body, outs, scratch, args, kinds=None, name=None):
    specs = [pl.BlockSpec(memory_space=kind) for kind in (kinds or [pltpu.VMEM] * len(args))]
    return pl.pallas_call(
        body,
        out_shape=outs,
        in_specs=specs,
        out_specs=[pl.BlockSpec(memory_space=pltpu.VMEM)] * len(outs),
        scratch_shapes=scratch,
        compiler_params=pltpu.CompilerParams(vmem_limit_bytes=VMEM_LIMIT),
        name=name,
    )(*args)


def exchange(pieces, source, target, count):
    received = []
    for step, piece in enumerate(pieces):
        if step == 0 and source == target:
            received.append(piece)
            continue
        pairs = [(source * count + place, target * count + (place + step) % count) for place in range(count)]
        received.append(lax.ppermute(piece, ("section", "seq"), pairs))
    return received


def shards(tokens, norm_gain, w_qkv, w_rate, rate_base, init_state, w_out):
    count = lax.axis_size("seq")
    heads = rate_base.shape[1]
    lw = heads // count * HD
    rows, model = tokens.shape
    width = heads * HD
    depth = w_qkv.shape[1]
    quads = width // QUAD
    shape = jax.ShapeDtypeStruct
    in_vmem = functools.partial(pltpu.with_memory_space_constraint, memory_space=pltpu.VMEM)
    pieces_out = [shape((HD, 2 * lw), BF16)] * count
    states_out = [shape((HD, lw), BF16)] * count
    rows_out = [shape((rows, model), BF16)] + [shape((rows, width), BF16)] * 3
    maps = pltpu.VMEM((count, HD, 2 * lw), BF16)
    states = pltpu.VMEM((count, HD, lw), BF16)

    w_out_first = lax.ppermute(w_out[0], "section", [(0, 1)])

    done = call(
        functools.partial(first_front, count, lw),
        pieces_out + [pltpu.VMEM((depth, 2 * width), BF16)] + rows_out,
        [maps, pltpu.SemaphoreType.DMA((quads, 2))],
        [tokens, norm_gain, w_qkv, w_rate, rate_base],
        [pltpu.VMEM, pltpu.VMEM, pl.ANY, pltpu.VMEM, pltpu.VMEM],
        name="first_front",
    )
    pieces, (wkv, normed, keys, x_all, y_all) = done[:count], done[count:]
    received = exchange(pieces, 0, 0, count)
    reads, wq = call(
        first_reads,
        [shape((rows, 2 * width), BF16), pltpu.VMEM((depth, width), BF16)],
        [pltpu.SemaphoreType.DMA((quads,))],
        [normed, keys, x_all, y_all, w_qkv],
        [pltpu.VMEM] * 4 + [pl.ANY],
        name="first_reads",
    )
    reads = lax.ppermute(reads, "section", [(0, 1)])
    begun = call(functools.partial(relay, count, lw, 0), states_out, [maps, states], received + [init_state], name="relay0")
    received = exchange(begun, 0, 1, count)

    done = call(
        functools.partial(later_front, count, lw),
        pieces_out + [shape((rows, model), BF16)] + rows_out,
        [states, maps],
        received + [reads, w_out_first, tokens, norm_gain, in_vmem(wkv), w_rate, rate_base],
        name="later_front",
    )
    pieces, (hidden, normed, keys, x_all, y_all) = done[:count], done[count:]
    received = exchange(pieces, 1, 1, count)
    back = lax.ppermute(hidden, "section", [(1, 0)])
    (reads,) = call(
        later_reads,
        [shape((rows, 2 * width), BF16)],
        [],
        [normed, keys, x_all, y_all, in_vmem(wq)],
        name="later_reads",
    )
    begun = call(functools.partial(relay, count, lw, 1), states_out, [maps, states], received + [init_state], name="relay1")
    received = exchange(begun, 1, 1, count)
    (result,) = call(
        functools.partial(last_finish, count, lw),
        [shape((1, rows, model), BF16)],
        [states],
        received + [reads, w_out, hidden, back],
        name="last_finish",
    )
    return result


def solution(mesh):
    return jax.shard_map(
        shards,
        mesh=mesh,
        in_specs=(
            P(("traj", "seq"), None),
            P("section", None),
            P("section", None, None),
            P("section", None, None),
            P("section", None),
            P("section", None, None, None),
            P("section", None, None),
        ),
        out_specs=P("section", ("traj", "seq"), None),
        check_vma=False,
    )
```

time: 344 us -> 140 us (0.41)
  the two profiles are of different devices: /device:TPU:8 before, /device:TPU:1 now
where the time goes in v1:
time: 140 us; the launch traced here: 139 us
  starting transfers between devices  64.3 us (46%)
  waiting for transfers between devices  44.2 us (32%)
  Pallas kernels  15.3 us (11%)
  local copies, waits for them, and re-layouts  14.5 us (10%)
    ppermute x29, starting transfers between devices, exchange(): received.append(lax.ppermute(piece, ('section', 'seq'), pairs))  59.9 us
    ppermute x29, waiting for transfers between devices, exchange(): received.append(lax.ppermute(piece, ('section', 'seq'), pairs))  44.2 us
    pallas_call x7, Pallas kernels, call(): pl.pallas_call(body, out_shape=outs, in_specs=specs, out_specs=[pl.BlockS...  15.3 us
    unnamed x23, local copies, waits for them, and re-layouts  14.5 us
  transfers between devices with their start and end apart: 32, of which 6 were waited for; matrix products, arithmetic and copies ran while one was open for 1% of the time, Pallas kernels for 4%

profile of v1, /device:TPU:1, one launch (start us, length us, event | category | flops | bytes accessed | tf_op | source)
XLA Modules:
  0.0 138.8 jit_solution(1572511356111192081)
XLA Ops:
  0.0 1.3 collective-permute-start.16
  1.3 1.1 copy.8.w_rate_ref.refs_13_
  2.4 4.6 %copy-done = bf16[1,2048,3072]{2,1,0:T(8,128)(2,1)S(1)} copy-done((bf16[1,2048,3072]{2,1,0:T(8,128)(2,1)S(1)}, bf16[1,2048,3072]{2,1,0:T(8,128)(2,1)}, u32[]{:S(2)}) %copy-start) | copy-done | bytes 12582936
  7.0 1.0 copy-done.6
  8.0 0.7 copy-done.8
  9.4 1.2 first_front.1
  10.6 4.2 %copy-done.2 = bf16[2048,2048]{1,0:T(8,128)(2,1)} copy-done((bf16[2048,2048]{1,0:T(8,128)(2,1)}, bf16[2048,2048]{1,0:T(8,128)(2,1)S(1)}, u32[]{:S(2)}) %copy-start.2) | copy-done | bytes 8388632
  14.8 2.2 %copy-done.1 = bf16[1,2048,3072]{2,1,0:T(8,128)(2,1)S(1)} copy-done((bf16[1,2048,3072]{2,1,0:T(8,128)(2,1)S(1)}, bf16[1,2048,3072]{2,1,0:T(8,128)(2,1)}, u32[]{:S(2)}) %copy-start.1) | copy-done | bytes 12582936
  17.6 1.6 %collective-permute-start.15 = (bf16[128,2048]{1,0:T(8,128)(2,1)S(1)}, bf16[128,2048]{1,0:T(8,128)(2,1)S(1)}, u32[]{:S(2)}, u32[]{:S(2)}) collective-permute-start(bf16[128,2048]{1,0:T(8,128)(2,1)S(1)} %get-tuple-element.69), channel_id=1, source_target_pairs={{0,16},{1,17},{2,18},{3,19},{4,20},{5,21},{6,22},{7,23},{8,24},{9,... | collective-permute-start | bytes 1572872 | tf_op jit(solution)/shard_map/ppermute | solution.py:341
  19.2 0.8 collective-permute-start
  20.0 0.7 collective-permute-start.1
  20.7 0.7 collective-permute-start.2
  21.3 0.7 collective-permute-start.3
  22.0 0.7 collective-permute-start.4
  22.7 0.7 collective-permute-start.5
  23.4 0.7 collective-permute-start.6
  24.1 1.3 collective-permute-start.7
  25.4 1.3 collective-permute-start.8
  26.7 1.3 collective-permute-start.9
  28.0 32.3 %collective-permute-done.7.refs_0_ = bf16[64,128]{1,0:T(8,128)(2,1)S(1)} collective-permute-done((bf16[64,128]{1,0:T(8,128)(2,1)S(1)}, bf16[64,128]{1,0:T(8,128)(2,1)S(1)}, u32[]{:S(2)}, u32[]{:S(2)}) %collective-permute-start.7) | collective-permute-done | bytes 16416 | tf_op jit(solution)/shard_map/ppermute | solution.py:301
  60.3 1.3 collective-permute-start.10
  61.6 4.5 %collective-permute-done.8.refs_1_ = bf16[64,128]{1,0:T(8,128)(2,1)S(1)} collective-permute-done((bf16[64,128]{1,0:T(8,128)(2,1)S(1)}, bf16[64,128]{1,0:T(8,128)(2,1)S(1)}, u32[]{:S(2)}, u32[]{:S(2)}) %collective-permute-start.8) | collective-permute-done | bytes 16416 | tf_op jit(solution)/shard_map/ppermute | solution.py:301
  66.1 1.3 collective-permute-start.11
  67.4 1.3 collective-permute-start.12
  68.7 1.3 collective-permute-start.13
  70.0 2.0 %collective-permute-done.11.refs_4_ = bf16[64,128]{1,0:T(8,128)(2,1)S(1)} collective-permute-done((bf16[64,128]{1,0:T(8,128)(2,1)S(1)}, bf16[64,128]{1,0:T(8,128)(2,1)S(1)}, u32[]{:S(2)}, u32[]{:S(2)}) %collective-permute-start.11) | collective-permute-done | bytes 16416 | tf_op jit(solution)/shard_map/ppermute | solution.py:301
  72.0 1.3 collective-permute-start.14
  73.8 3.3 %collective-permute-done.14.refs_7_ = bf16[64,128]{1,0:T(8,128)(2,1)S(1)} collective-permute-done((bf16[64,128]{1,0:T(8,128)(2,1)S(1)}, bf16[64,128]{1,0:T(8,128)(2,1)S(1)}, u32[]{:S(2)}, u32[]{:S(2)}) %collective-permute-start.14) | collective-permute-done | bytes 16416 | tf_op jit(solution)/shard_map/ppermute | solution.py:301
  77.1 7.4 %later_front.1 = (bf16[64,256]{1,0:T(8,128)(2,1)S(1)}, bf16[64,256]{1,0:T(8,128)(2,1)S(1)}, bf16[64,256]{1,0:T(8,128)(2,1)S(1)}, bf16[64,256]{1,0:T(8,128)(2,1)S...) custom-call(bf16[64,128]{1,0:T(8,128)(2,1)S(1)} %collective-permute-, ...), custom_call_target="tpu_custom_call" | custom-call | tf_op jit(solution)/shard_map/later_front/pallas_call | solution.py:283
  84.5 1.6 %collective-permute-start.31 = (bf16[128,2048]{1,0:T(8,128)(2,1)S(1)}, bf16[128,2048]{1,0:T(8,128)(2,1)S(1)}, u32[]{:S(2)}, u32[]{:S(2)}) collective-permute-start(bf16[128,2048]{1,0:T(8,128)(2,1)S(1)} %get-tuple-element.92.refs_10_), channel_id=1, source_target_pairs={{16,0},{17,1},{18,2},{19,3},{20,4},{21,5},{22,6},{23,7},{24,8},{25... | collective-permute-start | bytes 1572872 | tf_op jit(solution)/shard_map/ppermute | solution.py:354
  86.1 2.1 %collective-permute-start.17 = (bf16[64,256]{1,0:T(8,128)(2,1)S(1)}, bf16[64,256]{1,0:T(8,128)(2,1)S(1)}, u32[]{:S(2)}, u32[]{:S(2)}) collective-permute-start(bf16[64,256]{1,0:T(8,128)(2,1)S(1)} %get-tuple-element.72), channel_id=1, source_target_pairs={{16,18},{18,20},{20,22},{22,24},{24,26},{26,28},{28,30},{30,16},{1... | collective-permute-start | bytes 98312 | tf_op jit(solution)/shard_map/ppermute | solution.py:301
  88.2 2.1 %collective-permute-start.18 = (bf16[64,256]{1,0:T(8,128)(2,1)S(1)}, bf16[64,256]{1,0:T(8,128)(2,1)S(1)}, u32[]{:S(2)}, u32[]{:S(2)}) collective-permute-start(bf16[64,256]{1,0:T(8,128)(2,1)S(1)} %get-tuple-element.73), channel_id=1, source_target_pairs={{16,20},{18,22},{20,24},{22,26},{24,28},{26,30},{28,16},{30,18},{1... | collective-permute-start | bytes 98312 | tf_op jit(solution)/shard_map/ppermute | solution.py:301
  90.3 1.9 %collective-permute-start.19 = (bf16[64,256]{1,0:T(8,128)(2,1)S(1)}, bf16[64,256]{1,0:T(8,128)(2,1)S(1)}, u32[]{:S(2)}, u32[]{:S(2)}) collective-permute-start(bf16[64,256]{1,0:T(8,128)(2,1)S(1)} %get-tuple-element.74), channel_id=1, source_target_pairs={{16,22},{18,24},{20,26},{22,28},{24,30},{26,16},{28,18},{30,20},{1... | collective-permute-start | bytes 98312 | tf_op jit(solution)/shard_map/ppermute | solution.py:301
  92.2 6.0 %collective-permute-start.20 = (bf16[64,256]{1,0:T(8,128)(2,1)S(1)}, bf16[64,256]{1,0:T(8,128)(2,1)S(1)}, u32[]{:S(2)}, u32[]{:S(2)}) collective-permute-start(bf16[64,256]{1,0:T(8,128)(2,1)S(1)} %get-tuple-element.75), channel_id=1, source_target_pairs={{16,24},{18,26},{20,28},{22,30},{24,16},{26,18},{28,20},{30,22},{1... | collective-permute-start | bytes 98312 | tf_op jit(solution)/shard_map/ppermute | solution.py:301
  98.3 3.4 %collective-permute-start.21 = (bf16[64,256]{1,0:T(8,128)(2,1)S(1)}, bf16[64,256]{1,0:T(8,128)(2,1)S(1)}, u32[]{:S(2)}, u32[]{:S(2)}) collective-permute-start(bf16[64,256]{1,0:T(8,128)(2,1)S(1)} %get-tuple-element.76), channel_id=1, source_target_pairs={{16,26},{18,28},{20,30},{22,16},{24,18},{26,20},{28,22},{30,24},{1... | collective-permute-start | bytes 98312 | tf_op jit(solution)/shard_map/ppermute | solution.py:301
  101.6 2.8 %collective-permute-start.22 = (bf16[64,256]{1,0:T(8,128)(2,1)S(1)}, bf16[64,256]{1,0:T(8,128)(2,1)S(1)}, u32[]{:S(2)}, u32[]{:S(2)}) collective-permute-start(bf16[64,256]{1,0:T(8,128)(2,1)S(1)} %get-tuple-element.77), channel_id=1, source_target_pairs={{16,28},{18,30},{20,16},{22,18},{24,20},{26,22},{28,24},{30,26},{1... | collective-permute-start | bytes 98312 | tf_op jit(solution)/shard_map/ppermute | solution.py:301
  104.5 3.1 %collective-permute-start.23 = (bf16[64,256]{1,0:T(8,128)(2,1)S(1)}, bf16[64,256]{1,0:T(8,128)(2,1)S(1)}, u32[]{:S(2)}, u32[]{:S(2)}) collective-permute-start(bf16[64,256]{1,0:T(8,128)(2,1)S(1)} %get-tuple-element.78), channel_id=1, source_target_pairs={{16,30},{18,16},{20,18},{22,20},{24,22},{26,24},{28,26},{30,28},{1... | collective-permute-start | bytes 98312 | tf_op jit(solution)/shard_map/ppermute | solution.py:301
  107.6 1.5 %collective-permute-done.23.refs_7_ = bf16[64,256]{1,0:T(8,128)(2,1)S(1)} collective-permute-done((bf16[64,256]{1,0:T(8,128)(2,1)S(1)}, bf16[64,256]{1,0:T(8,128)(2,1)S(1)}, u32[]{:S(2)}, u32[]{:S(2)}) %collective-permute-start.23) | collective-permute-done | bytes 32800 | tf_op jit(solution)/shard_map/ppermute | solution.py:301
  109.1 1.0 relay1.1
  110.2 4.0 %collective-permute-start.24 = (bf16[64,128]{1,0:T(8,128)(2,1)S(1)}, bf16[64,128]{1,0:T(8,128)(2,1)S(1)}, u32[]{:S(2)}, u32[]{:S(2)}) collective-permute-start(bf16[64,128]{1,0:T(8,128)(2,1)S(1)} %get-tuple-element.80), channel_id=1, source_target_pairs={{16,18},{18,20},{20,22},{22,24},{24,26},{26,28},{28,30},{30,16},{1... | collective-permute-start | bytes 49160 | tf_op jit(solution)/shard_map/ppermute | solution.py:301
  114.2 3.4 %collective-permute-start.25 = (bf16[64,128]{1,0:T(8,128)(2,1)S(1)}, bf16[64,128]{1,0:T(8,128)(2,1)S(1)}, u32[]{:S(2)}, u32[]{:S(2)}) collective-permute-start(bf16[64,128]{1,0:T(8,128)(2,1)S(1)} %get-tuple-element.81), channel_id=1, source_target_pairs={{16,20},{18,22},{20,24},{22,26},{24,28},{26,30},{28,16},{30,18},{1... | collective-permute-start | bytes 49160 | tf_op jit(solution)/shard_map/ppermute | solution.py:301
  117.5 1.9 %collective-permute-start.26 = (bf16[64,128]{1,0:T(8,128)(2,1)S(1)}, bf16[64,128]{1,0:T(8,128)(2,1)S(1)}, u32[]{:S(2)}, u32[]{:S(2)}) collective-permute-start(bf16[64,128]{1,0:T(8,128)(2,1)S(1)} %get-tuple-element.82), channel_id=1, source_target_pairs={{16,22},{18,24},{20,26},{22,28},{24,30},{26,16},{28,18},{30,20},{1... | collective-permute-start | bytes 49160 | tf_op jit(solution)/shard_map/ppermute | solution.py:301
  119.5 4.0 %collective-permute-start.27 = (bf16[64,128]{1,0:T(8,128)(2,1)S(1)}, bf16[64,128]{1,0:T(8,128)(2,1)S(1)}, u32[]{:S(2)}, u32[]{:S(2)}) collective-permute-start(bf16[64,128]{1,0:T(8,128)(2,1)S(1)} %get-tuple-element.83), channel_id=1, source_target_pairs={{16,24},{18,26},{20,28},{22,30},{24,16},{26,18},{28,20},{30,22},{1... | collective-permute-start | bytes 49160 | tf_op jit(solution)/shard_map/ppermute | solution.py:301
  123.5 4.0 %collective-permute-start.28 = (bf16[64,128]{1,0:T(8,128)(2,1)S(1)}, bf16[64,128]{1,0:T(8,128)(2,1)S(1)}, u32[]{:S(2)}, u32[]{:S(2)}) collective-permute-start(bf16[64,128]{1,0:T(8,128)(2,1)S(1)} %get-tuple-element.84), channel_id=1, source_target_pairs={{16,26},{18,28},{20,30},{22,16},{24,18},{26,20},{28,22},{30,24},{1... | collective-permute-start | bytes 49160 | tf_op jit(solution)/shard_map/ppermute | solution.py:301
  127.5 3.1 %collective-permute-start.29 = (bf16[64,128]{1,0:T(8,128)(2,1)S(1)}, bf16[64,128]{1,0:T(8,128)(2,1)S(1)}, u32[]{:S(2)}, u32[]{:S(2)}) collective-permute-start(bf16[64,128]{1,0:T(8,128)(2,1)S(1)} %get-tuple-element.85), channel_id=1, source_target_pairs={{16,28},{18,30},{20,16},{22,18},{24,20},{26,22},{28,24},{30,26},{1... | collective-permute-start | bytes 49160 | tf_op jit(solution)/shard_map/ppermute | solution.py:301
  130.6 3.1 %collective-permute-start.30 = (bf16[64,128]{1,0:T(8,128)(2,1)S(1)}, bf16[64,128]{1,0:T(8,128)(2,1)S(1)}, u32[]{:S(2)}, u32[]{:S(2)}) collective-permute-start(bf16[64,128]{1,0:T(8,128)(2,1)S(1)} %get-tuple-element.86), channel_id=1, source_target_pairs={{16,30},{18,16},{20,18},{22,20},{24,22},{26,24},{28,26},{30,28},{1... | collective-permute-start | bytes 49160 | tf_op jit(solution)/shard_map/ppermute | solution.py:301
  133.7 3.3 %later_reads.1.refs_8_ = bf16[128,2048]{1,0:T(8,128)(2,1)S(1)} custom-call(bf16[128,2048]{1,0:T(8,128)(2,1)S(1)} %get-tuple-element.87.normed_ref, bf16[128,1024]{1,0:T(8,128)(2,1)S(1)} %get-tuple-element.88.keys_ref, bf16[128,1024]{1,0:T(8,128)(2,1)S(1)} %get-tuple-element.89.x_ref, bf16[128,1024]{1,0:T(8,128)(2,1)S(1)} %get-tuple-element.90.y_ref, ...), custom_call_target="tpu_custom_call" | custom-call | tf_op jit(solution)/shard_map/later_reads/pallas_call | solution.py:283
  137.1 1.7 %last_finish.1 = bf16[1,128,2048]{2,1,0:T(8,128)(2,1)} custom-call(bf16[64,128]{1,0:T(8,128)(2,1)S(1)} %get-tuple-element.79.refs_0_, bf16[64,128]{1,0:T(8,128)(2,1)S(1)} %collective-permute-done.24.refs_1_, bf16[64,128]{1,0:T(8,128)(2,1)S(1)} %collective-permute-done.25.refs_2_, bf16[64,128]{1,0:T(8,128)(2,1)S(1)} %collective-permute-done.26.refs_3_, ...), custom_call_target="tpu_custom_call" | custom-call | tf_op jit(solution)/shard_map/last_finish/pallas_call | solution.py:283
  (46 shorter events, 1.8 us)
Async XLA Ops:
  0.0 77.1 %collective-permute-start.16 = (bf16[1024,2048]{1,0:T(8,128)(2,1)}, bf16[1024,2048]{1,0:T(8,128)(2,1)}, u32[]{:S(2)}, u32[]{:S(2)}) collective-permute-start(bf16[1024,2048]{1,0:T(8,128)(2,1)} %bitcast.1), channel_id=1, source_target_pairs={{0,16},{1,17},{2,18},{3,19},{4,20},{5,21},{6,22},{7,23},{8,24},{9,... | collective-permute-start | bytes 12582920 | tf_op jit(solution)/shard_map/ppermute | solution.py:321
  2.4 4.6 %copy-start = (bf16[1,2048,3072]{2,1,0:T(8,128)(2,1)S(1)}, bf16[1,2048,3072]{2,1,0:T(8,128)(2,1)}, u32[]{:S(2)}) copy-start(bf16[1,2048,3072]{2,1,0:T(8,128)(2,1)} %w_hbm.3) | copy-start | bytes 37748740
  7.0 1.0 copy-start.6
  8.0 0.7 copy-start.8
  8.7 0.7 copy-start.9
  9.4 7.6 %copy-start.1 = (bf16[1,2048,3072]{2,1,0:T(8,128)(2,1)S(1)}, bf16[1,2048,3072]{2,1,0:T(8,128)(2,1)}, u32[]{:S(2)}) copy-start(bf16[1,2048,3072]{2,1,0:T(8,128)(2,1)} %w_hbm.3) | copy-start | bytes 37748740
  10.6 4.3 %copy-start.2 = (bf16[2048,2048]{1,0:T(8,128)(2,1)}, bf16[2048,2048]{1,0:T(8,128)(2,1)S(1)}, u32[]{:S(2)}) copy-start(bf16[2048,2048]{1,0:T(8,128)(2,1)S(1)} %get-tuple-element.70.refs_12_) | copy-start | bytes 25165828
  17.0 7.1 %copy-start.5 = (f32[1,16,64,64]{3,2,1,0:T(8,128)S(1)}, f32[1,16,64,64]{3,2,1,0:T(8,128)}, u32[]{:S(2)}) copy-start(f32[1,16,64,64]{3,2,1,0:T(8,128)} %refs_8_.3) | copy-start | bytes 786436
  17.0 60.1 %copy-start.3 = (bf16[2048,2048]{1,0:T(8,128)(2,1)S(1)}, bf16[2048,2048]{1,0:T(8,128)(2,1)}, u32[]{:S(2)}) copy-start(bf16[2048,2048]{1,0:T(8,128)(2,1)} %copy-done.2) | copy-start | bytes 25165828
  17.0 60.1 %copy-start.7 = (bf16[128,2048]{1,0:T(8,128)(2,1)S(1)}, bf16[128,2048]{1,0:T(8,128)(2,1)}, u32[]{:S(2)}) copy-start(bf16[128,2048]{1,0:T(8,128)(2,1)} %refs_10_.1) | copy-start | bytes 1572868
  17.0 60.1 %copy-start.10 = (f32[1,16]{1,0:T(1,128)S(1)}, f32[1,16]{1,0:T(1,128)}, u32[]{:S(2)}) copy-start(f32[1,16]{1,0:T(1,128)} %refs_14_.1) | copy-start | bytes 196
  17.6 59.5 %collective-permute-start.15 = (bf16[128,2048]{1,0:T(8,128)(2,1)S(1)}, bf16[128,2048]{1,0:T(8,128)(2,1)S(1)}, u32[]{:S(2)}, u32[]{:S(2)}) collective-permute-start(bf16[128,2048]{1,0:T(8,128)(2,1)S(1)} %get-tuple-element.69), channel_id=1, source_target_pairs={{0,16},{1,17},{2,18},{3,19},{4,20},{5,21},{6,22},{7,23},{8,24},{9,... | collective-permute-start | bytes 1572872 | tf_op jit(solution)/shard_map/ppermute | solution.py:341
  19.2 2.1 %collective-permute-start = (bf16[64,256]{1,0:T(8,128)(2,1)S(1)}, bf16[64,256]{1,0:T(8,128)(2,1)S(1)}, u32[]{:S(2)}, u32[]{:S(2)}) collective-permute-start(bf16[64,256]{1,0:T(8,128)(2,1)S(1)} %get-tuple-element.50), channel_id=1, source_target_pairs={{0,2},{2,4},{4,6},{6,8},{8,10},{10,12},{12,14},{14,0},{1,3},{3,5},... | collective-permute-start | bytes 98312 | tf_op jit(solution)/shard_map/ppermute | solution.py:301
  20.0 2.0 %collective-permute-start.1 = (bf16[64,256]{1,0:T(8,128)(2,1)S(1)}, bf16[64,256]{1,0:T(8,128)(2,1)S(1)}, u32[]{:S(2)}, u32[]{:S(2)}) collective-permute-start(bf16[64,256]{1,0:T(8,128)(2,1)S(1)} %get-tuple-element.51), channel_id=1, source_target_pairs={{0,4},{2,6},{4,8},{6,10},{8,12},{10,14},{12,0},{14,2},{1,5},{3,7},... | collective-permute-start | bytes 98312 | tf_op jit(solution)/shard_map/ppermute | solution.py:301
  20.7 2.0 %collective-permute-start.2 = (bf16[64,256]{1,0:T(8,128)(2,1)S(1)}, bf16[64,256]{1,0:T(8,128)(2,1)S(1)}, u32[]{:S(2)}, u32[]{:S(2)}) collective-permute-start(bf16[64,256]{1,0:T(8,128)(2,1)S(1)} %get-tuple-element.52), channel_id=1, source_target_pairs={{0,6},{2,8},{4,10},{6,12},{8,14},{10,0},{12,2},{14,4},{1,7},{3,9},... | collective-permute-start | bytes 98312 | tf_op jit(solution)/shard_map/ppermute | solution.py:301
  21.3 2.0 %collective-permute-start.3 = (bf16[64,256]{1,0:T(8,128)(2,1)S(1)}, bf16[64,256]{1,0:T(8,128)(2,1)S(1)}, u32[]{:S(2)}, u32[]{:S(2)}) collective-permute-start(bf16[64,256]{1,0:T(8,128)(2,1)S(1)} %get-tuple-element.53), channel_id=1, source_target_pairs={{0,8},{2,10},{4,12},{6,14},{8,0},{10,2},{12,4},{14,6},{1,9},{3,11}... | collective-permute-start | bytes 98312 | tf_op jit(solution)/shard_map/ppermute | solution.py:301
  22.0 2.0 %collective-permute-start.4 = (bf16[64,256]{1,0:T(8,128)(2,1)S(1)}, bf16[64,256]{1,0:T(8,128)(2,1)S(1)}, u32[]{:S(2)}, u32[]{:S(2)}) collective-permute-start(bf16[64,256]{1,0:T(8,128)(2,1)S(1)} %get-tuple-element.54), channel_id=1, source_target_pairs={{0,10},{2,12},{4,14},{6,0},{8,2},{10,4},{12,6},{14,8},{1,11},{3,13... | collective-permute-start | bytes 98312 | tf_op jit(solution)/shard_map/ppermute | solution.py:301
  22.7 1.4 collective-permute-start.5
  23.4 0.7 collective-permute-start.6
  24.1 36.2 %collective-permute-start.7 = (bf16[64,128]{1,0:T(8,128)(2,1)S(1)}, bf16[64,128]{1,0:T(8,128)(2,1)S(1)}, u32[]{:S(2)}, u32[]{:S(2)}) collective-permute-start(bf16[64,128]{1,0:T(8,128)(2,1)S(1)} %get-tuple-element.57), channel_id=1, source_target_pairs={{0,16},{2,18},{4,20},{6,22},{8,24},{10,26},{12,28},{14,30},{1,17},... | collective-permute-start | bytes 49160 | tf_op jit(solution)/shard_map/ppermute | solution.py:301
  25.4 40.7 %collective-permute-start.8 = (bf16[64,128]{1,0:T(8,128)(2,1)S(1)}, bf16[64,128]{1,0:T(8,128)(2,1)S(1)}, u32[]{:S(2)}, u32[]{:S(2)}) collective-permute-start(bf16[64,128]{1,0:T(8,128)(2,1)S(1)} %get-tuple-element.58), channel_id=1, source_target_pairs={{0,18},{2,20},{4,22},{6,24},{8,26},{10,28},{12,30},{14,16},{1,19},... | collective-permute-start | bytes 49160 | tf_op jit(solution)/shard_map/ppermute | solution.py:301
  26.7 40.7 %collective-permute-start.9 = (bf16[64,128]{1,0:T(8,128)(2,1)S(1)}, bf16[64,128]{1,0:T(8,128)(2,1)S(1)}, u32[]{:S(2)}, u32[]{:S(2)}) collective-permute-start(bf16[64,128]{1,0:T(8,128)(2,1)S(1)} %get-tuple-element.59), channel_id=1, source_target_pairs={{0,20},{2,22},{4,24},{6,26},{8,28},{10,30},{12,16},{14,18},{1,21},... | collective-permute-start | bytes 49160 | tf_op jit(solution)/shard_map/ppermute | solution.py:301
  60.3 8.4 %collective-permute-start.10 = (bf16[64,128]{1,0:T(8,128)(2,1)S(1)}, bf16[64,128]{1,0:T(8,128)(2,1)S(1)}, u32[]{:S(2)}, u32[]{:S(2)}) collective-permute-start(bf16[64,128]{1,0:T(8,128)(2,1)S(1)} %get-tuple-element.60), channel_id=1, source_target_pairs={{0,22},{2,24},{4,26},{6,28},{8,30},{10,16},{12,18},{14,20},{1,23},... | collective-permute-start | bytes 49160 | tf_op jit(solution)/shard_map/ppermute | solution.py:301
  66.1 5.9 %collective-permute-start.11 = (bf16[64,128]{1,0:T(8,128)(2,1)S(1)}, bf16[64,128]{1,0:T(8,128)(2,1)S(1)}, u32[]{:S(2)}, u32[]{:S(2)}) collective-permute-start(bf16[64,128]{1,0:T(8,128)(2,1)S(1)} %get-tuple-element.61), channel_id=1, source_target_pairs={{0,24},{2,26},{4,28},{6,30},{8,16},{10,18},{12,20},{14,22},{1,25},... | collective-permute-start | bytes 49160 | tf_op jit(solution)/shard_map/ppermute | solution.py:301
  67.4 6.0 %collective-permute-start.12 = (bf16[64,128]{1,0:T(8,128)(2,1)S(1)}, bf16[64,128]{1,0:T(8,128)(2,1)S(1)}, u32[]{:S(2)}, u32[]{:S(2)}) collective-permute-start(bf16[64,128]{1,0:T(8,128)(2,1)S(1)} %get-tuple-element.62), channel_id=1, source_target_pairs={{0,26},{2,28},{4,30},{6,16},{8,18},{10,20},{12,22},{14,24},{1,27},... | collective-permute-start | bytes 49160 | tf_op jit(solution)/shard_map/ppermute | solution.py:301
  68.7 5.1 %collective-permute-start.13 = (bf16[64,128]{1,0:T(8,128)(2,1)S(1)}, bf16[64,128]{1,0:T(8,128)(2,1)S(1)}, u32[]{:S(2)}, u32[]{:S(2)}) collective-permute-start(bf16[64,128]{1,0:T(8,128)(2,1)S(1)} %get-tuple-element.63), channel_id=1, source_target_pairs={{0,28},{2,30},{4,16},{6,18},{8,20},{10,22},{12,24},{14,26},{1,29},... | collective-permute-start | bytes 49160 | tf_op jit(solution)/shard_map/ppermute | solution.py:301
  72.0 5.0 %collective-permute-start.14 = (bf16[64,128]{1,0:T(8,128)(2,1)S(1)}, bf16[64,128]{1,0:T(8,128)(2,1)S(1)}, u32[]{:S(2)}, u32[]{:S(2)}) collective-permute-start(bf16[64,128]{1,0:T(8,128)(2,1)S(1)} %get-tuple-element.64), channel_id=1, source_target_pairs={{0,30},{2,16},{4,18},{6,20},{8,22},{10,24},{12,26},{14,28},{1,31},... | collective-permute-start | bytes 49160 | tf_op jit(solution)/shard_map/ppermute | solution.py:301
  84.5 52.6 %copy-start.4 = (bf16[1,1024,2048]{2,1,0:T(8,128)(2,1)S(1)}, bf16[1,1024,2048]{2,1,0:T(8,128)(2,1)}, u32[]{:S(2)}) copy-start(bf16[1,1024,2048]{2,1,0:T(8,128)(2,1)} %refs_9_.1) | copy-start | bytes 12582916
  84.5 52.5 %collective-permute-start.31 = (bf16[128,2048]{1,0:T(8,128)(2,1)S(1)}, bf16[128,2048]{1,0:T(8,128)(2,1)S(1)}, u32[]{:S(2)}, u32[]{:S(2)}) collective-permute-start(bf16[128,2048]{1,0:T(8,128)(2,1)S(1)} %get-tuple-element.92.refs_10_), channel_id=1, source_target_pairs={{16,0},{17,1},{18,2},{19,3},{20,4},{21,5},{22,6},{23,7},{24,8},{25... | collective-permute-start | bytes 1572872 | tf_op jit(solution)/shard_map/ppermute | solution.py:354
  86.1 12.1 %collective-permute-start.17 = (bf16[64,256]{1,0:T(8,128)(2,1)S(1)}, bf16[64,256]{1,0:T(8,128)(2,1)S(1)}, u32[]{:S(2)}, u32[]{:S(2)}) collective-permute-start(bf16[64,256]{1,0:T(8,128)(2,1)S(1)} %get-tuple-element.72), channel_id=1, source_target_pairs={{16,18},{18,20},{20,22},{22,24},{24,26},{26,28},{28,30},{30,16},{1... | collective-permute-start | bytes 98312 | tf_op jit(solution)/shard_map/ppermute | solution.py:301
  88.2 13.4 %collective-permute-start.18 = (bf16[64,256]{1,0:T(8,128)(2,1)S(1)}, bf16[64,256]{1,0:T(8,128)(2,1)S(1)}, u32[]{:S(2)}, u32[]{:S(2)}) collective-permute-start(bf16[64,256]{1,0:T(8,128)(2,1)S(1)} %get-tuple-element.73), channel_id=1, source_target_pairs={{16,20},{18,22},{20,24},{22,26},{24,28},{26,30},{28,16},{30,18},{1... | collective-permute-start | bytes 98312 | tf_op jit(solution)/shard_map/ppermute | solution.py:301
  90.3 14.2 %collective-permute-start.19 = (bf16[64,256]{1,0:T(8,128)(2,1)S(1)}, bf16[64,256]{1,0:T(8,128)(2,1)S(1)}, u32[]{:S(2)}, u32[]{:S(2)}) collective-permute-start(bf16[64,256]{1,0:T(8,128)(2,1)S(1)} %get-tuple-element.74), channel_id=1, source_target_pairs={{16,22},{18,24},{20,26},{22,28},{24,30},{26,16},{28,18},{30,20},{1... | collective-permute-start | bytes 98312 | tf_op jit(solution)/shard_map/ppermute | solution.py:301
  92.2 15.3 %collective-permute-start.20 = (bf16[64,256]{1,0:T(8,128)(2,1)S(1)}, bf16[64,256]{1,0:T(8,128)(2,1)S(1)}, u32[]{:S(2)}, u32[]{:S(2)}) collective-permute-start(bf16[64,256]{1,0:T(8,128)(2,1)S(1)} %get-tuple-element.75), channel_id=1, source_target_pairs={{16,24},{18,26},{20,28},{22,30},{24,16},{26,18},{28,20},{30,22},{1... | collective-permute-start | bytes 98312 | tf_op jit(solution)/shard_map/ppermute | solution.py:301
  98.3 9.3 %collective-permute-start.21 = (bf16[64,256]{1,0:T(8,128)(2,1)S(1)}, bf16[64,256]{1,0:T(8,128)(2,1)S(1)}, u32[]{:S(2)}, u32[]{:S(2)}) collective-permute-start(bf16[64,256]{1,0:T(8,128)(2,1)S(1)} %get-tuple-element.76), channel_id=1, source_target_pairs={{16,26},{18,28},{20,30},{22,16},{24,18},{26,20},{28,22},{30,24},{1... | collective-permute-start | bytes 98312 | tf_op jit(solution)/shard_map/ppermute | solution.py:301
  101.6 6.0 %collective-permute-start.22 = (bf16[64,256]{1,0:T(8,128)(2,1)S(1)}, bf16[64,256]{1,0:T(8,128)(2,1)S(1)}, u32[]{:S(2)}, u32[]{:S(2)}) collective-permute-start(bf16[64,256]{1,0:T(8,128)(2,1)S(1)} %get-tuple-element.77), channel_id=1, source_target_pairs={{16,28},{18,30},{20,16},{22,18},{24,20},{26,22},{28,24},{30,26},{1... | collective-permute-start | bytes 98312 | tf_op jit(solution)/shard_map/ppermute | solution.py:301
  104.5 4.7 %collective-permute-start.23 = (bf16[64,256]{1,0:T(8,128)(2,1)S(1)}, bf16[64,256]{1,0:T(8,128)(2,1)S(1)}, u32[]{:S(2)}, u32[]{:S(2)}) collective-permute-start(bf16[64,256]{1,0:T(8,128)(2,1)S(1)} %get-tuple-element.78), channel_id=1, source_target_pairs={{16,30},{18,16},{20,18},{22,20},{24,22},{26,24},{28,26},{30,28},{1... | collective-permute-start | bytes 98312 | tf_op jit(solution)/shard_map/ppermute | solution.py:301
  110.2 13.3 %collective-permute-start.24 = (bf16[64,128]{1,0:T(8,128)(2,1)S(1)}, bf16[64,128]{1,0:T(8,128)(2,1)S(1)}, u32[]{:S(2)}, u32[]{:S(2)}) collective-permute-start(bf16[64,128]{1,0:T(8,128)(2,1)S(1)} %get-tuple-element.80), channel_id=1, source_target_pairs={{16,18},{18,20},{20,22},{22,24},{24,26},{26,28},{28,30},{30,16},{1... | collective-permute-start | bytes 49160 | tf_op jit(solution)/shard_map/ppermute | solution.py:301
  114.2 13.3 %collective-permute-start.25 = (bf16[64,128]{1,0:T(8,128)(2,1)S(1)}, bf16[64,128]{1,0:T(8,128)(2,1)S(1)}, u32[]{:S(2)}, u32[]{:S(2)}) collective-permute-start(bf16[64,128]{1,0:T(8,128)(2,1)S(1)} %get-tuple-element.81), channel_id=1, source_target_pairs={{16,20},{18,22},{20,24},{22,26},{24,28},{26,30},{28,16},{30,18},{1... | collective-permute-start | bytes 49160 | tf_op jit(solution)/shard_map/ppermute | solution.py:301
  117.5 13.0 %collective-permute-start.26 = (bf16[64,128]{1,0:T(8,128)(2,1)S(1)}, bf16[64,128]{1,0:T(8,128)(2,1)S(1)}, u32[]{:S(2)}, u32[]{:S(2)}) collective-permute-start(bf16[64,128]{1,0:T(8,128)(2,1)S(1)} %get-tuple-element.82), channel_id=1, source_target_pairs={{16,22},{18,24},{20,26},{22,28},{24,30},{26,16},{28,18},{30,20},{1... | collective-permute-start | bytes 49160 | tf_op jit(solution)/shard_map/ppermute | solution.py:301
  119.5 17.6 %collective-permute-start.27 = (bf16[64,128]{1,0:T(8,128)(2,1)S(1)}, bf16[64,128]{1,0:T(8,128)(2,1)S(1)}, u32[]{:S(2)}, u32[]{:S(2)}) collective-permute-start(bf16[64,128]{1,0:T(8,128)(2,1)S(1)} %get-tuple-element.83), channel_id=1, source_target_pairs={{16,24},{18,26},{20,28},{22,30},{24,16},{26,18},{28,20},{30,22},{1... | collective-permute-start | bytes 49160 | tf_op jit(solution)/shard_map/ppermute | solution.py:301
  123.5 13.6 %collective-permute-start.28 = (bf16[64,128]{1,0:T(8,128)(2,1)S(1)}, bf16[64,128]{1,0:T(8,128)(2,1)S(1)}, u32[]{:S(2)}, u32[]{:S(2)}) collective-permute-start(bf16[64,128]{1,0:T(8,128)(2,1)S(1)} %get-tuple-element.84), channel_id=1, source_target_pairs={{16,26},{18,28},{20,30},{22,16},{24,18},{26,20},{28,22},{30,24},{1... | collective-permute-start | bytes 49160 | tf_op jit(solution)/shard_map/ppermute | solution.py:301
  127.5 9.6 %collective-permute-start.29 = (bf16[64,128]{1,0:T(8,128)(2,1)S(1)}, bf16[64,128]{1,0:T(8,128)(2,1)S(1)}, u32[]{:S(2)}, u32[]{:S(2)}) collective-permute-start(bf16[64,128]{1,0:T(8,128)(2,1)S(1)} %get-tuple-element.85), channel_id=1, source_target_pairs={{16,28},{18,30},{20,16},{22,18},{24,20},{26,22},{28,24},{30,26},{1... | collective-permute-start | bytes 49160 | tf_op jit(solution)/shard_map/ppermute | solution.py:301
  130.6 6.5 %collective-permute-start.30 = (bf16[64,128]{1,0:T(8,128)(2,1)S(1)}, bf16[64,128]{1,0:T(8,128)(2,1)S(1)}, u32[]{:S(2)}, u32[]{:S(2)}) collective-permute-start(bf16[64,128]{1,0:T(8,128)(2,1)S(1)} %get-tuple-element.86), channel_id=1, source_target_pairs={{16,30},{18,16},{20,18},{22,20},{24,22},{26,24},{28,26},{30,28},{1... | collective-permute-start | bytes 49160 | tf_op jit(solution)/shard_map/ppermute | solution.py:301

commit v2 on v1

--- a/solution.py
+++ b/solution.py
@@ -66,7 +66,7 @@
 
 
 def spread_rates(normed, w_rate, rate_base):
-    rates = rate_base * jax.nn.sigmoid(mm(normed, w_rate))
+    rates = rate_base * jax.nn.sigmoid(mm_nt(normed, w_rate))
     high = rates.astype(BF16)
     low = (rates - high.astype(F32)).astype(BF16)
     heads = rates.shape[1]
@@ -114,36 +114,28 @@
                 maps[pair * per_pair + part] = jnp.concatenate([s_map[:, cut], b_map[:, cut]], axis=1).astype(BF16)
 
 
-def place_out(refs, table, count):
-    me = lax.axis_index("seq")
-    for step, ref in enumerate(refs):
-        ref[...] = table[lax.rem(me + step, count)]
-
-
-def place_in(refs, table, count):
-    me = lax.axis_index("seq")
-    for step, ref in enumerate(refs):
-        table[lax.rem(me + count - step, count)] = ref[...]
-
-
-def first_front(count, lw, h_ref, gain_ref, w_hbm, w_rate_ref, base_ref, *rest):
-    outs = rest[:count]
-    wkv, normed_out, keys_out, x_out, y_out, maps, sems = rest[count:]
+def first_front(lw, h_hbm, gain_hbm, w_hbm, w_rate_hbm, base_hbm, maps, wkv, normed_out, keys_out, x_out, y_out, h_ref, gain_ref, w_rate_ref, base_ref, small_sems, sems):
     width = keys_out.shape[1]
     quads = width // QUAD
+    small = [
+        pltpu.make_async_copy(source, target, small_sems.at[index])
+        for index, (source, target) in enumerate(
+            [(h_hbm, h_ref), (gain_hbm, gain_ref), (w_rate_hbm, w_rate_ref), (base_hbm, base_ref)]
+        )
+    ]
 
     def copies(quad):
-        made = []
-        for side in range(2):
-            made.append(
-                pltpu.make_async_copy(
-                    w_hbm.at[0, :, pl.ds((side + 1) * width + quad * QUAD, QUAD)],
-                    wkv.at[:, pl.ds(side * width + quad * QUAD, QUAD)],
-                    sems.at[quad, side],
-                )
+        return [
+            pltpu.make_async_copy(
+                w_hbm.at[0, :, pl.ds((side + 1) * width + quad * QUAD, QUAD)],
+                wkv.at[:, pl.ds(side * width + quad * QUAD, QUAD)],
+                sems.at[quad, side],
             )
-        return made
-
+            for side in range(2)
+        ]
+
+    for copy in small:
+        copy.start()
     for quad in range(quads):
         for copy in copies(quad):
             copy.start()
@@ -151,6 +143,9 @@
     def wait_group(quad):
         for copy in copies(quad):
             copy.wait()
+
+    for copy in small:
+        copy.wait()
 
     @pl.when(lax.axis_index("section") == 0)
     def _():
@@ -158,7 +153,6 @@
         normed_out[...] = normed
         rates = spread_rates(normed, w_rate_ref[0], base_ref[...])
         slab_maps(normed, rates, wkv, wait_group, keys_out, x_out, y_out, maps, lw)
-        place_out(outs, maps, count)
 
     @pl.when(lax.axis_index("section") != 0)
     def _():
@@ -214,15 +208,9 @@
         read_out(normed_ref[...], wq, lambda quad: None, keys_ref, x_ref, y_ref, qo_out)
 
 
-def relay(count, lw, active, *refs):
-    pieces = refs[:count]
-    init_ref = refs[count]
-    outs = refs[count + 1 : 2 * count + 1]
-    table, states = refs[2 * count + 1 :]
-
+def relay(count, lw, active, table, init_ref, states):
     @pl.when(lax.axis_index("section") == active)
     def _():
-        place_in(pieces, table, count)
         heads = lw // HD
         me = lax.axis_index("seq")
         state = jnp.concatenate([init_ref[0, me * heads + index] for index in range(heads)], axis=1)
@@ -231,51 +219,39 @@
             step = table[slab]
             state = state - mm(step[:, :lw], spread(state.astype(BF16))) + step[:, lw:].astype(F32)
             states[slab + 1] = state.astype(BF16)
-        place_out(outs, states, count)
-
-
-def finish(pieces, table, qo_ref, w_out, h_ref, count, lw):
-    place_in(pieces, table, count)
-    width = qo_ref.shape[1] // 2
-    per_quad = QUAD // lw
-    parts = []
-    for quad in range(width // QUAD):
-        lanes = slice(quad * QUAD, (quad + 1) * QUAD)
-        state = jnp.concatenate([table[quad * per_quad + index] for index in range(per_quad)], axis=1)
-        inner = mm(qo_ref[:, lanes], spread(state)) + qo_ref[:, width + quad * QUAD : width + (quad + 1) * QUAD].astype(F32)
-        parts.append(inner.astype(BF16))
-    inner_bf = jnp.concatenate(parts, axis=1)
-    return (h_ref[...].astype(F32) + mm(inner_bf, w_out)).astype(BF16)
-
-
-def later_front(count, lw, *refs):
-    pieces = refs[:count]
-    qo_ref, w_out_ref, h_ref, gain_ref, wkv, w_rate_ref, base_ref = refs[count : count + 7]
-    outs = refs[count + 7 : 2 * count + 7]
-    h_out, normed_out, keys_out, x_out, y_out, table, maps = refs[2 * count + 7 :]
-
+
+
+def finish(lw, active, table, qo_ref, w_out_ref, h_ref, out_ref):
+    @pl.when(lax.axis_index("section") == active)
+    def _():
+        width = qo_ref.shape[1] // 2
+        per_quad = QUAD // lw
+        parts = []
+        for quad in range(width // QUAD):
+            lanes = slice(quad * QUAD, (quad + 1) * QUAD)
+            state = jnp.concatenate([table[quad * per_quad + index] for index in range(per_quad)], axis=1)
+            offset = qo_ref[:, width + quad * QUAD : width + (quad + 1) * QUAD]
+            inner = mm(qo_ref[:, lanes], spread(state)) + offset.astype(F32)
+            parts.append(inner.astype(BF16))
+        inner_bf = jnp.concatenate(parts, axis=1)
+        out_ref[...] = (h_ref[...].astype(F32) + mm(inner_bf, w_out_ref[0])).astype(BF16)
+
+
+def later_front(lw, h_ref, gain_ref, wkv, w_rate_ref, base_ref, maps, normed_out, keys_out, x_out, y_out):
     @pl.when(lax.axis_index("section") == 1)
     def _():
-        result = finish(pieces, table, qo_ref, w_out_ref[...], h_ref, count, lw)
-        h_out[...] = result
-        normed = norm_rows(result, gain_ref[...])
+        normed = norm_rows(h_ref[...], gain_ref[...])
         normed_out[...] = normed
         rates = spread_rates(normed, w_rate_ref[0], base_ref[...])
         slab_maps(normed, rates, wkv, lambda quad: None, keys_out, x_out, y_out, maps, lw)
-        place_out(outs, maps, count)
-
-
-def last_finish(count, lw, *refs):
-    pieces = refs[:count]
-    qo_ref, w_out_ref, h_ref, back_ref, out_ref, table = refs[count:]
-
-    @pl.when(lax.axis_index("section") == 1)
-    def _():
-        out_ref[0] = finish(pieces, table, qo_ref, w_out_ref[0], h_ref, count, lw)
+
+
+def last_finish(lw, table, qo_ref, w_out_ref, h_ref, first_ref, out_ref):
+    finish(lw, 1, table, qo_ref, w_out_ref, h_ref, out_ref.at[0])
 
     @pl.when(lax.axis_index("section") == 0)
     def _():
-        out_ref[0] = back_ref[...]
+        out_ref[0] = first_ref[...]
 
 
 def call(body, outs, scratch, args, kinds=None, name=None):
@@ -291,15 +267,8 @@
     )(*args)
 
 
-def exchange(pieces, source, target, count):
-    received = []
-    for step, piece in enumerate(pieces):
-        if step == 0 and source == target:
-            received.append(piece)
-            continue
-        pairs = [(source * count + place, target * count + (place + step) % count) for place in range(count)]
-        received.append(lax.ppermute(piece, ("section", "seq"), pairs))
-    return received
+def exchange(pieces):
+    return lax.all_to_all(pieces, "seq", 0, 0)
 
 
 def shards(tokens, norm_gain, w_qkv, w_rate, rate_base, init_state, w_out):
@@ -312,46 +281,55 @@
     quads = width // QUAD
     shape = jax.ShapeDtypeStruct
     in_vmem = functools.partial(pltpu.with_memory_space_constraint, memory_space=pltpu.VMEM)
-    pieces_out = [shape((HD, 2 * lw), BF16)] * count
-    states_out = [shape((HD, lw), BF16)] * count
+    in_hbm = functools.partial(pltpu.with_memory_space_constraint, memory_space=pltpu.HBM)
+    maps = shape((count, HD, 2 * lw), BF16)
+    states = shape((count, HD, lw), BF16)
     rows_out = [shape((rows, model), BF16)] + [shape((rows, width), BF16)] * 3
-    maps = pltpu.VMEM((count, HD, 2 * lw), BF16)
-    states = pltpu.VMEM((count, HD, lw), BF16)
-
-    w_out_first = lax.ppermute(w_out[0], "section", [(0, 1)])
-
-    done = call(
-        functools.partial(first_front, count, lw),
-        pieces_out + [pltpu.VMEM((depth, 2 * width), BF16)] + rows_out,
-        [maps, pltpu.SemaphoreType.DMA((quads, 2))],
-        [tokens, norm_gain, w_qkv, w_rate, rate_base],
-        [pltpu.VMEM, pltpu.VMEM, pl.ANY, pltpu.VMEM, pltpu.VMEM],
+    w_rate = jnp.swapaxes(w_rate, 1, 2)
+
+    sent, wkv, normed, keys, x_all, y_all = call(
+        functools.partial(first_front, lw),
+        [maps, pltpu.VMEM((depth, 2 * width), BF16)] + rows_out,
+        [
+            pltpu.VMEM(tokens.shape, tokens.dtype),
+            pltpu.VMEM(norm_gain.shape, norm_gain.dtype),
+            pltpu.VMEM(w_rate.shape, w_rate.dtype),
+            pltpu.VMEM(rate_base.shape, rate_base.dtype),
+            pltpu.SemaphoreType.DMA((4,)),
+            pltpu.SemaphoreType.DMA((quads, 2)),
+        ],
+        [in_hbm(value) for value in (tokens, norm_gain, w_qkv, w_rate, rate_base)],
+        [pltpu.HBM] * 5,
         name="first_front",
     )
-    pieces, (wkv, normed, keys, x_all, y_all) = done[:count], done[count:]
-    received = exchange(pieces, 0, 0, count)
+    received = exchange(sent)
     reads, wq = call(
         first_reads,
         [shape((rows, 2 * width), BF16), pltpu.VMEM((depth, width), BF16)],
         [pltpu.SemaphoreType.DMA((quads,))],
-        [normed, keys, x_all, y_all, w_qkv],
-        [pltpu.VMEM] * 4 + [pl.ANY],
+        [normed, keys, x_all, y_all, in_hbm(w_qkv)],
+        [pltpu.VMEM] * 4 + [pltpu.HBM],
         name="first_reads",
     )
-    reads = lax.ppermute(reads, "section", [(0, 1)])
-    begun = call(functools.partial(relay, count, lw, 0), states_out, [maps, states], received + [init_state], name="relay0")
-    received = exchange(begun, 0, 1, count)
-
-    done = call(
-        functools.partial(later_front, count, lw),
-        pieces_out + [shape((rows, model), BF16)] + rows_out,
-        [states, maps],
-        received + [reads, w_out_first, tokens, norm_gain, in_vmem(wkv), w_rate, rate_base],
+    (sent,) = call(functools.partial(relay, count, lw, 0), [states], [], [received, init_state], name="relay0")
+    received = exchange(sent)
+    (first,) = call(
+        functools.partial(finish, lw, 0),
+        [shape((rows, model), BF16)],
+        [],
+        [received, reads, w_out, tokens],
+        name="first_finish",
+    )
+    hidden = lax.ppermute(first, "section", [(0, 1)])
+
+    sent, normed, keys, x_all, y_all = call(
+        functools.partial(later_front, lw),
+        [maps] + rows_out,
+        [],
+        [hidden, norm_gain, in_vmem(wkv), w_rate, rate_base],
         name="later_front",
     )
-    pieces, (hidden, normed, keys, x_all, y_all) = done[:count], done[count:]
-    received = exchange(pieces, 1, 1, count)
-    back = lax.ppermute(hidden, "section", [(1, 0)])
+    received = exchange(sent)
     (reads,) = call(
         later_reads,
         [shape((rows, 2 * width), BF16)],
@@ -359,13 +337,13 @@
         [normed, keys, x_all, y_all, in_vmem(wq)],
         name="later_reads",
     )
-    begun = call(functools.partial(relay, count, lw, 1), states_out, [maps, states], received + [init_state], name="relay1")
-    received = exchange(begun, 1, 1, count)
+    (sent,) = call(functools.partial(relay, count, lw, 1), [states], [], [received, init_state], name="relay1")
+    received = exchange(sent)
     (result,) = call(
-        functools.partial(last_finish, count, lw),
+        functools.partial(last_finish, lw),
         [shape((1, rows, model), BF16)],
-        [states],
-        received + [reads, w_out, hidden, back],
+        [],
+        [received, reads, w_out, hidden, first],
         name="last_finish",
     )
     return result

time: 140 us -> 82.5 us (0.59)
  the two profiles are of different devices: /device:TPU:1 before, /device:TPU:25 now
where the time goes in v2:
time: 82.5 us; the launch traced here: 81 us
  blocking collectives  18.8 us (23%)
  Pallas kernels  17.9 us (22%)
  local copies, waits for them, and re-layouts  16.8 us (20%)
  starting transfers between devices  13.9 us (17%)
  waiting for transfers between devices  13.5 us (16%)
    all_to_all x2, blocking collectives, exchange(): return lax.all_to_all(pieces, 'seq', 0, 0)  18.8 us
    pallas_call x8, Pallas kernels, call(): pl.pallas_call(body, out_shape=outs, in_specs=specs, out_specs=[pl.BlockS...  17.9 us
    unnamed x26, local copies, waits for them, and re-layouts  16.8 us
    ppermute x1, waiting for transfers between devices, shards(): hidden = lax.ppermute(first, 'section', [(0, 1)])  13.5 us
    all_to_all x2, starting transfers between devices, exchange(): return lax.all_to_all(pieces, 'seq', 0, 0)  12.6 us
  transfers between devices with their start and end apart: 3, of which 1 were waited for; matrix products, arithmetic and copies ran while one was open for 0% of the time, Pallas kernels for 7%

profile of v2, /device:TPU:25, one launch (start us, length us, event | category | flops | bytes accessed | tf_op | source)
XLA Modules:
  0.0 81.0 jit_solution(7980460200623752757)
XLA Ops:
  0.0 0.0 copy-start.7
  0.0 3.9 %first_front.1 = (bf16[8,64,256]{2,1,0:T(8,128)(2,1)S(1)}, bf16[2048,2048]{1,0:T(8,128)(2,1)S(1)}, bf16[128,2048]{1,0:T(8,128)(2,1)S(1)}, bf16[128,1024]{1,0:T(8...) custom-call(bf16[128,2048]{1,0:T(8,128)(2,1)} %h_ref.1, f32[1,2048]{1,0:T(1,128)} %gain_ref.1, ...), custom_call_target="tpu_custom_call" | custom-call | tf_op jit(solution)/shard_map/first_front/pallas_call | solution.py:259
  3.9 0.0 copy-start.2
  3.9 3.2 %copy-done.2 = bf16[2048,2048]{1,0:T(8,128)(2,1)} copy-done((bf16[2048,2048]{1,0:T(8,128)(2,1)}, bf16[2048,2048]{1,0:T(8,128)(2,1)S(1)}, u32[]{:S(2)}) %copy-start.2) | copy-done | bytes 8388632
  7.1 0.0 copy-start.6
  7.1 9.5 %all_to_all.20.table = bf16[8,64,256]{2,1,0:T(8,128)(2,1)S(1)} all-to-all(bf16[8,64,256]{2,1,0:T(8,128)(2,1)S(1)} %get-tuple-element.18), channel_id=1, replica_groups=mesh['section'=2,'seq'=8,'traj'=2] {'seq'}, dimensions={0} | all-to-all | bytes 524288 | tf_op jit(solution)/shard_map/all_to_all | solution.py:271
  16.6 0.0 copy-done.7
  16.6 0.7 relay0.1
  17.2 6.3 %all-to-all-start.1 = ((bf16[8,64,128]{2,1,0:T(8,128)(2,1)}), bf16[8,64,128]{2,1,0:T(8,128)(2,1)S(1)}, u32[]{:S(2)}, u32[]{:S(2)}) async-start(bf16[8,64,128]{2,1,0:T(8,128)(2,1)} %relay0.1), calls=%async_computation.1 | async-start | bytes 262144 | tf_op jit(solution)/shard_map/all_to_all | solution.py:271
  23.5 0.0 copy-start.8
  23.5 0.0 copy-start.11
  23.5 0.0 copy-start.12
  23.5 2.3 %first_reads.1 = (bf16[128,2048]{1,0:T(8,128)(2,1)S(1)}, bf16[2048,1024]{1,0:T(8,128)(2,1)S(1)}) custom-call(bf16[128,2048]{1,0:T(8,128)(2,1)S(1)} %get-tuple-element.19.normed_ref, bf16[128,1024]{1,0:T(8,128)(2,1)S(1)} %get-tuple-element.20.keys_ref, bf16[128,1024]{1,0:T(8,128)(2,1)S(1)} %get-tuple-element.21.x_ref, ...), custom_call_target="tpu_custom_call" | custom-call | tf_op jit(solution)/shard_map/first_reads/pallas_call | solution.py:259
  25.9 0.0 copy-start.4
  25.9 2.0 %copy-done.4 = bf16[2048,1024]{1,0:T(8,128)(2,1)} copy-done((bf16[2048,1024]{1,0:T(8,128)(2,1)}, bf16[2048,1024]{1,0:T(8,128)(2,1)S(1)}, u32[]{:S(2)}) %copy-start.4) | copy-done | bytes 4194328
  27.8 0.0 all-to-all-done.1.table
  27.8 0.0 copy-done.6
  27.8 0.0 copy-start
  27.8 2.2 %copy-done = bf16[1,1024,2048]{2,1,0:T(8,128)(2,1)S(1)} copy-done((bf16[1,1024,2048]{2,1,0:T(8,128)(2,1)S(1)}, bf16[1,1024,2048]{2,1,0:T(8,128)(2,1)}, u32[]{:S(2)}) %copy-start) | copy-done | bytes 4194328
  30.0 1.3 %collective-permute-start = (bf16[128,2048]{1,0:T(8,128)(2,1)S(1)}, bf16[128,2048]{1,0:T(8,128)(2,1)S(1)}, u32[]{:S(2)}, u32[]{:S(2)}) collective-permute-start(bf16[128,2048]{1,0:T(8,128)(2,1)S(1)} %first_finish.1.first_ref), channel_id=1, source_target_pairs={{0,16},{1,17},{2,18},{3,19},{4,20},{5,21},{6,22},{7,23},{8,24},{9,... | collective-permute-start | bytes 1572872 | tf_op jit(solution)/shard_map/ppermute | solution.py:323
  31.3 13.5 %collective-permute-done.h_ref = bf16[128,2048]{1,0:T(8,128)(2,1)S(1)} collective-permute-done((bf16[128,2048]{1,0:T(8,128)(2,1)S(1)}, bf16[128,2048]{1,0:T(8,128)(2,1)S(1)}, u32[]{:S(2)}, u32[]{:S(2)}) %collective-permute-start) | collective-permute-done | bytes 524320 | tf_op jit(solution)/shard_map/ppermute | solution.py:323
  44.8 0.0 copy-done.8
  44.8 0.0 copy-done.11
  44.8 0.0 copy-done.12
  44.8 0.0 copy-start.3
  44.8 3.4 %copy-done.3 = bf16[2048,2048]{1,0:T(8,128)(2,1)S(1)} copy-done((bf16[2048,2048]{1,0:T(8,128)(2,1)S(1)}, bf16[2048,2048]{1,0:T(8,128)(2,1)}, u32[]{:S(2)}) %copy-start.3) | copy-done | bytes 8388632
  48.2 4.5 %later_front.1 = (bf16[8,64,256]{2,1,0:T(8,128)(2,1)S(1)}, bf16[128,2048]{1,0:T(8,128)(2,1)S(1)}, bf16[128,1024]{1,0:T(8,128)(2,1)S(1)}, bf16[128,1024]{1,0:T(8,128)(2,1)S(1)}, bf16[128,1024]{1,0:T(8,128)(2,1)S(1)}) custom-call(bf16[128,2048]{1,0:T(8,128)(2,1)S(1)} %collective-permute-done.h_ref, f32[1,2048]{1,0:T(1,128)S(1)} %copy-done.11, ...), custom_call_target="tpu_custom_call" | custom-call | tf_op jit(solution)/shard_map/later_front/pallas_call | solution.py:259
  52.7 0.0 copy-start.9
  52.7 0.7 copy-done.9
  53.4 9.3 %all_to_all.21.table = bf16[8,64,256]{2,1,0:T(8,128)(2,1)S(1)} all-to-all(bf16[8,64,256]{2,1,0:T(8,128)(2,1)S(1)} %get-tuple-element.25), channel_id=1, replica_groups=mesh['section'=2,'seq'=8,'traj'=2] {'seq'}, dimensions={0} | all-to-all | bytes 524288 | tf_op jit(solution)/shard_map/all_to_all | solution.py:271
  62.7 1.7 %relay1.1 = bf16[8,64,128]{2,1,0:T(8,128)(2,1)} custom-call(bf16[8,64,256]{2,1,0:T(8,128)(2,1)S(1)} %all_to_all.21.table, f32[1,16,64,64]{3,2,1,0:T(8,128)S(1)} %copy-done.7), custom_call_target="tpu_custom_call" | custom-call | tf_op jit(solution)/shard_map/relay1/pallas_call | solution.py:259
  64.4 6.3 %all-to-all-start.3 = ((bf16[8,64,128]{2,1,0:T(8,128)(2,1)}), bf16[8,64,128]{2,1,0:T(8,128)(2,1)S(1)}, u32[]{:S(2)}, u32[]{:S(2)}) async-start(bf16[8,64,128]{2,1,0:T(8,128)(2,1)} %relay1.1), calls=%async_computation.3 | async-start | bytes 262144 | tf_op jit(solution)/shard_map/all_to_all | solution.py:271
  70.7 0.0 copy-start.5
  70.7 2.2 %copy-done.5 = bf16[2048,1024]{1,0:T(8,128)(2,1)S(1)} copy-done((bf16[2048,1024]{1,0:T(8,128)(2,1)S(1)}, bf16[2048,1024]{1,0:T(8,128)(2,1)}, u32[]{:S(2)}) %copy-start.5) | copy-done | bytes 4194328
  72.9 0.0 copy-start.10
  72.9 0.9 %copy-done.10 = bf16[128,1024]{1,0:T(8,128)(2,1)S(1)} copy-done((bf16[128,1024]{1,0:T(8,128)(2,1)S(1)}, bf16[128,1024]{1,0:T(8,128)(2,1)}, u32[]{:S(2)}) %copy-start.10) | copy-done | bytes 262168
  73.8 3.3 %later_reads.1.qo_ref = bf16[128,2048]{1,0:T(8,128)(2,1)S(1)} custom-call(bf16[128,2048]{1,0:T(8,128)(2,1)S(1)} %get-tuple-element.26.normed_ref, bf16[128,1024]{1,0:T(8,128)(2,1)S(1)} %get-tuple-element.27.keys_ref, bf16[128,1024]{1,0:T(8,128)(2,1)S(1)} %get-tuple-element.28.x_ref, bf16[128,1024]{1,0:T(8,128)(2,1)S(1)} %copy-done.10, ...), custom_call_target="tpu_custom_call" | custom-call | tf_op jit(solution)/shard_map/later_reads/pallas_call | solution.py:259
  77.1 0.0 all-to-all-done.3.table
  77.1 0.0 copy-start.1
  77.1 2.2 %copy-done.1 = bf16[1,1024,2048]{2,1,0:T(8,128)(2,1)S(1)} copy-done((bf16[1,1024,2048]{2,1,0:T(8,128)(2,1)S(1)}, bf16[1,1024,2048]{2,1,0:T(8,128)(2,1)}, u32[]{:S(2)}) %copy-start.1) | copy-done | bytes 4194328
  79.3 1.7 %last_finish.1 = bf16[1,128,2048]{2,1,0:T(8,128)(2,1)} custom-call(bf16[8,64,128]{2,1,0:T(8,128)(2,1)S(1)} %all-to-all-done.3.table, bf16[128,2048]{1,0:T(8,128)(2,1)S(1)} %later_reads.1.qo_ref, bf16[1,1024,2048]{2,1,0:T(8,128)(2,1)S(1)} %copy-done.1, bf16[128,2048]{1,0:T(8,128)(2,1)S(1)} %collective-permute-done.h_ref, ...), custom_call_target="tpu_custom_call" | custom-call | tf_op jit(solution)/shard_map/last_finish/pallas_call | solution.py:259
  (1 shorter events, 0.0 us)
Async XLA Ops:
  0.0 16.6 %copy-start.7 = (f32[1,16,64,64]{3,2,1,0:T(8,128)S(1)}, f32[1,16,64,64]{3,2,1,0:T(8,128)}, u32[]{:S(2)}) copy-start(f32[1,16,64,64]{3,2,1,0:T(8,128)} %init_ref.3) | copy-start | bytes 786436
  3.9 3.2 %copy-start.2 = (bf16[2048,2048]{1,0:T(8,128)(2,1)}, bf16[2048,2048]{1,0:T(8,128)(2,1)S(1)}, u32[]{:S(2)}) copy-start(bf16[2048,2048]{1,0:T(8,128)(2,1)S(1)} %get-tuple-element.24.wkv) | copy-start | bytes 25165828
  7.1 20.7 %copy-start.6 = (bf16[128,2048]{1,0:T(8,128)(2,1)S(1)}, bf16[128,2048]{1,0:T(8,128)(2,1)}, u32[]{:S(2)}) copy-start(bf16[128,2048]{1,0:T(8,128)(2,1)} %h_ref.1) | copy-start | bytes 1572868
  17.2 10.6 %all-to-all-start.1 = ((bf16[8,64,128]{2,1,0:T(8,128)(2,1)}), bf16[8,64,128]{2,1,0:T(8,128)(2,1)S(1)}, u32[]{:S(2)}, u32[]{:S(2)}) async-start(bf16[8,64,128]{2,1,0:T(8,128)(2,1)} %relay0.1), calls=%async_computation.1 | async-start | bytes 262144 | tf_op jit(solution)/shard_map/all_to_all | solution.py:271
  23.5 21.3 %copy-start.8 = (bf16[1,2048,16]{1,2,0:T(8,128)(2,1)S(1)}, bf16[1,2048,16]{1,2,0:T(8,128)(2,1)}, u32[]{:S(2)}) copy-start(bf16[1,2048,16]{1,2,0:T(8,128)(2,1)} %param.10) | copy-start | bytes 196612
  23.5 21.3 %copy-start.11 = (f32[1,2048]{1,0:T(1,128)S(1)}, f32[1,2048]{1,0:T(1,128)}, u32[]{:S(2)}) copy-start(f32[1,2048]{1,0:T(1,128)} %gain_ref.1) | copy-start | bytes 24580
  23.5 21.3 %copy-start.12 = (f32[1,16]{1,0:T(1,128)S(1)}, f32[1,16]{1,0:T(1,128)}, u32[]{:S(2)}) copy-start(f32[1,16]{1,0:T(1,128)} %base_ref.1) | copy-start | bytes 196
  25.9 2.0 %copy-start.4 = (bf16[2048,1024]{1,0:T(8,128)(2,1)}, bf16[2048,1024]{1,0:T(8,128)(2,1)S(1)}, u32[]{:S(2)}) copy-start(bf16[2048,1024]{1,0:T(8,128)(2,1)S(1)} %get-tuple-element.30.wq) | copy-start | bytes 12582916
  27.8 2.2 %copy-start = (bf16[1,1024,2048]{2,1,0:T(8,128)(2,1)S(1)}, bf16[1,1024,2048]{2,1,0:T(8,128)(2,1)}, u32[]{:S(2)}) copy-start(bf16[1,1024,2048]{2,1,0:T(8,128)(2,1)} %w_out_ref.3) | copy-start | bytes 12582916
  30.0 14.8 %collective-permute-start = (bf16[128,2048]{1,0:T(8,128)(2,1)S(1)}, bf16[128,2048]{1,0:T(8,128)(2,1)S(1)}, u32[]{:S(2)}, u32[]{:S(2)}) collective-permute-start(bf16[128,2048]{1,0:T(8,128)(2,1)S(1)} %first_finish.1.first_ref), channel_id=1, source_target_pairs={{0,16},{1,17},{2,18},{3,19},{4,20},{5,21},{6,22},{7,23},{8,24},{9,... | collective-permute-start | bytes 1572872 | tf_op jit(solution)/shard_map/ppermute | solution.py:323
  44.8 3.4 %copy-start.3 = (bf16[2048,2048]{1,0:T(8,128)(2,1)S(1)}, bf16[2048,2048]{1,0:T(8,128)(2,1)}, u32[]{:S(2)}) copy-start(bf16[2048,2048]{1,0:T(8,128)(2,1)} %copy-done.2) | copy-start | bytes 25165828
  52.7 0.7 copy-start.9
  64.4 12.7 %all-to-all-start.3 = ((bf16[8,64,128]{2,1,0:T(8,128)(2,1)}), bf16[8,64,128]{2,1,0:T(8,128)(2,1)S(1)}, u32[]{:S(2)}, u32[]{:S(2)}) async-start(bf16[8,64,128]{2,1,0:T(8,128)(2,1)} %relay1.1), calls=%async_computation.3 | async-start | bytes 262144 | tf_op jit(solution)/shard_map/all_to_all | solution.py:271
  70.7 2.2 %copy-start.5 = (bf16[2048,1024]{1,0:T(8,128)(2,1)S(1)}, bf16[2048,1024]{1,0:T(8,128)(2,1)}, u32[]{:S(2)}) copy-start(bf16[2048,1024]{1,0:T(8,128)(2,1)} %copy-done.4) | copy-start | bytes 12582916
  72.9 0.9 %copy-start.10 = (bf16[128,1024]{1,0:T(8,128)(2,1)S(1)}, bf16[128,1024]{1,0:T(8,128)(2,1)}, u32[]{:S(2)}) copy-start(bf16[128,1024]{1,0:T(8,128)(2,1)} %copy-done.9) | copy-start | bytes 786436
  77.1 2.2 %copy-start.1 = (bf16[1,1024,2048]{2,1,0:T(8,128)(2,1)S(1)}, bf16[1,1024,2048]{2,1,0:T(8,128)(2,1)}, u32[]{:S(2)}) copy-start(bf16[1,1024,2048]{2,1,0:T(8,128)(2,1)} %w_out_ref.3) | copy-start | bytes 12582916

commit v3 on v0

v3 whole, which is shorter than its diff:
```python
import functools

import jax
import jax.numpy as jnp
from jax import lax
from jax.experimental import pallas as pl
from jax.experimental.pallas import tpu as pltpu
from jax.sharding import PartitionSpec as P

HD = 64
PAIR = 2 * HD
QUAD = 4 * HD
F32 = jnp.float32
BF16 = jnp.bfloat16
EPS = 1e-6
VMEM_LIMIT = 20 * 1024 * 1024


def mm(a, b):
    return jnp.dot(a, b, preferred_element_type=F32)


def mm_nt(a, b):
    return lax.dot_general(a, b, (((1,), (1,)), ((), ())), preferred_element_type=F32)


def mm_tn(a, b):
    return lax.dot_general(a, b, (((0,), (0,)), ((), ())), preferred_element_type=F32)


def head_masks(rows, lanes):
    lane = lax.broadcasted_iota(jnp.int32, (rows, lanes), 1)
    return [lane // HD == index for index in range(lanes // HD)]


def spread(value):
    zero = jnp.zeros_like(value)
    masks = head_masks(*value.shape)
    return jnp.concatenate([jnp.where(mask, value, zero) for mask in masks], axis=0)


def spread_two(left, right):
    return jnp.concatenate([spread(left), spread(right)], axis=1)


def diagonal(product):
    first = lax.broadcasted_iota(jnp.int32, (HD, PAIR), 1) < HD
    return jnp.where(first, product[:HD], product[HD:])


def head_ones():
    row = lax.broadcasted_iota(jnp.int32, (QUAD, QUAD), 0) // HD
    lane = lax.broadcasted_iota(jnp.int32, (QUAD, QUAD), 1) // HD
    return jnp.where(row == lane, 1.0, 0.0).astype(BF16)


def unit_heads(value, ones):
    squares = mm((value * value).astype(BF16), ones)
    return value * lax.rsqrt(squares + EPS)


def norm_rows(hidden, gain):
    wide = hidden.astype(F32)
    mean_sq = jnp.mean(wide * wide, axis=-1, keepdims=True)
    return (wide * lax.rsqrt(mean_sq + EPS) * gain).astype(BF16)


def spread_rates(normed, w_rate, rate_base):
    rates = rate_base * jax.nn.sigmoid(mm_nt(normed, w_rate))
    high = rates.astype(BF16)
    low = (rates - high.astype(F32)).astype(BF16)
    heads = rates.shape[1]
    row = lax.broadcasted_iota(jnp.int32, (heads, heads * HD), 0)
    lane = lax.broadcasted_iota(jnp.int32, (heads, heads * HD), 1) // HD
    pick = jnp.where(row == lane, 1.0, 0.0).astype(BF16)
    return mm(high, pick) + mm(low, pick)


def staged(groups):
    for group in groups[:2]:
        for copy in group:
            copy.start()

    def wait(index):
        for copy in groups[index]:
            copy.wait()
        if index + 2 < len(groups):
            for copy in groups[index + 2]:
                copy.start()

    return wait


def on_section(active, body):
    pl.when(lax.axis_index("section") == active)(body)


def front(active, h_ref, gain_hbm, w_hbm, w_rate_hbm, base_hbm, maps, normed_out, keys_out, x_out, y_out, wkv, h_in, gain, w_rate, base, small_sems, sems):
    width = keys_out.shape[1]
    quads = width // QUAD

    def body():
        sources = [(gain_hbm, gain), (w_rate_hbm, w_rate), (base_hbm, base)]
        if h_in is not None:
            sources.append((h_ref, h_in))
        small = [pltpu.make_async_copy(source, target, small_sems.at[index]) for index, (source, target) in enumerate(sources)]
        for copy in small:
            copy.start()
        wait_group = staged(
            [
                [
                    pltpu.make_async_copy(
                        w_hbm.at[0, :, pl.ds((side + 1) * width + quad * QUAD, QUAD)],
                        wkv.at[:, pl.ds(side * width + quad * QUAD, QUAD)],
                        sems.at[quad, side],
                    )
                    for side in range(2)
                ]
                for quad in range(quads)
            ]
        )
        for copy in small:
            copy.wait()
        normed = norm_rows((h_ref if h_in is None else h_in)[...], gain[...])
        normed_out[...] = normed
        rates = spread_rates(normed, w_rate[0], base[...])
        ones = head_ones()
        for quad in range(quads):
            wait_group(quad)
            lanes = slice(quad * QUAD, (quad + 1) * QUAD)
            keys = mm(normed, wkv[:, lanes])
            values = mm(normed, wkv[:, width + quad * QUAD : width + (quad + 1) * QUAD])
            keys = unit_heads(keys, ones)
            keys_bf = keys.astype(BF16)
            keys_out[:, lanes] = keys_bf
            rate = rates[:, lanes]
            x_all = rate * keys
            y_all = rate * values
            x_first, y_first = x_all[:HD].astype(BF16), y_all[:HD].astype(BF16)
            cross = mm_nt(keys_bf[HD:], spread(keys_bf[:HD])).astype(BF16)
            fix = mm(cross, spread_two(x_first, y_first))
            x_second = (x_all[HD:] - rate[HD:] * fix[:, :QUAD]).astype(BF16)
            y_second = (y_all[HD:] - rate[HD:] * fix[:, QUAD:]).astype(BF16)
            x_bf = jnp.concatenate([x_first, x_second], axis=0)
            y_bf = jnp.concatenate([y_first, y_second], axis=0)
            x_out[:, lanes] = x_bf
            y_out[:, lanes] = y_bf
            for half in range(2):
                own = slice(half * PAIR, (half + 1) * PAIR)
                start = quad * QUAD + half * PAIR
                both = mm_tn(keys_bf[:, own], jnp.concatenate([x_bf[:, own], y_bf[:, own]], axis=1))
                maps[:, start : start + PAIR] = diagonal(both[:, :PAIR]).astype(BF16)
                maps[:, width + start : width + start + PAIR] = diagonal(both[:, PAIR:]).astype(BF16)

    on_section(active, body)


def first_front(h_hbm, *rest):
    front(0, h_hbm, *rest)


def later_front(h_ref, *rest):
    *rest, small_sems, sems = rest
    front(1, h_ref, *rest[:10], None, *rest[10:], small_sems, sems)


def read_out(active, quads, normed_ref, keys_ref, x_ref, y_ref, w_hbm, reads_out, wq, sems):
    rows = keys_ref.shape[0]
    part = len(quads) * QUAD

    def body():
        wait_group = staged(
            [
                [
                    pltpu.make_async_copy(
                        w_hbm.at[0, :, pl.ds(quad * QUAD, QUAD)], wq.at[:, pl.ds(index * QUAD, QUAD)], sems.at[index]
                    )
                ]
                for index, quad in enumerate(quads)
            ]
        )
        normed = normed_ref[...]
        ones = head_ones()
        row = lax.broadcasted_iota(jnp.int32, (rows, 2 * rows), 0)
        lane = lax.rem(lax.broadcasted_iota(jnp.int32, (rows, 2 * rows), 1), rows)
        causal = row >= lane
        for index, quad in enumerate(quads):
            wait_group(index)
            queries = unit_heads(mm(normed, wq[:, index * QUAD : (index + 1) * QUAD]), ones)
            queries_bf = queries.astype(BF16)
            for half in range(2):
                own = slice(half * PAIR, (half + 1) * PAIR)
                place = slice(quad * QUAD + half * PAIR, quad * QUAD + (half + 1) * PAIR)
                start = index * QUAD + half * PAIR
                scores = mm_nt(queries_bf[:, own], spread(keys_ref[:, place]))
                scores = jnp.where(causal, scores, 0.0).astype(BF16)
                both = mm(scores, spread_two(x_ref[:, place], y_ref[:, place]))
                reads_out[:, start : start + PAIR] = (queries[:, own] - both[:, :PAIR]).astype(BF16)
                reads_out[:, part + start : part + start + PAIR] = both[:, PAIR:].astype(BF16)

    on_section(active, body)


def compose(active, own_ref, got_ref, after_ref, out_ref):
    width = own_ref.shape[1] // 2

    def body():
        for start in range(0, width, PAIR):
            s_lanes, b_lanes = slice(start, start + PAIR), slice(width + start, width + start + PAIR)
            s_own, s_got, b_got = own_ref[:, s_lanes], got_ref[:, s_lanes], got_ref[:, b_lanes]
            step = mm(s_own, spread_two(s_got, b_got))
            out_ref[:, s_lanes] = (s_own.astype(F32) + s_got.astype(F32) - step[:, :PAIR]).astype(BF16)
            out_ref[:, b_lanes] = (own_ref[:, b_lanes].astype(F32) + b_got.astype(F32) - step[:, PAIR:]).astype(BF16)

    on_section(active, body)


def pair_state(init_ref, pair):
    return jnp.concatenate([init_ref[0, 2 * pair], init_ref[0, 2 * pair + 1]], axis=1)


def end_state(active, own_ref, got_ref, init_ref, after_ref, out_ref):
    width = own_ref.shape[1] // 2

    def body():
        states = [pair_state(init_ref, pair) for pair in range(width // PAIR)]
        for ref in (got_ref, own_ref):
            for pair, state in enumerate(states):
                start = pair * PAIR
                step = mm(ref[:, start : start + PAIR], spread(state.astype(BF16)))
                states[pair] = state - step + ref[:, width + start : width + start + PAIR].astype(F32)
        for pair, state in enumerate(states):
            out_ref[:, pair * PAIR : (pair + 1) * PAIR] = state.astype(BF16)

    on_section(active, body)


def fold(active, count, *refs):
    got_refs = refs[:count]
    reads_refs = refs[count : count + 2]
    w_hbm, out_ref, w_out, sem = refs[count + 2 :]
    width = out_ref.shape[1] // 2
    part = width // 2

    def body():
        load = pltpu.make_async_copy(w_hbm.at[0], w_out, sem)
        load.start()
        for start in range(0, width, PAIR):
            reads_ref = reads_refs[start // part]
            inner = start % part
            left = reads_ref[:, inner : inner + PAIR].astype(F32)
            offset = reads_ref[:, part + inner : part + inner + PAIR].astype(F32)
            for ref in got_refs:
                step = mm(left.astype(BF16), spread_two(ref[:, start : start + PAIR], ref[:, width + start : width + start + PAIR]))
                left = left - step[:, :PAIR]
                offset = offset + step[:, PAIR:]
            out_ref[:, start : start + PAIR] = left.astype(BF16)
            out_ref[:, width + start : width + start + PAIR] = offset.astype(BF16)
        load.wait()

    on_section(active, body)


def finish(active, count, state_ref, init_ref, reads_ref, w_out_ref, h_ref, out_ref):
    width = reads_ref.shape[1] // 2

    def body():
        begins = lax.axis_index("seq") < count // 2
        parts = []
        for start in range(0, width, QUAD):
            lanes = slice(start, start + QUAD)
            init = jnp.concatenate([pair_state(init_ref, start // PAIR), pair_state(init_ref, start // PAIR + 1)], axis=1)
            state = jnp.where(begins, init.astype(BF16), state_ref[:, lanes])
            offset = reads_ref[:, width + start : width + start + QUAD]
            parts.append((mm(reads_ref[:, lanes], spread(state)) + offset.astype(F32)).astype(BF16))
        inner_bf = jnp.concatenate(parts, axis=1)
        out_ref[...] = (h_ref[...].astype(F32) + mm(inner_bf, w_out_ref[...])).astype(BF16)

    on_section(active, body)


def last_finish(count, state_ref, init_ref, reads_ref, w_out_ref, h_ref, first_ref, out_ref):
    finish(1, count, state_ref, init_ref, reads_ref, w_out_ref, h_ref, out_ref.at[0])

    @pl.when(lax.axis_index("section") == 0)
    def _():
        out_ref[0] = first_ref[...]


def call(body, outs, scratch, args, kinds=None, name=None):
    specs = [pl.BlockSpec(memory_space=kind) for kind in (kinds or [pltpu.VMEM] * len(args))]
    return pl.pallas_call(
        body,
        out_shape=outs,
        in_specs=specs,
        out_specs=[pl.BlockSpec(memory_space=pltpu.VMEM)] * len(outs),
        scratch_shapes=scratch,
        compiler_params=pltpu.CompilerParams(vmem_limit_bytes=VMEM_LIMIT),
        name=name,
    )(*args)


def shards(tokens, norm_gain, w_qkv, w_rate, rate_base, init_state, w_out):
    count = lax.axis_size("seq")
    heads = rate_base.shape[1]
    rows, model = tokens.shape
    width = heads * HD
    depth = w_qkv.shape[1]
    quads = width // QUAD
    shape = jax.ShapeDtypeStruct
    in_vmem = functools.partial(pltpu.with_memory_space_constraint, memory_space=pltpu.VMEM)
    in_hbm = functools.partial(pltpu.with_memory_space_constraint, memory_space=pltpu.HBM)
    maps = shape((HD, 2 * width), BF16)
    rows_out = [shape((rows, model), BF16)] + [shape((rows, width), BF16)] * 3
    w_rate = jnp.swapaxes(w_rate, 1, 2)
    norm_gain, w_qkv, w_rate, rate_base, w_out = [in_hbm(value) for value in (norm_gain, w_qkv, w_rate, rate_base, w_out)]

    def ahead(value, active, steps):
        pairs = [(active * count + place, active * count + place + steps) for place in range(count - steps)]
        return lax.ppermute(value, ("section", "seq"), pairs)

    def run(active, body, outs, scratch, args, kinds=None):
        return call(functools.partial(body, active), outs, scratch, args, kinds, name=body.__name__ + str(active))

    def layer(active, hidden):
        h_scratch = [] if active else [pltpu.VMEM(hidden.shape, hidden.dtype)]
        own, normed, keys, x_all, y_all = call(
            later_front if active else first_front,
            [maps] + rows_out,
            [pltpu.VMEM((depth, 2 * width), BF16)]
            + h_scratch
            + [pltpu.VMEM(value.shape, value.dtype) for value in (norm_gain, w_rate, rate_base)]
            + [pltpu.SemaphoreType.DMA((4,)), pltpu.SemaphoreType.DMA((quads, 2))],
            [hidden if active else in_hbm(hidden), norm_gain, w_qkv, w_rate, rate_base],
            [pltpu.VMEM if active else pltpu.HBM] + [pltpu.HBM] * 4,
            name="later_front" if active else "first_front",
        )

        def reads_of(picked):
            part = len(picked) * QUAD
            return call(
                functools.partial(read_out, active, picked),
                [shape((rows, 2 * part), BF16)],
                [pltpu.VMEM((depth, part), BF16), pltpu.SemaphoreType.DMA((len(picked),))],
                [normed, keys, x_all, y_all, w_qkv],
                [pltpu.VMEM] * 4 + [pltpu.HBM],
                name=f"reads{active}_{picked[0]}",
            )[0]

        reads = [reads_of(tuple(range(quads // 2))), reads_of(tuple(range(quads // 2, quads)))]
        got = [ahead(own, active, 1)]
        steps = 2
        while steps < count // 2:
            (own,) = run(active, compose, [maps], [], [own, got[-1], reads[0]], [pltpu.VMEM] * 2 + [pl.ANY])
            got.append(ahead(own, active, steps))
            steps *= 2
        (state,) = run(
            active, end_state, [shape((HD, width), BF16)], [], [own, got[-1], init_state, reads[1]], [pltpu.VMEM] * 3 + [pl.ANY]
        )
        state = ahead(state, active, steps)
        folded, w_out_near = call(
            functools.partial(fold, active, len(got)),
            [shape((rows, 2 * width), BF16), pltpu.VMEM(w_out.shape[1:], BF16)],
            [pltpu.SemaphoreType.DMA],
            got + reads + [w_out],
            [pltpu.VMEM] * (len(got) + 2) + [pltpu.HBM],
            name=f"fold{active}",
        )
        return [state, init_state, folded, in_vmem(w_out_near), hidden]

    (first,) = call(functools.partial(finish, 0, count), [shape((rows, model), BF16)], [], layer(0, tokens), name="first_finish")
    hidden = lax.ppermute(first, "section", [(0, 1)])
    (result,) = call(
        functools.partial(last_finish, count), [shape((1, rows, model), BF16)], [], layer(1, hidden) + [first], name="last_finish"
    )
    return result


def solution(mesh):
    return jax.shard_map(
        shards,
        mesh=mesh,
        in_specs=(
            P(("traj", "seq"), None),
            P("section", None),
            P("section", None, None),
            P("section", None, None),
            P("section", None),
            P("section", None, None, None),
            P("section", None, None),
        ),
        out_specs=P("section", ("traj", "seq"), None),
        check_vma=False,
    )
```

time: 344 us -> 71.6 us (0.21)
  the two profiles are of different devices: /device:TPU:8 before, /device:TPU:25 now
where the time goes in v3:
time: 71.6 us; the launch traced here: 71.3 us
  waiting for transfers between devices  44 us (61%)
  Pallas kernels  18.5 us (26%)
  starting transfers between devices  8.2 us (11%)
    ppermute x1, waiting for transfers between devices, shards(): hidden = lax.ppermute(first, 'section', [(0, 1)])  35 us
    pallas_call x14, Pallas kernels, call(): pl.pallas_call(body, out_shape=outs, in_specs=specs, out_specs=[pl.BlockS...  18.5 us
    ppermute x6, waiting for transfers between devices, ahead(): return lax.ppermute(value, ('section', 'seq'), pairs)  9.01 us
    ppermute x6, starting transfers between devices, ahead(): return lax.ppermute(value, ('section', 'seq'), pairs)  6.92 us
  transfers between devices with their start and end apart: 7, of which 4 were waited for; matrix products, arithmetic and copies ran while one was open for 0% of the time, Pallas kernels for 12%

profile of v3, /device:TPU:25, one launch (start us, length us, event | category | flops | bytes accessed | tf_op | source)
XLA Modules:
  0.0 71.3 jit_solution(14895472056926464712)
XLA Ops:
  0.0 0.1 first_front.1
  0.1 0.7 collective-permute-start
  0.8 0.0 collective-permute-done.got_ref.refs_0_
  0.9 0.0 copy-start
  0.9 0.8 %collective-permute-start.1 = (bf16[64,2048]{1,0:T(8,128)(2,1)S(1)}, bf16[64,2048]{1,0:T(8,128)(2,1)S(1)}, u32[]{:S(2)}, u32[]{:S(2)}) collective-permute-start(bf16[64,2048]{1,0:T(8,128)(2,1)S(1)} %compose0.1.own_ref), channel_id=1, source_target_pairs={{0,4},{2,6},{4,8},{6,10},{8,12},{10,14},{1,5},{3,7},{5,9},{7,11},{... | collective-permute-start | bytes 786440 | tf_op jit(solution)/shard_map/ppermute | solution.py:320
  1.7 0.0 copy-start.1
  1.8 0.0 collective-permute-done.1.got_ref.refs_1_
  1.8 0.2 copy-done
  1.9 0.7 collective-permute-start.2
  2.6 0.0 collective-permute-done.2.state_ref
  2.6 0.2 copy-done.1
  2.8 1.3 %collective-permute-start.3 = (bf16[128,2048]{1,0:T(8,128)(2,1)S(1)}, bf16[128,2048]{1,0:T(8,128)(2,1)S(1)}, u32[]{:S(2)}, u32[]{:S(2)}) collective-permute-start(bf16[128,2048]{1,0:T(8,128)(2,1)S(1)} %first_finish.1.first_ref), channel_id=1, source_target_pairs={{0,16},{1,17},{2,18},{3,19},{4,20},{5,21},{6,22},{7,23},{8,24},{9,... | collective-permute-start | bytes 1572872 | tf_op jit(solution)/shard_map/ppermute | solution.py:372
  4.1 35.0 %collective-permute-done.3.h_ref = bf16[128,2048]{1,0:T(8,128)(2,1)S(1)} collective-permute-done((bf16[128,2048]{1,0:T(8,128)(2,1)S(1)}, bf16[128,2048]{1,0:T(8,128)(2,1)S(1)}, u32[]{:S(2)}, u32[]{:S(2)}) %collective-permute-start.3) | collective-permute-done | bytes 524320 | tf_op jit(solution)/shard_map/ppermute | solution.py:372
  39.1 7.3 %later_front.1 = (bf16[64,2048]{1,0:T(8,128)(2,1)S(1)}, bf16[128,2048]{1,0:T(8,128)(2,1)S(1)}, bf16[128,1024]{1,0:T(8,128)(2,1)S(1)}, bf16[128,1024]{1,0:T(8,128)(2,1)S(1)}, bf16[128,1024]{1,0:T(8,128)(2,1)S(1)}) custom-call(bf16[128,2048]{1,0:T(8,128)(2,1)S(1)} %collective-permute-done.3.h_ref, f32[1,2048]{1,0:T(1,128)} %rest_0_.3, ...), custom_call_target="tpu_custom_call" | custom-call | tf_op jit(solution)/shard_map/later_front/pallas_call | solution.py:292
  46.4 2.2 %collective-permute-start.4 = (bf16[64,2048]{1,0:T(8,128)(2,1)S(1)}, bf16[64,2048]{1,0:T(8,128)(2,1)S(1)}, u32[]{:S(2)}, u32[]{:S(2)}) collective-permute-start(bf16[64,2048]{1,0:T(8,128)(2,1)S(1)} %get-tuple-element.26.own_ref), channel_id=1, source_target_pairs={{16,18},{18,20},{20,22},{22,24},{24,26},{26,28},{28,30},{17,19},{1... | collective-permute-start | bytes 786440 | tf_op jit(solution)/shard_map/ppermute | solution.py:320
  48.6 3.1 %reads1_0.1.after_ref.refs_2_ = bf16[128,1024]{1,0:T(8,128)(2,1)S(1)} custom-call(bf16[128,2048]{1,0:T(8,128)(2,1)S(1)} %get-tuple-element.27.normed_ref, bf16[128,1024]{1,0:T(8,128)(2,1)S(1)} %get-tuple-element.28.keys_ref, bf16[128,1024]{1,0:T(8,128)(2,1)S(1)} %get-tuple-element.29.x_ref, bf16[128,1024]{1,0:T(8,128)(2,1)S(1)} %get-tuple-element.30.y_ref, ...), custom_call_target="tpu_custom_call" | custom-call | tf_op jit(solution)/shard_map/reads1_0/pallas_call | solution.py:292
  51.8 2.7 %collective-permute-done.4.got_ref.refs_0_ = bf16[64,2048]{1,0:T(8,128)(2,1)S(1)} collective-permute-done((bf16[64,2048]{1,0:T(8,128)(2,1)S(1)}, bf16[64,2048]{1,0:T(8,128)(2,1)S(1)}, u32[]{:S(2)}, u32[]{:S(2)}) %collective-permute-start.4) | collective-permute-done | bytes 262176 | tf_op jit(solution)/shard_map/ppermute | solution.py:320
  54.4 0.2 compose1.1.own_ref
  54.7 1.3 %collective-permute-start.5 = (bf16[64,2048]{1,0:T(8,128)(2,1)S(1)}, bf16[64,2048]{1,0:T(8,128)(2,1)S(1)}, u32[]{:S(2)}, u32[]{:S(2)}) collective-permute-start(bf16[64,2048]{1,0:T(8,128)(2,1)S(1)} %compose1.1.own_ref), channel_id=1, source_target_pairs={{16,20},{18,22},{20,24},{22,26},{24,28},{26,30},{17,21},{19,23},{2... | collective-permute-start | bytes 786440 | tf_op jit(solution)/shard_map/ppermute | solution.py:320
  56.0 3.3 %reads1_2.1.after_ref.refs_3_ = bf16[128,1024]{1,0:T(8,128)(2,1)S(1)} custom-call(bf16[128,2048]{1,0:T(8,128)(2,1)S(1)} %get-tuple-element.27.normed_ref, bf16[128,1024]{1,0:T(8,128)(2,1)S(1)} %get-tuple-element.28.keys_ref, bf16[128,1024]{1,0:T(8,128)(2,1)S(1)} %get-tuple-element.29.x_ref, bf16[128,1024]{1,0:T(8,128)(2,1)S(1)} %get-tuple-element.30.y_ref, ...), custom_call_target="tpu_custom_call" | custom-call | tf_op jit(solution)/shard_map/reads1_2/pallas_call | solution.py:292
  59.3 2.5 %collective-permute-done.5.got_ref.refs_1_ = bf16[64,2048]{1,0:T(8,128)(2,1)S(1)} collective-permute-done((bf16[64,2048]{1,0:T(8,128)(2,1)S(1)}, bf16[64,2048]{1,0:T(8,128)(2,1)S(1)}, u32[]{:S(2)}, u32[]{:S(2)}) %collective-permute-start.5) | collective-permute-done | bytes 262176 | tf_op jit(solution)/shard_map/ppermute | solution.py:320
  61.8 0.4 end_state1.1
  62.2 1.3 %collective-permute-start.6 = (bf16[64,1024]{1,0:T(8,128)(2,1)S(1)}, bf16[64,1024]{1,0:T(8,128)(2,1)S(1)}, u32[]{:S(2)}, u32[]{:S(2)}) collective-permute-start(bf16[64,1024]{1,0:T(8,128)(2,1)S(1)} %end_state1.1), channel_id=1, source_target_pairs={{16,24},{18,26},{20,28},{22,30},{17,25},{19,27},{21,29},{23,31}} | collective-permute-start | bytes 393224 | tf_op jit(solution)/shard_map/ppermute | solution.py:320
  63.5 2.2 %fold1.1 = (bf16[128,2048]{1,0:T(8,128)(2,1)S(1)}, bf16[1024,2048]{1,0:T(8,128)(2,1)S(1)}) custom-call(bf16[64,2048]{1,0:T(8,128)(2,1)S(1)} %collective-permute-done.4.got_ref.refs_0_, bf16[64,2048]{1,0:T(8,128)(2,1)S(1)} %collective-permute-done.5.got_ref.refs_1_, bf16[128,1024]{1,0:T(8,128)(2,1)S(1)} %reads1_0.1.after_ref.refs_2_, ...), custom_call_target="tpu_custom_call" | custom-call | tf_op jit(solution)/shard_map/fold1/pallas_call | solution.py:292
  65.7 3.8 %collective-permute-done.6.state_ref = bf16[64,1024]{1,0:T(8,128)(2,1)S(1)} collective-permute-done((bf16[64,1024]{1,0:T(8,128)(2,1)S(1)}, bf16[64,1024]{1,0:T(8,128)(2,1)S(1)}, u32[]{:S(2)}, u32[]{:S(2)}) %collective-permute-start.6) | collective-permute-done | bytes 131104 | tf_op jit(solution)/shard_map/ppermute | solution.py:320
  69.6 1.7 %last_finish.1 = bf16[1,128,2048]{2,1,0:T(8,128)(2,1)} custom-call(bf16[64,1024]{1,0:T(8,128)(2,1)S(1)} %collective-permute-done.6.state_ref, f32[1,16,64,64]{3,2,1,0:T(8,128)S(1)} %copy-done, bf16[128,2048]{1,0:T(8,128)(2,1)S(1)} %get-tuple-element.31.reads_ref, bf16[1024,2048]{1,0:T(8,128)(2,1)S(1)} %get-tuple-element.32.w_out_ref, ...), custom_call_target="tpu_custom_call" | custom-call | tf_op jit(solution)/shard_map/last_finish/pallas_call | solution.py:292
  (6 shorter events, 0.1 us)
Async XLA Ops:
  0.1 0.7 %collective-permute-start = (bf16[64,2048]{1,0:T(8,128)(2,1)S(1)}, bf16[64,2048]{1,0:T(8,128)(2,1)S(1)}, u32[]{:S(2)}, u32[]{:S(2)}) collective-permute-start(bf16[64,2048]{1,0:T(8,128)(2,1)S(1)} %get-tuple-element.19.own_ref), channel_id=1, source_target_pairs={{0,2},{2,4},{4,6},{6,8},{8,10},{10,12},{12,14},{1,3},{3,5},{5,7},{... | collective-permute-start | bytes 786440 | tf_op jit(solution)/shard_map/ppermute | solution.py:320
  0.9 1.0 %copy-start = (f32[1,16,64,64]{3,2,1,0:T(8,128)S(1)}, f32[1,16,64,64]{3,2,1,0:T(8,128)}, u32[]{:S(2)}) copy-start(f32[1,16,64,64]{3,2,1,0:T(8,128)} %init_ref.7) | copy-start | bytes 786436
  0.9 0.9 %collective-permute-start.1 = (bf16[64,2048]{1,0:T(8,128)(2,1)S(1)}, bf16[64,2048]{1,0:T(8,128)(2,1)S(1)}, u32[]{:S(2)}, u32[]{:S(2)}) collective-permute-start(bf16[64,2048]{1,0:T(8,128)(2,1)S(1)} %compose0.1.own_ref), channel_id=1, source_target_pairs={{0,4},{2,6},{4,8},{6,10},{8,12},{10,14},{1,5},{3,7},{5,9},{7,11},{... | collective-permute-start | bytes 786440 | tf_op jit(solution)/shard_map/ppermute | solution.py:320
  1.7 1.1 %copy-start.1 = (bf16[128,2048]{1,0:T(8,128)(2,1)S(1)}, bf16[128,2048]{1,0:T(8,128)(2,1)}, u32[]{:S(2)}) copy-start(bf16[128,2048]{1,0:T(8,128)(2,1)} %h_ref.1) | copy-start | bytes 1572868
  1.9 0.7 collective-permute-start.2
  2.8 36.3 %collective-permute-start.3 = (bf16[128,2048]{1,0:T(8,128)(2,1)S(1)}, bf16[128,2048]{1,0:T(8,128)(2,1)S(1)}, u32[]{:S(2)}, u32[]{:S(2)}) collective-permute-start(bf16[128,2048]{1,0:T(8,128)(2,1)S(1)} %first_finish.1.first_ref), channel_id=1, source_target_pairs={{0,16},{1,17},{2,18},{3,19},{4,20},{5,21},{6,22},{7,23},{8,24},{9,... | collective-permute-start | bytes 1572872 | tf_op jit(solution)/shard_map/ppermute | solution.py:372
  46.4 8.0 %collective-permute-start.4 = (bf16[64,2048]{1,0:T(8,128)(2,1)S(1)}, bf16[64,2048]{1,0:T(8,128)(2,1)S(1)}, u32[]{:S(2)}, u32[]{:S(2)}) collective-permute-start(bf16[64,2048]{1,0:T(8,128)(2,1)S(1)} %get-tuple-element.26.own_ref), channel_id=1, source_target_pairs={{16,18},{18,20},{20,22},{22,24},{24,26},{26,28},{28,30},{17,19},{1... | collective-permute-start | bytes 786440 | tf_op jit(solution)/shard_map/ppermute | solution.py:320
  54.7 7.1 %collective-permute-start.5 = (bf16[64,2048]{1,0:T(8,128)(2,1)S(1)}, bf16[64,2048]{1,0:T(8,128)(2,1)S(1)}, u32[]{:S(2)}, u32[]{:S(2)}) collective-permute-start(bf16[64,2048]{1,0:T(8,128)(2,1)S(1)} %compose1.1.own_ref), channel_id=1, source_target_pairs={{16,20},{18,22},{20,24},{22,26},{24,28},{26,30},{17,21},{19,23},{2... | collective-permute-start | bytes 786440 | tf_op jit(solution)/shard_map/ppermute | solution.py:320
  62.2 7.3 %collective-permute-start.6 = (bf16[64,1024]{1,0:T(8,128)(2,1)S(1)}, bf16[64,1024]{1,0:T(8,128)(2,1)S(1)}, u32[]{:S(2)}, u32[]{:S(2)}) collective-permute-start(bf16[64,1024]{1,0:T(8,128)(2,1)S(1)} %end_state1.1), channel_id=1, source_target_pairs={{16,24},{18,26},{20,28},{22,30},{17,25},{19,27},{21,29},{23,31}} | collective-permute-start | bytes 393224 | tf_op jit(solution)/shard_map/ppermute | solution.py:320

commit v4 on v3

--- a/solution.py
+++ b/solution.py
@@ -201,86 +201,58 @@
     on_section(active, body)
 
 
-def compose(active, own_ref, got_ref, after_ref, out_ref):
-    width = own_ref.shape[1] // 2
-
-    def body():
-        for start in range(0, width, PAIR):
-            s_lanes, b_lanes = slice(start, start + PAIR), slice(width + start, width + start + PAIR)
-            s_own, s_got, b_got = own_ref[:, s_lanes], got_ref[:, s_lanes], got_ref[:, b_lanes]
-            step = mm(s_own, spread_two(s_got, b_got))
-            out_ref[:, s_lanes] = (s_own.astype(F32) + s_got.astype(F32) - step[:, :PAIR]).astype(BF16)
-            out_ref[:, b_lanes] = (own_ref[:, b_lanes].astype(F32) + b_got.astype(F32) - step[:, PAIR:]).astype(BF16)
-
-    on_section(active, body)
-
-
 def pair_state(init_ref, pair):
     return jnp.concatenate([init_ref[0, 2 * pair], init_ref[0, 2 * pair + 1]], axis=1)
 
 
-def end_state(active, own_ref, got_ref, init_ref, after_ref, out_ref):
-    width = own_ref.shape[1] // 2
+def finish(active, table, init_ref, reads_refs, w_hbm, h_ref, out_ref, state, w_out, sems):
+    width = state.shape[1]
+    part = width // 2
+    model = w_out.shape[1]
+    chunk = model // 4
 
     def body():
-        states = [pair_state(init_ref, pair) for pair in range(width // PAIR)]
-        for ref in (got_ref, own_ref):
-            for pair, state in enumerate(states):
-                start = pair * PAIR
-                step = mm(ref[:, start : start + PAIR], spread(state.astype(BF16)))
-                states[pair] = state - step + ref[:, width + start : width + start + PAIR].astype(F32)
-        for pair, state in enumerate(states):
-            out_ref[:, pair * PAIR : (pair + 1) * PAIR] = state.astype(BF16)
-
-    on_section(active, body)
-
-
-def fold(active, count, *refs):
-    got_refs = refs[:count]
-    reads_refs = refs[count : count + 2]
-    w_hbm, out_ref, w_out, sem = refs[count + 2 :]
-    width = out_ref.shape[1] // 2
-    part = width // 2
-
-    def body():
-        load = pltpu.make_async_copy(w_hbm.at[0], w_out, sem)
-        load.start()
-        for start in range(0, width, PAIR):
-            reads_ref = reads_refs[start // part]
-            inner = start % part
-            left = reads_ref[:, inner : inner + PAIR].astype(F32)
-            offset = reads_ref[:, part + inner : part + inner + PAIR].astype(F32)
-            for ref in got_refs:
-                step = mm(left.astype(BF16), spread_two(ref[:, start : start + PAIR], ref[:, width + start : width + start + PAIR]))
-                left = left - step[:, :PAIR]
-                offset = offset + step[:, PAIR:]
-            out_ref[:, start : start + PAIR] = left.astype(BF16)
-            out_ref[:, width + start : width + start + PAIR] = offset.astype(BF16)
-        load.wait()
-
-    on_section(active, body)
-
-
-def finish(active, count, state_ref, init_ref, reads_ref, w_out_ref, h_ref, out_ref):
-    width = reads_ref.shape[1] // 2
-
-    def body():
-        begins = lax.axis_index("seq") < count // 2
+        loads = [
+            pltpu.make_async_copy(
+                w_hbm.at[0, :, pl.ds(index * chunk, chunk)], w_out.at[:, pl.ds(index * chunk, chunk)], sems.at[index]
+            )
+            for index in range(4)
+        ]
+        for load in loads:
+            load.start()
+        for pair in range(width // PAIR):
+            state[:, pair * PAIR : (pair + 1) * PAIR] = pair_state(init_ref, pair)
+
+        @pl.loop(0, lax.axis_index("seq"))
+        def _(slab):
+            for start in range(0, width, PAIR):
+                lanes = slice(start, start + PAIR)
+                before = state[:, lanes]
+                step = mm(table[slab, :, lanes], spread(before.astype(BF16)))
+                state[:, lanes] = before - step + table[slab, :, width + start : width + start + PAIR].astype(F32)
+
         parts = []
         for start in range(0, width, QUAD):
             lanes = slice(start, start + QUAD)
-            init = jnp.concatenate([pair_state(init_ref, start // PAIR), pair_state(init_ref, start // PAIR + 1)], axis=1)
-            state = jnp.where(begins, init.astype(BF16), state_ref[:, lanes])
-            offset = reads_ref[:, width + start : width + start + QUAD]
-            parts.append((mm(reads_ref[:, lanes], spread(state)) + offset.astype(F32)).astype(BF16))
+            reads_ref, inner = reads_refs[start // part], start % part
+            offset = reads_ref[:, part + inner : part + inner + QUAD]
+            read = mm(reads_ref[:, inner : inner + QUAD], spread(state[:, lanes].astype(BF16)))
+            parts.append((read + offset.astype(F32)).astype(BF16))
         inner_bf = jnp.concatenate(parts, axis=1)
-        out_ref[...] = (h_ref[...].astype(F32) + mm(inner_bf, w_out_ref[...])).astype(BF16)
+        for index, load in enumerate(loads):
+            load.wait()
+            lanes = slice(index * chunk, (index + 1) * chunk)
+            out_ref[:, lanes] = (h_ref[:, lanes].astype(F32) + mm(inner_bf, w_out[:, lanes])).astype(BF16)
 
     on_section(active, body)
 
 
-def last_finish(count, state_ref, init_ref, reads_ref, w_out_ref, h_ref, first_ref, out_ref):
-    finish(1, count, state_ref, init_ref, reads_ref, w_out_ref, h_ref, out_ref.at[0])
+def first_finish(table, init_ref, reads_a, reads_b, w_hbm, h_ref, out_ref, state, w_out, sems):
+    finish(0, table, init_ref, (reads_a, reads_b), w_hbm, h_ref, out_ref, state, w_out, sems)
+
+
+def last_finish(table, init_ref, reads_a, reads_b, w_hbm, h_ref, first_ref, out_ref, state, w_out, sems):
+    finish(1, table, init_ref, (reads_a, reads_b), w_hbm, h_ref, out_ref.at[0], state, w_out, sems)
 
     @pl.when(lax.axis_index("section") == 0)
     def _():
@@ -301,26 +273,17 @@
 
 
 def shards(tokens, norm_gain, w_qkv, w_rate, rate_base, init_state, w_out):
-    count = lax.axis_size("seq")
     heads = rate_base.shape[1]
     rows, model = tokens.shape
     width = heads * HD
     depth = w_qkv.shape[1]
     quads = width // QUAD
     shape = jax.ShapeDtypeStruct
-    in_vmem = functools.partial(pltpu.with_memory_space_constraint, memory_space=pltpu.VMEM)
     in_hbm = functools.partial(pltpu.with_memory_space_constraint, memory_space=pltpu.HBM)
     maps = shape((HD, 2 * width), BF16)
     rows_out = [shape((rows, model), BF16)] + [shape((rows, width), BF16)] * 3
     w_rate = jnp.swapaxes(w_rate, 1, 2)
     norm_gain, w_qkv, w_rate, rate_base, w_out = [in_hbm(value) for value in (norm_gain, w_qkv, w_rate, rate_base, w_out)]
-
-    def ahead(value, active, steps):
-        pairs = [(active * count + place, active * count + place + steps) for place in range(count - steps)]
-        return lax.ppermute(value, ("section", "seq"), pairs)
-
-    def run(active, body, outs, scratch, args, kinds=None):
-        return call(functools.partial(body, active), outs, scratch, args, kinds, name=body.__name__ + str(active))
 
     def layer(active, hidden):
         h_scratch = [] if active else [pltpu.VMEM(hidden.shape, hidden.dtype)]
@@ -348,30 +311,14 @@
             )[0]
 
         reads = [reads_of(tuple(range(quads // 2))), reads_of(tuple(range(quads // 2, quads)))]
-        got = [ahead(own, active, 1)]
-        steps = 2
-        while steps < count // 2:
-            (own,) = run(active, compose, [maps], [], [own, got[-1], reads[0]], [pltpu.VMEM] * 2 + [pl.ANY])
-            got.append(ahead(own, active, steps))
-            steps *= 2
-        (state,) = run(
-            active, end_state, [shape((HD, width), BF16)], [], [own, got[-1], init_state, reads[1]], [pltpu.VMEM] * 3 + [pl.ANY]
-        )
-        state = ahead(state, active, steps)
-        folded, w_out_near = call(
-            functools.partial(fold, active, len(got)),
-            [shape((rows, 2 * width), BF16), pltpu.VMEM(w_out.shape[1:], BF16)],
-            [pltpu.SemaphoreType.DMA],
-            got + reads + [w_out],
-            [pltpu.VMEM] * (len(got) + 2) + [pltpu.HBM],
-            name=f"fold{active}",
-        )
-        return [state, init_state, folded, in_vmem(w_out_near), hidden]
-
-    (first,) = call(functools.partial(finish, 0, count), [shape((rows, model), BF16)], [], layer(0, tokens), name="first_finish")
+        return [lax.all_gather(own, "seq"), init_state, *reads, w_out, hidden]
+
+    scratch = [pltpu.VMEM((HD, width), F32), pltpu.VMEM(w_out.shape[1:], BF16), pltpu.SemaphoreType.DMA((4,))]
+    kinds = [pltpu.VMEM] * 4 + [pltpu.HBM] + [pltpu.VMEM]
+    (first,) = call(first_finish, [shape((rows, model), BF16)], scratch, layer(0, tokens), kinds, name="first_finish")
     hidden = lax.ppermute(first, "section", [(0, 1)])
     (result,) = call(
-        functools.partial(last_finish, count), [shape((1, rows, model), BF16)], [], layer(1, hidden) + [first], name="last_finish"
+        last_finish, [shape((1, rows, model), BF16)], scratch, layer(1, hidden) + [first], kinds + [pltpu.VMEM], name="last_finish"
     )
     return result
 

time: 71.6 us -> 141 us (1.97)
  waiting for transfers between devices: 44 us -> 102 us
  between operations: 0.19 us -> 13.5 us
  starting transfers between devices: 8.2 us -> 1.34 us
  local copies, waits for them, and re-layouts: 0.36 us -> 3.19 us
    all_gather x0 -> x2, waiting for transfers between devices: none -> 97.4 us  [layer(): return [lax.all_gather(own, 'seq'), init_state, *reads, w_out, hidden]]
    ppermute x1, waiting for transfers between devices: 35 us -> 5.07 us  [shards(): hidden = lax.ppermute(first, 'section', [(0, 1)])]
    ppermute x6 -> x0, waiting for transfers between devices: 9.01 us -> none  [ahead(): return lax.ppermute(value, ('section', 'seq'), pairs)]
    ppermute x6 -> x0, starting transfers between devices: 6.92 us -> none  [ahead(): return lax.ppermute(value, ('section', 'seq'), pairs)]
    unnamed x4 -> x8, local copies, waits for them, and re-layouts: 0.36 us -> 3.19 us
    pallas_call x14 -> x8, Pallas kernels: 18.5 us -> 19 us  [call(): pl.pallas_call(body, out_shape=outs, in_specs=specs, out_specs=[pl.BlockS...]
  transfers between devices with their start and end apart: 7 -> 3, of which waited for: 4 -> 3; matrix products, arithmetic and copies ran while one was open for 0% -> 0% of each run, Pallas kernels for 12% -> 5%
where the time goes in v4:
time: 141 us; the launch traced here: 139 us
  waiting for transfers between devices  102 us (72%)
  Pallas kernels  19 us (13%)
  between operations  13.5 us (10%)
  local copies, waits for them, and re-layouts  3.19 us (2%)
    all_gather x2, waiting for transfers between devices, layer(): return [lax.all_gather(own, 'seq'), init_state, *reads, w_out, hidden]  97.4 us
    pallas_call x8, Pallas kernels, call(): pl.pallas_call(body, out_shape=outs, in_specs=specs, out_specs=[pl.BlockS...  19 us
    ppermute x1, waiting for transfers between devices, shards(): hidden = lax.ppermute(first, 'section', [(0, 1)])  5.07 us
    unnamed x8, local copies, waits for them, and re-layouts  3.19 us
  transfers between devices with their start and end apart: 3, of which 3 were waited for; matrix products, arithmetic and copies ran while one was open for 0% of the time, Pallas kernels for 5%

profile of v4, /device:TPU:25, one launch (start us, length us, event | category | flops | bytes accessed | tf_op | source)
XLA Modules:
  0.0 139.5 jit_solution(1310257533371734421)
XLA Ops:
  6.5 0.0 all-gather.5.cloned.1.call-start
  6.5 0.8 first_front.1
  7.4 0.0 all-gather.5.cloned.1.call-update
  7.4 0.0 all-gather.7.cloned.1.call-start
  7.5 0.0 copy-start.1
  7.5 0.0 copy-start.2
  7.5 56.1 %all-gather.5.cloned.1.call-done = bf16[512,2048]{1,0:T(8,128)(2,1)} async-done(((bf16[64,2048]{1,0:T(8,128)(2,1)}), bf16[512,2048]{1,0:T(8,128)(2,1)}) %all-gather.5.cloned.1.call-update) | async-done | bytes 2097168 | tf_op jit(solution)/shard_map/all_gather | solution.py:314
  63.6 0.0 copy-done.1
  63.6 0.0 copy-done.2
  63.6 0.0 copy-start.3
  63.6 1.6 %copy-done.3 = bf16[512,2048]{1,0:T(8,128)(2,1)S(1)} copy-done((bf16[512,2048]{1,0:T(8,128)(2,1)S(1)}, bf16[512,2048]{1,0:T(8,128)(2,1)}, u32[]{:S(2)}) %copy-start.3) | copy-done | bytes 2097176
  65.3 1.3 collective-permute-start
  66.6 5.1 %collective-permute-done.h_ref = bf16[128,2048]{1,0:T(8,128)(2,1)S(1)} collective-permute-done((bf16[128,2048]{1,0:T(8,128)(2,1)S(1)}, bf16[128,2048]{1,0:T(8,128)(2,1)S(1)}, u32[]{:S(2)}, u32[]{:S(2)}) %collective-permute-start) | collective-permute-done | bytes 524320 | tf_op jit(solution)/shard_map/ppermute | solution.py:319
  71.6 8.0 %later_front.1 = (bf16[64,2048]{1,0:T(8,128)(2,1)}, bf16[128,2048]{1,0:T(8,128)(2,1)S(1)}, bf16[128,1024]{1,0:T(8,128)(2,1)S(1)}, bf16[128,1024]{1,0:T(8,128)(2,1)S(1)}, bf16[128,1024]{1,0:T(8,128)(2,1)S(1)}) custom-call(bf16[128,2048]{1,0:T(8,128)(2,1)S(1)} %collective-permute-done.h_ref, f32[1,2048]{1,0:T(1,128)} %rest_0_.3, ...), custom_call_target="tpu_custom_call" | custom-call | tf_op jit(solution)/shard_map/later_front/pallas_call | solution.py:264
  79.6 0.0 all-gather.7.cloned.1.call-update
  79.7 3.1 %reads1_2.1.reads_b = bf16[128,1024]{1,0:T(8,128)(2,1)S(1)} custom-call(bf16[128,2048]{1,0:T(8,128)(2,1)S(1)} %get-tuple-element.21.normed_ref, bf16[128,1024]{1,0:T(8,128)(2,1)S(1)} %get-tuple-element.22.keys_ref, bf16[128,1024]{1,0:T(8,128)(2,1)S(1)} %get-tuple-element.23.x_ref, bf16[128,1024]{1,0:T(8,128)(2,1)S(1)} %get-tuple-element.24.y_ref, ...), custom_call_target="tpu_custom_call" | custom-call | tf_op jit(solution)/shard_map/reads1_2/pallas_call | solution.py:264
  82.8 3.1 %reads1_0.1.reads_a = bf16[128,1024]{1,0:T(8,128)(2,1)S(1)} custom-call(bf16[128,2048]{1,0:T(8,128)(2,1)S(1)} %get-tuple-element.21.normed_ref, bf16[128,1024]{1,0:T(8,128)(2,1)S(1)} %get-tuple-element.22.keys_ref, bf16[128,1024]{1,0:T(8,128)(2,1)S(1)} %get-tuple-element.23.x_ref, bf16[128,1024]{1,0:T(8,128)(2,1)S(1)} %get-tuple-element.24.y_ref, ...), custom_call_target="tpu_custom_call" | custom-call | tf_op jit(solution)/shard_map/reads1_0/pallas_call | solution.py:264
  85.9 41.3 %all-gather.7.cloned.1.call-done = bf16[512,2048]{1,0:T(8,128)(2,1)} async-done(((bf16[64,2048]{1,0:T(8,128)(2,1)}), bf16[512,2048]{1,0:T(8,128)(2,1)}) %all-gather.7.cloned.1.call-update) | async-done | bytes 2097168 | tf_op jit(solution)/shard_map/all_gather | solution.py:314
  127.2 0.0 copy-start
  127.2 1.6 %copy-done = bf16[512,2048]{1,0:T(8,128)(2,1)S(1)} copy-done((bf16[512,2048]{1,0:T(8,128)(2,1)S(1)}, bf16[512,2048]{1,0:T(8,128)(2,1)}, u32[]{:S(2)}) %copy-start) | copy-done | bytes 2097176
  128.8 3.8 %last_finish.1 = bf16[1,128,2048]{2,1,0:T(8,128)(2,1)} custom-call(bf16[8,64,2048]{2,1,0:T(8,128)(2,1)S(1)} %bitcast.3, f32[1,16,64,64]{3,2,1,0:T(8,128)S(1)} %copy-done.2, bf16[128,1024]{1,0:T(8,128)(2,1)S(1)} %reads1_0.1.reads_a, bf16[128,1024]{1,0:T(8,128)(2,1)S(1)} %reads1_2.1.reads_b, bf16[1,1024,2048]{2,1,0:T(8,128)(2,1)} %w_hbm.11, ...), custom_call_target="tpu_custom_call" | custom-call | tf_op jit(solution)/shard_map/last_finish/pallas_call | solution.py:264
  (3 shorter events, 0.1 us)
Async XLA Ops:
  6.5 57.1 %all-gather.5.cloned.1.call-start = ((), (), s32[]{:S(2)}) async-start(), calls=%async_computation | async-start | bytes 2359296 | tf_op jit(solution)/shard_map/all_gather | solution.py:314
  7.4 119.9 %all-gather.7.cloned.1.call-start = ((), (), s32[]{:S(2)}) async-start(), calls=%async_computation.1 | async-start | bytes 2359296 | tf_op jit(solution)/shard_map/all_gather | solution.py:314
  7.5 56.2 %copy-start.1 = (bf16[128,2048]{1,0:T(8,128)(2,1)S(1)}, bf16[128,2048]{1,0:T(8,128)(2,1)}, u32[]{:S(2)}) copy-start(bf16[128,2048]{1,0:T(8,128)(2,1)} %h_ref.1) | copy-start | bytes 1572868
  7.5 56.1 %copy-start.2 = (f32[1,16,64,64]{3,2,1,0:T(8,128)S(1)}, f32[1,16,64,64]{3,2,1,0:T(8,128)}, u32[]{:S(2)}) copy-start(f32[1,16,64,64]{3,2,1,0:T(8,128)} %init_ref.3) | copy-start | bytes 786436
  63.6 1.6 %copy-start.3 = (bf16[512,2048]{1,0:T(8,128)(2,1)S(1)}, bf16[512,2048]{1,0:T(8,128)(2,1)}, u32[]{:S(2)}) copy-start(bf16[512,2048]{1,0:T(8,128)(2,1)} %all-gather.5.cloned.1.call-done) | copy-start | bytes 6291460
  65.3 6.4 %collective-permute-start = (bf16[128,2048]{1,0:T(8,128)(2,1)S(1)}, bf16[128,2048]{1,0:T(8,128)(2,1)S(1)}, u32[]{:S(2)}, u32[]{:S(2)}) collective-permute-start(bf16[128,2048]{1,0:T(8,128)(2,1)S(1)} %first_finish.1.first_ref), channel_id=1, source_target_pairs={{0,16},{1,17},{2,18},{3,19},{4,20},{5,21},{6,22},{7,23},{8,24},{9,... | collective-permute-start | bytes 1572872 | tf_op jit(solution)/shard_map/ppermute | solution.py:319
  127.2 1.6 %copy-start = (bf16[512,2048]{1,0:T(8,128)(2,1)S(1)}, bf16[512,2048]{1,0:T(8,128)(2,1)}, u32[]{:S(2)}) copy-start(bf16[512,2048]{1,0:T(8,128)(2,1)} %all-gather.7.cloned.1.call-done) | copy-start | bytes 6291460
Sparse Core Ops, SparseCore 0:
  9.5 54.0 all-gather.4
  79.8 47.3 all-gather.6

commit v5 on v3

--- a/solution.py
+++ b/solution.py
@@ -76,16 +76,16 @@
     return mm(high, pick) + mm(low, pick)
 
 
-def staged(groups):
-    for group in groups[:2]:
+def staged(groups, depth=3):
+    for group in groups[:depth]:
         for copy in group:
             copy.start()
 
     def wait(index):
         for copy in groups[index]:
             copy.wait()
-        if index + 2 < len(groups):
-            for copy in groups[index + 2]:
+        if index + depth < len(groups):
+            for copy in groups[index + depth]:
                 copy.start()
 
     return wait
@@ -125,11 +125,14 @@
         normed_out[...] = normed
         rates = spread_rates(normed, w_rate[0], base[...])
         ones = head_ones()
-        for quad in range(quads):
+
+        def project(quad):
             wait_group(quad)
             lanes = slice(quad * QUAD, (quad + 1) * QUAD)
-            keys = mm(normed, wkv[:, lanes])
-            values = mm(normed, wkv[:, width + quad * QUAD : width + (quad + 1) * QUAD])
+            return mm(normed, wkv[:, lanes]), mm(normed, wkv[:, width + quad * QUAD : width + (quad + 1) * QUAD])
+
+        def chain(quad, keys, values):
+            lanes = slice(quad * QUAD, (quad + 1) * QUAD)
             keys = unit_heads(keys, ones)
             keys_bf = keys.astype(BF16)
             keys_out[:, lanes] = keys_bf
@@ -151,6 +154,13 @@
                 both = mm_tn(keys_bf[:, own], jnp.concatenate([x_bf[:, own], y_bf[:, own]], axis=1))
                 maps[:, start : start + PAIR] = diagonal(both[:, :PAIR]).astype(BF16)
                 maps[:, width + start : width + start + PAIR] = diagonal(both[:, PAIR:]).astype(BF16)
+
+        before = project(0)
+        for quad in range(1, quads):
+            after = project(quad)
+            chain(quad - 1, *before)
+            before = after
+        chain(quads - 1, *before)
 
     on_section(active, body)
 
@@ -261,8 +271,10 @@
     on_section(active, body)
 
 
-def finish(active, count, state_ref, init_ref, reads_ref, w_out_ref, h_ref, out_ref):
+def finish(active, count, state_ref, init_ref, reads_ref, w_out_ref, h_ref, store):
     width = reads_ref.shape[1] // 2
+    model = h_ref.shape[1]
+    chunk = model // 4
 
     def body():
         begins = lax.axis_index("seq") < count // 2
@@ -274,26 +286,49 @@
             offset = reads_ref[:, width + start : width + start + QUAD]
             parts.append((mm(reads_ref[:, lanes], spread(state)) + offset.astype(F32)).astype(BF16))
         inner_bf = jnp.concatenate(parts, axis=1)
-        out_ref[...] = (h_ref[...].astype(F32) + mm(inner_bf, w_out_ref[...])).astype(BF16)
-
-    on_section(active, body)
-
-
-def last_finish(count, state_ref, init_ref, reads_ref, w_out_ref, h_ref, first_ref, out_ref):
-    finish(1, count, state_ref, init_ref, reads_ref, w_out_ref, h_ref, out_ref.at[0])
+        for start in range(0, model, chunk):
+            lanes = slice(start, start + chunk)
+            store(start, (h_ref[:, lanes].astype(F32) + mm(inner_bf, w_out_ref[:, lanes])).astype(BF16))
+
+    on_section(active, body)
+
+
+def first_finish(count, state_ref, init_ref, reads_ref, w_out_ref, h_ref, out_ref):
+    def store(start, value):
+        out_ref[:, start : start + value.shape[1]] = value
+
+    finish(0, count, state_ref, init_ref, reads_ref, w_out_ref, h_ref, store)
+
+
+def last_finish(count, state_ref, init_ref, reads_ref, w_out_ref, h_ref, first_ref, out_hbm, near, sems):
+    chunk = near.shape[1] // 4
+
+    def write(start):
+        lanes = pl.ds(start, chunk)
+        return pltpu.make_async_copy(near.at[:, lanes], out_hbm.at[0, :, lanes], sems.at[start // chunk])
+
+    def store(start, value):
+        near[:, start : start + chunk] = value
+        write(start).start()
+
+    finish(1, count, state_ref, init_ref, reads_ref, w_out_ref, h_ref, store)
 
     @pl.when(lax.axis_index("section") == 0)
     def _():
-        out_ref[0] = first_ref[...]
-
-
-def call(body, outs, scratch, args, kinds=None, name=None):
+        for start in range(0, near.shape[1], chunk):
+            store(start, first_ref[:, start : start + chunk])
+
+    for start in range(0, near.shape[1], chunk):
+        write(start).wait()
+
+
+def call(body, outs, scratch, args, kinds=None, name=None, out_kind=pltpu.VMEM):
     specs = [pl.BlockSpec(memory_space=kind) for kind in (kinds or [pltpu.VMEM] * len(args))]
     return pl.pallas_call(
         body,
         out_shape=outs,
         in_specs=specs,
-        out_specs=[pl.BlockSpec(memory_space=pltpu.VMEM)] * len(outs),
+        out_specs=[pl.BlockSpec(memory_space=out_kind)] * len(outs),
         scratch_shapes=scratch,
         compiler_params=pltpu.CompilerParams(vmem_limit_bytes=VMEM_LIMIT),
         name=name,
@@ -368,10 +403,15 @@
         )
         return [state, init_state, folded, in_vmem(w_out_near), hidden]
 
-    (first,) = call(functools.partial(finish, 0, count), [shape((rows, model), BF16)], [], layer(0, tokens), name="first_finish")
+    (first,) = call(functools.partial(first_finish, count), [shape((rows, model), BF16)], [], layer(0, tokens), name="first_finish")
     hidden = lax.ppermute(first, "section", [(0, 1)])
     (result,) = call(
-        functools.partial(last_finish, count), [shape((1, rows, model), BF16)], [], layer(1, hidden) + [first], name="last_finish"
+        functools.partial(last_finish, count),
+        [shape((1, rows, model), BF16)],
+        [pltpu.VMEM((rows, model), BF16), pltpu.SemaphoreType.DMA((4,))],
+        layer(1, hidden) + [first],
+        name="last_finish",
+        out_kind=pltpu.HBM,
     )
     return result
 

time: 71.6 us -> 72.2 us (level)
  no operation moved by 1% of the time
where the time goes in v5:
time: 72.2 us; the launch traced here: 71.9 us
  waiting for transfers between devices  44.2 us (61%)
  Pallas kernels  18.7 us (26%)
  starting transfers between devices  8.21 us (11%)
    ppermute x1, waiting for transfers between devices, shards(): hidden = lax.ppermute(first, 'section', [(0, 1)])  35.2 us
    pallas_call x14, Pallas kernels, call(): pl.pallas_call(body, out_shape=outs, in_specs=specs, out_specs=[pl.BlockS...  18.7 us
    ppermute x6, waiting for transfers between devices, ahead(): return lax.ppermute(value, ('section', 'seq'), pairs)  9 us
    ppermute x6, starting transfers between devices, ahead(): return lax.ppermute(value, ('section', 'seq'), pairs)  6.93 us
  transfers between devices with their start and end apart: 7, of which 4 were waited for; matrix products, arithmetic and copies ran while one was open for 0% of the time, Pallas kernels for 12%

profile of v5, /device:TPU:25, one launch (start us, length us, event | category | flops | bytes accessed | tf_op | source)
XLA Modules:
  0.0 71.9 jit_solution(7847120821903546324)
XLA Ops:
  0.0 0.1 first_front.1
  0.1 0.7 collective-permute-start
  0.8 0.0 collective-permute-done.got_ref.refs_0_
  0.9 0.0 copy-start
  0.9 0.8 %collective-permute-start.1 = (bf16[64,2048]{1,0:T(8,128)(2,1)S(1)}, bf16[64,2048]{1,0:T(8,128)(2,1)S(1)}, u32[]{:S(2)}, u32[]{:S(2)}) collective-permute-start(bf16[64,2048]{1,0:T(8,128)(2,1)S(1)} %compose0.1.own_ref), channel_id=1, source_target_pairs={{0,4},{2,6},{4,8},{6,10},{8,12},{10,14},{1,5},{3,7},{5,9},{7,11},{... | collective-permute-start | bytes 786440 | tf_op jit(solution)/shard_map/ppermute | solution.py:355
  1.7 0.0 copy-start.1
  1.8 0.0 collective-permute-done.1.got_ref.refs_1_
  1.8 0.2 copy-done
  1.9 0.7 collective-permute-start.2
  2.6 0.0 collective-permute-done.2.state_ref
  2.6 0.2 copy-done.1
  2.8 1.3 %collective-permute-start.3 = (bf16[128,2048]{1,0:T(8,128)(2,1)S(1)}, bf16[128,2048]{1,0:T(8,128)(2,1)S(1)}, u32[]{:S(2)}, u32[]{:S(2)}) collective-permute-start(bf16[128,2048]{1,0:T(8,128)(2,1)S(1)} %first_finish.1.first_ref), channel_id=1, source_target_pairs={{0,16},{1,17},{2,18},{3,19},{4,20},{5,21},{6,22},{7,23},{8,24},{9,... | collective-permute-start | bytes 1572872 | tf_op jit(solution)/shard_map/ppermute | solution.py:407
  4.1 35.2 %collective-permute-done.3.h_ref = bf16[128,2048]{1,0:T(8,128)(2,1)S(1)} collective-permute-done((bf16[128,2048]{1,0:T(8,128)(2,1)S(1)}, bf16[128,2048]{1,0:T(8,128)(2,1)S(1)}, u32[]{:S(2)}, u32[]{:S(2)}) %collective-permute-start.3) | collective-permute-done | bytes 524320 | tf_op jit(solution)/shard_map/ppermute | solution.py:407
  39.4 7.6 %later_front.1 = (bf16[64,2048]{1,0:T(8,128)(2,1)S(1)}, bf16[128,2048]{1,0:T(8,128)(2,1)S(1)}, bf16[128,1024]{1,0:T(8,128)(2,1)S(1)}, bf16[128,1024]{1,0:T(8,128)(2,1)S(1)}, bf16[128,1024]{1,0:T(8,128)(2,1)S(1)}) custom-call(bf16[128,2048]{1,0:T(8,128)(2,1)S(1)} %collective-permute-done.3.h_ref, f32[1,2048]{1,0:T(1,128)} %rest_0_.3, ...), custom_call_target="tpu_custom_call" | custom-call | tf_op jit(solution)/shard_map/later_front/pallas_call | solution.py:327
  46.9 2.2 %collective-permute-start.4 = (bf16[64,2048]{1,0:T(8,128)(2,1)S(1)}, bf16[64,2048]{1,0:T(8,128)(2,1)S(1)}, u32[]{:S(2)}, u32[]{:S(2)}) collective-permute-start(bf16[64,2048]{1,0:T(8,128)(2,1)S(1)} %get-tuple-element.26.own_ref), channel_id=1, source_target_pairs={{16,18},{18,20},{20,22},{22,24},{24,26},{26,28},{28,30},{17,19},{1... | collective-permute-start | bytes 786440 | tf_op jit(solution)/shard_map/ppermute | solution.py:355
  49.2 3.1 %reads1_0.1.after_ref.refs_2_ = bf16[128,1024]{1,0:T(8,128)(2,1)S(1)} custom-call(bf16[128,2048]{1,0:T(8,128)(2,1)S(1)} %get-tuple-element.27.normed_ref, bf16[128,1024]{1,0:T(8,128)(2,1)S(1)} %get-tuple-element.28.keys_ref, bf16[128,1024]{1,0:T(8,128)(2,1)S(1)} %get-tuple-element.29.x_ref, bf16[128,1024]{1,0:T(8,128)(2,1)S(1)} %get-tuple-element.30.y_ref, ...), custom_call_target="tpu_custom_call" | custom-call | tf_op jit(solution)/shard_map/reads1_0/pallas_call | solution.py:327
  52.3 2.7 %collective-permute-done.4.got_ref.refs_0_ = bf16[64,2048]{1,0:T(8,128)(2,1)S(1)} collective-permute-done((bf16[64,2048]{1,0:T(8,128)(2,1)S(1)}, bf16[64,2048]{1,0:T(8,128)(2,1)S(1)}, u32[]{:S(2)}, u32[]{:S(2)}) %collective-permute-start.4) | collective-permute-done | bytes 262176 | tf_op jit(solution)/shard_map/ppermute | solution.py:355
  55.0 0.2 compose1.1.own_ref
  55.2 1.3 %collective-permute-start.5 = (bf16[64,2048]{1,0:T(8,128)(2,1)S(1)}, bf16[64,2048]{1,0:T(8,128)(2,1)S(1)}, u32[]{:S(2)}, u32[]{:S(2)}) collective-permute-start(bf16[64,2048]{1,0:T(8,128)(2,1)S(1)} %compose1.1.own_ref), channel_id=1, source_target_pairs={{16,20},{18,22},{20,24},{22,26},{24,28},{26,30},{17,21},{19,23},{2... | collective-permute-start | bytes 786440 | tf_op jit(solution)/shard_map/ppermute | solution.py:355
  56.5 3.3 %reads1_2.1.after_ref.refs_3_ = bf16[128,1024]{1,0:T(8,128)(2,1)S(1)} custom-call(bf16[128,2048]{1,0:T(8,128)(2,1)S(1)} %get-tuple-element.27.normed_ref, bf16[128,1024]{1,0:T(8,128)(2,1)S(1)} %get-tuple-element.28.keys_ref, bf16[128,1024]{1,0:T(8,128)(2,1)S(1)} %get-tuple-element.29.x_ref, bf16[128,1024]{1,0:T(8,128)(2,1)S(1)} %get-tuple-element.30.y_ref, ...), custom_call_target="tpu_custom_call" | custom-call | tf_op jit(solution)/shard_map/reads1_2/pallas_call | solution.py:327
  59.8 2.5 %collective-permute-done.5.got_ref.refs_1_ = bf16[64,2048]{1,0:T(8,128)(2,1)S(1)} collective-permute-done((bf16[64,2048]{1,0:T(8,128)(2,1)S(1)}, bf16[64,2048]{1,0:T(8,128)(2,1)S(1)}, u32[]{:S(2)}, u32[]{:S(2)}) %collective-permute-start.5) | collective-permute-done | bytes 262176 | tf_op jit(solution)/shard_map/ppermute | solution.py:355
  62.3 0.4 end_state1.1
  62.7 1.3 %collective-permute-start.6 = (bf16[64,1024]{1,0:T(8,128)(2,1)S(1)}, bf16[64,1024]{1,0:T(8,128)(2,1)S(1)}, u32[]{:S(2)}, u32[]{:S(2)}) collective-permute-start(bf16[64,1024]{1,0:T(8,128)(2,1)S(1)} %end_state1.1), channel_id=1, source_target_pairs={{16,24},{18,26},{20,28},{22,30},{17,25},{19,27},{21,29},{23,31}} | collective-permute-start | bytes 393224 | tf_op jit(solution)/shard_map/ppermute | solution.py:355
  64.0 2.2 %fold1.1 = (bf16[128,2048]{1,0:T(8,128)(2,1)S(1)}, bf16[1024,2048]{1,0:T(8,128)(2,1)S(1)}) custom-call(bf16[64,2048]{1,0:T(8,128)(2,1)S(1)} %collective-permute-done.4.got_ref.refs_0_, bf16[64,2048]{1,0:T(8,128)(2,1)S(1)} %collective-permute-done.5.got_ref.refs_1_, bf16[128,1024]{1,0:T(8,128)(2,1)S(1)} %reads1_0.1.after_ref.refs_2_, ...), custom_call_target="tpu_custom_call" | custom-call | tf_op jit(solution)/shard_map/fold1/pallas_call | solution.py:327
  66.3 3.8 %collective-permute-done.6.state_ref = bf16[64,1024]{1,0:T(8,128)(2,1)S(1)} collective-permute-done((bf16[64,1024]{1,0:T(8,128)(2,1)S(1)}, bf16[64,1024]{1,0:T(8,128)(2,1)S(1)}, u32[]{:S(2)}, u32[]{:S(2)}) %collective-permute-start.6) | collective-permute-done | bytes 131104 | tf_op jit(solution)/shard_map/ppermute | solution.py:355
  70.1 1.6 %last_finish.1 = bf16[1,128,2048]{2,1,0:T(8,128)(2,1)} custom-call(bf16[64,1024]{1,0:T(8,128)(2,1)S(1)} %collective-permute-done.6.state_ref, f32[1,16,64,64]{3,2,1,0:T(8,128)S(1)} %copy-done, bf16[128,2048]{1,0:T(8,128)(2,1)S(1)} %get-tuple-element.31.reads_ref, bf16[1024,2048]{1,0:T(8,128)(2,1)S(1)} %get-tuple-element.32.w_out_ref, ...), custom_call_target="tpu_custom_call" | custom-call | tf_op jit(solution)/shard_map/last_finish/pallas_call | solution.py:327
  (6 shorter events, 0.1 us)
Async XLA Ops:
  0.1 0.7 %collective-permute-start = (bf16[64,2048]{1,0:T(8,128)(2,1)S(1)}, bf16[64,2048]{1,0:T(8,128)(2,1)S(1)}, u32[]{:S(2)}, u32[]{:S(2)}) collective-permute-start(bf16[64,2048]{1,0:T(8,128)(2,1)S(1)} %get-tuple-element.19.own_ref), channel_id=1, source_target_pairs={{0,2},{2,4},{4,6},{6,8},{8,10},{10,12},{12,14},{1,3},{3,5},{5,7},{... | collective-permute-start | bytes 786440 | tf_op jit(solution)/shard_map/ppermute | solution.py:355
  0.9 1.0 %copy-start = (f32[1,16,64,64]{3,2,1,0:T(8,128)S(1)}, f32[1,16,64,64]{3,2,1,0:T(8,128)}, u32[]{:S(2)}) copy-start(f32[1,16,64,64]{3,2,1,0:T(8,128)} %init_ref.7) | copy-start | bytes 786436
  0.9 0.9 %collective-permute-start.1 = (bf16[64,2048]{1,0:T(8,128)(2,1)S(1)}, bf16[64,2048]{1,0:T(8,128)(2,1)S(1)}, u32[]{:S(2)}, u32[]{:S(2)}) collective-permute-start(bf16[64,2048]{1,0:T(8,128)(2,1)S(1)} %compose0.1.own_ref), channel_id=1, source_target_pairs={{0,4},{2,6},{4,8},{6,10},{8,12},{10,14},{1,5},{3,7},{5,9},{7,11},{... | collective-permute-start | bytes 786440 | tf_op jit(solution)/shard_map/ppermute | solution.py:355
  1.7 1.1 %copy-start.1 = (bf16[128,2048]{1,0:T(8,128)(2,1)S(1)}, bf16[128,2048]{1,0:T(8,128)(2,1)}, u32[]{:S(2)}) copy-start(bf16[128,2048]{1,0:T(8,128)(2,1)} %h_ref.1) | copy-start | bytes 1572868
  1.9 0.7 collective-permute-start.2
  2.8 36.5 %collective-permute-start.3 = (bf16[128,2048]{1,0:T(8,128)(2,1)S(1)}, bf16[128,2048]{1,0:T(8,128)(2,1)S(1)}, u32[]{:S(2)}, u32[]{:S(2)}) collective-permute-start(bf16[128,2048]{1,0:T(8,128)(2,1)S(1)} %first_finish.1.first_ref), channel_id=1, source_target_pairs={{0,16},{1,17},{2,18},{3,19},{4,20},{5,21},{6,22},{7,23},{8,24},{9,... | collective-permute-start | bytes 1572872 | tf_op jit(solution)/shard_map/ppermute | solution.py:407
  46.9 8.0 %collective-permute-start.4 = (bf16[64,2048]{1,0:T(8,128)(2,1)S(1)}, bf16[64,2048]{1,0:T(8,128)(2,1)S(1)}, u32[]{:S(2)}, u32[]{:S(2)}) collective-permute-start(bf16[64,2048]{1,0:T(8,128)(2,1)S(1)} %get-tuple-element.26.own_ref), channel_id=1, source_target_pairs={{16,18},{18,20},{20,22},{22,24},{24,26},{26,28},{28,30},{17,19},{1... | collective-permute-start | bytes 786440 | tf_op jit(solution)/shard_map/ppermute | solution.py:355
  55.2 7.1 %collective-permute-start.5 = (bf16[64,2048]{1,0:T(8,128)(2,1)S(1)}, bf16[64,2048]{1,0:T(8,128)(2,1)S(1)}, u32[]{:S(2)}, u32[]{:S(2)}) collective-permute-start(bf16[64,2048]{1,0:T(8,128)(2,1)S(1)} %compose1.1.own_ref), channel_id=1, source_target_pairs={{16,20},{18,22},{20,24},{22,26},{24,28},{26,30},{17,21},{19,23},{2... | collective-permute-start | bytes 786440 | tf_op jit(solution)/shard_map/ppermute | solution.py:355
  62.7 7.3 %collective-permute-start.6 = (bf16[64,1024]{1,0:T(8,128)(2,1)S(1)}, bf16[64,1024]{1,0:T(8,128)(2,1)S(1)}, u32[]{:S(2)}, u32[]{:S(2)}) collective-permute-start(bf16[64,1024]{1,0:T(8,128)(2,1)S(1)} %end_state1.1), channel_id=1, source_target_pairs={{16,24},{18,26},{20,28},{22,30},{17,25},{19,27},{21,29},{23,31}} | collective-permute-start | bytes 393224 | tf_op jit(solution)/shard_map/ppermute | solution.py:355

commit v6 on v5

--- a/solution.py
+++ b/solution.py
@@ -174,7 +174,8 @@
     front(1, h_ref, *rest[:10], None, *rest[10:], small_sems, sems)
 
 
-def read_out(active, quads, normed_ref, keys_ref, x_ref, y_ref, w_hbm, reads_out, wq, sems):
+def read_out(active, quads, normed_ref, keys_ref, x_ref, y_ref, w_hbm, w_out_hbm, after_ref, reads_out, *rest):
+    w_out, (wq, sems, load_sem) = rest[:-3], rest[-3:]
     rows = keys_ref.shape[0]
     part = len(quads) * QUAD
 
@@ -187,8 +188,12 @@
                     )
                 ]
                 for index, quad in enumerate(quads)
-            ]
+            ],
+            len(quads),
         )
+        loads = [pltpu.make_async_copy(w_out_hbm.at[0], target, load_sem) for target in w_out]
+        for load in loads:
+            load.start()
         normed = normed_ref[...]
         ones = head_ones()
         row = lax.broadcasted_iota(jnp.int32, (rows, 2 * rows), 0)
@@ -207,6 +212,8 @@
                 both = mm(scores, spread_two(x_ref[:, place], y_ref[:, place]))
                 reads_out[:, start : start + PAIR] = (queries[:, own] - both[:, :PAIR]).astype(BF16)
                 reads_out[:, part + start : part + start + PAIR] = both[:, PAIR:].astype(BF16)
+        for load in loads:
+            load.wait()
 
     on_section(active, body)
 
@@ -214,77 +221,79 @@
 def compose(active, own_ref, got_ref, after_ref, out_ref):
     width = own_ref.shape[1] // 2
 
-    def body():
+    def body(first_ref, second_ref):
         for start in range(0, width, PAIR):
             s_lanes, b_lanes = slice(start, start + PAIR), slice(width + start, width + start + PAIR)
-            s_own, s_got, b_got = own_ref[:, s_lanes], got_ref[:, s_lanes], got_ref[:, b_lanes]
-            step = mm(s_own, spread_two(s_got, b_got))
-            out_ref[:, s_lanes] = (s_own.astype(F32) + s_got.astype(F32) - step[:, :PAIR]).astype(BF16)
-            out_ref[:, b_lanes] = (own_ref[:, b_lanes].astype(F32) + b_got.astype(F32) - step[:, PAIR:]).astype(BF16)
-
-    on_section(active, body)
+            s_second, s_first, b_first = second_ref[:, s_lanes], first_ref[:, s_lanes], first_ref[:, b_lanes]
+            step = mm(s_second, spread_two(s_first, b_first))
+            out_ref[:, s_lanes] = (s_second.astype(F32) + s_first.astype(F32) - step[:, :PAIR]).astype(BF16)
+            out_ref[:, b_lanes] = (second_ref[:, b_lanes].astype(F32) + b_first.astype(F32) - step[:, PAIR:]).astype(BF16)
+
+    here = lax.axis_index("section") == active
+    side = lax.rem(lax.axis_index("seq"), 2)
+    pl.when(here & (side == 0))(lambda: body(own_ref, got_ref))
+    pl.when(here & (side == 1))(lambda: body(got_ref, own_ref))
 
 
 def pair_state(init_ref, pair):
     return jnp.concatenate([init_ref[0, 2 * pair], init_ref[0, 2 * pair + 1]], axis=1)
 
 
-def end_state(active, own_ref, got_ref, init_ref, after_ref, out_ref):
-    width = own_ref.shape[1] // 2
-
-    def body():
-        states = [pair_state(init_ref, pair) for pair in range(width // PAIR)]
-        for ref in (got_ref, own_ref):
-            for pair, state in enumerate(states):
-                start = pair * PAIR
-                step = mm(ref[:, start : start + PAIR], spread(state.astype(BF16)))
-                states[pair] = state - step + ref[:, width + start : width + start + PAIR].astype(F32)
-        for pair, state in enumerate(states):
-            out_ref[:, pair * PAIR : (pair + 1) * PAIR] = state.astype(BF16)
-
-    on_section(active, body)
-
-
-def fold(active, count, *refs):
-    got_refs = refs[:count]
-    reads_refs = refs[count : count + 2]
-    w_hbm, out_ref, w_out, sem = refs[count + 2 :]
-    width = out_ref.shape[1] // 2
-    part = width // 2
-
-    def body():
-        load = pltpu.make_async_copy(w_hbm.at[0], w_out, sem)
-        load.start()
+def apply_map(state, ref, start, width):
+    step = mm(ref[:, start : start + PAIR], spread(state.astype(BF16)))
+    return state - step + ref[:, width + start : width + start + PAIR].astype(F32)
+
+
+def advance(active, place, own_ref, got_ref, state_ref, after_ref, out_ref):
+    width = out_ref.shape[1]
+
+    def body(refs):
         for start in range(0, width, PAIR):
-            reads_ref = reads_refs[start // part]
-            inner = start % part
-            left = reads_ref[:, inner : inner + PAIR].astype(F32)
-            offset = reads_ref[:, part + inner : part + inner + PAIR].astype(F32)
-            for ref in got_refs:
-                step = mm(left.astype(BF16), spread_two(ref[:, start : start + PAIR], ref[:, width + start : width + start + PAIR]))
-                left = left - step[:, :PAIR]
-                offset = offset + step[:, PAIR:]
-            out_ref[:, start : start + PAIR] = left.astype(BF16)
-            out_ref[:, width + start : width + start + PAIR] = offset.astype(BF16)
-        load.wait()
-
-    on_section(active, body)
-
-
-def finish(active, count, state_ref, init_ref, reads_ref, w_out_ref, h_ref, store):
-    width = reads_ref.shape[1] // 2
+            lanes = slice(start, start + PAIR)
+            state = state_ref[:, lanes].astype(F32) if place else pair_state(state_ref, start // PAIR)
+            for ref in refs:
+                state = apply_map(state, ref, start, width)
+            out_ref[:, lanes] = state.astype(BF16)
+
+    index = lax.axis_index("seq")
+    here = (lax.axis_index("section") == active) & (index // 2 == place)
+    if got_ref is None:
+        pl.when(here)(lambda: body((own_ref,)))
+    else:
+        side = lax.rem(index, 2)
+        pl.when(here & (side == 0))(lambda: body((own_ref, got_ref)))
+        pl.when(here & (side == 1))(lambda: body((got_ref, own_ref)))
+
+
+def finish(active, state_refs, got_refs, init_ref, reads_refs, w_out_ref, h_ref, store):
+    width = w_out_ref.shape[0]
+    part = width // len(reads_refs)
     model = h_ref.shape[1]
     chunk = model // 4
 
+    def total(refs, lanes):
+        value = refs[0][:, lanes].astype(F32)
+        for ref in refs[1:]:
+            value = value + ref[:, lanes].astype(F32)
+        return value
+
     def body():
-        begins = lax.axis_index("seq") < count // 2
+        index = lax.axis_index("seq")
+        begins = index // 2 == 0
+        follows = lax.rem(index, 2) == 1
         parts = []
         for start in range(0, width, QUAD):
-            lanes = slice(start, start + QUAD)
-            init = jnp.concatenate([pair_state(init_ref, start // PAIR), pair_state(init_ref, start // PAIR + 1)], axis=1)
-            state = jnp.where(begins, init.astype(BF16), state_ref[:, lanes])
-            offset = reads_ref[:, width + start : width + start + QUAD]
-            parts.append((mm(reads_ref[:, lanes], spread(state)) + offset.astype(F32)).astype(BF16))
+            pieces = []
+            for lane in range(start, start + QUAD, PAIR):
+                lanes = slice(lane, lane + PAIR)
+                state = jnp.where(begins, pair_state(init_ref, lane // PAIR), total(state_refs, lanes))
+                step = mm(total(got_refs, lanes).astype(BF16), spread(state.astype(BF16)))
+                moved = state - step + total(got_refs, slice(width + lane, width + lane + PAIR))
+                pieces.append(jnp.where(follows, moved, state).astype(BF16))
+            reads_ref, inner = reads_refs[start // part], start % part
+            offset = reads_ref[:, part + inner : part + inner + QUAD]
+            read = mm(reads_ref[:, inner : inner + QUAD], spread(jnp.concatenate(pieces, axis=1)))
+            parts.append((read + offset.astype(F32)).astype(BF16))
         inner_bf = jnp.concatenate(parts, axis=1)
         for start in range(0, model, chunk):
             lanes = slice(start, start + chunk)
@@ -293,14 +302,22 @@
     on_section(active, body)
 
 
-def first_finish(count, state_ref, init_ref, reads_ref, w_out_ref, h_ref, out_ref):
+def split_finish(counts, refs):
+    states, gots, reads = counts
+    return refs[:states], refs[states : states + gots], refs[states + gots], refs[states + gots + 1 :][:reads], refs[states + gots + 1 + reads :]
+
+
+def first_finish(counts, *refs):
+    states, gots, init_ref, reads, (w_out_ref, h_ref, out_ref) = split_finish(counts, refs)
+
     def store(start, value):
         out_ref[:, start : start + value.shape[1]] = value
 
-    finish(0, count, state_ref, init_ref, reads_ref, w_out_ref, h_ref, store)
-
-
-def last_finish(count, state_ref, init_ref, reads_ref, w_out_ref, h_ref, first_ref, out_hbm, near, sems):
+    finish(0, states, gots, init_ref, reads, w_out_ref, h_ref, store)
+
+
+def last_finish(counts, *refs):
+    states, gots, init_ref, reads, (w_out_ref, h_ref, first_ref, out_hbm, near, sems) = split_finish(counts, refs)
     chunk = near.shape[1] // 4
 
     def write(start):
@@ -311,7 +328,7 @@
         near[:, start : start + chunk] = value
         write(start).start()
 
-    finish(1, count, state_ref, init_ref, reads_ref, w_out_ref, h_ref, store)
+    finish(1, states, gots, init_ref, reads, w_out_ref, h_ref, store)
 
     @pl.when(lax.axis_index("section") == 0)
     def _():
@@ -350,12 +367,12 @@
     w_rate = jnp.swapaxes(w_rate, 1, 2)
     norm_gain, w_qkv, w_rate, rate_base, w_out = [in_hbm(value) for value in (norm_gain, w_qkv, w_rate, rate_base, w_out)]
 
-    def ahead(value, active, steps):
-        pairs = [(active * count + place, active * count + place + steps) for place in range(count - steps)]
-        return lax.ppermute(value, ("section", "seq"), pairs)
-
-    def run(active, body, outs, scratch, args, kinds=None):
-        return call(functools.partial(body, active), outs, scratch, args, kinds, name=body.__name__ + str(active))
+    def permute(value, active, pairs):
+        base = active * count
+        return lax.ppermute(value, ("section", "seq"), [(base + source, base + target) for source, target in pairs])
+
+    def swap(own, active, groups):
+        return permute(own, active, [(2 * group + side, 2 * group + 1 - side) for group in groups for side in range(2)])
 
     def layer(active, hidden):
         h_scratch = [] if active else [pltpu.VMEM(hidden.shape, hidden.dtype)]
@@ -371,45 +388,56 @@
             name="later_front" if active else "first_front",
         )
 
-        def reads_of(picked):
+        def reads_of(picked, load, after):
             part = len(picked) * QUAD
             return call(
                 functools.partial(read_out, active, picked),
-                [shape((rows, 2 * part), BF16)],
-                [pltpu.VMEM((depth, part), BF16), pltpu.SemaphoreType.DMA((len(picked),))],
-                [normed, keys, x_all, y_all, w_qkv],
-                [pltpu.VMEM] * 4 + [pltpu.HBM],
+                [shape((rows, 2 * part), BF16)] + [pltpu.VMEM(w_out.shape[1:], BF16)] * load,
+                [pltpu.VMEM((depth, part), BF16), pltpu.SemaphoreType.DMA((len(picked),)), pltpu.SemaphoreType.DMA],
+                [normed, keys, x_all, y_all, w_qkv, w_out, after],
+                [pltpu.VMEM] * 4 + [pltpu.HBM] * 2 + [pl.ANY],
                 name=f"reads{active}_{picked[0]}",
-            )[0]
-
-        reads = [reads_of(tuple(range(quads // 2))), reads_of(tuple(range(quads // 2, quads)))]
-        got = [ahead(own, active, 1)]
-        steps = 2
-        while steps < count // 2:
-            (own,) = run(active, compose, [maps], [], [own, got[-1], reads[0]], [pltpu.VMEM] * 2 + [pl.ANY])
-            got.append(ahead(own, active, steps))
-            steps *= 2
-        (state,) = run(
-            active, end_state, [shape((HD, width), BF16)], [], [own, got[-1], init_state, reads[1]], [pltpu.VMEM] * 3 + [pl.ANY]
-        )
-        state = ahead(state, active, steps)
-        folded, w_out_near = call(
-            functools.partial(fold, active, len(got)),
-            [shape((rows, 2 * width), BF16), pltpu.VMEM(w_out.shape[1:], BF16)],
-            [pltpu.SemaphoreType.DMA],
-            got + reads + [w_out],
-            [pltpu.VMEM] * (len(got) + 2) + [pltpu.HBM],
-            name=f"fold{active}",
-        )
-        return [state, init_state, folded, in_vmem(w_out_near), hidden]
-
-    (first,) = call(functools.partial(first_finish, count), [shape((rows, model), BF16)], [], layer(0, tokens), name="first_finish")
+            )
+
+        def hop(place, maps_here, state, after):
+            kinds = [pltpu.VMEM] * (len(maps_here) + 1) + [pl.ANY]
+
+            def body(*refs):
+                advance(active, place, refs[0], None if len(maps_here) == 1 else refs[1], *refs[len(maps_here) :])
+
+            (ahead,) = call(body, [shape((HD, width), BF16)], [], maps_here + [state, after], kinds, name=f"advance{active}_{place}")
+            pairs = [(2 * place + side, 2 * place + 2 + side) for side in range(2)]
+            return ahead, permute(ahead, active, pairs)
+
+        groups = count // 2
+        states, state = [], init_state
+        if active == 0:
+            got = [swap(own, active, range(groups))]
+            reads, near = reads_of(tuple(range(quads)), 1, init_state)
+            reads = [reads]
+            (both,) = call(functools.partial(compose, active), [maps], [], [own, got[0], reads[0]], [pltpu.VMEM] * 2 + [pl.ANY], name="compose")
+            for place in range(groups - 1):
+                ahead, state = hop(place, [both], state, both)
+                states.append(state)
+        else:
+            got = [swap(own, active, [group]) for group in range(groups)]
+            (reads,) = reads_of(tuple(range(quads // 2)), 0, init_state)
+            for place in range(groups - 1):
+                ahead, state = hop(place, [own, got[place]], state, reads)
+                states.append(state)
+            more, near = reads_of(tuple(range(quads // 2, quads)), 1, ahead)
+            reads = [reads, more]
+        return (len(states), len(got), len(reads)), [*states, *got, init_state, *reads, in_vmem(near), hidden]
+
+    counts, args = layer(0, tokens)
+    (first,) = call(functools.partial(first_finish, counts), [shape((rows, model), BF16)], [], args, name="first_finish")
     hidden = lax.ppermute(first, "section", [(0, 1)])
+    counts, args = layer(1, hidden)
     (result,) = call(
-        functools.partial(last_finish, count),
+        functools.partial(last_finish, counts),
         [shape((1, rows, model), BF16)],
         [pltpu.VMEM((rows, model), BF16), pltpu.SemaphoreType.DMA((4,))],
-        layer(1, hidden) + [first],
+        args + [first],
         name="last_finish",
         out_kind=pltpu.HBM,
     )

time: 72.2 us -> 65.5 us (0.907)
  waiting for transfers between devices: 44.2 us -> 36.1 us
  starting transfers between devices: 8.21 us -> 12 us
  Pallas kernels: 18.7 us -> 15.9 us
    ppermute x6 -> x11, waiting for transfers between devices: 9 us -> 3.18 us  [permute(): lax.ppermute(value, ('section', 'seq'), [(base + source, base + target) f...]
    ppermute x6 -> x11, starting transfers between devices: 6.93 us -> 10.7 us  [permute(): lax.ppermute(value, ('section', 'seq'), [(base + source, base + target) f...]
    pallas_call x14, Pallas kernels: 18.7 us -> 15.9 us  [call(): pl.pallas_call(body, out_shape=outs, in_specs=specs, out_specs=[pl.BlockS...]
    ppermute x1, waiting for transfers between devices: 35.2 us -> 32.9 us  [shards(): hidden = lax.ppermute(first, 'section', [(0, 1)])]
  transfers between devices with their start and end apart: 7 -> 12, of which waited for: 4 -> 2; matrix products, arithmetic and copies ran while one was open for 0% -> 0% of each run, Pallas kernels for 12% -> 10%
where the time goes in v6:
time: 65.5 us; the launch traced here: 64.6 us
  waiting for transfers between devices  36.1 us (55%)
  Pallas kernels  15.9 us (24%)
  starting transfers between devices  12 us (18%)
    ppermute x1, waiting for transfers between devices, shards(): hidden = lax.ppermute(first, 'section', [(0, 1)])  32.9 us
    pallas_call x14, Pallas kernels, call(): pl.pallas_call(body, out_shape=outs, in_specs=specs, out_specs=[pl.BlockS...  15.9 us
    ppermute x11, starting transfers between devices, permute(): lax.ppermute(value, ('section', 'seq'), [(base + source, base + target) f...  10.7 us
    ppermute x11, waiting for transfers between devices, permute(): lax.ppermute(value, ('section', 'seq'), [(base + source, base + target) f...  3.18 us
  transfers between devices with their start and end apart: 12, of which 2 were waited for; matrix products, arithmetic and copies ran while one was open for 0% of the time, Pallas kernels for 10%

profile of v6, /device:TPU:25, one launch (start us, length us, event | category | flops | bytes accessed | tf_op | source)
XLA Modules:
  0.0 64.6 jit_solution(14154314642422862222)
XLA Ops:
  0.0 0.0 copy-start
  0.0 0.1 first_front.1
  0.1 0.8 %collective-permute-start = (bf16[64,2048]{1,0:T(8,128)(2,1)S(1)}, bf16[64,2048]{1,0:T(8,128)(2,1)S(1)}, u32[]{:S(2)}, u32[]{:S(2)}) collective-permute-start(bf16[64,2048]{1,0:T(8,128)(2,1)S(1)} %get-tuple-element.19.own_ref), channel_id=1, source_target_pairs={{0,2},{2,0},{4,6},{6,4},{8,10},{10,8},{12,14},{14,12},{1,3},{3,1},... | collective-permute-start | bytes 786440 | tf_op jit(solution)/shard_map/ppermute | solution.py:372
  0.9 0.1 copy-done
  1.1 0.0 copy-start.1
  1.1 0.0 collective-permute-done.got_ref.refs_3_
  1.2 0.8 %collective-permute-start.1 = (bf16[64,1024]{1,0:T(8,128)(2,1)S(1)}, bf16[64,1024]{1,0:T(8,128)(2,1)S(1)}, u32[]{:S(2)}, u32[]{:S(2)}) collective-permute-start(bf16[64,1024]{1,0:T(8,128)(2,1)S(1)} %advance0_0.1), channel_id=1, source_target_pairs={{0,4},{2,6},{1,5},{3,7}} | collective-permute-start | bytes 393224 | tf_op jit(solution)/shard_map/ppermute | solution.py:372
  2.0 0.0 collective-permute-done.1.refs_1_.refs_0_
  2.0 0.7 %collective-permute-start.2 = (bf16[64,1024]{1,0:T(8,128)(2,1)S(1)}, bf16[64,1024]{1,0:T(8,128)(2,1)S(1)}, u32[]{:S(2)}, u32[]{:S(2)}) collective-permute-start(bf16[64,1024]{1,0:T(8,128)(2,1)S(1)} %advance0_1.1), channel_id=1, source_target_pairs={{4,8},{6,10},{5,9},{7,11}} | collective-permute-start | bytes 393224 | tf_op jit(solution)/shard_map/ppermute | solution.py:372
  2.7 0.0 collective-permute-done.2.refs_1_
  2.8 0.7 %collective-permute-start.3 = (bf16[64,1024]{1,0:T(8,128)(2,1)S(1)}, bf16[64,1024]{1,0:T(8,128)(2,1)S(1)}, u32[]{:S(2)}, u32[]{:S(2)}) collective-permute-start(bf16[64,1024]{1,0:T(8,128)(2,1)S(1)} %advance0_2.1), channel_id=1, source_target_pairs={{8,12},{10,14},{9,13},{11,15}} | collective-permute-start | bytes 393224 | tf_op jit(solution)/shard_map/ppermute | solution.py:372
  3.4 0.0 collective-permute-done.3.refs_2_
  3.4 0.0 copy-done.1
  3.5 1.3 %collective-permute-start.4 = (bf16[128,2048]{1,0:T(8,128)(2,1)S(1)}, bf16[128,2048]{1,0:T(8,128)(2,1)S(1)}, u32[]{:S(2)}, u32[]{:S(2)}) collective-permute-start(bf16[128,2048]{1,0:T(8,128)(2,1)S(1)} %first_finish.1.refs_12_), channel_id=1, source_target_pairs={{0,16},{1,17},{2,18},{3,19},{4,20},{5,21},{6,22},{7,23},{8,24},{9,... | collective-permute-start | bytes 1572872 | tf_op jit(solution)/shard_map/ppermute | solution.py:434
  4.8 32.9 %collective-permute-done.4.h_ref.refs_11_ = bf16[128,2048]{1,0:T(8,128)(2,1)S(1)} collective-permute-done((bf16[128,2048]{1,0:T(8,128)(2,1)S(1)}, bf16[128,2048]{1,0:T(8,128)(2,1)S(1)}, u32[]{:S(2)}, u32[]{:S(2)}) %collective-permute-start.4) | collective-permute-done | bytes 524320 | tf_op jit(solution)/shard_map/ppermute | solution.py:434
  37.7 7.6 %later_front.1 = (bf16[64,2048]{1,0:T(8,128)(2,1)S(1)}, bf16[128,2048]{1,0:T(8,128)(2,1)S(1)}, bf16[128,1024]{1,0:T(8,128)(2,1)S(1)}, bf16[128,1024]{1,0:T(8,128)(2,1)S(1)}, bf16[128,1024]{1,0:T(8,128)(2,1)S(1)}) custom-call(bf16[128,2048]{1,0:T(8,128)(2,1)S(1)} %collective-permute-done.4.h_ref.refs_11_, f32[1,2048]{1,0:T(1,128)} %rest_0_.3, ...), custom_call_target="tpu_custom_call" | custom-call | tf_op jit(solution)/shard_map/later_front/pallas_call | solution.py:344
  45.2 0.7 %collective-permute-start.5 = (bf16[64,2048]{1,0:T(8,128)(2,1)S(1)}, bf16[64,2048]{1,0:T(8,128)(2,1)S(1)}, u32[]{:S(2)}, u32[]{:S(2)}) collective-permute-start(bf16[64,2048]{1,0:T(8,128)(2,1)S(1)} %get-tuple-element.26.refs_0_), channel_id=1, source_target_pairs={{16,18},{18,16},{17,19},{19,17}} | collective-permute-start | bytes 786440 | tf_op jit(solution)/shard_map/ppermute | solution.py:372
  45.9 0.7 %collective-permute-start.7 = (bf16[64,2048]{1,0:T(8,128)(2,1)S(1)}, bf16[64,2048]{1,0:T(8,128)(2,1)S(1)}, u32[]{:S(2)}, u32[]{:S(2)}) collective-permute-start(bf16[64,2048]{1,0:T(8,128)(2,1)S(1)} %get-tuple-element.26.refs_0_), channel_id=1, source_target_pairs={{20,22},{22,20},{21,23},{23,21}} | collective-permute-start | bytes 786440 | tf_op jit(solution)/shard_map/ppermute | solution.py:372
  46.6 3.1 %reads1_0.1.refs_3_.refs_8_ = bf16[128,1024]{1,0:T(8,128)(2,1)S(1)} custom-call(bf16[128,2048]{1,0:T(8,128)(2,1)S(1)} %get-tuple-element.27.normed_ref, bf16[128,1024]{1,0:T(8,128)(2,1)S(1)} %get-tuple-element.28.keys_ref, bf16[128,1024]{1,0:T(8,128)(2,1)S(1)} %get-tuple-element.29.x_ref, bf16[128,1024]{1,0:T(8,128)(2,1)S(1)} %get-tuple-element.30.y_ref, ...), custom_call_target="tpu_custom_call" | custom-call | tf_op jit(solution)/shard_map/reads1_0/pallas_call | solution.py:344
  49.8 0.0 collective-permute-done.5.refs_1_.refs_3_
  49.8 0.8 %collective-permute-start.6 = (bf16[64,1024]{1,0:T(8,128)(2,1)S(1)}, bf16[64,1024]{1,0:T(8,128)(2,1)S(1)}, u32[]{:S(2)}, u32[]{:S(2)}) collective-permute-start(bf16[64,1024]{1,0:T(8,128)(2,1)S(1)} %advance1_0.1), channel_id=1, source_target_pairs={{16,20},{18,22},{17,21},{19,23}} | collective-permute-start | bytes 393224 | tf_op jit(solution)/shard_map/ppermute | solution.py:372
  50.7 0.7 %collective-permute-start.9 = (bf16[64,2048]{1,0:T(8,128)(2,1)S(1)}, bf16[64,2048]{1,0:T(8,128)(2,1)S(1)}, u32[]{:S(2)}, u32[]{:S(2)}) collective-permute-start(bf16[64,2048]{1,0:T(8,128)(2,1)S(1)} %get-tuple-element.26.refs_0_), channel_id=1, source_target_pairs={{24,26},{26,24},{25,27},{27,25}} | collective-permute-start | bytes 786440 | tf_op jit(solution)/shard_map/ppermute | solution.py:372
  51.3 0.0 collective-permute-done.7.refs_1_.refs_4_
  51.4 0.0 collective-permute-done.6.refs_2_.refs_0_
  51.4 0.7 %collective-permute-start.8 = (bf16[64,1024]{1,0:T(8,128)(2,1)S(1)}, bf16[64,1024]{1,0:T(8,128)(2,1)S(1)}, u32[]{:S(2)}, u32[]{:S(2)}) collective-permute-start(bf16[64,1024]{1,0:T(8,128)(2,1)S(1)} %advance1_1.1), channel_id=1, source_target_pairs={{20,24},{22,26},{21,25},{23,27}} | collective-permute-start | bytes 393224 | tf_op jit(solution)/shard_map/ppermute | solution.py:372
  52.1 2.9 %collective-permute-start.11 = (bf16[64,2048]{1,0:T(8,128)(2,1)S(1)}, bf16[64,2048]{1,0:T(8,128)(2,1)S(1)}, u32[]{:S(2)}, u32[]{:S(2)}) collective-permute-start(bf16[64,2048]{1,0:T(8,128)(2,1)S(1)} %get-tuple-element.26.refs_0_), channel_id=1, source_target_pairs={{28,30},{30,28},{29,31},{31,29}} | collective-permute-start | bytes 786440 | tf_op jit(solution)/shard_map/ppermute | solution.py:372
  55.0 0.0 collective-permute-done.9.refs_1_.refs_5_
  55.0 0.0 collective-permute-done.8.refs_2_.refs_1_
  55.1 1.3 %collective-permute-start.10 = (bf16[64,1024]{1,0:T(8,128)(2,1)S(1)}, bf16[64,1024]{1,0:T(8,128)(2,1)S(1)}, u32[]{:S(2)}, u32[]{:S(2)}) collective-permute-start(bf16[64,1024]{1,0:T(8,128)(2,1)S(1)} %advance1_2.1.after_ref), channel_id=1, source_target_pairs={{24,28},{26,30},{25,29},{27,31}} | collective-permute-start | bytes 393224 | tf_op jit(solution)/shard_map/ppermute | solution.py:372
  56.4 3.1 %reads1_2.1 = (bf16[128,1024]{1,0:T(8,128)(2,1)S(1)}, bf16[1024,2048]{1,0:T(8,128)(2,1)S(1)}) custom-call(bf16[128,2048]{1,0:T(8,128)(2,1)S(1)} %get-tuple-element.27.normed_ref, bf16[128,1024]{1,0:T(8,128)(2,1)S(1)} %get-tuple-element.28.keys_ref, bf16[128,1024]{1,0:T(8,128)(2,1)S(1)} %get-tuple-element.29.x_ref, ...), custom_call_target="tpu_custom_call" | custom-call | tf_op jit(solution)/shard_map/reads1_2/pallas_call | solution.py:344
  59.5 0.0 collective-permute-done.11.refs_6_
  59.5 3.2 %collective-permute-done.10.refs_2_ = bf16[64,1024]{1,0:T(8,128)(2,1)S(1)} collective-permute-done((bf16[64,1024]{1,0:T(8,128)(2,1)S(1)}, bf16[64,1024]{1,0:T(8,128)(2,1)S(1)}, u32[]{:S(2)}, u32[]{:S(2)}) %collective-permute-start.10) | collective-permute-done | bytes 131104 | tf_op jit(solution)/shard_map/ppermute | solution.py:372
  62.7 1.8 %last_finish.1 = bf16[1,128,2048]{2,1,0:T(8,128)(2,1)} custom-call(bf16[64,1024]{1,0:T(8,128)(2,1)S(1)} %collective-permute-done.6.refs_2_.refs_0_, bf16[64,1024]{1,0:T(8,128)(2,1)S(1)} %collective-permute-done.8.refs_2_.refs_1_, bf16[64,1024]{1,0:T(8,128)(2,1)S(1)} %collective-permute-done.10.refs_2_, ...), custom_call_target="tpu_custom_call" | custom-call | tf_op jit(solution)/shard_map/last_finish/pallas_call | solution.py:344
  (9 shorter events, 0.2 us)
Async XLA Ops:
  0.0 1.0 %copy-start = (f32[1,16,64,64]{3,2,1,0:T(8,128)S(1)}, f32[1,16,64,64]{3,2,1,0:T(8,128)}, u32[]{:S(2)}) copy-start(f32[1,16,64,64]{3,2,1,0:T(8,128)} %refs_7_.3) | copy-start | bytes 786436
  0.1 1.0 %collective-permute-start = (bf16[64,2048]{1,0:T(8,128)(2,1)S(1)}, bf16[64,2048]{1,0:T(8,128)(2,1)S(1)}, u32[]{:S(2)}, u32[]{:S(2)}) collective-permute-start(bf16[64,2048]{1,0:T(8,128)(2,1)S(1)} %get-tuple-element.19.own_ref), channel_id=1, source_target_pairs={{0,2},{2,0},{4,6},{6,4},{8,10},{10,8},{12,14},{14,12},{1,3},{3,1},... | collective-permute-start | bytes 786440 | tf_op jit(solution)/shard_map/ppermute | solution.py:372
  1.1 2.3 %copy-start.1 = (bf16[128,2048]{1,0:T(8,128)(2,1)S(1)}, bf16[128,2048]{1,0:T(8,128)(2,1)}, u32[]{:S(2)}) copy-start(bf16[128,2048]{1,0:T(8,128)(2,1)} %refs_7_.2) | copy-start | bytes 1572868
  1.2 0.8 %collective-permute-start.1 = (bf16[64,1024]{1,0:T(8,128)(2,1)S(1)}, bf16[64,1024]{1,0:T(8,128)(2,1)S(1)}, u32[]{:S(2)}, u32[]{:S(2)}) collective-permute-start(bf16[64,1024]{1,0:T(8,128)(2,1)S(1)} %advance0_0.1), channel_id=1, source_target_pairs={{0,4},{2,6},{1,5},{3,7}} | collective-permute-start | bytes 393224 | tf_op jit(solution)/shard_map/ppermute | solution.py:372
  2.0 0.7 %collective-permute-start.2 = (bf16[64,1024]{1,0:T(8,128)(2,1)S(1)}, bf16[64,1024]{1,0:T(8,128)(2,1)S(1)}, u32[]{:S(2)}, u32[]{:S(2)}) collective-permute-start(bf16[64,1024]{1,0:T(8,128)(2,1)S(1)} %advance0_1.1), channel_id=1, source_target_pairs={{4,8},{6,10},{5,9},{7,11}} | collective-permute-start | bytes 393224 | tf_op jit(solution)/shard_map/ppermute | solution.py:372
  2.8 0.7 %collective-permute-start.3 = (bf16[64,1024]{1,0:T(8,128)(2,1)S(1)}, bf16[64,1024]{1,0:T(8,128)(2,1)S(1)}, u32[]{:S(2)}, u32[]{:S(2)}) collective-permute-start(bf16[64,1024]{1,0:T(8,128)(2,1)S(1)} %advance0_2.1), channel_id=1, source_target_pairs={{8,12},{10,14},{9,13},{11,15}} | collective-permute-start | bytes 393224 | tf_op jit(solution)/shard_map/ppermute | solution.py:372
  3.5 34.2 %collective-permute-start.4 = (bf16[128,2048]{1,0:T(8,128)(2,1)S(1)}, bf16[128,2048]{1,0:T(8,128)(2,1)S(1)}, u32[]{:S(2)}, u32[]{:S(2)}) collective-permute-start(bf16[128,2048]{1,0:T(8,128)(2,1)S(1)} %first_finish.1.refs_12_), channel_id=1, source_target_pairs={{0,16},{1,17},{2,18},{3,19},{4,20},{5,21},{6,22},{7,23},{8,24},{9,... | collective-permute-start | bytes 1572872 | tf_op jit(solution)/shard_map/ppermute | solution.py:434
  45.2 4.5 %collective-permute-start.5 = (bf16[64,2048]{1,0:T(8,128)(2,1)S(1)}, bf16[64,2048]{1,0:T(8,128)(2,1)S(1)}, u32[]{:S(2)}, u32[]{:S(2)}) collective-permute-start(bf16[64,2048]{1,0:T(8,128)(2,1)S(1)} %get-tuple-element.26.refs_0_), channel_id=1, source_target_pairs={{16,18},{18,16},{17,19},{19,17}} | collective-permute-start | bytes 786440 | tf_op jit(solution)/shard_map/ppermute | solution.py:372
  45.9 5.4 %collective-permute-start.7 = (bf16[64,2048]{1,0:T(8,128)(2,1)S(1)}, bf16[64,2048]{1,0:T(8,128)(2,1)S(1)}, u32[]{:S(2)}, u32[]{:S(2)}) collective-permute-start(bf16[64,2048]{1,0:T(8,128)(2,1)S(1)} %get-tuple-element.26.refs_0_), channel_id=1, source_target_pairs={{20,22},{22,20},{21,23},{23,21}} | collective-permute-start | bytes 786440 | tf_op jit(solution)/shard_map/ppermute | solution.py:372
  49.8 1.6 %collective-permute-start.6 = (bf16[64,1024]{1,0:T(8,128)(2,1)S(1)}, bf16[64,1024]{1,0:T(8,128)(2,1)S(1)}, u32[]{:S(2)}, u32[]{:S(2)}) collective-permute-start(bf16[64,1024]{1,0:T(8,128)(2,1)S(1)} %advance1_0.1), channel_id=1, source_target_pairs={{16,20},{18,22},{17,21},{19,23}} | collective-permute-start | bytes 393224 | tf_op jit(solution)/shard_map/ppermute | solution.py:372
  50.7 4.3 %collective-permute-start.9 = (bf16[64,2048]{1,0:T(8,128)(2,1)S(1)}, bf16[64,2048]{1,0:T(8,128)(2,1)S(1)}, u32[]{:S(2)}, u32[]{:S(2)}) collective-permute-start(bf16[64,2048]{1,0:T(8,128)(2,1)S(1)} %get-tuple-element.26.refs_0_), channel_id=1, source_target_pairs={{24,26},{26,24},{25,27},{27,25}} | collective-permute-start | bytes 786440 | tf_op jit(solution)/shard_map/ppermute | solution.py:372
  51.4 3.6 %collective-permute-start.8 = (bf16[64,1024]{1,0:T(8,128)(2,1)S(1)}, bf16[64,1024]{1,0:T(8,128)(2,1)S(1)}, u32[]{:S(2)}, u32[]{:S(2)}) collective-permute-start(bf16[64,1024]{1,0:T(8,128)(2,1)S(1)} %advance1_1.1), channel_id=1, source_target_pairs={{20,24},{22,26},{21,25},{23,27}} | collective-permute-start | bytes 393224 | tf_op jit(solution)/shard_map/ppermute | solution.py:372
  52.1 7.4 %collective-permute-start.11 = (bf16[64,2048]{1,0:T(8,128)(2,1)S(1)}, bf16[64,2048]{1,0:T(8,128)(2,1)S(1)}, u32[]{:S(2)}, u32[]{:S(2)}) collective-permute-start(bf16[64,2048]{1,0:T(8,128)(2,1)S(1)} %get-tuple-element.26.refs_0_), channel_id=1, source_target_pairs={{28,30},{30,28},{29,31},{31,29}} | collective-permute-start | bytes 786440 | tf_op jit(solution)/shard_map/ppermute | solution.py:372
  55.1 7.6 %collective-permute-start.10 = (bf16[64,1024]{1,0:T(8,128)(2,1)S(1)}, bf16[64,1024]{1,0:T(8,128)(2,1)S(1)}, u32[]{:S(2)}, u32[]{:S(2)}) collective-permute-start(bf16[64,1024]{1,0:T(8,128)(2,1)S(1)} %advance1_2.1.after_ref), channel_id=1, source_target_pairs={{24,28},{26,30},{25,29},{27,31}} | collective-permute-start | bytes 393224 | tf_op jit(solution)/shard_map/ppermute | solution.py:372

commit v7 on v6

--- a/solution.py
+++ b/solution.py
@@ -13,7 +13,7 @@
 F32 = jnp.float32
 BF16 = jnp.bfloat16
 EPS = 1e-6
-VMEM_LIMIT = 20 * 1024 * 1024
+VMEM_LIMIT = 16 * 1024 * 1024
 
 
 def mm(a, b):
@@ -95,7 +95,7 @@
     pl.when(lax.axis_index("section") == active)(body)
 
 
-def front(active, h_ref, gain_hbm, w_hbm, w_rate_hbm, base_hbm, maps, normed_out, keys_out, x_out, y_out, wkv, h_in, gain, w_rate, base, small_sems, sems):
+def front(active, h_ref, gain_hbm, w_ref, w_rate_hbm, base_hbm, maps, normed_out, keys_out, x_out, y_out, wkv, h_in, gain, w_rate, base, small_sems, sems):
     width = keys_out.shape[1]
     quads = width // QUAD
 
@@ -106,19 +106,20 @@
         small = [pltpu.make_async_copy(source, target, small_sems.at[index]) for index, (source, target) in enumerate(sources)]
         for copy in small:
             copy.start()
-        wait_group = staged(
-            [
+        if wkv is not None:
+            wait_group = staged(
                 [
-                    pltpu.make_async_copy(
-                        w_hbm.at[0, :, pl.ds((side + 1) * width + quad * QUAD, QUAD)],
-                        wkv.at[:, pl.ds(side * width + quad * QUAD, QUAD)],
-                        sems.at[quad, side],
-                    )
-                    for side in range(2)
+                    [
+                        pltpu.make_async_copy(
+                            w_ref.at[0, :, pl.ds((side + 1) * width + quad * QUAD, QUAD)],
+                            wkv.at[:, pl.ds(side * width + quad * QUAD, QUAD)],
+                            sems.at[quad, side],
+                        )
+                        for side in range(2)
+                    ]
+                    for quad in range(quads)
                 ]
-                for quad in range(quads)
-            ]
-        )
+            )
         for copy in small:
             copy.wait()
         normed = norm_rows((h_ref if h_in is None else h_in)[...], gain[...])
@@ -127,9 +128,13 @@
         ones = head_ones()
 
         def project(quad):
-            wait_group(quad)
-            lanes = slice(quad * QUAD, (quad + 1) * QUAD)
-            return mm(normed, wkv[:, lanes]), mm(normed, wkv[:, width + quad * QUAD : width + (quad + 1) * QUAD])
+            if wkv is None:
+                weights, base_lane = w_ref, width
+            else:
+                weights, base_lane = wkv, 0
+                wait_group(quad)
+            key_lane = base_lane + quad * QUAD
+            return [mm(normed, weights[:, lane : lane + QUAD]) for lane in (key_lane, key_lane + width)]
 
         def chain(quad, keys, values):
             lanes = slice(quad * QUAD, (quad + 1) * QUAD)
@@ -170,50 +175,55 @@
 
 
 def later_front(h_ref, *rest):
-    *rest, small_sems, sems = rest
-    front(1, h_ref, *rest[:10], None, *rest[10:], small_sems, sems)
-
-
-def read_out(active, quads, normed_ref, keys_ref, x_ref, y_ref, w_hbm, w_out_hbm, after_ref, reads_out, *rest):
-    w_out, (wq, sems, load_sem) = rest[:-3], rest[-3:]
-    rows = keys_ref.shape[0]
-    part = len(quads) * QUAD
-
+    *rest, gain, w_rate, base, small_sems = rest
+    front(1, h_ref, *rest, None, None, gain, w_rate, base, small_sems, None)
+
+
+def load(w_hbm, after_ref, near, sem):
     def body():
-        wait_group = staged(
-            [
+        copy = pltpu.make_async_copy(w_hbm.at[0], near, sem)
+        copy.start()
+        copy.wait()
+
+    on_section(1, body)
+
+
+def read_out(active, normed_ref, keys_ref, x_ref, y_ref, w_ref, w_out_hbm, after_ref, reads_out, w_out, load_sem, wq=None, sems=None):
+    rows, width = keys_ref.shape
+    quads = width // QUAD
+
+    def body():
+        if wq is not None:
+            wait_group = staged(
                 [
-                    pltpu.make_async_copy(
-                        w_hbm.at[0, :, pl.ds(quad * QUAD, QUAD)], wq.at[:, pl.ds(index * QUAD, QUAD)], sems.at[index]
-                    )
-                ]
-                for index, quad in enumerate(quads)
-            ],
-            len(quads),
-        )
-        loads = [pltpu.make_async_copy(w_out_hbm.at[0], target, load_sem) for target in w_out]
-        for load in loads:
-            load.start()
+                    [pltpu.make_async_copy(w_ref.at[0, :, pl.ds(quad * QUAD, QUAD)], wq.at[:, pl.ds(quad * QUAD, QUAD)], sems.at[quad])]
+                    for quad in range(quads)
+                ],
+                quads,
+            )
+        fetch = pltpu.make_async_copy(w_out_hbm.at[0], w_out, load_sem)
+        fetch.start()
+        weights = w_ref if wq is None else wq
         normed = normed_ref[...]
         ones = head_ones()
         row = lax.broadcasted_iota(jnp.int32, (rows, 2 * rows), 0)
         lane = lax.rem(lax.broadcasted_iota(jnp.int32, (rows, 2 * rows), 1), rows)
         causal = row >= lane
-        for index, quad in enumerate(quads):
-            wait_group(index)
-            queries = unit_heads(mm(normed, wq[:, index * QUAD : (index + 1) * QUAD]), ones)
+        for quad in range(quads):
+            if wq is not None:
+                wait_group(quad)
+            queries = unit_heads(mm(normed, weights[:, quad * QUAD : (quad + 1) * QUAD]), ones)
             queries_bf = queries.astype(BF16)
             for half in range(2):
                 own = slice(half * PAIR, (half + 1) * PAIR)
-                place = slice(quad * QUAD + half * PAIR, quad * QUAD + (half + 1) * PAIR)
-                start = index * QUAD + half * PAIR
+                start = quad * QUAD + half * PAIR
+                place = slice(start, start + PAIR)
                 scores = mm_nt(queries_bf[:, own], spread(keys_ref[:, place]))
                 scores = jnp.where(causal, scores, 0.0).astype(BF16)
                 both = mm(scores, spread_two(x_ref[:, place], y_ref[:, place]))
-                reads_out[:, start : start + PAIR] = (queries[:, own] - both[:, :PAIR]).astype(BF16)
-                reads_out[:, part + start : part + start + PAIR] = both[:, PAIR:].astype(BF16)
-        for load in loads:
-            load.wait()
+                reads_out[:, place] = (queries[:, own] - both[:, :PAIR]).astype(BF16)
+                reads_out[:, width + start : width + start + PAIR] = both[:, PAIR:].astype(BF16)
+        fetch.wait()
 
     on_section(active, body)
 
@@ -265,9 +275,8 @@
         pl.when(here & (side == 1))(lambda: body((got_ref, own_ref)))
 
 
-def finish(active, state_refs, got_refs, init_ref, reads_refs, w_out_ref, h_ref, store):
+def finish(here, begins, state_refs, got_refs, init_ref, reads_ref, w_out_ref, h_ref, store):
     width = w_out_ref.shape[0]
-    part = width // len(reads_refs)
     model = h_ref.shape[1]
     chunk = model // 4
 
@@ -278,46 +287,45 @@
         return value
 
     def body():
-        index = lax.axis_index("seq")
-        begins = index // 2 == 0
-        follows = lax.rem(index, 2) == 1
+        follows = lax.rem(lax.axis_index("seq"), 2) == 1
         parts = []
         for start in range(0, width, QUAD):
             pieces = []
             for lane in range(start, start + QUAD, PAIR):
                 lanes = slice(lane, lane + PAIR)
-                state = jnp.where(begins, pair_state(init_ref, lane // PAIR), total(state_refs, lanes))
+                if begins is True:
+                    state = pair_state(init_ref, lane // PAIR)
+                else:
+                    state = total(state_refs, lanes)
+                    if begins is not False:
+                        state = jnp.where(begins, pair_state(init_ref, lane // PAIR), state)
                 step = mm(total(got_refs, lanes).astype(BF16), spread(state.astype(BF16)))
                 moved = state - step + total(got_refs, slice(width + lane, width + lane + PAIR))
                 pieces.append(jnp.where(follows, moved, state).astype(BF16))
-            reads_ref, inner = reads_refs[start // part], start % part
-            offset = reads_ref[:, part + inner : part + inner + QUAD]
-            read = mm(reads_ref[:, inner : inner + QUAD], spread(jnp.concatenate(pieces, axis=1)))
+            offset = reads_ref[:, width + start : width + start + QUAD]
+            read = mm(reads_ref[:, start : start + QUAD], spread(jnp.concatenate(pieces, axis=1)))
             parts.append((read + offset.astype(F32)).astype(BF16))
         inner_bf = jnp.concatenate(parts, axis=1)
         for start in range(0, model, chunk):
             lanes = slice(start, start + chunk)
             store(start, (h_ref[:, lanes].astype(F32) + mm(inner_bf, w_out_ref[:, lanes])).astype(BF16))
 
-    on_section(active, body)
-
-
-def split_finish(counts, refs):
-    states, gots, reads = counts
-    return refs[:states], refs[states : states + gots], refs[states + gots], refs[states + gots + 1 :][:reads], refs[states + gots + 1 + reads :]
-
-
-def first_finish(counts, *refs):
-    states, gots, init_ref, reads, (w_out_ref, h_ref, out_ref) = split_finish(counts, refs)
+    pl.when(here)(body)
+
+
+def first_finish(place, state_ref, got_ref, reads_ref, w_out_ref, h_ref, *rest):
+    out_ref = rest[-1]
 
     def store(start, value):
         out_ref[:, start : start + value.shape[1]] = value
 
-    finish(0, states, gots, init_ref, reads, w_out_ref, h_ref, store)
-
-
-def last_finish(counts, *refs):
-    states, gots, init_ref, reads, (w_out_ref, h_ref, first_ref, out_hbm, near, sems) = split_finish(counts, refs)
+    here = (lax.axis_index("section") == 0) & (lax.axis_index("seq") // 2 == place)
+    finish(here, place == 0, [state_ref], [got_ref], state_ref, reads_ref, w_out_ref, h_ref, store)
+
+
+def last_finish(count, *refs):
+    states, gots, refs = refs[: count - 1], refs[count - 1 : 2 * count - 1], refs[2 * count - 1 :]
+    init_ref, reads_ref, w_out_ref, h_ref, first_ref, out_hbm, near, sems = refs
     chunk = near.shape[1] // 4
 
     def write(start):
@@ -328,7 +336,8 @@
         near[:, start : start + chunk] = value
         write(start).start()
 
-    finish(1, states, gots, init_ref, reads, w_out_ref, h_ref, store)
+    begins = lax.axis_index("seq") // 2 == 0
+    finish(lax.axis_index("section") == 1, begins, states, gots, init_ref, reads_ref, w_out_ref, h_ref, store)
 
     @pl.when(lax.axis_index("section") == 0)
     def _():
@@ -339,7 +348,7 @@
         write(start).wait()
 
 
-def call(body, outs, scratch, args, kinds=None, name=None, out_kind=pltpu.VMEM):
+def call(body, outs, scratch, args, kinds=None, name=None, out_kind=pltpu.VMEM, aliases=None):
     specs = [pl.BlockSpec(memory_space=kind) for kind in (kinds or [pltpu.VMEM] * len(args))]
     return pl.pallas_call(
         body,
@@ -347,6 +356,7 @@
         in_specs=specs,
         out_specs=[pl.BlockSpec(memory_space=out_kind)] * len(outs),
         scratch_shapes=scratch,
+        input_output_aliases=aliases or {},
         compiler_params=pltpu.CompilerParams(vmem_limit_bytes=VMEM_LIMIT),
         name=name,
     )(*args)
@@ -374,70 +384,78 @@
     def swap(own, active, groups):
         return permute(own, active, [(2 * group + side, 2 * group + 1 - side) for group in groups for side in range(2)])
 
-    def layer(active, hidden):
-        h_scratch = [] if active else [pltpu.VMEM(hidden.shape, hidden.dtype)]
-        own, normed, keys, x_all, y_all = call(
+    def layer_front(active, hidden, weights):
+        small = [pltpu.VMEM(value.shape, value.dtype) for value in (norm_gain, w_rate, rate_base)]
+        near = [pltpu.VMEM((depth, 2 * width), BF16), pltpu.VMEM(hidden.shape, hidden.dtype)]
+        sems = [pltpu.SemaphoreType.DMA((quads, 2))]
+        return call(
             later_front if active else first_front,
             [maps] + rows_out,
-            [pltpu.VMEM((depth, 2 * width), BF16)]
-            + h_scratch
-            + [pltpu.VMEM(value.shape, value.dtype) for value in (norm_gain, w_rate, rate_base)]
-            + [pltpu.SemaphoreType.DMA((4,)), pltpu.SemaphoreType.DMA((quads, 2))],
-            [hidden if active else in_hbm(hidden), norm_gain, w_qkv, w_rate, rate_base],
-            [pltpu.VMEM if active else pltpu.HBM] + [pltpu.HBM] * 4,
+            (near if active == 0 else []) + small + [pltpu.SemaphoreType.DMA((4,))] + (sems if active == 0 else []),
+            [hidden, norm_gain, weights, w_rate, rate_base],
+            [pltpu.VMEM, pltpu.HBM, pltpu.VMEM, pltpu.HBM, pltpu.HBM] if active else [pltpu.HBM] * 5,
             name="later_front" if active else "first_front",
         )
 
-        def reads_of(picked, load, after):
-            part = len(picked) * QUAD
-            return call(
-                functools.partial(read_out, active, picked),
-                [shape((rows, 2 * part), BF16)] + [pltpu.VMEM(w_out.shape[1:], BF16)] * load,
-                [pltpu.VMEM((depth, part), BF16), pltpu.SemaphoreType.DMA((len(picked),)), pltpu.SemaphoreType.DMA],
-                [normed, keys, x_all, y_all, w_qkv, w_out, after],
-                [pltpu.VMEM] * 4 + [pltpu.HBM] * 2 + [pl.ANY],
-                name=f"reads{active}_{picked[0]}",
-            )
-
-        def hop(place, maps_here, state, after):
-            kinds = [pltpu.VMEM] * (len(maps_here) + 1) + [pl.ANY]
-
-            def body(*refs):
-                advance(active, place, refs[0], None if len(maps_here) == 1 else refs[1], *refs[len(maps_here) :])
-
-            (ahead,) = call(body, [shape((HD, width), BF16)], [], maps_here + [state, after], kinds, name=f"advance{active}_{place}")
-            pairs = [(2 * place + side, 2 * place + 2 + side) for side in range(2)]
-            return ahead, permute(ahead, active, pairs)
-
-        groups = count // 2
-        states, state = [], init_state
-        if active == 0:
-            got = [swap(own, active, range(groups))]
-            reads, near = reads_of(tuple(range(quads)), 1, init_state)
-            reads = [reads]
-            (both,) = call(functools.partial(compose, active), [maps], [], [own, got[0], reads[0]], [pltpu.VMEM] * 2 + [pl.ANY], name="compose")
-            for place in range(groups - 1):
-                ahead, state = hop(place, [both], state, both)
-                states.append(state)
-        else:
-            got = [swap(own, active, [group]) for group in range(groups)]
-            (reads,) = reads_of(tuple(range(quads // 2)), 0, init_state)
-            for place in range(groups - 1):
-                ahead, state = hop(place, [own, got[place]], state, reads)
-                states.append(state)
-            more, near = reads_of(tuple(range(quads // 2, quads)), 1, ahead)
-            reads = [reads, more]
-        return (len(states), len(got), len(reads)), [*states, *got, init_state, *reads, in_vmem(near), hidden]
-
-    counts, args = layer(0, tokens)
-    (first,) = call(functools.partial(first_finish, counts), [shape((rows, model), BF16)], [], args, name="first_finish")
+    def layer_reads(active, rows_of, weights, after):
+        near = [pltpu.VMEM((depth, width), BF16), pltpu.SemaphoreType.DMA((quads,))]
+        reads, w_out_near = call(
+            functools.partial(read_out, active),
+            [shape((rows, 2 * width), BF16), pltpu.VMEM(w_out.shape[1:], BF16)],
+            [pltpu.SemaphoreType.DMA] + (near if active == 0 else []),
+            [*rows_of, weights, w_out, after],
+            [pltpu.VMEM] * 4 + [pltpu.VMEM if active else pltpu.HBM, pltpu.HBM, pl.ANY],
+            name=f"reads{active}",
+        )
+        return reads, in_vmem(w_out_near)
+
+    def hop(active, place, maps_here, state, after):
+        def body(*refs):
+            advance(active, place, refs[0], None if len(maps_here) == 1 else refs[1], *refs[len(maps_here) :])
+
+        kinds = [pltpu.VMEM] * (len(maps_here) + 1) + [pl.ANY]
+        (ahead,) = call(body, [shape((HD, width), BF16)], [], maps_here + [state, after], kinds, name=f"advance{active}_{place}")
+        return ahead, permute(ahead, active, [(2 * place + side, 2 * place + 2 + side) for side in range(2)])
+
+    groups = count // 2
+
+    own, *rows_of = layer_front(0, in_hbm(tokens), w_qkv)
+    got = swap(own, 0, range(groups))
+    reads, w_out_near = layer_reads(0, rows_of, w_qkv, init_state)
+    (both,) = call(functools.partial(compose, 0), [maps], [], [own, got, reads], [pltpu.VMEM] * 2 + [pl.ANY], name="compose")
+    (w_near,) = call(
+        load, [pltpu.VMEM(w_qkv.shape[1:], BF16)], [pltpu.SemaphoreType.DMA], [w_qkv, both], [pltpu.HBM, pl.ANY], name="load"
+    )
+    w_near = in_vmem(w_near)
+    state, first = init_state, []
+    for place in range(groups):
+        here = state
+        if place + 1 < groups:
+            ahead, state = hop(0, place, [both], here, first[0] if first else both)
+        first = call(
+            functools.partial(first_finish, place),
+            [shape((rows, model), BF16)],
+            [],
+            [here, got, reads, w_out_near, tokens, ahead, *first],
+            [pltpu.VMEM] * 5 + [pl.ANY] + [pltpu.VMEM] * len(first),
+            name=f"first_finish_{place}",
+            aliases={6: 0} if first else None,
+        )
+    (first,) = first
     hidden = lax.ppermute(first, "section", [(0, 1)])
-    counts, args = layer(1, hidden)
+
+    own, *rows_of = layer_front(1, hidden, w_near)
+    gots = [swap(own, 1, [group]) for group in range(groups)]
+    states, state, ahead = [], init_state, own
+    for place in range(groups - 1):
+        ahead, state = hop(1, place, [own, gots[place]], state, ahead)
+        states.append(state)
+    reads, w_out_near = layer_reads(1, rows_of, w_near, ahead)
     (result,) = call(
-        functools.partial(last_finish, counts),
+        functools.partial(last_finish, groups),
         [shape((1, rows, model), BF16)],
         [pltpu.VMEM((rows, model), BF16), pltpu.SemaphoreType.DMA((4,))],
-        args + [first],
+        [*states, *gots, init_state, reads, w_out_near, hidden, first],
         name="last_finish",
         out_kind=pltpu.HBM,
     )

time: 65.5 us -> 58.9 us (0.90)
  the two profiles are of different devices: /device:TPU:25 before, /device:TPU:17 now
where the time goes in v7:
time: 58.9 us; the launch traced here: 58.5 us
  waiting for transfers between devices  30 us (51%)
  Pallas kernels  15.5 us (26%)
  starting transfers between devices  12.3 us (21%)
    ppermute x1, waiting for transfers between devices, shards(): hidden = lax.ppermute(first, 'section', [(0, 1)])  26.3 us
    pallas_call x17, Pallas kernels, call(): pl.pallas_call(body, out_shape=outs, in_specs=specs, out_specs=[pl.BlockS...  15.5 us
    ppermute x11, starting transfers between devices, permute(): lax.ppermute(value, ('section', 'seq'), [(base + source, base + target) f...  11 us
    ppermute x11, waiting for transfers between devices, permute(): lax.ppermute(value, ('section', 'seq'), [(base + source, base + target) f...  3.75 us
    ppermute x1, starting transfers between devices, shards(): hidden = lax.ppermute(first, 'section', [(0, 1)])  1.29 us
  transfers between devices with their start and end apart: 12, of which 3 were waited for; matrix products, arithmetic and copies ran while one was open for 0% of the time, Pallas kernels for 14%

profile of v7, /device:TPU:17, one launch (start us, length us, event | category | flops | bytes accessed | tf_op | source)
XLA Modules:
  0.0 58.5 jit_solution(10616138902878576444)
XLA Ops:
  0.0 0.0 copy-start
  0.0 0.1 first_front.1
  0.1 0.8 %collective-permute-start = (bf16[64,2048]{1,0:T(8,128)(2,1)S(1)}, bf16[64,2048]{1,0:T(8,128)(2,1)S(1)}, u32[]{:S(2)}, u32[]{:S(2)}) collective-permute-start(bf16[64,2048]{1,0:T(8,128)(2,1)S(1)} %get-tuple-element.19.own_ref), channel_id=1, source_target_pairs={{0,2},{2,0},{4,6},{6,4},{8,10},{10,8},{12,14},{14,12},{1,3},{3,1},... | collective-permute-start | bytes 786440 | tf_op jit(solution)/shard_map/ppermute | solution.py:382
  0.9 0.1 copy-done
  1.0 0.0 copy-start.1
  1.1 0.0 collective-permute-done.got_ref
  1.2 0.8 %collective-permute-start.1 = (bf16[64,1024]{1,0:T(8,128)(2,1)S(1)}, bf16[64,1024]{1,0:T(8,128)(2,1)S(1)}, u32[]{:S(2)}, u32[]{:S(2)}) collective-permute-start(bf16[64,1024]{1,0:T(8,128)(2,1)S(1)} %advance0_0.1.rest_0_), channel_id=1, source_target_pairs={{0,4},{2,6},{1,5},{3,7}} | collective-permute-start | bytes 393224 | tf_op jit(solution)/shard_map/ppermute | solution.py:382
  2.0 0.1 copy-done.1
  2.1 0.0 collective-permute-done.1.refs_1_.state_ref
  2.1 0.7 %collective-permute-start.2 = (bf16[64,1024]{1,0:T(8,128)(2,1)S(1)}, bf16[64,1024]{1,0:T(8,128)(2,1)S(1)}, u32[]{:S(2)}, u32[]{:S(2)}) collective-permute-start(bf16[64,1024]{1,0:T(8,128)(2,1)S(1)} %advance0_1.1.rest_0_), channel_id=1, source_target_pairs={{4,8},{6,10},{5,9},{7,11}} | collective-permute-start | bytes 393224 | tf_op jit(solution)/shard_map/ppermute | solution.py:382
  2.8 0.0 collective-permute-done.2.refs_1_.state_ref
  2.8 0.7 %collective-permute-start.3 = (bf16[64,1024]{1,0:T(8,128)(2,1)S(1)}, bf16[64,1024]{1,0:T(8,128)(2,1)S(1)}, u32[]{:S(2)}, u32[]{:S(2)}) collective-permute-start(bf16[64,1024]{1,0:T(8,128)(2,1)S(1)} %advance0_2.1.rest_0_), channel_id=1, source_target_pairs={{8,12},{10,14},{9,13},{11,15}} | collective-permute-start | bytes 393224 | tf_op jit(solution)/shard_map/ppermute | solution.py:382
  3.5 0.0 collective-permute-done.3.state_ref
  3.6 1.3 %collective-permute-start.4 = (bf16[128,2048]{1,0:T(8,128)(2,1)S(1)}, bf16[128,2048]{1,0:T(8,128)(2,1)S(1)}, u32[]{:S(2)}, u32[]{:S(2)}) collective-permute-start(bf16[128,2048]{1,0:T(8,128)(2,1)S(1)} %first_finish_3.1.refs_11_), channel_id=1, source_target_pairs={{0,16},{1,17},{2,18},{3,19},{4,20},{5,21},{6,22},{7,23},{8,24},{9,... | collective-permute-start | bytes 1572872 | tf_op jit(solution)/shard_map/ppermute | solution.py:445
  4.9 4.6 %load.1.rest_1_.w_ref = bf16[2048,3072]{1,0:T(8,128)(2,1)S(1)} custom-call(bf16[1,2048,3072]{2,1,0:T(8,128)(2,1)} %w_hbm.1, bf16[64,2048]{1,0:T(8,128)(2,1)S(1)} %compose.1.refs_0_.refs_2_.after_ref), custom_call_target="tpu_custom_call" | custom-call | tf_op jit(solution)/shard_map/load/pallas_call | solution.py:353
  9.5 26.3 %collective-permute-done.4.h_ref.refs_10_ = bf16[128,2048]{1,0:T(8,128)(2,1)S(1)} collective-permute-done((bf16[128,2048]{1,0:T(8,128)(2,1)S(1)}, bf16[128,2048]{1,0:T(8,128)(2,1)S(1)}, u32[]{:S(2)}, u32[]{:S(2)}) %collective-permute-start.4) | collective-permute-done | bytes 524320 | tf_op jit(solution)/shard_map/ppermute | solution.py:445
  35.8 5.1 %later_front.1 = (bf16[64,2048]{1,0:T(8,128)(2,1)S(1)}, bf16[128,2048]{1,0:T(8,128)(2,1)S(1)}, bf16[128,1024]{1,0:T(8,128)(2,1)S(1)}, bf16[128,1024]{1,0:T(8,128)(2,1)S(1)}, bf16[128,1024]{1,0:T(8,128)(2,1)S(1)}) custom-call(bf16[128,2048]{1,0:T(8,128)(2,1)S(1)} %collective-permute-done.4.h_ref.refs_10_, f32[1,2048]{1,0:T(1,128)} %rest_0_.3, ...), custom_call_target="tpu_custom_call" | custom-call | tf_op jit(solution)/shard_map/later_front/pallas_call | solution.py:353
  40.8 0.7 %collective-permute-start.5 = (bf16[64,2048]{1,0:T(8,128)(2,1)S(1)}, bf16[64,2048]{1,0:T(8,128)(2,1)S(1)}, u32[]{:S(2)}, u32[]{:S(2)}) collective-permute-start(bf16[64,2048]{1,0:T(8,128)(2,1)S(1)} %get-tuple-element.26.refs_0_.refs_3_), channel_id=1, source_target_pairs={{16,18},{18,16},{17,19},{19,17}} | collective-permute-start | bytes 786440 | tf_op jit(solution)/shard_map/ppermute | solution.py:382
  41.5 0.7 %collective-permute-start.7 = (bf16[64,2048]{1,0:T(8,128)(2,1)S(1)}, bf16[64,2048]{1,0:T(8,128)(2,1)S(1)}, u32[]{:S(2)}, u32[]{:S(2)}) collective-permute-start(bf16[64,2048]{1,0:T(8,128)(2,1)S(1)} %get-tuple-element.26.refs_0_.refs_3_), channel_id=1, source_target_pairs={{20,22},{22,20},{21,23},{23,21}} | collective-permute-start | bytes 786440 | tf_op jit(solution)/shard_map/ppermute | solution.py:382
  42.2 0.0 collective-permute-done.5.refs_1_.refs_3_
  42.3 0.7 %collective-permute-start.6 = (bf16[64,1024]{1,0:T(8,128)(2,1)S(1)}, bf16[64,1024]{1,0:T(8,128)(2,1)S(1)}, u32[]{:S(2)}, u32[]{:S(2)}) collective-permute-start(bf16[64,1024]{1,0:T(8,128)(2,1)S(1)} %advance1_0.1.refs_3_), channel_id=1, source_target_pairs={{16,20},{18,22},{17,21},{19,23}} | collective-permute-start | bytes 393224 | tf_op jit(solution)/shard_map/ppermute | solution.py:382
  42.9 2.8 %collective-permute-start.9 = (bf16[64,2048]{1,0:T(8,128)(2,1)S(1)}, bf16[64,2048]{1,0:T(8,128)(2,1)S(1)}, u32[]{:S(2)}, u32[]{:S(2)}) collective-permute-start(bf16[64,2048]{1,0:T(8,128)(2,1)S(1)} %get-tuple-element.26.refs_0_.refs_3_), channel_id=1, source_target_pairs={{24,26},{26,24},{25,27},{27,25}} | collective-permute-start | bytes 786440 | tf_op jit(solution)/shard_map/ppermute | solution.py:382
  45.8 0.0 collective-permute-done.7.refs_1_.refs_4_
  45.8 0.0 collective-permute-done.6.refs_2_.refs_0_
  45.8 1.3 %collective-permute-start.8 = (bf16[64,1024]{1,0:T(8,128)(2,1)S(1)}, bf16[64,1024]{1,0:T(8,128)(2,1)S(1)}, u32[]{:S(2)}, u32[]{:S(2)}) collective-permute-start(bf16[64,1024]{1,0:T(8,128)(2,1)S(1)} %advance1_1.1.refs_3_), channel_id=1, source_target_pairs={{20,24},{22,26},{21,25},{23,27}} | collective-permute-start | bytes 393224 | tf_op jit(solution)/shard_map/ppermute | solution.py:382
  47.1 0.7 %collective-permute-start.11 = (bf16[64,2048]{1,0:T(8,128)(2,1)S(1)}, bf16[64,2048]{1,0:T(8,128)(2,1)S(1)}, u32[]{:S(2)}, u32[]{:S(2)}) collective-permute-start(bf16[64,2048]{1,0:T(8,128)(2,1)S(1)} %get-tuple-element.26.refs_0_.refs_3_), channel_id=1, source_target_pairs={{28,30},{30,28},{29,31},{31,29}} | collective-permute-start | bytes 786440 | tf_op jit(solution)/shard_map/ppermute | solution.py:382
  47.8 2.2 %collective-permute-done.9.refs_1_.refs_5_ = bf16[64,2048]{1,0:T(8,128)(2,1)S(1)} collective-permute-done((bf16[64,2048]{1,0:T(8,128)(2,1)S(1)}, bf16[64,2048]{1,0:T(8,128)(2,1)S(1)}, u32[]{:S(2)}, u32[]{:S(2)}) %collective-permute-start.9) | collective-permute-done | bytes 262176 | tf_op jit(solution)/shard_map/ppermute | solution.py:382
  50.1 1.5 %collective-permute-done.8.refs_2_.refs_1_ = bf16[64,1024]{1,0:T(8,128)(2,1)S(1)} collective-permute-done((bf16[64,1024]{1,0:T(8,128)(2,1)S(1)}, bf16[64,1024]{1,0:T(8,128)(2,1)S(1)}, u32[]{:S(2)}, u32[]{:S(2)}) %collective-permute-start.8) | collective-permute-done | bytes 131104 | tf_op jit(solution)/shard_map/ppermute | solution.py:382
  51.5 0.4 advance1_2.1.after_ref
  51.9 1.3 %collective-permute-start.10 = (bf16[64,1024]{1,0:T(8,128)(2,1)S(1)}, bf16[64,1024]{1,0:T(8,128)(2,1)S(1)}, u32[]{:S(2)}, u32[]{:S(2)}) collective-permute-start(bf16[64,1024]{1,0:T(8,128)(2,1)S(1)} %advance1_2.1.after_ref), channel_id=1, source_target_pairs={{24,28},{26,30},{25,29},{27,31}} | collective-permute-start | bytes 393224 | tf_op jit(solution)/shard_map/ppermute | solution.py:382
  53.2 3.3 %reads1.1 = (bf16[128,2048]{1,0:T(8,128)(2,1)S(1)}, bf16[1024,2048]{1,0:T(8,128)(2,1)S(1)}) custom-call(bf16[128,2048]{1,0:T(8,128)(2,1)S(1)} %get-tuple-element.27.normed_ref, bf16[128,1024]{1,0:T(8,128)(2,1)S(1)} %get-tuple-element.28.keys_ref, bf16[128,1024]{1,0:T(8,128)(2,1)S(1)} %get-tuple-element.29.x_ref, ...), custom_call_target="tpu_custom_call" | custom-call | tf_op jit(solution)/shard_map/reads1/pallas_call | solution.py:353
  56.6 0.0 collective-permute-done.11.refs_6_
  56.6 0.0 collective-permute-done.10.refs_2_
  56.6 1.8 %last_finish.1 = bf16[1,128,2048]{2,1,0:T(8,128)(2,1)} custom-call(bf16[64,1024]{1,0:T(8,128)(2,1)S(1)} %collective-permute-done.6.refs_2_.refs_0_, bf16[64,1024]{1,0:T(8,128)(2,1)S(1)} %collective-permute-done.8.refs_2_.refs_1_, bf16[64,1024]{1,0:T(8,128)(2,1)S(1)} %collective-permute-done.10.refs_2_, ...), custom_call_target="tpu_custom_call" | custom-call | tf_op jit(solution)/shard_map/last_finish/pallas_call | solution.py:353
  (11 shorter events, 0.3 us)
Async XLA Ops:
  0.0 1.0 %copy-start = (f32[1,16,64,64]{3,2,1,0:T(8,128)S(1)}, f32[1,16,64,64]{3,2,1,0:T(8,128)}, u32[]{:S(2)}) copy-start(f32[1,16,64,64]{3,2,1,0:T(8,128)} %refs_7_.1) | copy-start | bytes 786436
  0.1 1.0 %collective-permute-start = (bf16[64,2048]{1,0:T(8,128)(2,1)S(1)}, bf16[64,2048]{1,0:T(8,128)(2,1)S(1)}, u32[]{:S(2)}, u32[]{:S(2)}) collective-permute-start(bf16[64,2048]{1,0:T(8,128)(2,1)S(1)} %get-tuple-element.19.own_ref), channel_id=1, source_target_pairs={{0,2},{2,0},{4,6},{6,4},{8,10},{10,8},{12,14},{14,12},{1,3},{3,1},... | collective-permute-start | bytes 786440 | tf_op jit(solution)/shard_map/ppermute | solution.py:382
  1.0 1.0 %copy-start.1 = (bf16[128,2048]{1,0:T(8,128)(2,1)S(1)}, bf16[128,2048]{1,0:T(8,128)(2,1)}, u32[]{:S(2)}) copy-start(bf16[128,2048]{1,0:T(8,128)(2,1)} %h_ref.7) | copy-start | bytes 1572868
  1.2 0.9 %collective-permute-start.1 = (bf16[64,1024]{1,0:T(8,128)(2,1)S(1)}, bf16[64,1024]{1,0:T(8,128)(2,1)S(1)}, u32[]{:S(2)}, u32[]{:S(2)}) collective-permute-start(bf16[64,1024]{1,0:T(8,128)(2,1)S(1)} %advance0_0.1.rest_0_), channel_id=1, source_target_pairs={{0,4},{2,6},{1,5},{3,7}} | collective-permute-start | bytes 393224 | tf_op jit(solution)/shard_map/ppermute | solution.py:382
  2.1 0.7 %collective-permute-start.2 = (bf16[64,1024]{1,0:T(8,128)(2,1)S(1)}, bf16[64,1024]{1,0:T(8,128)(2,1)S(1)}, u32[]{:S(2)}, u32[]{:S(2)}) collective-permute-start(bf16[64,1024]{1,0:T(8,128)(2,1)S(1)} %advance0_1.1.rest_0_), channel_id=1, source_target_pairs={{4,8},{6,10},{5,9},{7,11}} | collective-permute-start | bytes 393224 | tf_op jit(solution)/shard_map/ppermute | solution.py:382
  2.8 0.7 %collective-permute-start.3 = (bf16[64,1024]{1,0:T(8,128)(2,1)S(1)}, bf16[64,1024]{1,0:T(8,128)(2,1)S(1)}, u32[]{:S(2)}, u32[]{:S(2)}) collective-permute-start(bf16[64,1024]{1,0:T(8,128)(2,1)S(1)} %advance0_2.1.rest_0_), channel_id=1, source_target_pairs={{8,12},{10,14},{9,13},{11,15}} | collective-permute-start | bytes 393224 | tf_op jit(solution)/shard_map/ppermute | solution.py:382
  3.6 32.2 %collective-permute-start.4 = (bf16[128,2048]{1,0:T(8,128)(2,1)S(1)}, bf16[128,2048]{1,0:T(8,128)(2,1)S(1)}, u32[]{:S(2)}, u32[]{:S(2)}) collective-permute-start(bf16[128,2048]{1,0:T(8,128)(2,1)S(1)} %first_finish_3.1.refs_11_), channel_id=1, source_target_pairs={{0,16},{1,17},{2,18},{3,19},{4,20},{5,21},{6,22},{7,23},{8,24},{9,... | collective-permute-start | bytes 1572872 | tf_op jit(solution)/shard_map/ppermute | solution.py:445
  40.8 1.4 %collective-permute-start.5 = (bf16[64,2048]{1,0:T(8,128)(2,1)S(1)}, bf16[64,2048]{1,0:T(8,128)(2,1)S(1)}, u32[]{:S(2)}, u32[]{:S(2)}) collective-permute-start(bf16[64,2048]{1,0:T(8,128)(2,1)S(1)} %get-tuple-element.26.refs_0_.refs_3_), channel_id=1, source_target_pairs={{16,18},{18,16},{17,19},{19,17}} | collective-permute-start | bytes 786440 | tf_op jit(solution)/shard_map/ppermute | solution.py:382
  41.5 4.2 %collective-permute-start.7 = (bf16[64,2048]{1,0:T(8,128)(2,1)S(1)}, bf16[64,2048]{1,0:T(8,128)(2,1)S(1)}, u32[]{:S(2)}, u32[]{:S(2)}) collective-permute-start(bf16[64,2048]{1,0:T(8,128)(2,1)S(1)} %get-tuple-element.26.refs_0_.refs_3_), channel_id=1, source_target_pairs={{20,22},{22,20},{21,23},{23,21}} | collective-permute-start | bytes 786440 | tf_op jit(solution)/shard_map/ppermute | solution.py:382
  42.3 3.5 %collective-permute-start.6 = (bf16[64,1024]{1,0:T(8,128)(2,1)S(1)}, bf16[64,1024]{1,0:T(8,128)(2,1)S(1)}, u32[]{:S(2)}, u32[]{:S(2)}) collective-permute-start(bf16[64,1024]{1,0:T(8,128)(2,1)S(1)} %advance1_0.1.refs_3_), channel_id=1, source_target_pairs={{16,20},{18,22},{17,21},{19,23}} | collective-permute-start | bytes 393224 | tf_op jit(solution)/shard_map/ppermute | solution.py:382
  42.9 7.1 %collective-permute-start.9 = (bf16[64,2048]{1,0:T(8,128)(2,1)S(1)}, bf16[64,2048]{1,0:T(8,128)(2,1)S(1)}, u32[]{:S(2)}, u32[]{:S(2)}) collective-permute-start(bf16[64,2048]{1,0:T(8,128)(2,1)S(1)} %get-tuple-element.26.refs_0_.refs_3_), channel_id=1, source_target_pairs={{24,26},{26,24},{25,27},{27,25}} | collective-permute-start | bytes 786440 | tf_op jit(solution)/shard_map/ppermute | solution.py:382
  45.8 5.7 %collective-permute-start.8 = (bf16[64,1024]{1,0:T(8,128)(2,1)S(1)}, bf16[64,1024]{1,0:T(8,128)(2,1)S(1)}, u32[]{:S(2)}, u32[]{:S(2)}) collective-permute-start(bf16[64,1024]{1,0:T(8,128)(2,1)S(1)} %advance1_1.1.refs_3_), channel_id=1, source_target_pairs={{20,24},{22,26},{21,25},{23,27}} | collective-permute-start | bytes 393224 | tf_op jit(solution)/shard_map/ppermute | solution.py:382
  47.1 9.5 %collective-permute-start.11 = (bf16[64,2048]{1,0:T(8,128)(2,1)S(1)}, bf16[64,2048]{1,0:T(8,128)(2,1)S(1)}, u32[]{:S(2)}, u32[]{:S(2)}) collective-permute-start(bf16[64,2048]{1,0:T(8,128)(2,1)S(1)} %get-tuple-element.26.refs_0_.refs_3_), channel_id=1, source_target_pairs={{28,30},{30,28},{29,31},{31,29}} | collective-permute-start | bytes 786440 | tf_op jit(solution)/shard_map/ppermute | solution.py:382
  51.9 4.7 %collective-permute-start.10 = (bf16[64,1024]{1,0:T(8,128)(2,1)S(1)}, bf16[64,1024]{1,0:T(8,128)(2,1)S(1)}, u32[]{:S(2)}, u32[]{:S(2)}) collective-permute-start(bf16[64,1024]{1,0:T(8,128)(2,1)S(1)} %advance1_2.1.after_ref), channel_id=1, source_target_pairs={{24,28},{26,30},{25,29},{27,31}} | collective-permute-start | bytes 393224 | tf_op jit(solution)/shard_map/ppermute | solution.py:382

commit v8 on v7

--- a/solution.py
+++ b/solution.py
@@ -76,63 +76,69 @@
     return mm(high, pick) + mm(low, pick)
 
 
-def staged(groups, depth=3):
-    for group in groups[:depth]:
-        for copy in group:
-            copy.start()
-
-    def wait(index):
-        for copy in groups[index]:
-            copy.wait()
-        if index + depth < len(groups):
-            for copy in groups[index + depth]:
-                copy.start()
-
-    return wait
+def start_all(copies):
+    for copy in copies:
+        copy.start()
+
+
+def wait_all(copies):
+    for copy in copies:
+        copy.wait()
 
 
 def on_section(active, body):
     pl.when(lax.axis_index("section") == active)(body)
 
 
-def front(active, h_ref, gain_hbm, w_ref, w_rate_hbm, base_hbm, maps, normed_out, keys_out, x_out, y_out, wkv, h_in, gain, w_rate, base, small_sems, sems):
+def at_pair(places, active):
+    pair = lax.axis_index("seq") // 2
+    first, last = places[0], places[-1]
+    return (lax.axis_index("section") == active) & (pair >= first) & (pair <= last)
+
+
+def front(here, h_refs, gain_ref, w_ref, w_rate_ref, base_ref, maps, normed_out, keys_out, x_out, y_out, h_in, near=None):
     width = keys_out.shape[1]
     quads = width // QUAD
 
     def body():
-        sources = [(gain_hbm, gain), (w_rate_hbm, w_rate), (base_hbm, base)]
-        if h_in is not None:
-            sources.append((h_ref, h_in))
-        small = [pltpu.make_async_copy(source, target, small_sems.at[index]) for index, (source, target) in enumerate(sources)]
-        for copy in small:
-            copy.start()
-        if wkv is not None:
-            wait_group = staged(
+        if near is None:
+            groups = []
+            gain, w_rate, base, weights, base_lane = gain_ref, w_rate_ref, base_ref, w_ref, width
+            for place, ref in enumerate(h_refs):
+
+                @pl.when(lax.axis_index("seq") // 2 == place)
+                def _():
+                    h_in[...] = ref[...]
+        else:
+            gain, w_rate, base, weights, small_sems, sems = near
+            base_lane = 0
+            pairs = [(gain_ref, gain), (w_rate_ref, w_rate), (base_ref, base), (h_refs[0], h_in)]
+            small = [pltpu.make_async_copy(source, target, small_sems.at[index]) for index, (source, target) in enumerate(pairs)]
+            groups = [
                 [
-                    [
-                        pltpu.make_async_copy(
-                            w_ref.at[0, :, pl.ds((side + 1) * width + quad * QUAD, QUAD)],
-                            wkv.at[:, pl.ds(side * width + quad * QUAD, QUAD)],
-                            sems.at[quad, side],
-                        )
-                        for side in range(2)
-                    ]
-                    for quad in range(quads)
+                    pltpu.make_async_copy(
+                        w_ref.at[0, :, pl.ds((side + 1) * width + quad * QUAD, QUAD)],
+                        weights.at[:, pl.ds(side * width + quad * QUAD, QUAD)],
+                        sems.at[quad, side],
+                    )
+                    for side in range(2)
                 ]
-            )
-        for copy in small:
-            copy.wait()
-        normed = norm_rows((h_ref if h_in is None else h_in)[...], gain[...])
+                for quad in range(quads)
+            ]
+            start_all(small)
+            start_all(groups[0])
+            wait_all(small)
+            start_all(groups[1])
+        normed = norm_rows(h_in[...], gain[...])
         normed_out[...] = normed
         rates = spread_rates(normed, w_rate[0], base[...])
         ones = head_ones()
 
         def project(quad):
-            if wkv is None:
-                weights, base_lane = w_ref, width
-            else:
-                weights, base_lane = wkv, 0
-                wait_group(quad)
+            if groups:
+                wait_all(groups[quad])
+                if quad + 2 < quads:
+                    start_all(groups[quad + 2])
             key_lane = base_lane + quad * QUAD
             return [mm(normed, weights[:, lane : lane + QUAD]) for lane in (key_lane, key_lane + width)]
 
@@ -167,51 +173,64 @@
             before = after
         chain(quads - 1, *before)
 
-    on_section(active, body)
-
-
-def first_front(h_hbm, *rest):
-    front(0, h_hbm, *rest)
-
-
-def later_front(h_ref, *rest):
-    *rest, gain, w_rate, base, small_sems = rest
-    front(1, h_ref, *rest, None, None, gain, w_rate, base, small_sems, None)
-
-
-def load(w_hbm, after_ref, near, sem):
+    pl.when(here)(body)
+
+
+def first_front(h_hbm, gain, weights, w_rate, base, maps, normed_out, keys_out, x_out, y_out, h_in, *near):
+    here = lax.axis_index("section") == 0
+    front(here, [h_hbm], gain, weights, w_rate, base, maps, normed_out, keys_out, x_out, y_out, h_in, near)
+
+
+def later_front(*refs):
+    refs, rest = refs[:-10], refs[-10:]
+    front(lax.axis_index("section") == 1, refs, *rest)
+
+
+def load(*refs):
+    count = (len(refs) - 2) // 2
+    sources, targets, sems = refs[:count], refs[count + 1 : -1], refs[-1]
+
     def body():
-        copy = pltpu.make_async_copy(w_hbm.at[0], near, sem)
-        copy.start()
-        copy.wait()
+        copies = [pltpu.make_async_copy(source, target, sems.at[index]) for index, (source, target) in enumerate(zip(sources, targets))]
+        start_all(copies)
+        wait_all(copies)
 
     on_section(1, body)
 
 
-def read_out(active, normed_ref, keys_ref, x_ref, y_ref, w_ref, w_out_hbm, after_ref, reads_out, w_out, load_sem, wq=None, sems=None):
+def read_out(active, places, normed_ref, keys_ref, x_ref, y_ref, w_ref, w_out_hbm, after_ref, *rest):
+    if active:
+        reads_out, w_out, load_sem = rest
+    else:
+        reads_out, w_out, load_sem, wq, sems = rest[-5:]
     rows, width = keys_ref.shape
     quads = width // QUAD
 
     def body():
-        if wq is not None:
-            wait_group = staged(
-                [
-                    [pltpu.make_async_copy(w_ref.at[0, :, pl.ds(quad * QUAD, QUAD)], wq.at[:, pl.ds(quad * QUAD, QUAD)], sems.at[quad])]
-                    for quad in range(quads)
-                ],
-                quads,
-            )
-        fetch = pltpu.make_async_copy(w_out_hbm.at[0], w_out, load_sem)
-        fetch.start()
-        weights = w_ref if wq is None else wq
+        fetch = [pltpu.make_async_copy(w_out_hbm.at[0], w_out, load_sem)]
+        if active:
+            weights, groups = w_ref, []
+            start_all(fetch)
+        else:
+            weights = wq
+            groups = [
+                [pltpu.make_async_copy(w_ref.at[0, :, pl.ds(quad * QUAD, QUAD)], wq.at[:, pl.ds(quad * QUAD, QUAD)], sems.at[quad])]
+                for quad in range(quads)
+            ]
+            start_all(groups[0])
+            start_all(groups[1])
         normed = normed_ref[...]
         ones = head_ones()
         row = lax.broadcasted_iota(jnp.int32, (rows, 2 * rows), 0)
         lane = lax.rem(lax.broadcasted_iota(jnp.int32, (rows, 2 * rows), 1), rows)
         causal = row >= lane
         for quad in range(quads):
-            if wq is not None:
-                wait_group(quad)
+            if groups:
+                wait_all(groups[quad])
+                if quad + 2 < quads:
+                    start_all(groups[quad + 2])
+                if quad + 3 == quads:
+                    start_all(fetch)
             queries = unit_heads(mm(normed, weights[:, quad * QUAD : (quad + 1) * QUAD]), ones)
             queries_bf = queries.astype(BF16)
             for half in range(2):
@@ -223,9 +242,9 @@
                 both = mm(scores, spread_two(x_ref[:, place], y_ref[:, place]))
                 reads_out[:, place] = (queries[:, own] - both[:, :PAIR]).astype(BF16)
                 reads_out[:, width + start : width + start + PAIR] = both[:, PAIR:].astype(BF16)
-        fetch.wait()
-
-    on_section(active, body)
+        wait_all(fetch)
+
+    pl.when(at_pair(places, active))(body)
 
 
 def compose(active, own_ref, got_ref, after_ref, out_ref):
@@ -313,19 +332,16 @@
     pl.when(here)(body)
 
 
-def first_finish(place, state_ref, got_ref, reads_ref, w_out_ref, h_ref, *rest):
-    out_ref = rest[-1]
-
+def first_finish(place, state_ref, got_ref, reads_ref, w_out_ref, h_ref, after_ref, out_ref):
     def store(start, value):
         out_ref[:, start : start + value.shape[1]] = value
 
-    here = (lax.axis_index("section") == 0) & (lax.axis_index("seq") // 2 == place)
-    finish(here, place == 0, [state_ref], [got_ref], state_ref, reads_ref, w_out_ref, h_ref, store)
+    finish(at_pair([place], 0), place == 0, [state_ref], [got_ref], state_ref, reads_ref, w_out_ref, h_ref, store)
 
 
 def last_finish(count, *refs):
     states, gots, refs = refs[: count - 1], refs[count - 1 : 2 * count - 1], refs[2 * count - 1 :]
-    init_ref, reads_ref, w_out_ref, h_ref, first_ref, out_hbm, near, sems = refs
+    init_ref, reads_ref, w_out_ref, h_ref, *first_refs, out_hbm, near, sems = refs
     chunk = near.shape[1] // 4
 
     def write(start):
@@ -339,16 +355,18 @@
     begins = lax.axis_index("seq") // 2 == 0
     finish(lax.axis_index("section") == 1, begins, states, gots, init_ref, reads_ref, w_out_ref, h_ref, store)
 
-    @pl.when(lax.axis_index("section") == 0)
-    def _():
-        for start in range(0, near.shape[1], chunk):
-            store(start, first_ref[:, start : start + chunk])
+    for place, first_ref in enumerate(first_refs):
+
+        @pl.when(at_pair([place], 0))
+        def _():
+            for start in range(0, near.shape[1], chunk):
+                store(start, first_ref[:, start : start + chunk])
 
     for start in range(0, near.shape[1], chunk):
         write(start).wait()
 
 
-def call(body, outs, scratch, args, kinds=None, name=None, out_kind=pltpu.VMEM, aliases=None):
+def call(body, outs, scratch, args, kinds=None, name=None, out_kind=pltpu.VMEM):
     specs = [pl.BlockSpec(memory_space=kind) for kind in (kinds or [pltpu.VMEM] * len(args))]
     return pl.pallas_call(
         body,
@@ -356,7 +374,6 @@
         in_specs=specs,
         out_specs=[pl.BlockSpec(memory_space=out_kind)] * len(outs),
         scratch_shapes=scratch,
-        input_output_aliases=aliases or {},
         compiler_params=pltpu.CompilerParams(vmem_limit_bytes=VMEM_LIMIT),
         name=name,
     )(*args)
@@ -384,28 +401,15 @@
     def swap(own, active, groups):
         return permute(own, active, [(2 * group + side, 2 * group + 1 - side) for group in groups for side in range(2)])
 
-    def layer_front(active, hidden, weights):
-        small = [pltpu.VMEM(value.shape, value.dtype) for value in (norm_gain, w_rate, rate_base)]
-        near = [pltpu.VMEM((depth, 2 * width), BF16), pltpu.VMEM(hidden.shape, hidden.dtype)]
-        sems = [pltpu.SemaphoreType.DMA((quads, 2))]
-        return call(
-            later_front if active else first_front,
-            [maps] + rows_out,
-            (near if active == 0 else []) + small + [pltpu.SemaphoreType.DMA((4,))] + (sems if active == 0 else []),
-            [hidden, norm_gain, weights, w_rate, rate_base],
-            [pltpu.VMEM, pltpu.HBM, pltpu.VMEM, pltpu.HBM, pltpu.HBM] if active else [pltpu.HBM] * 5,
-            name="later_front" if active else "first_front",
-        )
-
-    def layer_reads(active, rows_of, weights, after):
+    def layer_reads(active, places, rows_of, weights, after):
         near = [pltpu.VMEM((depth, width), BF16), pltpu.SemaphoreType.DMA((quads,))]
         reads, w_out_near = call(
-            functools.partial(read_out, active),
+            functools.partial(read_out, active, places),
             [shape((rows, 2 * width), BF16), pltpu.VMEM(w_out.shape[1:], BF16)],
             [pltpu.SemaphoreType.DMA] + (near if active == 0 else []),
             [*rows_of, weights, w_out, after],
             [pltpu.VMEM] * 4 + [pltpu.VMEM if active else pltpu.HBM, pltpu.HBM, pl.ANY],
-            name=f"reads{active}",
+            name=f"reads{active}_{places[0]}",
         )
         return reads, in_vmem(w_out_near)
 
@@ -419,43 +423,64 @@
 
     groups = count // 2
 
-    own, *rows_of = layer_front(0, in_hbm(tokens), w_qkv)
-    got = swap(own, 0, range(groups))
-    reads, w_out_near = layer_reads(0, rows_of, w_qkv, init_state)
-    (both,) = call(functools.partial(compose, 0), [maps], [], [own, got, reads], [pltpu.VMEM] * 2 + [pl.ANY], name="compose")
-    (w_near,) = call(
-        load, [pltpu.VMEM(w_qkv.shape[1:], BF16)], [pltpu.SemaphoreType.DMA], [w_qkv, both], [pltpu.HBM, pl.ANY], name="load"
+    own, *rows_of = call(
+        first_front,
+        [maps] + rows_out,
+        [pltpu.VMEM(value.shape, value.dtype) for value in (tokens, norm_gain, w_rate, rate_base)]
+        + [pltpu.VMEM((depth, 2 * width), BF16), pltpu.SemaphoreType.DMA((4,)), pltpu.SemaphoreType.DMA((quads, 2))],
+        [in_hbm(tokens), norm_gain, w_qkv, w_rate, rate_base],
+        [pltpu.HBM] * 5,
+        name="first_front",
     )
-    w_near = in_vmem(w_near)
-    state, first = init_state, []
+    got_first = swap(own, 0, [0])
+    got_rest = swap(own, 0, range(1, groups))
+    read_first = layer_reads(0, [0], rows_of, w_qkv, init_state)
+    ahead, state = hop(0, 0, [own, got_first], init_state, read_first[0])
+    read_rest = layer_reads(0, range(1, groups), rows_of, w_qkv, ahead)
+    (both,) = call(
+        functools.partial(compose, 0), [maps], [], [own, got_rest, read_rest[0]], [pltpu.VMEM] * 2 + [pl.ANY], name="compose"
+    )
+    firsts, hiddens, here = [], [], init_state
     for place in range(groups):
-        here = state
-        if place + 1 < groups:
-            ahead, state = hop(0, place, [both], here, first[0] if first else both)
-        first = call(
+        got, (reads, w_out_near) = (got_rest, read_rest) if place else (got_first, read_first)
+        if 0 < place < groups - 1:
+            ahead, state = hop(0, place, [both], here, firsts[-1])
+        (first,) = call(
             functools.partial(first_finish, place),
             [shape((rows, model), BF16)],
             [],
-            [here, got, reads, w_out_near, tokens, ahead, *first],
-            [pltpu.VMEM] * 5 + [pl.ANY] + [pltpu.VMEM] * len(first),
+            [here, got, reads, w_out_near, tokens, ahead],
+            [pltpu.VMEM] * 5 + [pl.ANY],
             name=f"first_finish_{place}",
-            aliases={6: 0} if first else None,
         )
-    (first,) = first
-    hidden = lax.ppermute(first, "section", [(0, 1)])
-
-    own, *rows_of = layer_front(1, hidden, w_near)
+        firsts.append(first)
+        hiddens.append(lax.ppermute(first, ("section", "seq"), [(2 * place + side, count + 2 * place + side) for side in range(2)]))
+        here = state
+
+    params = [norm_gain, w_qkv, w_rate, rate_base]
+    gain_near, w_near, rate_near, base_near = call(
+        load,
+        [pltpu.VMEM(value.shape, value.dtype) for value in params],
+        [pltpu.SemaphoreType.DMA((4,))],
+        params + [both],
+        [pltpu.HBM] * 4 + [pl.ANY],
+        name="load",
+    )
+    params = [in_vmem(value) for value in (gain_near, w_near.reshape(w_qkv.shape[1:]), rate_near, base_near)]
+    own, *rows_of, hidden = call(
+        later_front, [maps] + rows_out + [shape((rows, model), BF16)], [], [*hiddens, *params], name="later_front"
+    )
     gots = [swap(own, 1, [group]) for group in range(groups)]
     states, state, ahead = [], init_state, own
     for place in range(groups - 1):
         ahead, state = hop(1, place, [own, gots[place]], state, ahead)
         states.append(state)
-    reads, w_out_near = layer_reads(1, rows_of, w_near, ahead)
+    reads, w_out_near = layer_reads(1, range(groups), rows_of, params[1], ahead)
     (result,) = call(
         functools.partial(last_finish, groups),
         [shape((1, rows, model), BF16)],
         [pltpu.VMEM((rows, model), BF16), pltpu.SemaphoreType.DMA((4,))],
-        [*states, *gots, init_state, reads, w_out_near, hidden, first],
+        [*states, *gots, init_state, reads, w_out_near, hidden, *firsts],
         name="last_finish",
         out_kind=pltpu.HBM,
     )

time: 58.9 us -> 55 us (0.934)
  waiting for transfers between devices: 30 us -> 24.6 us
  starting transfers between devices: 12.3 us -> 14.5 us
    ppermute x1 -> x4, waiting for transfers between devices: 26.3 us -> 20.8 us  [shards(): lax.ppermute(first, ('section', 'seq'), [(2 * place + side, count + 2 * p...]
    ppermute x1 -> x4, starting transfers between devices: 1.29 us -> 3.37 us  [shards(): lax.ppermute(first, ('section', 'seq'), [(2 * place + side, count + 2 * p...]
    pallas_call x17 -> x18, Pallas kernels: 15.5 us -> 15 us  [call(): pl.pallas_call(body, out_shape=outs, in_specs=specs, out_specs=[pl.BlockS...]
    ppermute x11 -> x12, starting transfers between devices: 11 us -> 11.1 us  [permute(): lax.ppermute(value, ('section', 'seq'), [(base + source, base + target) f...]
    ppermute x11 -> x12, waiting for transfers between devices: 3.75 us -> 3.75 us  [permute(): lax.ppermute(value, ('section', 'seq'), [(base + source, base + target) f...]
  transfers between devices with their start and end apart: 12 -> 16, of which waited for: 3 -> 3; matrix products, arithmetic and copies ran while one was open for 0% -> 0% of each run, Pallas kernels for 14% -> 16%
where the time goes in v8:
time: 55 us; the launch traced here: 54.7 us
  waiting for transfers between devices  24.6 us (45%)
  Pallas kernels  15 us (27%)
  starting transfers between devices  14.5 us (26%)
    ppermute x4, waiting for transfers between devices, shards(): lax.ppermute(first, ('section', 'seq'), [(2 * place + side, count + 2 * p...  20.8 us
    pallas_call x18, Pallas kernels, call(): pl.pallas_call(body, out_shape=outs, in_specs=specs, out_specs=[pl.BlockS...  15 us
    ppermute x12, starting transfers between devices, permute(): lax.ppermute(value, ('section', 'seq'), [(base + source, base + target) f...  11.1 us
    ppermute x12, waiting for transfers between devices, permute(): lax.ppermute(value, ('section', 'seq'), [(base + source, base + target) f...  3.75 us
    ppermute x4, starting transfers between devices, shards(): lax.ppermute(first, ('section', 'seq'), [(2 * place + side, count + 2 * p...  3.37 us
  transfers between devices with their start and end apart: 16, of which 3 were waited for; matrix products, arithmetic and copies ran while one was open for 0% of the time, Pallas kernels for 16%

profile of v8, /device:TPU:17, one launch (start us, length us, event | category | flops | bytes accessed | tf_op | source)
XLA Modules:
  0.0 54.7 jit_solution(12779375317392017589)
XLA Ops:
  0.0 0.0 copy-start.1
  0.0 0.1 first_front.1
  0.1 0.8 %collective-permute-start = (bf16[64,2048]{1,0:T(8,128)(2,1)S(1)}, bf16[64,2048]{1,0:T(8,128)(2,1)S(1)}, u32[]{:S(2)}, u32[]{:S(2)}) collective-permute-start(bf16[64,2048]{1,0:T(8,128)(2,1)S(1)} %get-tuple-element.26.refs_0_.own_ref), channel_id=1, source_target_pairs={{0,2},{2,0},{1,3},{3,1}} | collective-permute-start | bytes 786440 | tf_op jit(solution)/shard_map/ppermute | solution.py:399
  0.9 0.7 %collective-permute-start.3 = (bf16[64,2048]{1,0:T(8,128)(2,1)S(1)}, bf16[64,2048]{1,0:T(8,128)(2,1)S(1)}, u32[]{:S(2)}, u32[]{:S(2)}) collective-permute-start(bf16[64,2048]{1,0:T(8,128)(2,1)S(1)} %get-tuple-element.26.refs_0_.own_ref), channel_id=1, source_target_pairs={{4,6},{6,4},{8,10},{10,8},{12,14},{14,12},{5,7},{7,5},{9,11},{11,9... | collective-permute-start | bytes 786440 | tf_op jit(solution)/shard_map/ppermute | solution.py:399
  1.6 0.0 copy-done.1
  1.6 0.1 reads0_0.1
  1.7 0.0 collective-permute-done.refs_1_.got_ref
  1.8 0.0 copy-start
  1.8 0.8 %collective-permute-start.2 = (bf16[64,1024]{1,0:T(8,128)(2,1)S(1)}, bf16[64,1024]{1,0:T(8,128)(2,1)S(1)}, u32[]{:S(2)}, u32[]{:S(2)}) collective-permute-start(bf16[64,1024]{1,0:T(8,128)(2,1)S(1)} %advance0_0.1.after_ref), channel_id=1, source_target_pairs={{0,4},{2,6},{1,5},{3,7}} | collective-permute-start | bytes 393224 | tf_op jit(solution)/shard_map/ppermute | solution.py:399
  2.6 0.1 reads0_1.1
  2.7 0.1 copy-done
  2.8 0.0 collective-permute-done.3.got_ref
  2.8 0.0 collective-permute-done.2.refs_1_.state_ref
  2.8 0.7 %collective-permute-start.5 = (bf16[64,1024]{1,0:T(8,128)(2,1)S(1)}, bf16[64,1024]{1,0:T(8,128)(2,1)S(1)}, u32[]{:S(2)}, u32[]{:S(2)}) collective-permute-start(bf16[64,1024]{1,0:T(8,128)(2,1)S(1)} %advance0_1.1.after_ref), channel_id=1, source_target_pairs={{4,8},{6,10},{5,9},{7,11}} | collective-permute-start | bytes 393224 | tf_op jit(solution)/shard_map/ppermute | solution.py:399
  3.6 0.0 collective-permute-done.5.refs_1_.state_ref
  3.6 0.7 %collective-permute-start.7 = (bf16[64,1024]{1,0:T(8,128)(2,1)S(1)}, bf16[64,1024]{1,0:T(8,128)(2,1)S(1)}, u32[]{:S(2)}, u32[]{:S(2)}) collective-permute-start(bf16[64,1024]{1,0:T(8,128)(2,1)S(1)} %advance0_2.1.after_ref), channel_id=1, source_target_pairs={{8,12},{10,14},{9,13},{11,15}} | collective-permute-start | bytes 393224 | tf_op jit(solution)/shard_map/ppermute | solution.py:399
  4.3 0.7 %collective-permute-start.1 = (bf16[128,2048]{1,0:T(8,128)(2,1)S(1)}, bf16[128,2048]{1,0:T(8,128)(2,1)S(1)}, u32[]{:S(2)}, u32[]{:S(2)}) collective-permute-start(bf16[128,2048]{1,0:T(8,128)(2,1)S(1)} %first_finish_0.1.refs_2_.refs_11_), channel_id=1, source_target_pairs={{0,16},{2,18},{1,17},{3,19}} | collective-permute-start | bytes 1572872 | tf_op jit(solution)/shard_map/ppermute | solution.py:457
  5.0 0.7 %collective-permute-start.4 = (bf16[128,2048]{1,0:T(8,128)(2,1)S(1)}, bf16[128,2048]{1,0:T(8,128)(2,1)S(1)}, u32[]{:S(2)}, u32[]{:S(2)}) collective-permute-start(bf16[128,2048]{1,0:T(8,128)(2,1)S(1)} %first_finish_1.1.refs_2_.refs_12_), channel_id=1, source_target_pairs={{4,20},{6,22},{5,21},{7,23}} | collective-permute-start | bytes 1572872 | tf_op jit(solution)/shard_map/ppermute | solution.py:457
  5.7 1.3 %collective-permute-start.6 = (bf16[128,2048]{1,0:T(8,128)(2,1)S(1)}, bf16[128,2048]{1,0:T(8,128)(2,1)S(1)}, u32[]{:S(2)}, u32[]{:S(2)}) collective-permute-start(bf16[128,2048]{1,0:T(8,128)(2,1)S(1)} %first_finish_2.1.refs_13_), channel_id=1, source_target_pairs={{8,24},{10,26},{9,25},{11,27}} | collective-permute-start | bytes 1572872 | tf_op jit(solution)/shard_map/ppermute | solution.py:457
  7.0 0.0 collective-permute-done.7.state_ref
  7.0 0.2 first_finish_3.1.refs_14_
  7.2 0.7 %collective-permute-start.8 = (bf16[128,2048]{1,0:T(8,128)(2,1)S(1)}, bf16[128,2048]{1,0:T(8,128)(2,1)S(1)}, u32[]{:S(2)}, u32[]{:S(2)}) collective-permute-start(bf16[128,2048]{1,0:T(8,128)(2,1)S(1)} %first_finish_3.1.refs_14_), channel_id=1, source_target_pairs={{12,28},{14,30},{13,29},{15,31}} | collective-permute-start | bytes 1572872 | tf_op jit(solution)/shard_map/ppermute | solution.py:457
  7.9 4.6 %load.1 = (f32[1,2048]{1,0:T(1,128)S(1)}, bf16[1,2048,3072]{2,1,0:T(8,128)(2,1)S(1)}, bf16[1,16,2048]{2,1,0:T(8,128)(2,1)S(1)}, f32[1,16]{1,0:T(1,128)S(1)}) custom-call(f32[1,2048]{1,0:T(1,128)} %refs_0_.1, bf16[1,2048,3072]{2,1,0:T(8,128)(2,1)} %refs_1_.1, bf16[1,16,2048]{2,1,0:T(8,128)(2,1)} %bitcast.5, f32[1,16]{1,0:T(1,128)} %refs_3_.1, ...), custom_call_target="tpu_custom_call" | custom-call | tf_op jit(solution)/shard_map/load/pallas_call | solution.py:371
  12.6 0.0 collective-permute-done.1.refs_0_
  12.6 0.0 collective-permute-done.4.refs_1_
  12.6 20.8 %collective-permute-done.6.refs_2_ = bf16[128,2048]{1,0:T(8,128)(2,1)S(1)} collective-permute-done((bf16[128,2048]{1,0:T(8,128)(2,1)S(1)}, bf16[128,2048]{1,0:T(8,128)(2,1)S(1)}, u32[]{:S(2)}, u32[]{:S(2)}) %collective-permute-start.6) | collective-permute-done | bytes 524320 | tf_op jit(solution)/shard_map/ppermute | solution.py:457
  33.4 0.0 collective-permute-done.8.refs_3_
  33.4 4.2 %later_front.1 = (bf16[64,2048]{1,0:T(8,128)(2,1)S(1)}, bf16[128,2048]{1,0:T(8,128)(2,1)S(1)}, bf16[128,1024]{1,0:T(8,128)(2,1)S(1)}, bf16[128,1024]{1,0:T(8,128...) custom-call(bf16[128,2048]{1,0:T(8,128)(2,1)S(1)} %collective-permute-done.1.refs_0_, ...), custom_call_target="tpu_custom_call" | custom-call | tf_op jit(solution)/shard_map/later_front/pallas_call | solution.py:371
  37.6 0.7 %collective-permute-start.9 = (bf16[64,2048]{1,0:T(8,128)(2,1)S(1)}, bf16[64,2048]{1,0:T(8,128)(2,1)S(1)}, u32[]{:S(2)}, u32[]{:S(2)}) collective-permute-start(bf16[64,2048]{1,0:T(8,128)(2,1)S(1)} %get-tuple-element.39.refs_0_.refs_3_), channel_id=1, source_target_pairs={{16,18},{18,16},{17,19},{19,17}} | collective-permute-start | bytes 786440 | tf_op jit(solution)/shard_map/ppermute | solution.py:399
  38.3 0.7 %collective-permute-start.11 = (bf16[64,2048]{1,0:T(8,128)(2,1)S(1)}, bf16[64,2048]{1,0:T(8,128)(2,1)S(1)}, u32[]{:S(2)}, u32[]{:S(2)}) collective-permute-start(bf16[64,2048]{1,0:T(8,128)(2,1)S(1)} %get-tuple-element.39.refs_0_.refs_3_), channel_id=1, source_target_pairs={{20,22},{22,20},{21,23},{23,21}} | collective-permute-start | bytes 786440 | tf_op jit(solution)/shard_map/ppermute | solution.py:399
  39.0 0.0 collective-permute-done.9.refs_1_.refs_3_
  39.0 0.7 %collective-permute-start.10 = (bf16[64,1024]{1,0:T(8,128)(2,1)S(1)}, bf16[64,1024]{1,0:T(8,128)(2,1)S(1)}, u32[]{:S(2)}, u32[]{:S(2)}) collective-permute-start(bf16[64,1024]{1,0:T(8,128)(2,1)S(1)} %advance1_0.1.refs_3_), channel_id=1, source_target_pairs={{16,20},{18,22},{17,21},{19,23}} | collective-permute-start | bytes 393224 | tf_op jit(solution)/shard_map/ppermute | solution.py:399
  39.7 2.2 %collective-permute-start.13 = (bf16[64,2048]{1,0:T(8,128)(2,1)S(1)}, bf16[64,2048]{1,0:T(8,128)(2,1)S(1)}, u32[]{:S(2)}, u32[]{:S(2)}) collective-permute-start(bf16[64,2048]{1,0:T(8,128)(2,1)S(1)} %get-tuple-element.39.refs_0_.refs_3_), channel_id=1, source_target_pairs={{24,26},{26,24},{25,27},{27,25}} | collective-permute-start | bytes 786440 | tf_op jit(solution)/shard_map/ppermute | solution.py:399
  41.9 0.0 collective-permute-done.11.refs_1_.refs_4_
  41.9 0.0 collective-permute-done.10.refs_2_.refs_0_
  42.0 1.3 %collective-permute-start.12 = (bf16[64,1024]{1,0:T(8,128)(2,1)S(1)}, bf16[64,1024]{1,0:T(8,128)(2,1)S(1)}, u32[]{:S(2)}, u32[]{:S(2)}) collective-permute-start(bf16[64,1024]{1,0:T(8,128)(2,1)S(1)} %advance1_1.1.refs_3_), channel_id=1, source_target_pairs={{20,24},{22,26},{21,25},{23,27}} | collective-permute-start | bytes 393224 | tf_op jit(solution)/shard_map/ppermute | solution.py:399
  43.3 0.7 %collective-permute-start.15 = (bf16[64,2048]{1,0:T(8,128)(2,1)S(1)}, bf16[64,2048]{1,0:T(8,128)(2,1)S(1)}, u32[]{:S(2)}, u32[]{:S(2)}) collective-permute-start(bf16[64,2048]{1,0:T(8,128)(2,1)S(1)} %get-tuple-element.39.refs_0_.refs_3_), channel_id=1, source_target_pairs={{28,30},{30,28},{29,31},{31,29}} | collective-permute-start | bytes 786440 | tf_op jit(solution)/shard_map/ppermute | solution.py:399
  44.0 2.9 %collective-permute-done.13.refs_1_.refs_5_ = bf16[64,2048]{1,0:T(8,128)(2,1)S(1)} collective-permute-done((bf16[64,2048]{1,0:T(8,128)(2,1)S(1)}, bf16[64,2048]{1,0:T(8,128)(2,1)S(1)}, u32[]{:S(2)}, u32[]{:S(2)}) %collective-permute-start.13) | collective-permute-done | bytes 262176 | tf_op jit(solution)/shard_map/ppermute | solution.py:399
  46.8 0.9 %collective-permute-done.12.refs_2_.refs_1_ = bf16[64,1024]{1,0:T(8,128)(2,1)S(1)} collective-permute-done((bf16[64,1024]{1,0:T(8,128)(2,1)S(1)}, bf16[64,1024]{1,0:T(8,128)(2,1)S(1)}, u32[]{:S(2)}, u32[]{:S(2)}) %collective-permute-start.12) | collective-permute-done | bytes 131104 | tf_op jit(solution)/shard_map/ppermute | solution.py:399
  47.7 0.4 advance1_2.1.after_ref
  48.1 1.3 %collective-permute-start.14 = (bf16[64,1024]{1,0:T(8,128)(2,1)S(1)}, bf16[64,1024]{1,0:T(8,128)(2,1)S(1)}, u32[]{:S(2)}, u32[]{:S(2)}) collective-permute-start(bf16[64,1024]{1,0:T(8,128)(2,1)S(1)} %advance1_2.1.after_ref), channel_id=1, source_target_pairs={{24,28},{26,30},{25,29},{27,31}} | collective-permute-start | bytes 393224 | tf_op jit(solution)/shard_map/ppermute | solution.py:399
  49.4 3.3 %reads1_0.1 = (bf16[128,2048]{1,0:T(8,128)(2,1)S(1)}, bf16[1024,2048]{1,0:T(8,128)(2,1)S(1)}) custom-call(bf16[128,2048]{1,0:T(8,128)(2,1)S(1)} %get-tuple-element.40.normed_ref, bf16[128,1024]{1,0:T(8,128)(2,1)S(1)} %get-tuple-element.41.keys_ref, bf16[128,1024]{1,0:T(8,128)(2,1)S(1)} %get-tuple-element.42.x_ref, ...), custom_call_target="tpu_custom_call" | custom-call | tf_op jit(solution)/shard_map/reads1_0/pallas_call | solution.py:371
  52.7 0.0 collective-permute-done.15.refs_6_
  52.8 0.0 collective-permute-done.14.refs_2_
  52.8 1.8 %last_finish.1 = bf16[1,128,2048]{2,1,0:T(8,128)(2,1)} custom-call(bf16[64,1024]{1,0:T(8,128)(2,1)S(1)} %collective-permute-done.10.refs_2_.refs_0_, bf16[64,1024]{1,0:T(8,128)(2,1)S(1)} %collective-permute-done.12.refs_2_.refs_1_, bf16[64,1024]{1,0:T(8,128)(2,1)S(1)} %collective-permute-done.14.refs_2_, ...), custom_call_target="tpu_custom_call" | custom-call | tf_op jit(solution)/shard_map/last_finish/pallas_call | solution.py:371
  (9 shorter events, 0.2 us)
Async XLA Ops:
  0.0 1.6 %copy-start.1 = (f32[1,16,64,64]{3,2,1,0:T(8,128)S(1)}, f32[1,16,64,64]{3,2,1,0:T(8,128)}, u32[]{:S(2)}) copy-start(f32[1,16,64,64]{3,2,1,0:T(8,128)} %refs_7_.1) | copy-start | bytes 786436
  0.1 1.6 %collective-permute-start = (bf16[64,2048]{1,0:T(8,128)(2,1)S(1)}, bf16[64,2048]{1,0:T(8,128)(2,1)S(1)}, u32[]{:S(2)}, u32[]{:S(2)}) collective-permute-start(bf16[64,2048]{1,0:T(8,128)(2,1)S(1)} %get-tuple-element.26.refs_0_.own_ref), channel_id=1, source_target_pairs={{0,2},{2,0},{1,3},{3,1}} | collective-permute-start | bytes 786440 | tf_op jit(solution)/shard_map/ppermute | solution.py:399
  0.9 1.9 %collective-permute-start.3 = (bf16[64,2048]{1,0:T(8,128)(2,1)S(1)}, bf16[64,2048]{1,0:T(8,128)(2,1)S(1)}, u32[]{:S(2)}, u32[]{:S(2)}) collective-permute-start(bf16[64,2048]{1,0:T(8,128)(2,1)S(1)} %get-tuple-element.26.refs_0_.own_ref), channel_id=1, source_target_pairs={{4,6},{6,4},{8,10},{10,8},{12,14},{14,12},{5,7},{7,5},{9,11},{11,9... | collective-permute-start | bytes 786440 | tf_op jit(solution)/shard_map/ppermute | solution.py:399
  1.8 1.0 %copy-start = (bf16[128,2048]{1,0:T(8,128)(2,1)S(1)}, bf16[128,2048]{1,0:T(8,128)(2,1)}, u32[]{:S(2)}) copy-start(bf16[128,2048]{1,0:T(8,128)(2,1)} %h_ref.7) | copy-start | bytes 1572868
  1.8 1.0 %collective-permute-start.2 = (bf16[64,1024]{1,0:T(8,128)(2,1)S(1)}, bf16[64,1024]{1,0:T(8,128)(2,1)S(1)}, u32[]{:S(2)}, u32[]{:S(2)}) collective-permute-start(bf16[64,1024]{1,0:T(8,128)(2,1)S(1)} %advance0_0.1.after_ref), channel_id=1, source_target_pairs={{0,4},{2,6},{1,5},{3,7}} | collective-permute-start | bytes 393224 | tf_op jit(solution)/shard_map/ppermute | solution.py:399
  2.8 0.7 %collective-permute-start.5 = (bf16[64,1024]{1,0:T(8,128)(2,1)S(1)}, bf16[64,1024]{1,0:T(8,128)(2,1)S(1)}, u32[]{:S(2)}, u32[]{:S(2)}) collective-permute-start(bf16[64,1024]{1,0:T(8,128)(2,1)S(1)} %advance0_1.1.after_ref), channel_id=1, source_target_pairs={{4,8},{6,10},{5,9},{7,11}} | collective-permute-start | bytes 393224 | tf_op jit(solution)/shard_map/ppermute | solution.py:399
  3.6 3.4 %collective-permute-start.7 = (bf16[64,1024]{1,0:T(8,128)(2,1)S(1)}, bf16[64,1024]{1,0:T(8,128)(2,1)S(1)}, u32[]{:S(2)}, u32[]{:S(2)}) collective-permute-start(bf16[64,1024]{1,0:T(8,128)(2,1)S(1)} %advance0_2.1.after_ref), channel_id=1, source_target_pairs={{8,12},{10,14},{9,13},{11,15}} | collective-permute-start | bytes 393224 | tf_op jit(solution)/shard_map/ppermute | solution.py:399
  4.3 8.3 %collective-permute-start.1 = (bf16[128,2048]{1,0:T(8,128)(2,1)S(1)}, bf16[128,2048]{1,0:T(8,128)(2,1)S(1)}, u32[]{:S(2)}, u32[]{:S(2)}) collective-permute-start(bf16[128,2048]{1,0:T(8,128)(2,1)S(1)} %first_finish_0.1.refs_2_.refs_11_), channel_id=1, source_target_pairs={{0,16},{2,18},{1,17},{3,19}} | collective-permute-start | bytes 1572872 | tf_op jit(solution)/shard_map/ppermute | solution.py:457
  5.0 7.6 %collective-permute-start.4 = (bf16[128,2048]{1,0:T(8,128)(2,1)S(1)}, bf16[128,2048]{1,0:T(8,128)(2,1)S(1)}, u32[]{:S(2)}, u32[]{:S(2)}) collective-permute-start(bf16[128,2048]{1,0:T(8,128)(2,1)S(1)} %first_finish_1.1.refs_2_.refs_12_), channel_id=1, source_target_pairs={{4,20},{6,22},{5,21},{7,23}} | collective-permute-start | bytes 1572872 | tf_op jit(solution)/shard_map/ppermute | solution.py:457
  5.7 27.7 %collective-permute-start.6 = (bf16[128,2048]{1,0:T(8,128)(2,1)S(1)}, bf16[128,2048]{1,0:T(8,128)(2,1)S(1)}, u32[]{:S(2)}, u32[]{:S(2)}) collective-permute-start(bf16[128,2048]{1,0:T(8,128)(2,1)S(1)} %first_finish_2.1.refs_13_), channel_id=1, source_target_pairs={{8,24},{10,26},{9,25},{11,27}} | collective-permute-start | bytes 1572872 | tf_op jit(solution)/shard_map/ppermute | solution.py:457
  7.2 26.2 %collective-permute-start.8 = (bf16[128,2048]{1,0:T(8,128)(2,1)S(1)}, bf16[128,2048]{1,0:T(8,128)(2,1)S(1)}, u32[]{:S(2)}, u32[]{:S(2)}) collective-permute-start(bf16[128,2048]{1,0:T(8,128)(2,1)S(1)} %first_finish_3.1.refs_14_), channel_id=1, source_target_pairs={{12,28},{14,30},{13,29},{15,31}} | collective-permute-start | bytes 1572872 | tf_op jit(solution)/shard_map/ppermute | solution.py:457
  37.6 1.4 %collective-permute-start.9 = (bf16[64,2048]{1,0:T(8,128)(2,1)S(1)}, bf16[64,2048]{1,0:T(8,128)(2,1)S(1)}, u32[]{:S(2)}, u32[]{:S(2)}) collective-permute-start(bf16[64,2048]{1,0:T(8,128)(2,1)S(1)} %get-tuple-element.39.refs_0_.refs_3_), channel_id=1, source_target_pairs={{16,18},{18,16},{17,19},{19,17}} | collective-permute-start | bytes 786440 | tf_op jit(solution)/shard_map/ppermute | solution.py:399
  38.3 3.6 %collective-permute-start.11 = (bf16[64,2048]{1,0:T(8,128)(2,1)S(1)}, bf16[64,2048]{1,0:T(8,128)(2,1)S(1)}, u32[]{:S(2)}, u32[]{:S(2)}) collective-permute-start(bf16[64,2048]{1,0:T(8,128)(2,1)S(1)} %get-tuple-element.39.refs_0_.refs_3_), channel_id=1, source_target_pairs={{20,22},{22,20},{21,23},{23,21}} | collective-permute-start | bytes 786440 | tf_op jit(solution)/shard_map/ppermute | solution.py:399
  39.0 2.9 %collective-permute-start.10 = (bf16[64,1024]{1,0:T(8,128)(2,1)S(1)}, bf16[64,1024]{1,0:T(8,128)(2,1)S(1)}, u32[]{:S(2)}, u32[]{:S(2)}) collective-permute-start(bf16[64,1024]{1,0:T(8,128)(2,1)S(1)} %advance1_0.1.refs_3_), channel_id=1, source_target_pairs={{16,20},{18,22},{17,21},{19,23}} | collective-permute-start | bytes 393224 | tf_op jit(solution)/shard_map/ppermute | solution.py:399
  39.7 7.1 %collective-permute-start.13 = (bf16[64,2048]{1,0:T(8,128)(2,1)S(1)}, bf16[64,2048]{1,0:T(8,128)(2,1)S(1)}, u32[]{:S(2)}, u32[]{:S(2)}) collective-permute-start(bf16[64,2048]{1,0:T(8,128)(2,1)S(1)} %get-tuple-element.39.refs_0_.refs_3_), channel_id=1, source_target_pairs={{24,26},{26,24},{25,27},{27,25}} | collective-permute-start | bytes 786440 | tf_op jit(solution)/shard_map/ppermute | solution.py:399
  42.0 5.7 %collective-permute-start.12 = (bf16[64,1024]{1,0:T(8,128)(2,1)S(1)}, bf16[64,1024]{1,0:T(8,128)(2,1)S(1)}, u32[]{:S(2)}, u32[]{:S(2)}) collective-permute-start(bf16[64,1024]{1,0:T(8,128)(2,1)S(1)} %advance1_1.1.refs_3_), channel_id=1, source_target_pairs={{20,24},{22,26},{21,25},{23,27}} | collective-permute-start | bytes 393224 | tf_op jit(solution)/shard_map/ppermute | solution.py:399
  43.3 9.5 %collective-permute-start.15 = (bf16[64,2048]{1,0:T(8,128)(2,1)S(1)}, bf16[64,2048]{1,0:T(8,128)(2,1)S(1)}, u32[]{:S(2)}, u32[]{:S(2)}) collective-permute-start(bf16[64,2048]{1,0:T(8,128)(2,1)S(1)} %get-tuple-element.39.refs_0_.refs_3_), channel_id=1, source_target_pairs={{28,30},{30,28},{29,31},{31,29}} | collective-permute-start | bytes 786440 | tf_op jit(solution)/shard_map/ppermute | solution.py:399
  48.1 4.7 %collective-permute-start.14 = (bf16[64,1024]{1,0:T(8,128)(2,1)S(1)}, bf16[64,1024]{1,0:T(8,128)(2,1)S(1)}, u32[]{:S(2)}, u32[]{:S(2)}) collective-permute-start(bf16[64,1024]{1,0:T(8,128)(2,1)S(1)} %advance1_2.1.after_ref), channel_id=1, source_target_pairs={{24,28},{26,30},{25,29},{27,31}} | collective-permute-start | bytes 393224 | tf_op jit(solution)/shard_map/ppermute | solution.py:399

commit v9 on v8

--- a/solution.py
+++ b/solution.py
@@ -104,9 +104,10 @@
         if near is None:
             groups = []
             gain, w_rate, base, weights, base_lane = gain_ref, w_rate_ref, base_ref, w_ref, width
-            for place, ref in enumerate(h_refs):
-
-                @pl.when(lax.axis_index("seq") // 2 == place)
+            last = lax.axis_index("seq") // 2 == lax.axis_size("seq") // 2 - 1
+            for picked, ref in zip((jnp.logical_not(last), last), h_refs):
+
+                @pl.when(picked)
                 def _():
                     h_in[...] = ref[...]
         else:
@@ -131,14 +132,16 @@
             start_all(groups[1])
         normed = norm_rows(h_in[...], gain[...])
         normed_out[...] = normed
+        if groups:
+            start_all(groups[2])
         rates = spread_rates(normed, w_rate[0], base[...])
         ones = head_ones()
 
         def project(quad):
             if groups:
                 wait_all(groups[quad])
-                if quad + 2 < quads:
-                    start_all(groups[quad + 2])
+                if quad + 3 < quads:
+                    start_all(groups[quad + 3])
             key_lane = base_lane + quad * QUAD
             return [mm(normed, weights[:, lane : lane + QUAD]) for lane in (key_lane, key_lane + width)]
 
@@ -198,23 +201,21 @@
     on_section(1, body)
 
 
-def read_out(active, places, normed_ref, keys_ref, x_ref, y_ref, w_ref, w_out_hbm, after_ref, *rest):
-    if active:
-        reads_out, w_out, load_sem = rest
-    else:
-        reads_out, w_out, load_sem, wq, sems = rest[-5:]
+def read_out(active, places, fetches, normed_ref, keys_ref, x_ref, y_ref, w_ref, w_out_hbm, after_ref, reads_out, *rest):
     rows, width = keys_ref.shape
     quads = width // QUAD
+    w_out, rest = rest[:fetches], rest[fetches:]
+    load_sem, *near = rest
 
     def body():
-        fetch = [pltpu.make_async_copy(w_out_hbm.at[0], w_out, load_sem)]
+        fetch = [pltpu.make_async_copy(w_out_hbm.at[0], target, load_sem) for target in w_out]
         if active:
             weights, groups = w_ref, []
             start_all(fetch)
         else:
-            weights = wq
+            weights, sems = near
             groups = [
-                [pltpu.make_async_copy(w_ref.at[0, :, pl.ds(quad * QUAD, QUAD)], wq.at[:, pl.ds(quad * QUAD, QUAD)], sems.at[quad])]
+                [pltpu.make_async_copy(w_ref.at[0, :, pl.ds(quad * QUAD, QUAD)], weights.at[:, pl.ds(quad * QUAD, QUAD)], sems.at[quad])]
                 for quad in range(quads)
             ]
             start_all(groups[0])
@@ -294,37 +295,27 @@
         pl.when(here & (side == 1))(lambda: body((got_ref, own_ref)))
 
 
-def finish(here, begins, state_refs, got_refs, init_ref, reads_ref, w_out_ref, h_ref, store):
+def finish(here, begins, state_ref, got_ref, reads_ref, w_out_ref, h_ref, store, fetch=()):
     width = w_out_ref.shape[0]
     model = h_ref.shape[1]
     chunk = model // 4
 
-    def total(refs, lanes):
-        value = refs[0][:, lanes].astype(F32)
-        for ref in refs[1:]:
-            value = value + ref[:, lanes].astype(F32)
-        return value
-
     def body():
+        start_all(fetch)
         follows = lax.rem(lax.axis_index("seq"), 2) == 1
         parts = []
         for start in range(0, width, QUAD):
             pieces = []
             for lane in range(start, start + QUAD, PAIR):
                 lanes = slice(lane, lane + PAIR)
-                if begins is True:
-                    state = pair_state(init_ref, lane // PAIR)
-                else:
-                    state = total(state_refs, lanes)
-                    if begins is not False:
-                        state = jnp.where(begins, pair_state(init_ref, lane // PAIR), state)
-                step = mm(total(got_refs, lanes).astype(BF16), spread(state.astype(BF16)))
-                moved = state - step + total(got_refs, slice(width + lane, width + lane + PAIR))
+                state = pair_state(state_ref, lane // PAIR) if begins else state_ref[:, lanes].astype(F32)
+                moved = apply_map(state, got_ref, lane, width)
                 pieces.append(jnp.where(follows, moved, state).astype(BF16))
             offset = reads_ref[:, width + start : width + start + QUAD]
             read = mm(reads_ref[:, start : start + QUAD], spread(jnp.concatenate(pieces, axis=1)))
             parts.append((read + offset.astype(F32)).astype(BF16))
         inner_bf = jnp.concatenate(parts, axis=1)
+        wait_all(fetch)
         for start in range(0, model, chunk):
             lanes = slice(start, start + chunk)
             store(start, (h_ref[:, lanes].astype(F32) + mm(inner_bf, w_out_ref[:, lanes])).astype(BF16))
@@ -332,16 +323,22 @@
     pl.when(here)(body)
 
 
-def first_finish(place, state_ref, got_ref, reads_ref, w_out_ref, h_ref, after_ref, out_ref):
+def first_finish(place, passed, state_ref, got_ref, reads_ref, w_out_ref, h_ref, after_ref, *rest):
+    out_ref, *near = rest[passed:]
+
     def store(start, value):
         out_ref[:, start : start + value.shape[1]] = value
 
-    finish(at_pair([place], 0), place == 0, [state_ref], [got_ref], state_ref, reads_ref, w_out_ref, h_ref, store)
+    fetch = []
+    if near:
+        fetch = [pltpu.make_async_copy(w_out_ref.at[0], *near)]
+        w_out_ref = near[0]
+    finish(at_pair([place], 0), place == 0, state_ref, got_ref, reads_ref, w_out_ref, h_ref, store, fetch)
 
 
 def last_finish(count, *refs):
-    states, gots, refs = refs[: count - 1], refs[count - 1 : 2 * count - 1], refs[2 * count - 1 :]
-    init_ref, reads_ref, w_out_ref, h_ref, *first_refs, out_hbm, near, sems = refs
+    states, gots, refs = refs[:count], refs[count : 2 * count], refs[2 * count :]
+    reads_early, reads_late, w_out_early, w_out_late, h_ref, first_early, first_late, out_hbm, near, sems = refs
     chunk = near.shape[1] // 4
 
     def write(start):
@@ -352,12 +349,13 @@
         near[:, start : start + chunk] = value
         write(start).start()
 
-    begins = lax.axis_index("seq") // 2 == 0
-    finish(lax.axis_index("section") == 1, begins, states, gots, init_ref, reads_ref, w_out_ref, h_ref, store)
-
-    for place, first_ref in enumerate(first_refs):
-
-        @pl.when(at_pair([place], 0))
+    for place in range(count):
+        reads_ref, w_out_ref = (reads_early, w_out_early) if place + 1 < count else (reads_late, w_out_late)
+        finish(at_pair([place], 1), place == 0, states[place], gots[place], reads_ref, w_out_ref, h_ref, store)
+
+    for places, first_ref in ((range(count - 1), first_early), ([count - 1], first_late)):
+
+        @pl.when(at_pair(places, 0))
         def _():
             for start in range(0, near.shape[1], chunk):
                 store(start, first_ref[:, start : start + chunk])
@@ -366,7 +364,7 @@
         write(start).wait()
 
 
-def call(body, outs, scratch, args, kinds=None, name=None, out_kind=pltpu.VMEM):
+def call(body, outs, scratch, args, kinds=None, name=None, out_kind=pltpu.VMEM, aliases=None):
     specs = [pl.BlockSpec(memory_space=kind) for kind in (kinds or [pltpu.VMEM] * len(args))]
     return pl.pallas_call(
         body,
@@ -374,6 +372,7 @@
         in_specs=specs,
         out_specs=[pl.BlockSpec(memory_space=out_kind)] * len(outs),
         scratch_shapes=scratch,
+        input_output_aliases=aliases or {},
         compiler_params=pltpu.CompilerParams(vmem_limit_bytes=VMEM_LIMIT),
         name=name,
     )(*args)
@@ -401,17 +400,17 @@
     def swap(own, active, groups):
         return permute(own, active, [(2 * group + side, 2 * group + 1 - side) for group in groups for side in range(2)])
 
-    def layer_reads(active, places, rows_of, weights, after):
+    def layer_reads(active, places, fetches, rows_of, weights, after):
         near = [pltpu.VMEM((depth, width), BF16), pltpu.SemaphoreType.DMA((quads,))]
-        reads, w_out_near = call(
-            functools.partial(read_out, active, places),
-            [shape((rows, 2 * width), BF16), pltpu.VMEM(w_out.shape[1:], BF16)],
+        reads, *w_out_near = call(
+            functools.partial(read_out, active, places, fetches),
+            [shape((rows, 2 * width), BF16)] + [pltpu.VMEM(w_out.shape[1:], BF16)] * fetches,
             [pltpu.SemaphoreType.DMA] + (near if active == 0 else []),
             [*rows_of, weights, w_out, after],
             [pltpu.VMEM] * 4 + [pltpu.VMEM if active else pltpu.HBM, pltpu.HBM, pl.ANY],
             name=f"reads{active}_{places[0]}",
         )
-        return reads, in_vmem(w_out_near)
+        return [reads] + [in_vmem(value) for value in w_out_near]
 
     def hop(active, place, maps_here, state, after):
         def body(*refs):
@@ -434,28 +433,35 @@
     )
     got_first = swap(own, 0, [0])
     got_rest = swap(own, 0, range(1, groups))
-    read_first = layer_reads(0, [0], rows_of, w_qkv, init_state)
+    read_first = layer_reads(0, [0], 0, rows_of, w_qkv, init_state)
     ahead, state = hop(0, 0, [own, got_first], init_state, read_first[0])
-    read_rest = layer_reads(0, range(1, groups), rows_of, w_qkv, ahead)
+    read_rest = layer_reads(0, range(1, groups), 1, rows_of, w_qkv, ahead)
     (both,) = call(
         functools.partial(compose, 0), [maps], [], [own, got_rest, read_rest[0]], [pltpu.VMEM] * 2 + [pl.ANY], name="compose"
     )
-    firsts, hiddens, here = [], [], init_state
+    early, here = [], init_state
     for place in range(groups):
-        got, (reads, w_out_near) = (got_rest, read_rest) if place else (got_first, read_first)
+        got, (reads, w_out_near) = (got_rest, read_rest) if place else (got_first, read_first + [w_out])
         if 0 < place < groups - 1:
-            ahead, state = hop(0, place, [both], here, firsts[-1])
+            ahead, state = hop(0, place, [both], here, early[0])
+        passed = early if place + 1 < groups else []
         (first,) = call(
-            functools.partial(first_finish, place),
+            functools.partial(first_finish, place, len(passed)),
             [shape((rows, model), BF16)],
-            [],
-            [here, got, reads, w_out_near, tokens, ahead],
-            [pltpu.VMEM] * 5 + [pl.ANY],
+            [] if place else [pltpu.VMEM(w_out.shape[1:], BF16), pltpu.SemaphoreType.DMA],
+            [here, got, reads, w_out_near, tokens, ahead, *passed],
+            [pltpu.VMEM] * 3 + [pltpu.VMEM if place else pltpu.HBM, pltpu.VMEM, pl.ANY] + [pltpu.VMEM] * len(passed),
             name=f"first_finish_{place}",
+            aliases={6: 0} if passed else None,
         )
-        firsts.append(first)
-        hiddens.append(lax.ppermute(first, ("section", "seq"), [(2 * place + side, count + 2 * place + side) for side in range(2)]))
+        if place + 1 < groups:
+            early = [first]
         here = state
+    firsts = [early[0], first]
+    spans = [range(2 * (groups - 1)), range(2 * (groups - 1), count)]
+    hiddens = [
+        lax.ppermute(value, ("section", "seq"), [(place, count + place) for place in span]) for value, span in zip(firsts, spans)
+    ]
 
     params = [norm_gain, w_qkv, w_rate, rate_base]
     gain_near, w_near, rate_near, base_near = call(
@@ -471,16 +477,19 @@
         later_front, [maps] + rows_out + [shape((rows, model), BF16)], [], [*hiddens, *params], name="later_front"
     )
     gots = [swap(own, 1, [group]) for group in range(groups)]
-    states, state, ahead = [], init_state, own
+    states, after = [init_state], own
     for place in range(groups - 1):
-        ahead, state = hop(1, place, [own, gots[place]], state, ahead)
+        if place + 2 == groups:
+            reads_early = layer_reads(1, range(groups - 1), 1, rows_of, params[1], after)
+            after = reads_early[0]
+        after, state = hop(1, place, [own, gots[place]], states[-1], after)
         states.append(state)
-    reads, w_out_near = layer_reads(1, range(groups), rows_of, params[1], ahead)
+    reads_late = layer_reads(1, [groups - 1], 1, rows_of, params[1], after)
     (result,) = call(
         functools.partial(last_finish, groups),
         [shape((1, rows, model), BF16)],
         [pltpu.VMEM((rows, model), BF16), pltpu.SemaphoreType.DMA((4,))],
-        [*states, *gots, init_state, reads, w_out_near, hidden, *firsts],
+        [*states, *gots, reads_early[0], reads_late[0], reads_early[1], reads_late[1], hidden, *firsts],
         name="last_finish",
         out_kind=pltpu.HBM,
     )

time: 55 us -> 53.2 us (0.967)
  the two profiles are of different devices: /device:TPU:17 before, /device:TPU:25 now
where the time goes in v9:
time: 53.2 us; the launch traced here: 52.9 us
  waiting for transfers between devices  25.2 us (47%)
  Pallas kernels  14.6 us (27%)
  starting transfers between devices  12.5 us (23%)
    ppermute x2, waiting for transfers between devices, shards(): lax.ppermute(value, ('section', 'seq'), [(place, count + place) for place...  24.1 us
    pallas_call x19, Pallas kernels, call(): pl.pallas_call(body, out_shape=outs, in_specs=specs, out_specs=[pl.BlockS...  14.6 us
    ppermute x12, starting transfers between devices, permute(): lax.ppermute(value, ('section', 'seq'), [(base + source, base + target) f...  10.5 us
    ppermute x2, starting transfers between devices, shards(): lax.ppermute(value, ('section', 'seq'), [(place, count + place) for place...  1.99 us
    ppermute x12, waiting for transfers between devices, permute(): lax.ppermute(value, ('section', 'seq'), [(base + source, base + target) f...  1.1 us
  transfers between devices with their start and end apart: 14, of which 3 were waited for; matrix products, arithmetic and copies ran while one was open for 0% of the time, Pallas kernels for 16%

profile of v9, /device:TPU:25, one launch (start us, length us, event | category | flops | bytes accessed | tf_op | source)
XLA Modules:
  0.0 52.9 jit_solution(17173675438908214810)
XLA Ops:
  0.0 0.0 copy-start
  0.0 0.1 first_front.1
  0.1 0.8 %collective-permute-start.1 = (bf16[64,2048]{1,0:T(8,128)(2,1)S(1)}, bf16[64,2048]{1,0:T(8,128)(2,1)S(1)}, u32[]{:S(2)}, u32[]{:S(2)}) collective-permute-start(bf16[64,2048]{1,0:T(8,128)(2,1)S(1)} %get-tuple-element.26.refs_0_.own_ref), channel_id=1, source_target_pairs={{0,2},{2,0},{1,3},{3,1}} | collective-permute-start | bytes 786440 | tf_op jit(solution)/shard_map/ppermute | solution.py:398
  0.9 0.7 %collective-permute-start = (bf16[64,2048]{1,0:T(8,128)(2,1)S(1)}, bf16[64,2048]{1,0:T(8,128)(2,1)S(1)}, u32[]{:S(2)}, u32[]{:S(2)}) collective-permute-start(bf16[64,2048]{1,0:T(8,128)(2,1)S(1)} %get-tuple-element.26.refs_0_.own_ref), channel_id=1, source_target_pairs={{4,6},{6,4},{8,10},{10,8},{12,14},{14,12},{5,7},{7,5},{9,11},{11,9... | collective-permute-start | bytes 786440 | tf_op jit(solution)/shard_map/ppermute | solution.py:398
  1.6 0.0 copy-done
  1.6 0.1 reads0_0.1.refs_3_.reads_ref
  1.7 0.0 collective-permute-done.1.refs_1_.got_ref
  1.8 0.0 copy-start.1
  1.8 0.8 %collective-permute-start.2 = (bf16[64,1024]{1,0:T(8,128)(2,1)S(1)}, bf16[64,1024]{1,0:T(8,128)(2,1)S(1)}, u32[]{:S(2)}, u32[]{:S(2)}) collective-permute-start(bf16[64,1024]{1,0:T(8,128)(2,1)S(1)} %advance0_0.1.after_ref), channel_id=1, source_target_pairs={{0,4},{2,6},{1,5},{3,7}} | collective-permute-start | bytes 393224 | tf_op jit(solution)/shard_map/ppermute | solution.py:398
  2.6 0.1 reads0_1.1
  2.7 0.1 copy-done.1
  2.8 0.0 collective-permute-done.got_ref
  2.9 0.0 collective-permute-done.2.refs_1_.state_ref
  2.9 0.7 %collective-permute-start.3 = (bf16[64,1024]{1,0:T(8,128)(2,1)S(1)}, bf16[64,1024]{1,0:T(8,128)(2,1)S(1)}, u32[]{:S(2)}, u32[]{:S(2)}) collective-permute-start(bf16[64,1024]{1,0:T(8,128)(2,1)S(1)} %advance0_1.1.after_ref), channel_id=1, source_target_pairs={{4,8},{6,10},{5,9},{7,11}} | collective-permute-start | bytes 393224 | tf_op jit(solution)/shard_map/ppermute | solution.py:398
  3.6 0.0 collective-permute-done.3.refs_1_.state_ref
  3.7 0.7 %collective-permute-start.5 = (bf16[64,1024]{1,0:T(8,128)(2,1)S(1)}, bf16[64,1024]{1,0:T(8,128)(2,1)S(1)}, u32[]{:S(2)}, u32[]{:S(2)}) collective-permute-start(bf16[64,1024]{1,0:T(8,128)(2,1)S(1)} %advance0_2.1.after_ref), channel_id=1, source_target_pairs={{8,12},{10,14},{9,13},{11,15}} | collective-permute-start | bytes 393224 | tf_op jit(solution)/shard_map/ppermute | solution.py:398
  4.4 0.7 %collective-permute-start.4 = (bf16[128,2048]{1,0:T(8,128)(2,1)S(1)}, bf16[128,2048]{1,0:T(8,128)(2,1)S(1)}, u32[]{:S(2)}, u32[]{:S(2)}) collective-permute-start(bf16[128,2048]{1,0:T(8,128)(2,1)S(1)} %first_finish_2.1.refs_13_), channel_id=1, source_target_pairs={{0,16},{2,18},{4,20},{6,22},{8,24},{10,26},{1,17},{3,19},{5,21},{7... | collective-permute-start | bytes 1572872 | tf_op jit(solution)/shard_map/ppermute | solution.py:463
  5.1 0.0 collective-permute-done.5.state_ref
  5.1 0.2 first_finish_3.1.refs_14_
  5.3 1.3 %collective-permute-start.6 = (bf16[128,2048]{1,0:T(8,128)(2,1)S(1)}, bf16[128,2048]{1,0:T(8,128)(2,1)S(1)}, u32[]{:S(2)}, u32[]{:S(2)}) collective-permute-start(bf16[128,2048]{1,0:T(8,128)(2,1)S(1)} %first_finish_3.1.refs_14_), channel_id=1, source_target_pairs={{12,28},{14,30},{13,29},{15,31}} | collective-permute-start | bytes 1572872 | tf_op jit(solution)/shard_map/ppermute | solution.py:463
  6.6 4.6 %load.1 = (f32[1,2048]{1,0:T(1,128)S(1)}, bf16[1,2048,3072]{2,1,0:T(8,128)(2,1)S(1)}, bf16[1,16,2048]{2,1,0:T(8,128)(2,1)S(1)}, f32[1,16]{1,0:T(1,128)S(1)}) custom-call(f32[1,2048]{1,0:T(1,128)} %refs_0_.2, bf16[1,2048,3072]{2,1,0:T(8,128)(2,1)} %refs_1_.1, bf16[1,16,2048]{2,1,0:T(8,128)(2,1)} %bitcast.6, f32[1,16]{1,0:T(1,128)} %refs_3_.1, ...), custom_call_target="tpu_custom_call" | custom-call | tf_op jit(solution)/shard_map/load/pallas_call | solution.py:369
  11.2 0.0 collective-permute-done.4.refs_0_
  11.3 24.1 %collective-permute-done.6.refs_1_ = bf16[128,2048]{1,0:T(8,128)(2,1)S(1)} collective-permute-done((bf16[128,2048]{1,0:T(8,128)(2,1)S(1)}, bf16[128,2048]{1,0:T(8,128)(2,1)S(1)}, u32[]{:S(2)}, u32[]{:S(2)}) %collective-permute-start.6) | collective-permute-done | bytes 524320 | tf_op jit(solution)/shard_map/ppermute | solution.py:463
  35.3 4.2 %later_front.1 = (bf16[64,2048]{1,0:T(8,128)(2,1)S(1)}, bf16[128,2048]{1,0:T(8,128)(2,1)S(1)}, bf16[128,1024]{1,0:T(8,128)(2,1)S(1)}, bf16[128,1024]{1,0:T(8,128...) custom-call(bf16[128,2048]{1,0:T(8,128)(2,1)S(1)} %collective-permute-done.4.refs_0_, ...), custom_call_target="tpu_custom_call" | custom-call | tf_op jit(solution)/shard_map/later_front/pallas_call | solution.py:369
  39.5 0.7 %collective-permute-start.7 = (bf16[64,2048]{1,0:T(8,128)(2,1)S(1)}, bf16[64,2048]{1,0:T(8,128)(2,1)S(1)}, u32[]{:S(2)}, u32[]{:S(2)}) collective-permute-start(bf16[64,2048]{1,0:T(8,128)(2,1)S(1)} %get-tuple-element.37.refs_0_.refs_3_), channel_id=1, source_target_pairs={{16,18},{18,16},{17,19},{19,17}} | collective-permute-start | bytes 786440 | tf_op jit(solution)/shard_map/ppermute | solution.py:398
  40.2 0.7 %collective-permute-start.9 = (bf16[64,2048]{1,0:T(8,128)(2,1)S(1)}, bf16[64,2048]{1,0:T(8,128)(2,1)S(1)}, u32[]{:S(2)}, u32[]{:S(2)}) collective-permute-start(bf16[64,2048]{1,0:T(8,128)(2,1)S(1)} %get-tuple-element.37.refs_0_.refs_3_), channel_id=1, source_target_pairs={{20,22},{22,20},{21,23},{23,21}} | collective-permute-start | bytes 786440 | tf_op jit(solution)/shard_map/ppermute | solution.py:398
  40.9 0.0 collective-permute-done.7.refs_1_.refs_4_
  41.0 0.7 %collective-permute-start.8 = (bf16[64,1024]{1,0:T(8,128)(2,1)S(1)}, bf16[64,1024]{1,0:T(8,128)(2,1)S(1)}, u32[]{:S(2)}, u32[]{:S(2)}) collective-permute-start(bf16[64,1024]{1,0:T(8,128)(2,1)S(1)} %advance1_0.1.refs_3_), channel_id=1, source_target_pairs={{16,20},{18,22},{17,21},{19,23}} | collective-permute-start | bytes 393224 | tf_op jit(solution)/shard_map/ppermute | solution.py:398
  41.6 0.7 %collective-permute-start.11 = (bf16[64,2048]{1,0:T(8,128)(2,1)S(1)}, bf16[64,2048]{1,0:T(8,128)(2,1)S(1)}, u32[]{:S(2)}, u32[]{:S(2)}) collective-permute-start(bf16[64,2048]{1,0:T(8,128)(2,1)S(1)} %get-tuple-element.37.refs_0_.refs_3_), channel_id=1, source_target_pairs={{24,26},{26,24},{25,27},{27,25}} | collective-permute-start | bytes 786440 | tf_op jit(solution)/shard_map/ppermute | solution.py:398
  42.3 0.0 collective-permute-done.9.refs_1_.refs_5_
  42.3 0.0 collective-permute-done.8.refs_2_.refs_1_
  42.4 0.7 %collective-permute-start.10 = (bf16[64,1024]{1,0:T(8,128)(2,1)S(1)}, bf16[64,1024]{1,0:T(8,128)(2,1)S(1)}, u32[]{:S(2)}, u32[]{:S(2)}) collective-permute-start(bf16[64,1024]{1,0:T(8,128)(2,1)S(1)} %advance1_1.1.after_ref), channel_id=1, source_target_pairs={{20,24},{22,26},{21,25},{23,27}} | collective-permute-start | bytes 393224 | tf_op jit(solution)/shard_map/ppermute | solution.py:398
  43.0 2.2 %collective-permute-start.13 = (bf16[64,2048]{1,0:T(8,128)(2,1)S(1)}, bf16[64,2048]{1,0:T(8,128)(2,1)S(1)}, u32[]{:S(2)}, u32[]{:S(2)}) collective-permute-start(bf16[64,2048]{1,0:T(8,128)(2,1)S(1)} %get-tuple-element.37.refs_0_.refs_3_), channel_id=1, source_target_pairs={{28,30},{30,28},{29,31},{31,29}} | collective-permute-start | bytes 786440 | tf_op jit(solution)/shard_map/ppermute | solution.py:398
  45.3 0.0 collective-permute-done.11.refs_1_.refs_6_
  45.3 0.0 collective-permute-done.10.refs_2_
  45.3 1.3 %collective-permute-start.12 = (bf16[64,1024]{1,0:T(8,128)(2,1)S(1)}, bf16[64,1024]{1,0:T(8,128)(2,1)S(1)}, u32[]{:S(2)}, u32[]{:S(2)}) collective-permute-start(bf16[64,1024]{1,0:T(8,128)(2,1)S(1)} %advance1_2.1.after_ref), channel_id=1, source_target_pairs={{24,28},{26,30},{25,29},{27,31}} | collective-permute-start | bytes 393224 | tf_op jit(solution)/shard_map/ppermute | solution.py:398
  46.6 3.3 %reads1_3.1 = (bf16[128,2048]{1,0:T(8,128)(2,1)S(1)}, bf16[1024,2048]{1,0:T(8,128)(2,1)S(1)}) custom-call(bf16[128,2048]{1,0:T(8,128)(2,1)S(1)} %get-tuple-element.38.normed_ref, bf16[128,1024]{1,0:T(8,128)(2,1)S(1)} %get-tuple-element.39.keys_ref, bf16[128,1024]{1,0:T(8,128)(2,1)S(1)} %get-tuple-element.40.x_ref, ...), custom_call_target="tpu_custom_call" | custom-call | tf_op jit(solution)/shard_map/reads1_3/pallas_call | solution.py:369
  50.0 0.2 collective-permute-done.13.refs_7_
  50.2 0.9 %collective-permute-done.12.refs_3_ = bf16[64,1024]{1,0:T(8,128)(2,1)S(1)} collective-permute-done((bf16[64,1024]{1,0:T(8,128)(2,1)S(1)}, bf16[64,1024]{1,0:T(8,128)(2,1)S(1)}, u32[]{:S(2)}, u32[]{:S(2)}) %collective-permute-start.12) | collective-permute-done | bytes 131104 | tf_op jit(solution)/shard_map/ppermute | solution.py:398
  51.1 1.7 %last_finish.1 = bf16[1,128,2048]{2,1,0:T(8,128)(2,1)} custom-call(f32[1,16,64,64]{3,2,1,0:T(8,128)S(1)} %copy-done, bf16[64,1024]{1,0:T(8,128)(2,1)S(1)} %collective-permute-done.8.refs_2_.refs_1_, bf16[64,1024]{1,0:T(8,128)(2,1)S(1)} %collective-permute-done.10.refs_2_, bf16[64,1024]{1,0:T(8,128)(2,1)S(1)} %collective-permute-done.12.refs_3_, ...), custom_call_target="tpu_custom_call" | custom-call | tf_op jit(solution)/shard_map/last_finish/pallas_call | solution.py:369
  (11 shorter events, 0.3 us)
Async XLA Ops:
  0.0 1.6 %copy-start = (f32[1,16,64,64]{3,2,1,0:T(8,128)S(1)}, f32[1,16,64,64]{3,2,1,0:T(8,128)}, u32[]{:S(2)}) copy-start(f32[1,16,64,64]{3,2,1,0:T(8,128)} %refs_0_.3) | copy-start | bytes 786436
  0.1 1.6 %collective-permute-start.1 = (bf16[64,2048]{1,0:T(8,128)(2,1)S(1)}, bf16[64,2048]{1,0:T(8,128)(2,1)S(1)}, u32[]{:S(2)}, u32[]{:S(2)}) collective-permute-start(bf16[64,2048]{1,0:T(8,128)(2,1)S(1)} %get-tuple-element.26.refs_0_.own_ref), channel_id=1, source_target_pairs={{0,2},{2,0},{1,3},{3,1}} | collective-permute-start | bytes 786440 | tf_op jit(solution)/shard_map/ppermute | solution.py:398
  0.9 1.9 %collective-permute-start = (bf16[64,2048]{1,0:T(8,128)(2,1)S(1)}, bf16[64,2048]{1,0:T(8,128)(2,1)S(1)}, u32[]{:S(2)}, u32[]{:S(2)}) collective-permute-start(bf16[64,2048]{1,0:T(8,128)(2,1)S(1)} %get-tuple-element.26.refs_0_.own_ref), channel_id=1, source_target_pairs={{4,6},{6,4},{8,10},{10,8},{12,14},{14,12},{5,7},{7,5},{9,11},{11,9... | collective-permute-start | bytes 786440 | tf_op jit(solution)/shard_map/ppermute | solution.py:398
  1.8 1.0 %copy-start.1 = (bf16[128,2048]{1,0:T(8,128)(2,1)S(1)}, bf16[128,2048]{1,0:T(8,128)(2,1)}, u32[]{:S(2)}) copy-start(bf16[128,2048]{1,0:T(8,128)(2,1)} %h_ref.7) | copy-start | bytes 1572868
  1.8 1.1 %collective-permute-start.2 = (bf16[64,1024]{1,0:T(8,128)(2,1)S(1)}, bf16[64,1024]{1,0:T(8,128)(2,1)S(1)}, u32[]{:S(2)}, u32[]{:S(2)}) collective-permute-start(bf16[64,1024]{1,0:T(8,128)(2,1)S(1)} %advance0_0.1.after_ref), channel_id=1, source_target_pairs={{0,4},{2,6},{1,5},{3,7}} | collective-permute-start | bytes 393224 | tf_op jit(solution)/shard_map/ppermute | solution.py:398
  2.9 0.7 %collective-permute-start.3 = (bf16[64,1024]{1,0:T(8,128)(2,1)S(1)}, bf16[64,1024]{1,0:T(8,128)(2,1)S(1)}, u32[]{:S(2)}, u32[]{:S(2)}) collective-permute-start(bf16[64,1024]{1,0:T(8,128)(2,1)S(1)} %advance0_1.1.after_ref), channel_id=1, source_target_pairs={{4,8},{6,10},{5,9},{7,11}} | collective-permute-start | bytes 393224 | tf_op jit(solution)/shard_map/ppermute | solution.py:398
  3.7 1.4 %collective-permute-start.5 = (bf16[64,1024]{1,0:T(8,128)(2,1)S(1)}, bf16[64,1024]{1,0:T(8,128)(2,1)S(1)}, u32[]{:S(2)}, u32[]{:S(2)}) collective-permute-start(bf16[64,1024]{1,0:T(8,128)(2,1)S(1)} %advance0_2.1.after_ref), channel_id=1, source_target_pairs={{8,12},{10,14},{9,13},{11,15}} | collective-permute-start | bytes 393224 | tf_op jit(solution)/shard_map/ppermute | solution.py:398
  4.4 6.9 %collective-permute-start.4 = (bf16[128,2048]{1,0:T(8,128)(2,1)S(1)}, bf16[128,2048]{1,0:T(8,128)(2,1)S(1)}, u32[]{:S(2)}, u32[]{:S(2)}) collective-permute-start(bf16[128,2048]{1,0:T(8,128)(2,1)S(1)} %first_finish_2.1.refs_13_), channel_id=1, source_target_pairs={{0,16},{2,18},{4,20},{6,22},{8,24},{10,26},{1,17},{3,19},{5,21},{7... | collective-permute-start | bytes 1572872 | tf_op jit(solution)/shard_map/ppermute | solution.py:463
  5.3 30.0 %collective-permute-start.6 = (bf16[128,2048]{1,0:T(8,128)(2,1)S(1)}, bf16[128,2048]{1,0:T(8,128)(2,1)S(1)}, u32[]{:S(2)}, u32[]{:S(2)}) collective-permute-start(bf16[128,2048]{1,0:T(8,128)(2,1)S(1)} %first_finish_3.1.refs_14_), channel_id=1, source_target_pairs={{12,28},{14,30},{13,29},{15,31}} | collective-permute-start | bytes 1572872 | tf_op jit(solution)/shard_map/ppermute | solution.py:463
  39.5 1.4 %collective-permute-start.7 = (bf16[64,2048]{1,0:T(8,128)(2,1)S(1)}, bf16[64,2048]{1,0:T(8,128)(2,1)S(1)}, u32[]{:S(2)}, u32[]{:S(2)}) collective-permute-start(bf16[64,2048]{1,0:T(8,128)(2,1)S(1)} %get-tuple-element.37.refs_0_.refs_3_), channel_id=1, source_target_pairs={{16,18},{18,16},{17,19},{19,17}} | collective-permute-start | bytes 786440 | tf_op jit(solution)/shard_map/ppermute | solution.py:398
  40.2 2.1 %collective-permute-start.9 = (bf16[64,2048]{1,0:T(8,128)(2,1)S(1)}, bf16[64,2048]{1,0:T(8,128)(2,1)S(1)}, u32[]{:S(2)}, u32[]{:S(2)}) collective-permute-start(bf16[64,2048]{1,0:T(8,128)(2,1)S(1)} %get-tuple-element.37.refs_0_.refs_3_), channel_id=1, source_target_pairs={{20,22},{22,20},{21,23},{23,21}} | collective-permute-start | bytes 786440 | tf_op jit(solution)/shard_map/ppermute | solution.py:398
  41.0 1.4 %collective-permute-start.8 = (bf16[64,1024]{1,0:T(8,128)(2,1)S(1)}, bf16[64,1024]{1,0:T(8,128)(2,1)S(1)}, u32[]{:S(2)}, u32[]{:S(2)}) collective-permute-start(bf16[64,1024]{1,0:T(8,128)(2,1)S(1)} %advance1_0.1.refs_3_), channel_id=1, source_target_pairs={{16,20},{18,22},{17,21},{19,23}} | collective-permute-start | bytes 393224 | tf_op jit(solution)/shard_map/ppermute | solution.py:398
  41.6 3.7 %collective-permute-start.11 = (bf16[64,2048]{1,0:T(8,128)(2,1)S(1)}, bf16[64,2048]{1,0:T(8,128)(2,1)S(1)}, u32[]{:S(2)}, u32[]{:S(2)}) collective-permute-start(bf16[64,2048]{1,0:T(8,128)(2,1)S(1)} %get-tuple-element.37.refs_0_.refs_3_), channel_id=1, source_target_pairs={{24,26},{26,24},{25,27},{27,25}} | collective-permute-start | bytes 786440 | tf_op jit(solution)/shard_map/ppermute | solution.py:398
  42.4 2.9 %collective-permute-start.10 = (bf16[64,1024]{1,0:T(8,128)(2,1)S(1)}, bf16[64,1024]{1,0:T(8,128)(2,1)S(1)}, u32[]{:S(2)}, u32[]{:S(2)}) collective-permute-start(bf16[64,1024]{1,0:T(8,128)(2,1)S(1)} %advance1_1.1.after_ref), channel_id=1, source_target_pairs={{20,24},{22,26},{21,25},{23,27}} | collective-permute-start | bytes 393224 | tf_op jit(solution)/shard_map/ppermute | solution.py:398
  43.0 7.1 %collective-permute-start.13 = (bf16[64,2048]{1,0:T(8,128)(2,1)S(1)}, bf16[64,2048]{1,0:T(8,128)(2,1)S(1)}, u32[]{:S(2)}, u32[]{:S(2)}) collective-permute-start(bf16[64,2048]{1,0:T(8,128)(2,1)S(1)} %get-tuple-element.37.refs_0_.refs_3_), channel_id=1, source_target_pairs={{28,30},{30,28},{29,31},{31,29}} | collective-permute-start | bytes 786440 | tf_op jit(solution)/shard_map/ppermute | solution.py:398
  45.3 5.7 %collective-permute-start.12 = (bf16[64,1024]{1,0:T(8,128)(2,1)S(1)}, bf16[64,1024]{1,0:T(8,128)(2,1)S(1)}, u32[]{:S(2)}, u32[]{:S(2)}) collective-permute-start(bf16[64,1024]{1,0:T(8,128)(2,1)S(1)} %advance1_2.1.after_ref), channel_id=1, source_target_pairs={{24,28},{26,30},{25,29},{27,31}} | collective-permute-start | bytes 393224 | tf_op jit(solution)/shard_map/ppermute | solution.py:398

commit v10 on v9

--- a/solution.py
+++ b/solution.py
@@ -96,25 +96,20 @@
     return (lax.axis_index("section") == active) & (pair >= first) & (pair <= last)
 
 
-def front(here, h_refs, gain_ref, w_ref, w_rate_ref, base_ref, maps, normed_out, keys_out, x_out, y_out, h_in, near=None):
+def front(here, h_ref, gain_ref, w_ref, w_rate_ref, base_ref, maps, normed_out, keys_out, x_out, y_out, near=None):
     width = keys_out.shape[1]
     quads = width // QUAD
 
     def body():
         if near is None:
-            groups = []
-            gain, w_rate, base, weights, base_lane = gain_ref, w_rate_ref, base_ref, w_ref, width
-            last = lax.axis_index("seq") // 2 == lax.axis_size("seq") // 2 - 1
-            for picked, ref in zip((jnp.logical_not(last), last), h_refs):
-
-                @pl.when(picked)
-                def _():
-                    h_in[...] = ref[...]
+            groups, last = [], []
+            h_in, gain, w_rate, base, weights, base_lane = h_ref, gain_ref, w_rate_ref, base_ref, w_ref, width
         else:
-            gain, w_rate, base, weights, small_sems, sems = near
+            wq, h_in, gain, w_rate, base, weights, small_sems, sems = near
             base_lane = 0
-            pairs = [(gain_ref, gain), (w_rate_ref, w_rate), (base_ref, base), (h_refs[0], h_in)]
+            pairs = [(gain_ref, gain), (w_rate_ref, w_rate), (base_ref, base), (h_ref, h_in)]
             small = [pltpu.make_async_copy(source, target, small_sems.at[index]) for index, (source, target) in enumerate(pairs)]
+            last = [pltpu.make_async_copy(w_ref.at[0, :, pl.ds(0, width)], wq, small_sems.at[len(pairs)])]
             groups = [
                 [
                     pltpu.make_async_copy(
@@ -142,6 +137,8 @@
                 wait_all(groups[quad])
                 if quad + 3 < quads:
                     start_all(groups[quad + 3])
+                if quad + 1 == quads:
+                    start_all(last)
             key_lane = base_lane + quad * QUAD
             return [mm(normed, weights[:, lane : lane + QUAD]) for lane in (key_lane, key_lane + width)]
 
@@ -176,17 +173,18 @@
             before = after
         chain(quads - 1, *before)
 
+        wait_all(last)
+
     pl.when(here)(body)
 
 
-def first_front(h_hbm, gain, weights, w_rate, base, maps, normed_out, keys_out, x_out, y_out, h_in, *near):
+def first_front(h_hbm, gain, weights, w_rate, base, maps, normed_out, keys_out, x_out, y_out, *near):
     here = lax.axis_index("section") == 0
-    front(here, [h_hbm], gain, weights, w_rate, base, maps, normed_out, keys_out, x_out, y_out, h_in, near)
-
-
-def later_front(*refs):
-    refs, rest = refs[:-10], refs[-10:]
-    front(lax.axis_index("section") == 1, refs, *rest)
+    front(here, h_hbm, gain, weights, w_rate, base, maps, normed_out, keys_out, x_out, y_out, near)
+
+
+def later_front(places, h_ref, gain, weights, w_rate, base, after_ref, *outs):
+    front(at_pair(places, 1), h_ref, gain, weights, w_rate, base, *outs)
 
 
 def load(*refs):
@@ -201,37 +199,19 @@
     on_section(1, body)
 
 
-def read_out(active, places, fetches, normed_ref, keys_ref, x_ref, y_ref, w_ref, w_out_hbm, after_ref, reads_out, *rest):
+def read_out(active, places, fetches, normed_ref, keys_ref, x_ref, y_ref, weights, w_out_hbm, after_ref, reads_out, *rest):
     rows, width = keys_ref.shape
-    quads = width // QUAD
-    w_out, rest = rest[:fetches], rest[fetches:]
-    load_sem, *near = rest
+    *w_out, load_sem = rest
 
     def body():
         fetch = [pltpu.make_async_copy(w_out_hbm.at[0], target, load_sem) for target in w_out]
-        if active:
-            weights, groups = w_ref, []
-            start_all(fetch)
-        else:
-            weights, sems = near
-            groups = [
-                [pltpu.make_async_copy(w_ref.at[0, :, pl.ds(quad * QUAD, QUAD)], weights.at[:, pl.ds(quad * QUAD, QUAD)], sems.at[quad])]
-                for quad in range(quads)
-            ]
-            start_all(groups[0])
-            start_all(groups[1])
+        start_all(fetch)
         normed = normed_ref[...]
         ones = head_ones()
         row = lax.broadcasted_iota(jnp.int32, (rows, 2 * rows), 0)
         lane = lax.rem(lax.broadcasted_iota(jnp.int32, (rows, 2 * rows), 1), rows)
         causal = row >= lane
-        for quad in range(quads):
-            if groups:
-                wait_all(groups[quad])
-                if quad + 2 < quads:
-                    start_all(groups[quad + 2])
-                if quad + 3 == quads:
-                    start_all(fetch)
+        for quad in range(width // QUAD):
             queries = unit_heads(mm(normed, weights[:, quad * QUAD : (quad + 1) * QUAD]), ones)
             queries_bf = queries.astype(BF16)
             for half in range(2):
@@ -295,13 +275,12 @@
         pl.when(here & (side == 1))(lambda: body((got_ref, own_ref)))
 
 
-def finish(here, begins, state_ref, got_ref, reads_ref, w_out_ref, h_ref, store, fetch=()):
+def finish(here, begins, state_ref, got_ref, reads_ref, w_out_ref, h_ref, store):
     width = w_out_ref.shape[0]
     model = h_ref.shape[1]
     chunk = model // 4
 
     def body():
-        start_all(fetch)
         follows = lax.rem(lax.axis_index("seq"), 2) == 1
         parts = []
         for start in range(0, width, QUAD):
@@ -315,7 +294,6 @@
             read = mm(reads_ref[:, start : start + QUAD], spread(jnp.concatenate(pieces, axis=1)))
             parts.append((read + offset.astype(F32)).astype(BF16))
         inner_bf = jnp.concatenate(parts, axis=1)
-        wait_all(fetch)
         for start in range(0, model, chunk):
             lanes = slice(start, start + chunk)
             store(start, (h_ref[:, lanes].astype(F32) + mm(inner_bf, w_out_ref[:, lanes])).astype(BF16))
@@ -323,22 +301,19 @@
     pl.when(here)(body)
 
 
-def first_finish(place, passed, state_ref, got_ref, reads_ref, w_out_ref, h_ref, after_ref, *rest):
-    out_ref, *near = rest[passed:]
+def first_finish(place, state_ref, got_ref, reads_ref, w_out_ref, h_ref, after_ref, *rest):
+    out_ref = rest[-1]
 
     def store(start, value):
         out_ref[:, start : start + value.shape[1]] = value
 
-    fetch = []
-    if near:
-        fetch = [pltpu.make_async_copy(w_out_ref.at[0], *near)]
-        w_out_ref = near[0]
-    finish(at_pair([place], 0), place == 0, state_ref, got_ref, reads_ref, w_out_ref, h_ref, store, fetch)
-
-
-def last_finish(count, *refs):
+    finish(at_pair([place], 0), place == 0, state_ref, got_ref, reads_ref, w_out_ref, h_ref, store)
+
+
+def last_finish(count, w_out_ref, *refs):
     states, gots, refs = refs[:count], refs[count : 2 * count], refs[2 * count :]
-    reads_early, reads_late, w_out_early, w_out_late, h_ref, first_early, first_late, out_hbm, near, sems = refs
+    reads, hiddens, firsts = [[refs[index]] * (count - 1) + [refs[index + 1]] for index in (0, 2, 4)]
+    out_hbm, near, sems = refs[6:]
     chunk = near.shape[1] // 4
 
     def write(start):
@@ -350,15 +325,12 @@
         write(start).start()
 
     for place in range(count):
-        reads_ref, w_out_ref = (reads_early, w_out_early) if place + 1 < count else (reads_late, w_out_late)
-        finish(at_pair([place], 1), place == 0, states[place], gots[place], reads_ref, w_out_ref, h_ref, store)
-
-    for places, first_ref in ((range(count - 1), first_early), ([count - 1], first_late)):
-
-        @pl.when(at_pair(places, 0))
+        finish(at_pair([place], 1), place == 0, states[place], gots[place], reads[place], w_out_ref, hiddens[place], store)
+
+        @pl.when(at_pair([place], 0))
         def _():
             for start in range(0, near.shape[1], chunk):
-                store(start, first_ref[:, start : start + chunk])
+                store(start, firsts[place][:, start : start + chunk])
 
     for start in range(0, near.shape[1], chunk):
         write(start).wait()
@@ -401,13 +373,12 @@
         return permute(own, active, [(2 * group + side, 2 * group + 1 - side) for group in groups for side in range(2)])
 
     def layer_reads(active, places, fetches, rows_of, weights, after):
-        near = [pltpu.VMEM((depth, width), BF16), pltpu.SemaphoreType.DMA((quads,))]
         reads, *w_out_near = call(
             functools.partial(read_out, active, places, fetches),
             [shape((rows, 2 * width), BF16)] + [pltpu.VMEM(w_out.shape[1:], BF16)] * fetches,
-            [pltpu.SemaphoreType.DMA] + (near if active == 0 else []),
+            [pltpu.SemaphoreType.DMA],
             [*rows_of, weights, w_out, after],
-            [pltpu.VMEM] * 4 + [pltpu.VMEM if active else pltpu.HBM, pltpu.HBM, pl.ANY],
+            [pltpu.VMEM] * 5 + [pltpu.HBM, pl.ANY],
             name=f"reads{active}_{places[0]}",
         )
         return [reads] + [in_vmem(value) for value in w_out_near]
@@ -422,74 +393,86 @@
 
     groups = count // 2
 
-    own, *rows_of = call(
+    own, *rows_of, wq_near = call(
         first_front,
-        [maps] + rows_out,
+        [maps] + rows_out + [pltpu.VMEM((depth, width), BF16)],
         [pltpu.VMEM(value.shape, value.dtype) for value in (tokens, norm_gain, w_rate, rate_base)]
-        + [pltpu.VMEM((depth, 2 * width), BF16), pltpu.SemaphoreType.DMA((4,)), pltpu.SemaphoreType.DMA((quads, 2))],
+        + [pltpu.VMEM((depth, 2 * width), BF16), pltpu.SemaphoreType.DMA((5,)), pltpu.SemaphoreType.DMA((quads, 2))],
         [in_hbm(tokens), norm_gain, w_qkv, w_rate, rate_base],
         [pltpu.HBM] * 5,
         name="first_front",
     )
+    wq_near = in_vmem(wq_near)
     got_first = swap(own, 0, [0])
     got_rest = swap(own, 0, range(1, groups))
-    read_first = layer_reads(0, [0], 0, rows_of, w_qkv, init_state)
+    read_first = layer_reads(0, [0], 1, rows_of, wq_near, init_state)
     ahead, state = hop(0, 0, [own, got_first], init_state, read_first[0])
-    read_rest = layer_reads(0, range(1, groups), 1, rows_of, w_qkv, ahead)
+    read_rest = layer_reads(0, range(1, groups), 1, rows_of, wq_near, ahead)
     (both,) = call(
         functools.partial(compose, 0), [maps], [], [own, got_rest, read_rest[0]], [pltpu.VMEM] * 2 + [pl.ANY], name="compose"
     )
-    early, here = [], init_state
+
+    params = [norm_gain, w_qkv, w_rate, rate_base, w_out]
+    gain_near, w_near, rate_near, base_near, w_out_near = call(
+        load,
+        [pltpu.VMEM(value.shape, value.dtype) for value in params],
+        [pltpu.SemaphoreType.DMA((5,))],
+        params + [both],
+        [pltpu.HBM] * 5 + [pl.ANY],
+        name="load",
+    )
+    params = [in_vmem(value) for value in (gain_near, w_near.reshape(w_qkv.shape[1:]), rate_near, base_near)]
+    w_out_near = in_vmem(w_out_near.reshape(w_out.shape[1:]))
+
+    def begin(places, first, after):
+        span = range(2 * places[0], 2 * places[-1] + 2)
+        hidden = lax.ppermute(first, ("section", "seq"), [(place, count + place) for place in span])
+        own, *rows_of = call(
+            functools.partial(later_front, places),
+            [maps] + rows_out,
+            [],
+            [hidden, *params, after],
+            [pltpu.VMEM] * 5 + [pl.ANY],
+            name=f"later_front_{places[0]}",
+        )
+        return hidden, own, rows_of, [swap(own, 1, [place]) for place in places]
+
+    here, passed = init_state, []
     for place in range(groups):
-        got, (reads, w_out_near) = (got_rest, read_rest) if place else (got_first, read_first + [w_out])
+        got, (reads, near) = (got_rest, read_rest) if place else (got_first, read_first)
         if 0 < place < groups - 1:
-            ahead, state = hop(0, place, [both], here, early[0])
-        passed = early if place + 1 < groups else []
+            ahead, state = hop(0, place, [both], here, passed[0])
+        if place + 1 == groups:
+            firsts, passed = passed, []
         (first,) = call(
-            functools.partial(first_finish, place, len(passed)),
+            functools.partial(first_finish, place),
             [shape((rows, model), BF16)],
-            [] if place else [pltpu.VMEM(w_out.shape[1:], BF16), pltpu.SemaphoreType.DMA],
-            [here, got, reads, w_out_near, tokens, ahead, *passed],
-            [pltpu.VMEM] * 3 + [pltpu.VMEM if place else pltpu.HBM, pltpu.VMEM, pl.ANY] + [pltpu.VMEM] * len(passed),
+            [],
+            [here, got, reads, near, tokens, ahead, *passed],
+            [pltpu.VMEM] * 5 + [pl.ANY] + [pltpu.VMEM] * len(passed),
             name=f"first_finish_{place}",
             aliases={6: 0} if passed else None,
         )
-        if place + 1 < groups:
-            early = [first]
-        here = state
-    firsts = [early[0], first]
-    spans = [range(2 * (groups - 1)), range(2 * (groups - 1), count)]
-    hiddens = [
-        lax.ppermute(value, ("section", "seq"), [(place, count + place) for place in span]) for value, span in zip(firsts, spans)
-    ]
-
-    params = [norm_gain, w_qkv, w_rate, rate_base]
-    gain_near, w_near, rate_near, base_near = call(
-        load,
-        [pltpu.VMEM(value.shape, value.dtype) for value in params],
-        [pltpu.SemaphoreType.DMA((4,))],
-        params + [both],
-        [pltpu.HBM] * 4 + [pl.ANY],
-        name="load",
-    )
-    params = [in_vmem(value) for value in (gain_near, w_near.reshape(w_qkv.shape[1:]), rate_near, base_near)]
-    own, *rows_of, hidden = call(
-        later_front, [maps] + rows_out + [shape((rows, model), BF16)], [], [*hiddens, *params], name="later_front"
-    )
-    gots = [swap(own, 1, [group]) for group in range(groups)]
-    states, after = [init_state], own
+        passed, here = [first], state
+    firsts += passed
+
+    hidden, own_later, rows_later, gots = begin(range(groups - 1), firsts[0], own)
+    hiddens, states, after = [hidden], [init_state], own_later
     for place in range(groups - 1):
         if place + 2 == groups:
-            reads_early = layer_reads(1, range(groups - 1), 1, rows_of, params[1], after)
-            after = reads_early[0]
-        after, state = hop(1, place, [own, gots[place]], states[-1], after)
+            hidden, own_last, rows_last, got = begin([groups - 1], firsts[1], after)
+            hiddens.append(hidden)
+            gots += got
+            reads = layer_reads(1, range(groups - 1), 0, rows_later, params[1], after)
+            after = reads[0]
+        after, state = hop(1, place, [own_later, gots[place]], states[-1], after)
         states.append(state)
-    reads_late = layer_reads(1, [groups - 1], 1, rows_of, params[1], after)
+    reads += layer_reads(1, [groups - 1], 0, rows_last, params[1], after)
     (result,) = call(
         functools.partial(last_finish, groups),
         [shape((1, rows, model), BF16)],
         [pltpu.VMEM((rows, model), BF16), pltpu.SemaphoreType.DMA((4,))],
-        [*states, *gots, reads_early[0], reads_late[0], reads_early[1], reads_late[1], hidden, *firsts],
+        [w_out_near, *states, *gots, *reads, *hiddens, *firsts],
         name="last_finish",
         out_kind=pltpu.HBM,
     )

time: 53.2 us -> 52.8 us (level)
  waiting for transfers between devices: 25.2 us -> 21.8 us
  Pallas kernels: 14.6 us -> 16 us
  starting transfers between devices: 12.5 us -> 13.9 us
    ppermute x2, waiting for transfers between devices: 24.1 us -> 21 us  [begin(): lax.ppermute(first, ('section', 'seq'), [(place, count + place) for place...]
    ppermute x12, starting transfers between devices: 10.5 us -> 11.9 us  [permute(): lax.ppermute(value, ('section', 'seq'), [(base + source, base + target) f...]
    pallas_call x19 -> x20, Pallas kernels: 14.6 us -> 16 us  [call(): pl.pallas_call(body, out_shape=outs, in_specs=specs, out_specs=[pl.BlockS...]
  transfers between devices with their start and end apart: 14 -> 14, of which waited for: 3 -> 2; matrix products, arithmetic and copies ran while one was open for 0% -> 0% of each run, Pallas kernels for 16% -> 27%
where the time goes in v10:
time: 52.8 us; the launch traced here: 52.5 us
  waiting for transfers between devices  21.8 us (41%)
  Pallas kernels  16 us (30%)
  starting transfers between devices  13.9 us (26%)
    ppermute x2, waiting for transfers between devices, begin(): lax.ppermute(first, ('section', 'seq'), [(place, count + place) for place...  21 us
    pallas_call x20, Pallas kernels, call(): pl.pallas_call(body, out_shape=outs, in_specs=specs, out_specs=[pl.BlockS...  16 us
    ppermute x12, starting transfers between devices, permute(): lax.ppermute(value, ('section', 'seq'), [(base + source, base + target) f...  11.9 us
    ppermute x2, starting transfers between devices, begin(): lax.ppermute(first, ('section', 'seq'), [(place, count + place) for place...  1.99 us
  transfers between devices with their start and end apart: 14, of which 2 were waited for; matrix products, arithmetic and copies ran while one was open for 0% of the time, Pallas kernels for 27%

profile of v10, /device:TPU:25, one launch (start us, length us, event | category | flops | bytes accessed | tf_op | source)
XLA Modules:
  0.0 52.5 jit_solution(2862942698872320052)
XLA Ops:
  0.0 0.0 copy-start
  0.0 0.1 first_front.1
  0.1 0.8 %collective-permute-start.1 = (bf16[64,2048]{1,0:T(8,128)(2,1)S(1)}, bf16[64,2048]{1,0:T(8,128)(2,1)S(1)}, u32[]{:S(2)}, u32[]{:S(2)}) collective-permute-start(bf16[64,2048]{1,0:T(8,128)(2,1)S(1)} %get-tuple-element.30.refs_0_.own_ref.after_ref), channel_id=1, source_target_pairs={{0,2},{2,0},{1,3},{3,1}} | collective-permute-start | bytes 786440 | tf_op jit(solution)/shard_map/ppermute | solution.py:370
  0.9 0.7 %collective-permute-start = (bf16[64,2048]{1,0:T(8,128)(2,1)S(1)}, bf16[64,2048]{1,0:T(8,128)(2,1)S(1)}, u32[]{:S(2)}, u32[]{:S(2)}) collective-permute-start(bf16[64,2048]{1,0:T(8,128)(2,1)S(1)} %get-tuple-element.30.refs_0_.own_ref.after_ref), channel_id=1, source_target_pairs={{4,6},{6,4},{8,10},{10,8},{12,14},{14,12},{5,7},{7,5},{9,11},{11,9... | collective-permute-start | bytes 786440 | tf_op jit(solution)/shard_map/ppermute | solution.py:370
  1.6 0.0 copy-done
  1.7 0.0 collective-permute-done.1.refs_1_.got_ref
  1.7 0.0 copy-start.1
  1.7 0.8 %collective-permute-start.2 = (bf16[64,1024]{1,0:T(8,128)(2,1)S(1)}, bf16[64,1024]{1,0:T(8,128)(2,1)S(1)}, u32[]{:S(2)}, u32[]{:S(2)}) collective-permute-start(bf16[64,1024]{1,0:T(8,128)(2,1)S(1)} %advance0_0.1.after_ref), channel_id=1, source_target_pairs={{0,4},{2,6},{1,5},{3,7}} | collective-permute-start | bytes 393224 | tf_op jit(solution)/shard_map/ppermute | solution.py:370
  2.6 0.2 copy-done.1
  2.8 0.0 collective-permute-done.got_ref
  2.8 0.0 collective-permute-done.2.refs_1_.state_ref
  2.8 0.7 %collective-permute-start.3 = (bf16[64,1024]{1,0:T(8,128)(2,1)S(1)}, bf16[64,1024]{1,0:T(8,128)(2,1)S(1)}, u32[]{:S(2)}, u32[]{:S(2)}) collective-permute-start(bf16[64,1024]{1,0:T(8,128)(2,1)S(1)} %advance0_1.1.after_ref), channel_id=1, source_target_pairs={{4,8},{6,10},{5,9},{7,11}} | collective-permute-start | bytes 393224 | tf_op jit(solution)/shard_map/ppermute | solution.py:370
  3.5 0.0 collective-permute-done.3.refs_1_.state_ref
  3.6 0.7 %collective-permute-start.4 = (bf16[128,2048]{1,0:T(8,128)(2,1)S(1)}, bf16[128,2048]{1,0:T(8,128)(2,1)S(1)}, u32[]{:S(2)}, u32[]{:S(2)}) collective-permute-start(bf16[128,2048]{1,0:T(8,128)(2,1)S(1)} %first_finish_2.1.refs_12_), channel_id=1, source_target_pairs={{0,16},{2,18},{4,20},{6,22},{8,24},{10,26},{1,17},{3,19},{5,21},{7... | collective-permute-start | bytes 1572872 | tf_op jit(solution)/shard_map/ppermute | solution.py:429
  4.3 0.7 %collective-permute-start.11 = (bf16[64,1024]{1,0:T(8,128)(2,1)S(1)}, bf16[64,1024]{1,0:T(8,128)(2,1)S(1)}, u32[]{:S(2)}, u32[]{:S(2)}) collective-permute-start(bf16[64,1024]{1,0:T(8,128)(2,1)S(1)} %advance0_2.1.after_ref), channel_id=1, source_target_pairs={{8,12},{10,14},{9,13},{11,15}} | collective-permute-start | bytes 393224 | tf_op jit(solution)/shard_map/ppermute | solution.py:370
  5.0 0.0 collective-permute-done.11.state_ref
  5.0 0.2 first_finish_3.1.refs_13_
  5.2 1.3 %collective-permute-start.12 = (bf16[128,2048]{1,0:T(8,128)(2,1)S(1)}, bf16[128,2048]{1,0:T(8,128)(2,1)S(1)}, u32[]{:S(2)}, u32[]{:S(2)}) collective-permute-start(bf16[128,2048]{1,0:T(8,128)(2,1)S(1)} %first_finish_3.1.refs_13_), channel_id=1, source_target_pairs={{12,28},{14,30},{13,29},{15,31}} | collective-permute-start | bytes 1572872 | tf_op jit(solution)/shard_map/ppermute | solution.py:429
  6.5 5.9 %load.1 = (f32[1,2048]{1,0:T(1,128)S(1)}, bf16[1,2048,3072]{2,1,0:T(8,128)(2,1)S(1)}, bf16[1,16,2048]{2,1,0:T(8,128)(2,1)S(1)}, f32[1,16]{1,0:T(1,128)S(1)}, bf16[1,1024,2048]{2,1,0:T(8,128)(2,1)S(1)}) custom-call(f32[1,2048]{1,0:T(1,128)} %refs_0_.2, bf16[1,2048,3072]{2,1,0:T(8,128)(2,1)} %refs_1_.1, bf16[1,16,2048]{2,1,0:T(8,128)(2,1)} %bitcast.9, ...), custom_call_target="tpu_custom_call" | custom-call | tf_op jit(solution)/shard_map/load/pallas_call | solution.py:341
  12.4 0.0 collective-permute-done.4.h_ref.refs_10_
  12.4 0.7 %collective-permute-start.5 = (bf16[64,2048]{1,0:T(8,128)(2,1)S(1)}, bf16[64,2048]{1,0:T(8,128)(2,1)S(1)}, u32[]{:S(2)}, u32[]{:S(2)}) collective-permute-start(bf16[64,2048]{1,0:T(8,128)(2,1)S(1)} %get-tuple-element.45.refs_0_.refs_3_), channel_id=1, source_target_pairs={{16,18},{18,16},{17,19},{19,17}} | collective-permute-start | bytes 786440 | tf_op jit(solution)/shard_map/ppermute | solution.py:370
  13.1 0.7 %collective-permute-start.7 = (bf16[64,2048]{1,0:T(8,128)(2,1)S(1)}, bf16[64,2048]{1,0:T(8,128)(2,1)S(1)}, u32[]{:S(2)}, u32[]{:S(2)}) collective-permute-start(bf16[64,2048]{1,0:T(8,128)(2,1)S(1)} %get-tuple-element.45.refs_0_.refs_3_), channel_id=1, source_target_pairs={{20,22},{22,20},{21,23},{23,21}} | collective-permute-start | bytes 786440 | tf_op jit(solution)/shard_map/ppermute | solution.py:370
  13.8 0.0 collective-permute-done.5.refs_1_.refs_4_
  13.9 0.7 %collective-permute-start.6 = (bf16[64,1024]{1,0:T(8,128)(2,1)S(1)}, bf16[64,1024]{1,0:T(8,128)(2,1)S(1)}, u32[]{:S(2)}, u32[]{:S(2)}) collective-permute-start(bf16[64,1024]{1,0:T(8,128)(2,1)S(1)} %advance1_0.1.refs_3_), channel_id=1, source_target_pairs={{16,20},{18,22},{17,21},{19,23}} | collective-permute-start | bytes 393224 | tf_op jit(solution)/shard_map/ppermute | solution.py:370
  14.5 0.7 %collective-permute-start.9 = (bf16[64,2048]{1,0:T(8,128)(2,1)S(1)}, bf16[64,2048]{1,0:T(8,128)(2,1)S(1)}, u32[]{:S(2)}, u32[]{:S(2)}) collective-permute-start(bf16[64,2048]{1,0:T(8,128)(2,1)S(1)} %get-tuple-element.45.refs_0_.refs_3_), channel_id=1, source_target_pairs={{24,26},{26,24},{25,27},{27,25}} | collective-permute-start | bytes 786440 | tf_op jit(solution)/shard_map/ppermute | solution.py:370
  15.2 0.0 collective-permute-done.7.refs_1_.refs_5_
  15.2 0.0 collective-permute-done.6.refs_2_.refs_1_
  15.3 0.7 %collective-permute-start.8 = (bf16[64,1024]{1,0:T(8,128)(2,1)S(1)}, bf16[64,1024]{1,0:T(8,128)(2,1)S(1)}, u32[]{:S(2)}, u32[]{:S(2)}) collective-permute-start(bf16[64,1024]{1,0:T(8,128)(2,1)S(1)} %advance1_1.1.after_ref), channel_id=1, source_target_pairs={{20,24},{22,26},{21,25},{23,27}} | collective-permute-start | bytes 393224 | tf_op jit(solution)/shard_map/ppermute | solution.py:370
  16.0 21.0 %collective-permute-done.12.h_ref.refs_11_ = bf16[128,2048]{1,0:T(8,128)(2,1)S(1)} collective-permute-done((bf16[128,2048]{1,0:T(8,128)(2,1)S(1)}, bf16[128,2048]{1,0:T(8,128)(2,1)S(1)}, u32[]{:S(2)}, u32[]{:S(2)}) %collective-permute-start.12) | collective-permute-done | bytes 524320 | tf_op jit(solution)/shard_map/ppermute | solution.py:429
  36.9 4.2 %later_front_3.1 = (bf16[64,2048]{1,0:T(8,128)(2,1)S(1)}, bf16[128,2048]{1,0:T(8,128)(2,1)S(1)}, bf16[128,1024]{1,0:T(8,128)(2,1)S(1)}, bf16[128,1024]{1,0:T(8,128)(2,1)S(1)}, bf16[128,1024]{1,0:T(8,128)(2,1)S(1)}) custom-call(bf16[128,2048]{1,0:T(8,128)(2,1)S(1)} %collective-permute-done.12.h_ref.refs_11_, f32[1,2048]{1,0:T(1,128)S(1)} %get-tuple-element.41.gain, ...), custom_call_target="tpu_custom_call" | custom-call | tf_op jit(solution)/shard_map/later_front_3/pallas_call | solution.py:341
  41.1 3.6 %collective-permute-start.13 = (bf16[64,2048]{1,0:T(8,128)(2,1)S(1)}, bf16[64,2048]{1,0:T(8,128)(2,1)S(1)}, u32[]{:S(2)}, u32[]{:S(2)}) collective-permute-start(bf16[64,2048]{1,0:T(8,128)(2,1)S(1)} %get-tuple-element.50), channel_id=1, source_target_pairs={{28,30},{30,28},{29,31},{31,29}} | collective-permute-start | bytes 786440 | tf_op jit(solution)/shard_map/ppermute | solution.py:370
  44.8 0.0 collective-permute-done.9.refs_1_.refs_6_
  44.8 0.0 collective-permute-done.8.refs_2_
  44.9 1.3 %collective-permute-start.10 = (bf16[64,1024]{1,0:T(8,128)(2,1)S(1)}, bf16[64,1024]{1,0:T(8,128)(2,1)S(1)}, u32[]{:S(2)}, u32[]{:S(2)}) collective-permute-start(bf16[64,1024]{1,0:T(8,128)(2,1)S(1)} %advance1_2.1.after_ref), channel_id=1, source_target_pairs={{24,28},{26,30},{25,29},{27,31}} | collective-permute-start | bytes 393224 | tf_op jit(solution)/shard_map/ppermute | solution.py:370
  46.2 3.6 %reads1_3.1.refs_9_ = bf16[128,2048]{1,0:T(8,128)(2,1)S(1)} custom-call(bf16[128,2048]{1,0:T(8,128)(2,1)S(1)} %get-tuple-element.51.normed_ref, bf16[128,1024]{1,0:T(8,128)(2,1)S(1)} %get-tuple-element.52.keys_ref, bf16[128,1024]{1,0:T(8,128)(2,1)S(1)} %get-tuple-element.53.x_ref, bf16[128,1024]{1,0:T(8,128)(2,1)S(1)} %get-tuple-element.54.y_ref, ...), custom_call_target="tpu_custom_call" | custom-call | tf_op jit(solution)/shard_map/reads1_3/pallas_call | solution.py:341
  49.7 0.8 %collective-permute-done.10.refs_3_ = bf16[64,1024]{1,0:T(8,128)(2,1)S(1)} collective-permute-done((bf16[64,1024]{1,0:T(8,128)(2,1)S(1)}, bf16[64,1024]{1,0:T(8,128)(2,1)S(1)}, u32[]{:S(2)}, u32[]{:S(2)}) %collective-permute-start.10) | collective-permute-done | bytes 131104 | tf_op jit(solution)/shard_map/ppermute | solution.py:370
  50.6 0.0 collective-permute-done.13.refs_7_
  50.6 1.7 %last_finish.1 = bf16[1,128,2048]{2,1,0:T(8,128)(2,1)} custom-call(bf16[1024,2048]{1,0:T(8,128)(2,1)S(1)} %bitcast.7, f32[1,16,64,64]{3,2,1,0:T(8,128)S(1)} %copy-done, bf16[64,1024]{1,0:T(8,128)(2,1)S(1)} %collective-permute-done.6.refs_2_.refs_1_, bf16[64,1024]{1,0:T(8,128)(2,1)S(1)} %collective-permute-done.8.refs_2_, ...), custom_call_target="tpu_custom_call" | custom-call | tf_op jit(solution)/shard_map/last_finish/pallas_call | solution.py:341
  (14 shorter events, 0.3 us)
Async XLA Ops:
  0.0 1.6 %copy-start = (f32[1,16,64,64]{3,2,1,0:T(8,128)S(1)}, f32[1,16,64,64]{3,2,1,0:T(8,128)}, u32[]{:S(2)}) copy-start(f32[1,16,64,64]{3,2,1,0:T(8,128)} %refs_0_.3) | copy-start | bytes 786436
  0.1 1.6 %collective-permute-start.1 = (bf16[64,2048]{1,0:T(8,128)(2,1)S(1)}, bf16[64,2048]{1,0:T(8,128)(2,1)S(1)}, u32[]{:S(2)}, u32[]{:S(2)}) collective-permute-start(bf16[64,2048]{1,0:T(8,128)(2,1)S(1)} %get-tuple-element.30.refs_0_.own_ref.after_ref), channel_id=1, source_target_pairs={{0,2},{2,0},{1,3},{3,1}} | collective-permute-start | bytes 786440 | tf_op jit(solution)/shard_map/ppermute | solution.py:370
  0.9 1.8 %collective-permute-start = (bf16[64,2048]{1,0:T(8,128)(2,1)S(1)}, bf16[64,2048]{1,0:T(8,128)(2,1)S(1)}, u32[]{:S(2)}, u32[]{:S(2)}) collective-permute-start(bf16[64,2048]{1,0:T(8,128)(2,1)S(1)} %get-tuple-element.30.refs_0_.own_ref.after_ref), channel_id=1, source_target_pairs={{4,6},{6,4},{8,10},{10,8},{12,14},{14,12},{5,7},{7,5},{9,11},{11,9... | collective-permute-start | bytes 786440 | tf_op jit(solution)/shard_map/ppermute | solution.py:370
  1.7 1.0 %copy-start.1 = (bf16[128,2048]{1,0:T(8,128)(2,1)S(1)}, bf16[128,2048]{1,0:T(8,128)(2,1)}, u32[]{:S(2)}) copy-start(bf16[128,2048]{1,0:T(8,128)(2,1)} %h_ref.7) | copy-start | bytes 1572868
  1.7 1.0 %collective-permute-start.2 = (bf16[64,1024]{1,0:T(8,128)(2,1)S(1)}, bf16[64,1024]{1,0:T(8,128)(2,1)S(1)}, u32[]{:S(2)}, u32[]{:S(2)}) collective-permute-start(bf16[64,1024]{1,0:T(8,128)(2,1)S(1)} %advance0_0.1.after_ref), channel_id=1, source_target_pairs={{0,4},{2,6},{1,5},{3,7}} | collective-permute-start | bytes 393224 | tf_op jit(solution)/shard_map/ppermute | solution.py:370
  2.8 0.7 %collective-permute-start.3 = (bf16[64,1024]{1,0:T(8,128)(2,1)S(1)}, bf16[64,1024]{1,0:T(8,128)(2,1)S(1)}, u32[]{:S(2)}, u32[]{:S(2)}) collective-permute-start(bf16[64,1024]{1,0:T(8,128)(2,1)S(1)} %advance0_1.1.after_ref), channel_id=1, source_target_pairs={{4,8},{6,10},{5,9},{7,11}} | collective-permute-start | bytes 393224 | tf_op jit(solution)/shard_map/ppermute | solution.py:370
  3.6 8.8 %collective-permute-start.4 = (bf16[128,2048]{1,0:T(8,128)(2,1)S(1)}, bf16[128,2048]{1,0:T(8,128)(2,1)S(1)}, u32[]{:S(2)}, u32[]{:S(2)}) collective-permute-start(bf16[128,2048]{1,0:T(8,128)(2,1)S(1)} %first_finish_2.1.refs_12_), channel_id=1, source_target_pairs={{0,16},{2,18},{4,20},{6,22},{8,24},{10,26},{1,17},{3,19},{5,21},{7... | collective-permute-start | bytes 1572872 | tf_op jit(solution)/shard_map/ppermute | solution.py:429
  4.3 0.7 %collective-permute-start.11 = (bf16[64,1024]{1,0:T(8,128)(2,1)S(1)}, bf16[64,1024]{1,0:T(8,128)(2,1)S(1)}, u32[]{:S(2)}, u32[]{:S(2)}) collective-permute-start(bf16[64,1024]{1,0:T(8,128)(2,1)S(1)} %advance0_2.1.after_ref), channel_id=1, source_target_pairs={{8,12},{10,14},{9,13},{11,15}} | collective-permute-start | bytes 393224 | tf_op jit(solution)/shard_map/ppermute | solution.py:370
  5.2 31.7 %collective-permute-start.12 = (bf16[128,2048]{1,0:T(8,128)(2,1)S(1)}, bf16[128,2048]{1,0:T(8,128)(2,1)S(1)}, u32[]{:S(2)}, u32[]{:S(2)}) collective-permute-start(bf16[128,2048]{1,0:T(8,128)(2,1)S(1)} %first_finish_3.1.refs_13_), channel_id=1, source_target_pairs={{12,28},{14,30},{13,29},{15,31}} | collective-permute-start | bytes 1572872 | tf_op jit(solution)/shard_map/ppermute | solution.py:429
  12.4 1.4 %collective-permute-start.5 = (bf16[64,2048]{1,0:T(8,128)(2,1)S(1)}, bf16[64,2048]{1,0:T(8,128)(2,1)S(1)}, u32[]{:S(2)}, u32[]{:S(2)}) collective-permute-start(bf16[64,2048]{1,0:T(8,128)(2,1)S(1)} %get-tuple-element.45.refs_0_.refs_3_), channel_id=1, source_target_pairs={{16,18},{18,16},{17,19},{19,17}} | collective-permute-start | bytes 786440 | tf_op jit(solution)/shard_map/ppermute | solution.py:370
  13.1 2.1 %collective-permute-start.7 = (bf16[64,2048]{1,0:T(8,128)(2,1)S(1)}, bf16[64,2048]{1,0:T(8,128)(2,1)S(1)}, u32[]{:S(2)}, u32[]{:S(2)}) collective-permute-start(bf16[64,2048]{1,0:T(8,128)(2,1)S(1)} %get-tuple-element.45.refs_0_.refs_3_), channel_id=1, source_target_pairs={{20,22},{22,20},{21,23},{23,21}} | collective-permute-start | bytes 786440 | tf_op jit(solution)/shard_map/ppermute | solution.py:370
  13.9 1.4 %collective-permute-start.6 = (bf16[64,1024]{1,0:T(8,128)(2,1)S(1)}, bf16[64,1024]{1,0:T(8,128)(2,1)S(1)}, u32[]{:S(2)}, u32[]{:S(2)}) collective-permute-start(bf16[64,1024]{1,0:T(8,128)(2,1)S(1)} %advance1_0.1.refs_3_), channel_id=1, source_target_pairs={{16,20},{18,22},{17,21},{19,23}} | collective-permute-start | bytes 393224 | tf_op jit(solution)/shard_map/ppermute | solution.py:370
  14.5 30.3 %collective-permute-start.9 = (bf16[64,2048]{1,0:T(8,128)(2,1)S(1)}, bf16[64,2048]{1,0:T(8,128)(2,1)S(1)}, u32[]{:S(2)}, u32[]{:S(2)}) collective-permute-start(bf16[64,2048]{1,0:T(8,128)(2,1)S(1)} %get-tuple-element.45.refs_0_.refs_3_), channel_id=1, source_target_pairs={{24,26},{26,24},{25,27},{27,25}} | collective-permute-start | bytes 786440 | tf_op jit(solution)/shard_map/ppermute | solution.py:370
  15.3 29.6 %collective-permute-start.8 = (bf16[64,1024]{1,0:T(8,128)(2,1)S(1)}, bf16[64,1024]{1,0:T(8,128)(2,1)S(1)}, u32[]{:S(2)}, u32[]{:S(2)}) collective-permute-start(bf16[64,1024]{1,0:T(8,128)(2,1)S(1)} %advance1_1.1.after_ref), channel_id=1, source_target_pairs={{20,24},{22,26},{21,25},{23,27}} | collective-permute-start | bytes 393224 | tf_op jit(solution)/shard_map/ppermute | solution.py:370
  41.1 9.5 %collective-permute-start.13 = (bf16[64,2048]{1,0:T(8,128)(2,1)S(1)}, bf16[64,2048]{1,0:T(8,128)(2,1)S(1)}, u32[]{:S(2)}, u32[]{:S(2)}) collective-permute-start(bf16[64,2048]{1,0:T(8,128)(2,1)S(1)} %get-tuple-element.50), channel_id=1, source_target_pairs={{28,30},{30,28},{29,31},{31,29}} | collective-permute-start | bytes 786440 | tf_op jit(solution)/shard_map/ppermute | solution.py:370
  44.9 5.7 %collective-permute-start.10 = (bf16[64,1024]{1,0:T(8,128)(2,1)S(1)}, bf16[64,1024]{1,0:T(8,128)(2,1)S(1)}, u32[]{:S(2)}, u32[]{:S(2)}) collective-permute-start(bf16[64,1024]{1,0:T(8,128)(2,1)S(1)} %advance1_2.1.after_ref), channel_id=1, source_target_pairs={{24,28},{26,30},{25,29},{27,31}} | collective-permute-start | bytes 393224 | tf_op jit(solution)/shard_map/ppermute | solution.py:370

commit v11 on v10

--- a/solution.py
+++ b/solution.py
@@ -109,7 +109,8 @@
             base_lane = 0
             pairs = [(gain_ref, gain), (w_rate_ref, w_rate), (base_ref, base), (h_ref, h_in)]
             small = [pltpu.make_async_copy(source, target, small_sems.at[index]) for index, (source, target) in enumerate(pairs)]
-            last = [pltpu.make_async_copy(w_ref.at[0, :, pl.ds(0, width)], wq, small_sems.at[len(pairs)])]
+            half = wq.shape[1]
+            last = [pltpu.make_async_copy(w_ref.at[0, :, pl.ds(0, half)], wq, small_sems.at[len(pairs)])]
             groups = [
                 [
                     pltpu.make_async_copy(
@@ -142,23 +143,31 @@
             key_lane = base_lane + quad * QUAD
             return [mm(normed, weights[:, lane : lane + QUAD]) for lane in (key_lane, key_lane + width)]
 
-        def chain(quad, keys, values):
+        def unit(quad, keys, values):
             lanes = slice(quad * QUAD, (quad + 1) * QUAD)
             keys = unit_heads(keys, ones)
             keys_bf = keys.astype(BF16)
             keys_out[:, lanes] = keys_bf
             rate = rates[:, lanes]
-            x_all = rate * keys
-            y_all = rate * values
+            return keys_bf, rate * keys, rate * values
+
+        def crossed(quad, keys_bf, x_all, y_all):
+            return mm_nt(keys_bf[HD:], spread(keys_bf[:HD])).astype(BF16)
+
+        def fixed(quad, cross, keys_bf, x_all, y_all):
+            lanes = slice(quad * QUAD, (quad + 1) * QUAD)
+            rate = rates[HD:, lanes]
             x_first, y_first = x_all[:HD].astype(BF16), y_all[:HD].astype(BF16)
-            cross = mm_nt(keys_bf[HD:], spread(keys_bf[:HD])).astype(BF16)
             fix = mm(cross, spread_two(x_first, y_first))
-            x_second = (x_all[HD:] - rate[HD:] * fix[:, :QUAD]).astype(BF16)
-            y_second = (y_all[HD:] - rate[HD:] * fix[:, QUAD:]).astype(BF16)
+            x_second = (x_all[HD:] - rate * fix[:, :QUAD]).astype(BF16)
+            y_second = (y_all[HD:] - rate * fix[:, QUAD:]).astype(BF16)
             x_bf = jnp.concatenate([x_first, x_second], axis=0)
             y_bf = jnp.concatenate([y_first, y_second], axis=0)
             x_out[:, lanes] = x_bf
             y_out[:, lanes] = y_bf
+            return x_bf, y_bf
+
+        def mapped(quad, keys_bf, x_bf, y_bf):
             for half in range(2):
                 own = slice(half * PAIR, (half + 1) * PAIR)
                 start = quad * QUAD + half * PAIR
@@ -166,13 +175,22 @@
                 maps[:, start : start + PAIR] = diagonal(both[:, :PAIR]).astype(BF16)
                 maps[:, width + start : width + start + PAIR] = diagonal(both[:, PAIR:]).astype(BF16)
 
-        before = project(0)
-        for quad in range(1, quads):
-            after = project(quad)
-            chain(quad - 1, *before)
-            before = after
-        chain(quads - 1, *before)
-
+        def stages(picked, projected):
+            units = [unit(quad, *projected[quad]) for quad in picked]
+            crosses = [crossed(quad, *value) for quad, value in zip(picked, units)]
+            fixes = [fixed(quad, cross, *value) for quad, cross, value in zip(picked, crosses, units)]
+            for quad, value, fix in zip(picked, units, fixes):
+                mapped(quad, value[0], *fix)
+
+        if groups:
+            projected = {0: project(0)}
+            for quad in range(1, quads):
+                projected[quad] = project(quad)
+                if quad + 1 < quads:
+                    stages([quad - 1], projected)
+            stages([quads - 2, quads - 1], projected)
+        else:
+            stages(range(quads), [project(quad) for quad in range(quads)])
         wait_all(last)
 
     pl.when(here)(body)
@@ -199,31 +217,41 @@
     on_section(1, body)
 
 
-def read_out(active, places, fetches, normed_ref, keys_ref, x_ref, y_ref, weights, w_out_hbm, after_ref, reads_out, *rest):
+def read_out(active, places, fetches, normed_ref, keys_ref, x_ref, y_ref, weights, w_hbm, w_out_hbm, after_ref, reads_out, *rest):
     rows, width = keys_ref.shape
-    *w_out, load_sem = rest
+    *w_out, wq, sems = rest
+    half = width // 2
 
     def body():
-        fetch = [pltpu.make_async_copy(w_out_hbm.at[0], target, load_sem) for target in w_out]
-        start_all(fetch)
+        late = [pltpu.make_async_copy(w_hbm.at[0, :, pl.ds(half, half)], wq, sems.at[0])] * fetches
+        fetch = [pltpu.make_async_copy(w_out_hbm.at[0], target, sems.at[1]) for target in w_out]
+        start_all(late)
         normed = normed_ref[...]
         ones = head_ones()
         row = lax.broadcasted_iota(jnp.int32, (rows, 2 * rows), 0)
         lane = lax.rem(lax.broadcasted_iota(jnp.int32, (rows, 2 * rows), 1), rows)
         causal = row >= lane
-        for quad in range(width // QUAD):
-            queries = unit_heads(mm(normed, weights[:, quad * QUAD : (quad + 1) * QUAD]), ones)
-            queries_bf = queries.astype(BF16)
-            for half in range(2):
-                own = slice(half * PAIR, (half + 1) * PAIR)
-                start = quad * QUAD + half * PAIR
-                place = slice(start, start + PAIR)
-                scores = mm_nt(queries_bf[:, own], spread(keys_ref[:, place]))
-                scores = jnp.where(causal, scores, 0.0).astype(BF16)
-                both = mm(scores, spread_two(x_ref[:, place], y_ref[:, place]))
-                reads_out[:, place] = (queries[:, own] - both[:, :PAIR]).astype(BF16)
-                reads_out[:, width + start : width + start + PAIR] = both[:, PAIR:].astype(BF16)
-        wait_all(fetch)
+
+        def stages(start, stop, source, base):
+            quads = range(start, stop, QUAD)
+            queries = [unit_heads(mm(normed, source[:, lane - base : lane - base + QUAD]), ones) for lane in quads]
+            parts = [value[:, own : own + PAIR] for value in queries for own in range(0, QUAD, PAIR)]
+            places = [slice(lane, lane + PAIR) for lane in range(start, stop, PAIR)]
+            scores = [mm_nt(part.astype(BF16), spread(keys_ref[:, place])) for part, place in zip(parts, places)]
+            scores = [jnp.where(causal, score, 0.0).astype(BF16) for score in scores]
+            both = [mm(score, spread_two(x_ref[:, place], y_ref[:, place])) for score, place in zip(scores, places)]
+            for part, place, value in zip(parts, places, both):
+                reads_out[:, place] = (part - value[:, :PAIR]).astype(BF16)
+                reads_out[:, width + place.start : width + place.stop] = value[:, PAIR:].astype(BF16)
+
+        if fetches:
+            stages(0, half, weights, 0)
+            wait_all(late)
+            start_all(fetch)
+            stages(half, width, wq, half)
+            wait_all(fetch)
+        else:
+            stages(0, width, weights, 0)
 
     pl.when(at_pair(places, active))(body)
 
@@ -258,12 +286,12 @@
     width = out_ref.shape[1]
 
     def body(refs):
-        for start in range(0, width, PAIR):
-            lanes = slice(start, start + PAIR)
-            state = state_ref[:, lanes].astype(F32) if place else pair_state(state_ref, start // PAIR)
-            for ref in refs:
-                state = apply_map(state, ref, start, width)
-            out_ref[:, lanes] = state.astype(BF16)
+        starts = range(0, width, PAIR)
+        states = [state_ref[:, start : start + PAIR].astype(F32) if place else pair_state(state_ref, start // PAIR) for start in starts]
+        for ref in refs:
+            states = [apply_map(state, ref, start, width) for state, start in zip(states, starts)]
+        for state, start in zip(states, starts):
+            out_ref[:, start : start + PAIR] = state.astype(BF16)
 
     index = lax.axis_index("seq")
     here = (lax.axis_index("section") == active) & (index // 2 == place)
@@ -282,18 +310,20 @@
 
     def body():
         follows = lax.rem(lax.axis_index("seq"), 2) == 1
-        parts = []
-        for start in range(0, width, QUAD):
-            pieces = []
-            for lane in range(start, start + QUAD, PAIR):
-                lanes = slice(lane, lane + PAIR)
-                state = pair_state(state_ref, lane // PAIR) if begins else state_ref[:, lanes].astype(F32)
-                moved = apply_map(state, got_ref, lane, width)
-                pieces.append(jnp.where(follows, moved, state).astype(BF16))
-            offset = reads_ref[:, width + start : width + start + QUAD]
-            read = mm(reads_ref[:, start : start + QUAD], spread(jnp.concatenate(pieces, axis=1)))
-            parts.append((read + offset.astype(F32)).astype(BF16))
-        inner_bf = jnp.concatenate(parts, axis=1)
+        starts = range(0, width, PAIR)
+        states = [pair_state(state_ref, start // PAIR) if begins else state_ref[:, start : start + PAIR].astype(F32) for start in starts]
+        moved = [apply_map(state, got_ref, start, width) for state, start in zip(states, starts)]
+        states = [jnp.where(follows, after, state).astype(BF16) for after, state in zip(moved, states)]
+        quads = range(0, width, QUAD)
+        spreads = [spread(jnp.concatenate(states[start // PAIR : (start + QUAD) // PAIR], axis=1)) for start in quads]
+        reads = [mm(reads_ref[:, start : start + QUAD], value) for start, value in zip(quads, spreads)]
+        inner_bf = jnp.concatenate(
+            [
+                (read + reads_ref[:, width + start : width + start + QUAD].astype(F32)).astype(BF16)
+                for start, read in zip(quads, reads)
+            ],
+            axis=1,
+        )
         for start in range(0, model, chunk):
             lanes = slice(start, start + chunk)
             store(start, (h_ref[:, lanes].astype(F32) + mm(inner_bf, w_out_ref[:, lanes])).astype(BF16))
@@ -376,9 +406,9 @@
         reads, *w_out_near = call(
             functools.partial(read_out, active, places, fetches),
             [shape((rows, 2 * width), BF16)] + [pltpu.VMEM(w_out.shape[1:], BF16)] * fetches,
-            [pltpu.SemaphoreType.DMA],
-            [*rows_of, weights, w_out, after],
-            [pltpu.VMEM] * 5 + [pltpu.HBM, pl.ANY],
+            [pltpu.VMEM((depth, width // 2), BF16) if fetches else pltpu.VMEM((16, 128), BF16), pltpu.SemaphoreType.DMA((2,))],
+            [*rows_of, weights, w_qkv, w_out, after],
+            [pltpu.VMEM] * 5 + [pltpu.HBM, pltpu.HBM, pl.ANY],
             name=f"reads{active}_{places[0]}",
         )
         return [reads] + [in_vmem(value) for value in w_out_near]
@@ -395,7 +425,7 @@
 
     own, *rows_of, wq_near = call(
         first_front,
-        [maps] + rows_out + [pltpu.VMEM((depth, width), BF16)],
+        [maps] + rows_out + [pltpu.VMEM((depth, width // 2), BF16)],
         [pltpu.VMEM(value.shape, value.dtype) for value in (tokens, norm_gain, w_rate, rate_base)]
         + [pltpu.VMEM((depth, 2 * width), BF16), pltpu.SemaphoreType.DMA((5,)), pltpu.SemaphoreType.DMA((quads, 2))],
         [in_hbm(tokens), norm_gain, w_qkv, w_rate, rate_base],

time: 52.8 us -> 51.4 us (0.973)
  Pallas kernels: 16 us -> 13.1 us
  waiting for transfers between devices: 21.8 us -> 24.2 us
  starting transfers between devices: 13.9 us -> 13 us
    pallas_call x20, Pallas kernels: 16 us -> 13.1 us  [call(): pl.pallas_call(body, out_shape=outs, in_specs=specs, out_specs=[pl.BlockS...]
    ppermute x12, waiting for transfers between devices: 0.87 us -> 2.35 us  [permute(): lax.ppermute(value, ('section', 'seq'), [(base + source, base + target) f...]
    ppermute x2, waiting for transfers between devices: 21 us -> 21.9 us  [begin(): lax.ppermute(first, ('section', 'seq'), [(place, count + place) for place...]
    ppermute x12, starting transfers between devices: 11.9 us -> 11 us  [permute(): lax.ppermute(value, ('section', 'seq'), [(base + source, base + target) f...]
  transfers between devices with their start and end apart: 14 -> 14, of which waited for: 2 -> 2; matrix products, arithmetic and copies ran while one was open for 0% -> 0% of each run, Pallas kernels for 27% -> 22%
where the time goes in v11:
time: 51.4 us; the launch traced here: 51.1 us
  waiting for transfers between devices  24.2 us (47%)
  Pallas kernels  13.1 us (25%)
  starting transfers between devices  13 us (25%)
    ppermute x2, waiting for transfers between devices, begin(): lax.ppermute(first, ('section', 'seq'), [(place, count + place) for place...  21.9 us
    pallas_call x20, Pallas kernels, call(): pl.pallas_call(body, out_shape=outs, in_specs=specs, out_specs=[pl.BlockS...  13.1 us
    ppermute x12, starting transfers between devices, permute(): lax.ppermute(value, ('section', 'seq'), [(base + source, base + target) f...  11 us
    ppermute x12, waiting for transfers between devices, permute(): lax.ppermute(value, ('section', 'seq'), [(base + source, base + target) f...  2.35 us
    ppermute x2, starting transfers between devices, begin(): lax.ppermute(first, ('section', 'seq'), [(place, count + place) for place...  1.99 us
  transfers between devices with their start and end apart: 14, of which 2 were waited for; matrix products, arithmetic and copies ran while one was open for 0% of the time, Pallas kernels for 22%

profile of v11, /device:TPU:25, one launch (start us, length us, event | category | flops | bytes accessed | tf_op | source)
XLA Modules:
  0.0 51.1 jit_solution(4550390713523739496)
XLA Ops:
  0.0 0.0 copy-start
  0.0 0.1 first_front.1
  0.1 0.8 %collective-permute-start.1 = (bf16[64,2048]{1,0:T(8,128)(2,1)S(1)}, bf16[64,2048]{1,0:T(8,128)(2,1)S(1)}, u32[]{:S(2)}, u32[]{:S(2)}) collective-permute-start(bf16[64,2048]{1,0:T(8,128)(2,1)S(1)} %get-tuple-element.30.refs_0_.own_ref.after_ref), channel_id=1, source_target_pairs={{0,2},{2,0},{1,3},{3,1}} | collective-permute-start | bytes 786440 | tf_op jit(solution)/shard_map/ppermute | solution.py:400
  0.9 0.7 %collective-permute-start = (bf16[64,2048]{1,0:T(8,128)(2,1)S(1)}, bf16[64,2048]{1,0:T(8,128)(2,1)S(1)}, u32[]{:S(2)}, u32[]{:S(2)}) collective-permute-start(bf16[64,2048]{1,0:T(8,128)(2,1)S(1)} %get-tuple-element.30.refs_0_.own_ref.after_ref), channel_id=1, source_target_pairs={{4,6},{6,4},{8,10},{10,8},{12,14},{14,12},{5,7},{7,5},{9,11},{11,9... | collective-permute-start | bytes 786440 | tf_op jit(solution)/shard_map/ppermute | solution.py:400
  1.6 0.0 copy-done
  1.7 0.0 collective-permute-done.1.refs_1_.got_ref
  1.7 0.0 copy-start.1
  1.8 0.8 %collective-permute-start.2 = (bf16[64,1024]{1,0:T(8,128)(2,1)S(1)}, bf16[64,1024]{1,0:T(8,128)(2,1)S(1)}, u32[]{:S(2)}, u32[]{:S(2)}) collective-permute-start(bf16[64,1024]{1,0:T(8,128)(2,1)S(1)} %advance0_0.1.after_ref), channel_id=1, source_target_pairs={{0,4},{2,6},{1,5},{3,7}} | collective-permute-start | bytes 393224 | tf_op jit(solution)/shard_map/ppermute | solution.py:400
  2.6 0.2 copy-done.1
  2.8 0.0 collective-permute-done.got_ref
  2.8 0.0 collective-permute-done.2.refs_1_.state_ref
  2.8 0.7 %collective-permute-start.3 = (bf16[64,1024]{1,0:T(8,128)(2,1)S(1)}, bf16[64,1024]{1,0:T(8,128)(2,1)S(1)}, u32[]{:S(2)}, u32[]{:S(2)}) collective-permute-start(bf16[64,1024]{1,0:T(8,128)(2,1)S(1)} %advance0_1.1.after_ref), channel_id=1, source_target_pairs={{4,8},{6,10},{5,9},{7,11}} | collective-permute-start | bytes 393224 | tf_op jit(solution)/shard_map/ppermute | solution.py:400
  3.5 0.0 collective-permute-done.3.refs_1_.state_ref
  3.6 0.7 %collective-permute-start.4 = (bf16[128,2048]{1,0:T(8,128)(2,1)S(1)}, bf16[128,2048]{1,0:T(8,128)(2,1)S(1)}, u32[]{:S(2)}, u32[]{:S(2)}) collective-permute-start(bf16[128,2048]{1,0:T(8,128)(2,1)S(1)} %first_finish_2.1.refs_12_), channel_id=1, source_target_pairs={{0,16},{2,18},{4,20},{6,22},{8,24},{10,26},{1,17},{3,19},{5,21},{7... | collective-permute-start | bytes 1572872 | tf_op jit(solution)/shard_map/ppermute | solution.py:459
  4.3 0.7 %collective-permute-start.11 = (bf16[64,1024]{1,0:T(8,128)(2,1)S(1)}, bf16[64,1024]{1,0:T(8,128)(2,1)S(1)}, u32[]{:S(2)}, u32[]{:S(2)}) collective-permute-start(bf16[64,1024]{1,0:T(8,128)(2,1)S(1)} %advance0_2.1.after_ref), channel_id=1, source_target_pairs={{8,12},{10,14},{9,13},{11,15}} | collective-permute-start | bytes 393224 | tf_op jit(solution)/shard_map/ppermute | solution.py:400
  5.0 0.0 collective-permute-done.11.state_ref
  5.0 1.3 %collective-permute-start.12 = (bf16[128,2048]{1,0:T(8,128)(2,1)S(1)}, bf16[128,2048]{1,0:T(8,128)(2,1)S(1)}, u32[]{:S(2)}, u32[]{:S(2)}) collective-permute-start(bf16[128,2048]{1,0:T(8,128)(2,1)S(1)} %first_finish_3.1.refs_13_), channel_id=1, source_target_pairs={{12,28},{14,30},{13,29},{15,31}} | collective-permute-start | bytes 1572872 | tf_op jit(solution)/shard_map/ppermute | solution.py:459
  6.3 5.9 %load.1 = (f32[1,2048]{1,0:T(1,128)S(1)}, bf16[1,2048,3072]{2,1,0:T(8,128)(2,1)S(1)}, bf16[1,16,2048]{2,1,0:T(8,128)(2,1)S(1)}, f32[1,16]{1,0:T(1,128)S(1)}, bf16[1,1024,2048]{2,1,0:T(8,128)(2,1)S(1)}) custom-call(f32[1,2048]{1,0:T(1,128)} %refs_0_.2, bf16[1,2048,3072]{2,1,0:T(8,128)(2,1)} %w_hbm.7, bf16[1,16,2048]{2,1,0:T(8,128)(2,1)} %bitcast.9, ...), custom_call_target="tpu_custom_call" | custom-call | tf_op jit(solution)/shard_map/load/pallas_call | solution.py:371
  12.2 0.0 collective-permute-done.4.h_ref.refs_10_
  12.2 0.2 later_front_0.1
  12.4 0.7 %collective-permute-start.5 = (bf16[64,2048]{1,0:T(8,128)(2,1)S(1)}, bf16[64,2048]{1,0:T(8,128)(2,1)S(1)}, u32[]{:S(2)}, u32[]{:S(2)}) collective-permute-start(bf16[64,2048]{1,0:T(8,128)(2,1)S(1)} %get-tuple-element.45.refs_0_.refs_3_), channel_id=1, source_target_pairs={{16,18},{18,16},{17,19},{19,17}} | collective-permute-start | bytes 786440 | tf_op jit(solution)/shard_map/ppermute | solution.py:400
  13.1 0.7 %collective-permute-start.7 = (bf16[64,2048]{1,0:T(8,128)(2,1)S(1)}, bf16[64,2048]{1,0:T(8,128)(2,1)S(1)}, u32[]{:S(2)}, u32[]{:S(2)}) collective-permute-start(bf16[64,2048]{1,0:T(8,128)(2,1)S(1)} %get-tuple-element.45.refs_0_.refs_3_), channel_id=1, source_target_pairs={{20,22},{22,20},{21,23},{23,21}} | collective-permute-start | bytes 786440 | tf_op jit(solution)/shard_map/ppermute | solution.py:400
  13.8 0.0 collective-permute-done.5.refs_1_.refs_4_
  13.9 0.7 %collective-permute-start.6 = (bf16[64,1024]{1,0:T(8,128)(2,1)S(1)}, bf16[64,1024]{1,0:T(8,128)(2,1)S(1)}, u32[]{:S(2)}, u32[]{:S(2)}) collective-permute-start(bf16[64,1024]{1,0:T(8,128)(2,1)S(1)} %advance1_0.1.refs_3_), channel_id=1, source_target_pairs={{16,20},{18,22},{17,21},{19,23}} | collective-permute-start | bytes 393224 | tf_op jit(solution)/shard_map/ppermute | solution.py:400
  14.5 0.7 %collective-permute-start.9 = (bf16[64,2048]{1,0:T(8,128)(2,1)S(1)}, bf16[64,2048]{1,0:T(8,128)(2,1)S(1)}, u32[]{:S(2)}, u32[]{:S(2)}) collective-permute-start(bf16[64,2048]{1,0:T(8,128)(2,1)S(1)} %get-tuple-element.45.refs_0_.refs_3_), channel_id=1, source_target_pairs={{24,26},{26,24},{25,27},{27,25}} | collective-permute-start | bytes 786440 | tf_op jit(solution)/shard_map/ppermute | solution.py:400
  15.2 0.0 collective-permute-done.7.refs_1_.refs_5_
  15.2 0.0 collective-permute-done.6.refs_2_.refs_1_
  15.3 0.7 %collective-permute-start.8 = (bf16[64,1024]{1,0:T(8,128)(2,1)S(1)}, bf16[64,1024]{1,0:T(8,128)(2,1)S(1)}, u32[]{:S(2)}, u32[]{:S(2)}) collective-permute-start(bf16[64,1024]{1,0:T(8,128)(2,1)S(1)} %advance1_1.1.after_ref), channel_id=1, source_target_pairs={{20,24},{22,26},{21,25},{23,27}} | collective-permute-start | bytes 393224 | tf_op jit(solution)/shard_map/ppermute | solution.py:400
  16.0 21.9 %collective-permute-done.12.h_ref.refs_11_ = bf16[128,2048]{1,0:T(8,128)(2,1)S(1)} collective-permute-done((bf16[128,2048]{1,0:T(8,128)(2,1)S(1)}, bf16[128,2048]{1,0:T(8,128)(2,1)S(1)}, u32[]{:S(2)}, u32[]{:S(2)}) %collective-permute-start.12) | collective-permute-done | bytes 524320 | tf_op jit(solution)/shard_map/ppermute | solution.py:459
  37.8 2.7 %later_front_3.1 = (bf16[64,2048]{1,0:T(8,128)(2,1)S(1)}, bf16[128,2048]{1,0:T(8,128)(2,1)S(1)}, bf16[128,1024]{1,0:T(8,128)(2,1)S(1)}, bf16[128,1024]{1,0:T(8,128)(2,1)S(1)}, bf16[128,1024]{1,0:T(8,128)(2,1)S(1)}) custom-call(bf16[128,2048]{1,0:T(8,128)(2,1)S(1)} %collective-permute-done.12.h_ref.refs_11_, f32[1,2048]{1,0:T(1,128)S(1)} %get-tuple-element.41.gain, ...), custom_call_target="tpu_custom_call" | custom-call | tf_op jit(solution)/shard_map/later_front_3/pallas_call | solution.py:371
  40.6 2.8 %collective-permute-start.13 = (bf16[64,2048]{1,0:T(8,128)(2,1)S(1)}, bf16[64,2048]{1,0:T(8,128)(2,1)S(1)}, u32[]{:S(2)}, u32[]{:S(2)}) collective-permute-start(bf16[64,2048]{1,0:T(8,128)(2,1)S(1)} %get-tuple-element.50), channel_id=1, source_target_pairs={{28,30},{30,28},{29,31},{31,29}} | collective-permute-start | bytes 786440 | tf_op jit(solution)/shard_map/ppermute | solution.py:400
  43.4 0.0 collective-permute-done.9.refs_1_.refs_6_
  43.4 0.0 collective-permute-done.8.refs_2_
  43.5 1.3 %collective-permute-start.10 = (bf16[64,1024]{1,0:T(8,128)(2,1)S(1)}, bf16[64,1024]{1,0:T(8,128)(2,1)S(1)}, u32[]{:S(2)}, u32[]{:S(2)}) collective-permute-start(bf16[64,1024]{1,0:T(8,128)(2,1)S(1)} %advance1_2.1.after_ref), channel_id=1, source_target_pairs={{24,28},{26,30},{25,29},{27,31}} | collective-permute-start | bytes 393224 | tf_op jit(solution)/shard_map/ppermute | solution.py:400
  44.8 2.1 %reads1_3.1.refs_9_ = bf16[128,2048]{1,0:T(8,128)(2,1)S(1)} custom-call(bf16[128,2048]{1,0:T(8,128)(2,1)S(1)} %get-tuple-element.51.normed_ref, bf16[128,1024]{1,0:T(8,128)(2,1)S(1)} %get-tuple-element.52.keys_ref, bf16[128,1024]{1,0:T(8,128)(2,1)S(1)} %get-tuple-element.53.x_ref, bf16[128,1024]{1,0:T(8,128)(2,1)S(1)} %get-tuple-element.54.y_ref, ...), custom_call_target="tpu_custom_call" | custom-call | tf_op jit(solution)/shard_map/reads1_3/pallas_call | solution.py:371
  46.8 2.3 %collective-permute-done.10.refs_3_ = bf16[64,1024]{1,0:T(8,128)(2,1)S(1)} collective-permute-done((bf16[64,1024]{1,0:T(8,128)(2,1)S(1)}, bf16[64,1024]{1,0:T(8,128)(2,1)S(1)}, u32[]{:S(2)}, u32[]{:S(2)}) %collective-permute-start.10) | collective-permute-done | bytes 131104 | tf_op jit(solution)/shard_map/ppermute | solution.py:400
  49.2 0.0 collective-permute-done.13.refs_7_
  49.2 1.7 %last_finish.1 = bf16[1,128,2048]{2,1,0:T(8,128)(2,1)} custom-call(bf16[1024,2048]{1,0:T(8,128)(2,1)S(1)} %bitcast.7, f32[1,16,64,64]{3,2,1,0:T(8,128)S(1)} %copy-done, bf16[64,1024]{1,0:T(8,128)(2,1)S(1)} %collective-permute-done.6.refs_2_.refs_1_, bf16[64,1024]{1,0:T(8,128)(2,1)S(1)} %collective-permute-done.8.refs_2_, ...), custom_call_target="tpu_custom_call" | custom-call | tf_op jit(solution)/shard_map/last_finish/pallas_call | solution.py:371
  (14 shorter events, 0.4 us)
Async XLA Ops:
  0.0 1.6 %copy-start = (f32[1,16,64,64]{3,2,1,0:T(8,128)S(1)}, f32[1,16,64,64]{3,2,1,0:T(8,128)}, u32[]{:S(2)}) copy-start(f32[1,16,64,64]{3,2,1,0:T(8,128)} %refs_0_.3) | copy-start | bytes 786436
  0.1 1.6 %collective-permute-start.1 = (bf16[64,2048]{1,0:T(8,128)(2,1)S(1)}, bf16[64,2048]{1,0:T(8,128)(2,1)S(1)}, u32[]{:S(2)}, u32[]{:S(2)}) collective-permute-start(bf16[64,2048]{1,0:T(8,128)(2,1)S(1)} %get-tuple-element.30.refs_0_.own_ref.after_ref), channel_id=1, source_target_pairs={{0,2},{2,0},{1,3},{3,1}} | collective-permute-start | bytes 786440 | tf_op jit(solution)/shard_map/ppermute | solution.py:400
  0.9 1.8 %collective-permute-start = (bf16[64,2048]{1,0:T(8,128)(2,1)S(1)}, bf16[64,2048]{1,0:T(8,128)(2,1)S(1)}, u32[]{:S(2)}, u32[]{:S(2)}) collective-permute-start(bf16[64,2048]{1,0:T(8,128)(2,1)S(1)} %get-tuple-element.30.refs_0_.own_ref.after_ref), channel_id=1, source_target_pairs={{4,6},{6,4},{8,10},{10,8},{12,14},{14,12},{5,7},{7,5},{9,11},{11,9... | collective-permute-start | bytes 786440 | tf_op jit(solution)/shard_map/ppermute | solution.py:400
  1.7 1.0 %copy-start.1 = (bf16[128,2048]{1,0:T(8,128)(2,1)S(1)}, bf16[128,2048]{1,0:T(8,128)(2,1)}, u32[]{:S(2)}) copy-start(bf16[128,2048]{1,0:T(8,128)(2,1)} %h_ref.7) | copy-start | bytes 1572868
  1.8 1.0 %collective-permute-start.2 = (bf16[64,1024]{1,0:T(8,128)(2,1)S(1)}, bf16[64,1024]{1,0:T(8,128)(2,1)S(1)}, u32[]{:S(2)}, u32[]{:S(2)}) collective-permute-start(bf16[64,1024]{1,0:T(8,128)(2,1)S(1)} %advance0_0.1.after_ref), channel_id=1, source_target_pairs={{0,4},{2,6},{1,5},{3,7}} | collective-permute-start | bytes 393224 | tf_op jit(solution)/shard_map/ppermute | solution.py:400
  2.8 0.7 %collective-permute-start.3 = (bf16[64,1024]{1,0:T(8,128)(2,1)S(1)}, bf16[64,1024]{1,0:T(8,128)(2,1)S(1)}, u32[]{:S(2)}, u32[]{:S(2)}) collective-permute-start(bf16[64,1024]{1,0:T(8,128)(2,1)S(1)} %advance0_1.1.after_ref), channel_id=1, source_target_pairs={{4,8},{6,10},{5,9},{7,11}} | collective-permute-start | bytes 393224 | tf_op jit(solution)/shard_map/ppermute | solution.py:400
  3.6 8.6 %collective-permute-start.4 = (bf16[128,2048]{1,0:T(8,128)(2,1)S(1)}, bf16[128,2048]{1,0:T(8,128)(2,1)S(1)}, u32[]{:S(2)}, u32[]{:S(2)}) collective-permute-start(bf16[128,2048]{1,0:T(8,128)(2,1)S(1)} %first_finish_2.1.refs_12_), channel_id=1, source_target_pairs={{0,16},{2,18},{4,20},{6,22},{8,24},{10,26},{1,17},{3,19},{5,21},{7... | collective-permute-start | bytes 1572872 | tf_op jit(solution)/shard_map/ppermute | solution.py:459
  4.3 0.7 %collective-permute-start.11 = (bf16[64,1024]{1,0:T(8,128)(2,1)S(1)}, bf16[64,1024]{1,0:T(8,128)(2,1)S(1)}, u32[]{:S(2)}, u32[]{:S(2)}) collective-permute-start(bf16[64,1024]{1,0:T(8,128)(2,1)S(1)} %advance0_2.1.after_ref), channel_id=1, source_target_pairs={{8,12},{10,14},{9,13},{11,15}} | collective-permute-start | bytes 393224 | tf_op jit(solution)/shard_map/ppermute | solution.py:400
  5.0 32.8 %collective-permute-start.12 = (bf16[128,2048]{1,0:T(8,128)(2,1)S(1)}, bf16[128,2048]{1,0:T(8,128)(2,1)S(1)}, u32[]{:S(2)}, u32[]{:S(2)}) collective-permute-start(bf16[128,2048]{1,0:T(8,128)(2,1)S(1)} %first_finish_3.1.refs_13_), channel_id=1, source_target_pairs={{12,28},{14,30},{13,29},{15,31}} | collective-permute-start | bytes 1572872 | tf_op jit(solution)/shard_map/ppermute | solution.py:459
  12.4 1.4 %collective-permute-start.5 = (bf16[64,2048]{1,0:T(8,128)(2,1)S(1)}, bf16[64,2048]{1,0:T(8,128)(2,1)S(1)}, u32[]{:S(2)}, u32[]{:S(2)}) collective-permute-start(bf16[64,2048]{1,0:T(8,128)(2,1)S(1)} %get-tuple-element.45.refs_0_.refs_3_), channel_id=1, source_target_pairs={{16,18},{18,16},{17,19},{19,17}} | collective-permute-start | bytes 786440 | tf_op jit(solution)/shard_map/ppermute | solution.py:400
  13.1 2.1 %collective-permute-start.7 = (bf16[64,2048]{1,0:T(8,128)(2,1)S(1)}, bf16[64,2048]{1,0:T(8,128)(2,1)S(1)}, u32[]{:S(2)}, u32[]{:S(2)}) collective-permute-start(bf16[64,2048]{1,0:T(8,128)(2,1)S(1)} %get-tuple-element.45.refs_0_.refs_3_), channel_id=1, source_target_pairs={{20,22},{22,20},{21,23},{23,21}} | collective-permute-start | bytes 786440 | tf_op jit(solution)/shard_map/ppermute | solution.py:400
  13.9 1.4 %collective-permute-start.6 = (bf16[64,1024]{1,0:T(8,128)(2,1)S(1)}, bf16[64,1024]{1,0:T(8,128)(2,1)S(1)}, u32[]{:S(2)}, u32[]{:S(2)}) collective-permute-start(bf16[64,1024]{1,0:T(8,128)(2,1)S(1)} %advance1_0.1.refs_3_), channel_id=1, source_target_pairs={{16,20},{18,22},{17,21},{19,23}} | collective-permute-start | bytes 393224 | tf_op jit(solution)/shard_map/ppermute | solution.py:400
  14.5 28.9 %collective-permute-start.9 = (bf16[64,2048]{1,0:T(8,128)(2,1)S(1)}, bf16[64,2048]{1,0:T(8,128)(2,1)S(1)}, u32[]{:S(2)}, u32[]{:S(2)}) collective-permute-start(bf16[64,2048]{1,0:T(8,128)(2,1)S(1)} %get-tuple-element.45.refs_0_.refs_3_), channel_id=1, source_target_pairs={{24,26},{26,24},{25,27},{27,25}} | collective-permute-start | bytes 786440 | tf_op jit(solution)/shard_map/ppermute | solution.py:400
  15.3 28.1 %collective-permute-start.8 = (bf16[64,1024]{1,0:T(8,128)(2,1)S(1)}, bf16[64,1024]{1,0:T(8,128)(2,1)S(1)}, u32[]{:S(2)}, u32[]{:S(2)}) collective-permute-start(bf16[64,1024]{1,0:T(8,128)(2,1)S(1)} %advance1_1.1.after_ref), channel_id=1, source_target_pairs={{20,24},{22,26},{21,25},{23,27}} | collective-permute-start | bytes 393224 | tf_op jit(solution)/shard_map/ppermute | solution.py:400
  40.6 8.6 %collective-permute-start.13 = (bf16[64,2048]{1,0:T(8,128)(2,1)S(1)}, bf16[64,2048]{1,0:T(8,128)(2,1)S(1)}, u32[]{:S(2)}, u32[]{:S(2)}) collective-permute-start(bf16[64,2048]{1,0:T(8,128)(2,1)S(1)} %get-tuple-element.50), channel_id=1, source_target_pairs={{28,30},{30,28},{29,31},{31,29}} | collective-permute-start | bytes 786440 | tf_op jit(solution)/shard_map/ppermute | solution.py:400
  43.5 5.7 %collective-permute-start.10 = (bf16[64,1024]{1,0:T(8,128)(2,1)S(1)}, bf16[64,1024]{1,0:T(8,128)(2,1)S(1)}, u32[]{:S(2)}, u32[]{:S(2)}) collective-permute-start(bf16[64,1024]{1,0:T(8,128)(2,1)S(1)} %advance1_2.1.after_ref), channel_id=1, source_target_pairs={{24,28},{26,30},{25,29},{27,31}} | collective-permute-start | bytes 393224 | tf_op jit(solution)/shard_map/ppermute | solution.py:400

commit v12 on v11

--- a/solution.py
+++ b/solution.py
@@ -125,19 +125,16 @@
             start_all(small)
             start_all(groups[0])
             wait_all(small)
-            start_all(groups[1])
+            for group in groups[1:]:
+                start_all(group)
         normed = norm_rows(h_in[...], gain[...])
         normed_out[...] = normed
-        if groups:
-            start_all(groups[2])
         rates = spread_rates(normed, w_rate[0], base[...])
         ones = head_ones()
 
         def project(quad):
             if groups:
                 wait_all(groups[quad])
-                if quad + 3 < quads:
-                    start_all(groups[quad + 3])
                 if quad + 1 == quads:
                     start_all(last)
             key_lane = base_lane + quad * QUAD
@@ -175,22 +172,12 @@
                 maps[:, start : start + PAIR] = diagonal(both[:, :PAIR]).astype(BF16)
                 maps[:, width + start : width + start + PAIR] = diagonal(both[:, PAIR:]).astype(BF16)
 
-        def stages(picked, projected):
-            units = [unit(quad, *projected[quad]) for quad in picked]
-            crosses = [crossed(quad, *value) for quad, value in zip(picked, units)]
-            fixes = [fixed(quad, cross, *value) for quad, cross, value in zip(picked, crosses, units)]
-            for quad, value, fix in zip(picked, units, fixes):
-                mapped(quad, value[0], *fix)
-
-        if groups:
-            projected = {0: project(0)}
-            for quad in range(1, quads):
-                projected[quad] = project(quad)
-                if quad + 1 < quads:
-                    stages([quad - 1], projected)
-            stages([quads - 2, quads - 1], projected)
-        else:
-            stages(range(quads), [project(quad) for quad in range(quads)])
+        picked = range(quads)
+        units = [unit(quad, *value) for quad, value in zip(picked, [project(quad) for quad in picked])]
+        crosses = [crossed(quad, *value) for quad, value in zip(picked, units)]
+        fixes = [fixed(quad, cross, *value) for quad, cross, value in zip(picked, crosses, units)]
+        for quad, value, fix in zip(picked, units, fixes):
+            mapped(quad, value[0], *fix)
         wait_all(last)
 
     pl.when(here)(body)
@@ -225,7 +212,7 @@
     def body():
         late = [pltpu.make_async_copy(w_hbm.at[0, :, pl.ds(half, half)], wq, sems.at[0])] * fetches
         fetch = [pltpu.make_async_copy(w_out_hbm.at[0], target, sems.at[1]) for target in w_out]
-        start_all(late)
+        start_all(late + fetch)
         normed = normed_ref[...]
         ones = head_ones()
         row = lax.broadcasted_iota(jnp.int32, (rows, 2 * rows), 0)
@@ -247,7 +234,6 @@
         if fetches:
             stages(0, half, weights, 0)
             wait_all(late)
-            start_all(fetch)
             stages(half, width, wq, half)
             wait_all(fetch)
         else:
@@ -282,28 +268,60 @@
     return state - step + ref[:, width + start : width + start + PAIR].astype(F32)
 
 
+def moved_states(state_of, refs, width):
+    starts = range(0, width, PAIR)
+    states = [state_of(start) for start in starts]
+    for ref in refs:
+        states = [apply_map(state, ref, start, width) for state, start in zip(states, starts)]
+    return states
+
+
+def put_states(out_ref, states):
+    for index, state in enumerate(states):
+        out_ref[:, index * PAIR : (index + 1) * PAIR] = state.astype(BF16)
+
+
 def advance(active, place, own_ref, got_ref, state_ref, after_ref, out_ref):
     width = out_ref.shape[1]
 
     def body(refs):
-        starts = range(0, width, PAIR)
-        states = [state_ref[:, start : start + PAIR].astype(F32) if place else pair_state(state_ref, start // PAIR) for start in starts]
-        for ref in refs:
-            states = [apply_map(state, ref, start, width) for state, start in zip(states, starts)]
-        for state, start in zip(states, starts):
-            out_ref[:, start : start + PAIR] = state.astype(BF16)
-
-    index = lax.axis_index("seq")
-    here = (lax.axis_index("section") == active) & (index // 2 == place)
+        def state_of(start):
+            return state_ref[:, start : start + PAIR].astype(F32) if place else pair_state(state_ref, start // PAIR)
+
+        put_states(out_ref, moved_states(state_of, refs, width))
+
+    here = at_pair([place], active)
     if got_ref is None:
         pl.when(here)(lambda: body((own_ref,)))
     else:
-        side = lax.rem(index, 2)
+        side = lax.rem(lax.axis_index("seq"), 2)
         pl.when(here & (side == 0))(lambda: body((own_ref, got_ref)))
         pl.when(here & (side == 1))(lambda: body((got_ref, own_ref)))
 
 
-def finish(here, begins, state_ref, got_ref, reads_ref, w_out_ref, h_ref, store):
+def first_step(own_ref, init_ref, out_ref):
+    width = out_ref.shape[1]
+
+    @pl.when((lax.axis_index("section") == 0) & (lax.axis_index("seq") == 0))
+    def _():
+        put_states(out_ref, moved_states(lambda start: pair_state(init_ref, start // PAIR), (own_ref,), width))
+
+
+def first_advance(own_ref, got_ref, init_ref, state_ref, after_ref, out_ref):
+    width = out_ref.shape[1]
+    here = at_pair([0], 0)
+    side = lax.rem(lax.axis_index("seq"), 2)
+
+    @pl.when(here & (side == 0))
+    def _():
+        put_states(out_ref, moved_states(lambda start: pair_state(init_ref, start // PAIR), (own_ref, got_ref), width))
+
+    @pl.when(here & (side == 1))
+    def _():
+        put_states(out_ref, moved_states(lambda start: state_ref[:, start : start + PAIR].astype(F32), (own_ref,), width))
+
+
+def finish(here, begins, state_ref, got_ref, reads_ref, w_out_ref, h_ref, store, followed=None):
     width = w_out_ref.shape[0]
     model = h_ref.shape[1]
     chunk = model // 4
@@ -312,7 +330,10 @@
         follows = lax.rem(lax.axis_index("seq"), 2) == 1
         starts = range(0, width, PAIR)
         states = [pair_state(state_ref, start // PAIR) if begins else state_ref[:, start : start + PAIR].astype(F32) for start in starts]
-        moved = [apply_map(state, got_ref, start, width) for state, start in zip(states, starts)]
+        if followed is None:
+            moved = [apply_map(state, got_ref, start, width) for state, start in zip(states, starts)]
+        else:
+            moved = [followed[:, start : start + PAIR].astype(F32) for start in starts]
         states = [jnp.where(follows, after, state).astype(BF16) for after, state in zip(moved, states)]
         quads = range(0, width, QUAD)
         spreads = [spread(jnp.concatenate(states[start // PAIR : (start + QUAD) // PAIR], axis=1)) for start in quads]
@@ -337,7 +358,8 @@
     def store(start, value):
         out_ref[:, start : start + value.shape[1]] = value
 
-    finish(at_pair([place], 0), place == 0, state_ref, got_ref, reads_ref, w_out_ref, h_ref, store)
+    followed = None if place else got_ref
+    finish(at_pair([place], 0), place == 0, state_ref, got_ref, reads_ref, w_out_ref, h_ref, store, followed)
 
 
 def last_finish(count, w_out_ref, *refs):
@@ -433,10 +455,21 @@
         name="first_front",
     )
     wq_near = in_vmem(wq_near)
-    got_first = swap(own, 0, [0])
+    state_out = shape((HD, width), BF16)
+    got_first = permute(own, 0, [(1, 0)])
+    (stepped,) = call(first_step, [state_out], [], [own, init_state], name="first_step")
+    stepped = permute(stepped, 0, [(0, 1)])
     got_rest = swap(own, 0, range(1, groups))
     read_first = layer_reads(0, [0], 1, rows_of, wq_near, init_state)
-    ahead, state = hop(0, 0, [own, got_first], init_state, read_first[0])
+    (ahead,) = call(
+        first_advance,
+        [state_out],
+        [],
+        [own, got_first, init_state, stepped, read_first[0]],
+        [pltpu.VMEM] * 4 + [pl.ANY],
+        name="first_advance",
+    )
+    state = permute(ahead, 0, [(side, 2 + side) for side in range(2)])
     read_rest = layer_reads(0, range(1, groups), 1, rows_of, wq_near, ahead)
     (both,) = call(
         functools.partial(compose, 0), [maps], [], [own, got_rest, read_rest[0]], [pltpu.VMEM] * 2 + [pl.ANY], name="compose"
@@ -469,7 +502,7 @@
 
     here, passed = init_state, []
     for place in range(groups):
-        got, (reads, near) = (got_rest, read_rest) if place else (got_first, read_first)
+        got, (reads, near) = (got_rest, read_rest) if place else (stepped, read_first)
         if 0 < place < groups - 1:
             ahead, state = hop(0, place, [both], here, passed[0])
         if place + 1 == groups:

time: 51.4 us -> 51.1 us (level)
  the two profiles are of different devices: /device:TPU:25 before, /device:TPU:31 now
where the time goes in v12:
time: 51.1 us; the launch traced here: 50.8 us
  waiting for transfers between devices  22.7 us (44%)
  starting transfers between devices  14.1 us (28%)
  Pallas kernels  13.1 us (26%)
    ppermute x2, waiting for transfers between devices, begin(): lax.ppermute(first, ('section', 'seq'), [(place, count + place) for place...  20.4 us
    pallas_call x21, Pallas kernels, call(): pl.pallas_call(body, out_shape=outs, in_specs=specs, out_specs=[pl.BlockS...  13.1 us
    ppermute x13, starting transfers between devices, permute(): lax.ppermute(value, ('section', 'seq'), [(base + source, base + target) f...  12.2 us
    ppermute x13, waiting for transfers between devices, permute(): lax.ppermute(value, ('section', 'seq'), [(base + source, base + target) f...  2.35 us
    ppermute x2, starting transfers between devices, begin(): lax.ppermute(first, ('section', 'seq'), [(place, count + place) for place...  1.99 us
  transfers between devices with their start and end apart: 15, of which 2 were waited for; matrix products, arithmetic and copies ran while one was open for 0% of the time, Pallas kernels for 22%

profile of v12, /device:TPU:31, one launch (start us, length us, event | category | flops | bytes accessed | tf_op | source)
XLA Modules:
  0.0 50.8 jit_solution(9985612929921407142)
XLA Ops:
  0.0 0.0 copy-start
  0.0 0.1 first_front.1
  0.1 0.8 %collective-permute-start.1 = (bf16[64,2048]{1,0:T(8,128)(2,1)S(1)}, bf16[64,2048]{1,0:T(8,128)(2,1)S(1)}, u32[]{:S(2)}, u32[]{:S(2)}) collective-permute-start(bf16[64,2048]{1,0:T(8,128)(2,1)S(1)} %get-tuple-element.30.own_ref.after_ref), channel_id=1, source_target_pairs={{2,0},{3,1}} | collective-permute-start | bytes 786440 | tf_op jit(solution)/shard_map/ppermute | solution.py:422
  0.9 0.1 copy-done
  1.0 0.7 %collective-permute-start.2 = (bf16[64,1024]{1,0:T(8,128)(2,1)S(1)}, bf16[64,1024]{1,0:T(8,128)(2,1)S(1)}, u32[]{:S(2)}, u32[]{:S(2)}) collective-permute-start(bf16[64,1024]{1,0:T(8,128)(2,1)S(1)} %first_step.1), channel_id=1, source_target_pairs={{0,2},{1,3}} | collective-permute-start | bytes 393224 | tf_op jit(solution)/shard_map/ppermute | solution.py:422
  1.7 0.7 %collective-permute-start = (bf16[64,2048]{1,0:T(8,128)(2,1)S(1)}, bf16[64,2048]{1,0:T(8,128)(2,1)S(1)}, u32[]{:S(2)}, u32[]{:S(2)}) collective-permute-start(bf16[64,2048]{1,0:T(8,128)(2,1)S(1)} %get-tuple-element.30.own_ref.after_ref), channel_id=1, source_target_pairs={{4,6},{6,4},{8,10},{10,8},{12,14},{14,12},{5,7},{7,5},{9,11},{11,9... | collective-permute-start | bytes 786440 | tf_op jit(solution)/shard_map/ppermute | solution.py:422
  2.4 0.0 collective-permute-done.2.state_ref.got_ref
  2.5 0.0 collective-permute-done.1.got_ref
  2.5 0.0 copy-start.1
  2.5 0.8 %collective-permute-start.3 = (bf16[64,1024]{1,0:T(8,128)(2,1)S(1)}, bf16[64,1024]{1,0:T(8,128)(2,1)S(1)}, u32[]{:S(2)}, u32[]{:S(2)}) collective-permute-start(bf16[64,1024]{1,0:T(8,128)(2,1)S(1)} %first_advance.1.after_ref), channel_id=1, source_target_pairs={{0,4},{2,6},{1,5},{3,7}} | collective-permute-start | bytes 393224 | tf_op jit(solution)/shard_map/ppermute | solution.py:422
  3.4 0.2 copy-done.1
  3.6 0.0 collective-permute-done.got_ref
  3.6 0.0 collective-permute-done.3.refs_1_.state_ref
  3.6 0.7 %collective-permute-start.4 = (bf16[64,1024]{1,0:T(8,128)(2,1)S(1)}, bf16[64,1024]{1,0:T(8,128)(2,1)S(1)}, u32[]{:S(2)}, u32[]{:S(2)}) collective-permute-start(bf16[64,1024]{1,0:T(8,128)(2,1)S(1)} %advance0_1.1.after_ref), channel_id=1, source_target_pairs={{4,8},{6,10},{5,9},{7,11}} | collective-permute-start | bytes 393224 | tf_op jit(solution)/shard_map/ppermute | solution.py:422
  4.3 0.0 collective-permute-done.4.refs_1_.state_ref
  4.4 0.7 %collective-permute-start.5 = (bf16[128,2048]{1,0:T(8,128)(2,1)S(1)}, bf16[128,2048]{1,0:T(8,128)(2,1)S(1)}, u32[]{:S(2)}, u32[]{:S(2)}) collective-permute-start(bf16[128,2048]{1,0:T(8,128)(2,1)S(1)} %first_finish_2.1.refs_12_), channel_id=1, source_target_pairs={{0,16},{2,18},{4,20},{6,22},{8,24},{10,26},{1,17},{3,19},{5,21},{7... | collective-permute-start | bytes 1572872 | tf_op jit(solution)/shard_map/ppermute | solution.py:492
  5.1 0.7 %collective-permute-start.12 = (bf16[64,1024]{1,0:T(8,128)(2,1)S(1)}, bf16[64,1024]{1,0:T(8,128)(2,1)S(1)}, u32[]{:S(2)}, u32[]{:S(2)}) collective-permute-start(bf16[64,1024]{1,0:T(8,128)(2,1)S(1)} %advance0_2.1.after_ref), channel_id=1, source_target_pairs={{8,12},{10,14},{9,13},{11,15}} | collective-permute-start | bytes 393224 | tf_op jit(solution)/shard_map/ppermute | solution.py:422
  5.8 0.0 collective-permute-done.12.state_ref
  5.8 1.3 %collective-permute-start.13 = (bf16[128,2048]{1,0:T(8,128)(2,1)S(1)}, bf16[128,2048]{1,0:T(8,128)(2,1)S(1)}, u32[]{:S(2)}, u32[]{:S(2)}) collective-permute-start(bf16[128,2048]{1,0:T(8,128)(2,1)S(1)} %first_finish_3.1.refs_13_), channel_id=1, source_target_pairs={{12,28},{14,30},{13,29},{15,31}} | collective-permute-start | bytes 1572872 | tf_op jit(solution)/shard_map/ppermute | solution.py:492
  7.1 5.9 %load.1 = (f32[1,2048]{1,0:T(1,128)S(1)}, bf16[1,2048,3072]{2,1,0:T(8,128)(2,1)S(1)}, bf16[1,16,2048]{2,1,0:T(8,128)(2,1)S(1)}, f32[1,16]{1,0:T(1,128)S(1)}, bf16[1,1024,2048]{2,1,0:T(8,128)(2,1)S(1)}) custom-call(f32[1,2048]{1,0:T(1,128)} %refs_0_.2, bf16[1,2048,3072]{2,1,0:T(8,128)(2,1)} %w_hbm.7, bf16[1,16,2048]{2,1,0:T(8,128)(2,1)} %bitcast.9, ...), custom_call_target="tpu_custom_call" | custom-call | tf_op jit(solution)/shard_map/load/pallas_call | solution.py:393
  13.0 0.0 collective-permute-done.5.h_ref.refs_10_
  13.0 0.2 later_front_0.1
  13.2 0.7 %collective-permute-start.6 = (bf16[64,2048]{1,0:T(8,128)(2,1)S(1)}, bf16[64,2048]{1,0:T(8,128)(2,1)S(1)}, u32[]{:S(2)}, u32[]{:S(2)}) collective-permute-start(bf16[64,2048]{1,0:T(8,128)(2,1)S(1)} %get-tuple-element.45.refs_0_.refs_3_), channel_id=1, source_target_pairs={{16,18},{18,16},{17,19},{19,17}} | collective-permute-start | bytes 786440 | tf_op jit(solution)/shard_map/ppermute | solution.py:422
  13.9 0.7 %collective-permute-start.8 = (bf16[64,2048]{1,0:T(8,128)(2,1)S(1)}, bf16[64,2048]{1,0:T(8,128)(2,1)S(1)}, u32[]{:S(2)}, u32[]{:S(2)}) collective-permute-start(bf16[64,2048]{1,0:T(8,128)(2,1)S(1)} %get-tuple-element.45.refs_0_.refs_3_), channel_id=1, source_target_pairs={{20,22},{22,20},{21,23},{23,21}} | collective-permute-start | bytes 786440 | tf_op jit(solution)/shard_map/ppermute | solution.py:422
  14.6 0.0 collective-permute-done.6.refs_1_.refs_4_
  14.6 0.7 %collective-permute-start.7 = (bf16[64,1024]{1,0:T(8,128)(2,1)S(1)}, bf16[64,1024]{1,0:T(8,128)(2,1)S(1)}, u32[]{:S(2)}, u32[]{:S(2)}) collective-permute-start(bf16[64,1024]{1,0:T(8,128)(2,1)S(1)} %advance1_0.1.refs_3_), channel_id=1, source_target_pairs={{16,20},{18,22},{17,21},{19,23}} | collective-permute-start | bytes 393224 | tf_op jit(solution)/shard_map/ppermute | solution.py:422
  15.3 0.7 %collective-permute-start.10 = (bf16[64,2048]{1,0:T(8,128)(2,1)S(1)}, bf16[64,2048]{1,0:T(8,128)(2,1)S(1)}, u32[]{:S(2)}, u32[]{:S(2)}) collective-permute-start(bf16[64,2048]{1,0:T(8,128)(2,1)S(1)} %get-tuple-element.45.refs_0_.refs_3_), channel_id=1, source_target_pairs={{24,26},{26,24},{25,27},{27,25}} | collective-permute-start | bytes 786440 | tf_op jit(solution)/shard_map/ppermute | solution.py:422
  16.0 0.0 collective-permute-done.8.refs_1_.refs_5_
  16.0 0.0 collective-permute-done.7.refs_2_.refs_1_
  16.1 0.7 %collective-permute-start.9 = (bf16[64,1024]{1,0:T(8,128)(2,1)S(1)}, bf16[64,1024]{1,0:T(8,128)(2,1)S(1)}, u32[]{:S(2)}, u32[]{:S(2)}) collective-permute-start(bf16[64,1024]{1,0:T(8,128)(2,1)S(1)} %advance1_1.1.after_ref), channel_id=1, source_target_pairs={{20,24},{22,26},{21,25},{23,27}} | collective-permute-start | bytes 393224 | tf_op jit(solution)/shard_map/ppermute | solution.py:422
  16.7 20.4 %collective-permute-done.13.h_ref.refs_11_ = bf16[128,2048]{1,0:T(8,128)(2,1)S(1)} collective-permute-done((bf16[128,2048]{1,0:T(8,128)(2,1)S(1)}, bf16[128,2048]{1,0:T(8,128)(2,1)S(1)}, u32[]{:S(2)}, u32[]{:S(2)}) %collective-permute-start.13) | collective-permute-done | bytes 524320 | tf_op jit(solution)/shard_map/ppermute | solution.py:492
  37.1 2.7 %later_front_3.1 = (bf16[64,2048]{1,0:T(8,128)(2,1)S(1)}, bf16[128,2048]{1,0:T(8,128)(2,1)S(1)}, bf16[128,1024]{1,0:T(8,128)(2,1)S(1)}, bf16[128,1024]{1,0:T(8,128)(2,1)S(1)}, bf16[128,1024]{1,0:T(8,128)(2,1)S(1)}) custom-call(bf16[128,2048]{1,0:T(8,128)(2,1)S(1)} %collective-permute-done.13.h_ref.refs_11_, f32[1,2048]{1,0:T(1,128)S(1)} %get-tuple-element.41.gain, ...), custom_call_target="tpu_custom_call" | custom-call | tf_op jit(solution)/shard_map/later_front_3/pallas_call | solution.py:393
  39.8 3.2 %collective-permute-start.14 = (bf16[64,2048]{1,0:T(8,128)(2,1)S(1)}, bf16[64,2048]{1,0:T(8,128)(2,1)S(1)}, u32[]{:S(2)}, u32[]{:S(2)}) collective-permute-start(bf16[64,2048]{1,0:T(8,128)(2,1)S(1)} %get-tuple-element.50), channel_id=1, source_target_pairs={{28,30},{30,28},{29,31},{31,29}} | collective-permute-start | bytes 786440 | tf_op jit(solution)/shard_map/ppermute | solution.py:422
  43.1 0.0 collective-permute-done.10.refs_1_.refs_6_
  43.1 0.0 collective-permute-done.9.refs_2_
  43.2 1.3 %collective-permute-start.11 = (bf16[64,1024]{1,0:T(8,128)(2,1)S(1)}, bf16[64,1024]{1,0:T(8,128)(2,1)S(1)}, u32[]{:S(2)}, u32[]{:S(2)}) collective-permute-start(bf16[64,1024]{1,0:T(8,128)(2,1)S(1)} %advance1_2.1.after_ref), channel_id=1, source_target_pairs={{24,28},{26,30},{25,29},{27,31}} | collective-permute-start | bytes 393224 | tf_op jit(solution)/shard_map/ppermute | solution.py:422
  44.5 2.1 %reads1_3.1.refs_9_ = bf16[128,2048]{1,0:T(8,128)(2,1)S(1)} custom-call(bf16[128,2048]{1,0:T(8,128)(2,1)S(1)} %get-tuple-element.51.normed_ref, bf16[128,1024]{1,0:T(8,128)(2,1)S(1)} %get-tuple-element.52.keys_ref, bf16[128,1024]{1,0:T(8,128)(2,1)S(1)} %get-tuple-element.53.x_ref, bf16[128,1024]{1,0:T(8,128)(2,1)S(1)} %get-tuple-element.54.y_ref, ...), custom_call_target="tpu_custom_call" | custom-call | tf_op jit(solution)/shard_map/reads1_3/pallas_call | solution.py:393
  46.6 2.3 %collective-permute-done.11.refs_3_ = bf16[64,1024]{1,0:T(8,128)(2,1)S(1)} collective-permute-done((bf16[64,1024]{1,0:T(8,128)(2,1)S(1)}, bf16[64,1024]{1,0:T(8,128)(2,1)S(1)}, u32[]{:S(2)}, u32[]{:S(2)}) %collective-permute-start.11) | collective-permute-done | bytes 131104 | tf_op jit(solution)/shard_map/ppermute | solution.py:422
  48.9 0.0 collective-permute-done.14.refs_7_
  48.9 1.7 %last_finish.1 = bf16[1,128,2048]{2,1,0:T(8,128)(2,1)} custom-call(bf16[1024,2048]{1,0:T(8,128)(2,1)S(1)} %bitcast.7, f32[1,16,64,64]{3,2,1,0:T(8,128)S(1)} %copy-done, bf16[64,1024]{1,0:T(8,128)(2,1)S(1)} %collective-permute-done.7.refs_2_.refs_1_, bf16[64,1024]{1,0:T(8,128)(2,1)S(1)} %collective-permute-done.9.refs_2_, ...), custom_call_target="tpu_custom_call" | custom-call | tf_op jit(solution)/shard_map/last_finish/pallas_call | solution.py:393
  (15 shorter events, 0.4 us)
Async XLA Ops:
  0.0 1.0 %copy-start = (f32[1,16,64,64]{3,2,1,0:T(8,128)S(1)}, f32[1,16,64,64]{3,2,1,0:T(8,128)}, u32[]{:S(2)}) copy-start(f32[1,16,64,64]{3,2,1,0:T(8,128)} %refs_0_.3) | copy-start | bytes 786436
  0.1 2.3 %collective-permute-start.1 = (bf16[64,2048]{1,0:T(8,128)(2,1)S(1)}, bf16[64,2048]{1,0:T(8,128)(2,1)S(1)}, u32[]{:S(2)}, u32[]{:S(2)}) collective-permute-start(bf16[64,2048]{1,0:T(8,128)(2,1)S(1)} %get-tuple-element.30.own_ref.after_ref), channel_id=1, source_target_pairs={{2,0},{3,1}} | collective-permute-start | bytes 786440 | tf_op jit(solution)/shard_map/ppermute | solution.py:422
  1.0 1.4 %collective-permute-start.2 = (bf16[64,1024]{1,0:T(8,128)(2,1)S(1)}, bf16[64,1024]{1,0:T(8,128)(2,1)S(1)}, u32[]{:S(2)}, u32[]{:S(2)}) collective-permute-start(bf16[64,1024]{1,0:T(8,128)(2,1)S(1)} %first_step.1), channel_id=1, source_target_pairs={{0,2},{1,3}} | collective-permute-start | bytes 393224 | tf_op jit(solution)/shard_map/ppermute | solution.py:422
  1.7 1.8 %collective-permute-start = (bf16[64,2048]{1,0:T(8,128)(2,1)S(1)}, bf16[64,2048]{1,0:T(8,128)(2,1)S(1)}, u32[]{:S(2)}, u32[]{:S(2)}) collective-permute-start(bf16[64,2048]{1,0:T(8,128)(2,1)S(1)} %get-tuple-element.30.own_ref.after_ref), channel_id=1, source_target_pairs={{4,6},{6,4},{8,10},{10,8},{12,14},{14,12},{5,7},{7,5},{9,11},{11,9... | collective-permute-start | bytes 786440 | tf_op jit(solution)/shard_map/ppermute | solution.py:422
  2.5 1.0 %copy-start.1 = (bf16[128,2048]{1,0:T(8,128)(2,1)S(1)}, bf16[128,2048]{1,0:T(8,128)(2,1)}, u32[]{:S(2)}) copy-start(bf16[128,2048]{1,0:T(8,128)(2,1)} %h_ref.7) | copy-start | bytes 1572868
  2.5 1.0 %collective-permute-start.3 = (bf16[64,1024]{1,0:T(8,128)(2,1)S(1)}, bf16[64,1024]{1,0:T(8,128)(2,1)S(1)}, u32[]{:S(2)}, u32[]{:S(2)}) collective-permute-start(bf16[64,1024]{1,0:T(8,128)(2,1)S(1)} %first_advance.1.after_ref), channel_id=1, source_target_pairs={{0,4},{2,6},{1,5},{3,7}} | collective-permute-start | bytes 393224 | tf_op jit(solution)/shard_map/ppermute | solution.py:422
  3.6 0.7 %collective-permute-start.4 = (bf16[64,1024]{1,0:T(8,128)(2,1)S(1)}, bf16[64,1024]{1,0:T(8,128)(2,1)S(1)}, u32[]{:S(2)}, u32[]{:S(2)}) collective-permute-start(bf16[64,1024]{1,0:T(8,128)(2,1)S(1)} %advance0_1.1.after_ref), channel_id=1, source_target_pairs={{4,8},{6,10},{5,9},{7,11}} | collective-permute-start | bytes 393224 | tf_op jit(solution)/shard_map/ppermute | solution.py:422
  4.4 8.6 %collective-permute-start.5 = (bf16[128,2048]{1,0:T(8,128)(2,1)S(1)}, bf16[128,2048]{1,0:T(8,128)(2,1)S(1)}, u32[]{:S(2)}, u32[]{:S(2)}) collective-permute-start(bf16[128,2048]{1,0:T(8,128)(2,1)S(1)} %first_finish_2.1.refs_12_), channel_id=1, source_target_pairs={{0,16},{2,18},{4,20},{6,22},{8,24},{10,26},{1,17},{3,19},{5,21},{7... | collective-permute-start | bytes 1572872 | tf_op jit(solution)/shard_map/ppermute | solution.py:492
  5.1 0.7 %collective-permute-start.12 = (bf16[64,1024]{1,0:T(8,128)(2,1)S(1)}, bf16[64,1024]{1,0:T(8,128)(2,1)S(1)}, u32[]{:S(2)}, u32[]{:S(2)}) collective-permute-start(bf16[64,1024]{1,0:T(8,128)(2,1)S(1)} %advance0_2.1.after_ref), channel_id=1, source_target_pairs={{8,12},{10,14},{9,13},{11,15}} | collective-permute-start | bytes 393224 | tf_op jit(solution)/shard_map/ppermute | solution.py:422
  5.8 31.3 %collective-permute-start.13 = (bf16[128,2048]{1,0:T(8,128)(2,1)S(1)}, bf16[128,2048]{1,0:T(8,128)(2,1)S(1)}, u32[]{:S(2)}, u32[]{:S(2)}) collective-permute-start(bf16[128,2048]{1,0:T(8,128)(2,1)S(1)} %first_finish_3.1.refs_13_), channel_id=1, source_target_pairs={{12,28},{14,30},{13,29},{15,31}} | collective-permute-start | bytes 1572872 | tf_op jit(solution)/shard_map/ppermute | solution.py:492
  13.2 1.4 %collective-permute-start.6 = (bf16[64,2048]{1,0:T(8,128)(2,1)S(1)}, bf16[64,2048]{1,0:T(8,128)(2,1)S(1)}, u32[]{:S(2)}, u32[]{:S(2)}) collective-permute-start(bf16[64,2048]{1,0:T(8,128)(2,1)S(1)} %get-tuple-element.45.refs_0_.refs_3_), channel_id=1, source_target_pairs={{16,18},{18,16},{17,19},{19,17}} | collective-permute-start | bytes 786440 | tf_op jit(solution)/shard_map/ppermute | solution.py:422
  13.9 2.1 %collective-permute-start.8 = (bf16[64,2048]{1,0:T(8,128)(2,1)S(1)}, bf16[64,2048]{1,0:T(8,128)(2,1)S(1)}, u32[]{:S(2)}, u32[]{:S(2)}) collective-permute-start(bf16[64,2048]{1,0:T(8,128)(2,1)S(1)} %get-tuple-element.45.refs_0_.refs_3_), channel_id=1, source_target_pairs={{20,22},{22,20},{21,23},{23,21}} | collective-permute-start | bytes 786440 | tf_op jit(solution)/shard_map/ppermute | solution.py:422
  14.6 1.4 %collective-permute-start.7 = (bf16[64,1024]{1,0:T(8,128)(2,1)S(1)}, bf16[64,1024]{1,0:T(8,128)(2,1)S(1)}, u32[]{:S(2)}, u32[]{:S(2)}) collective-permute-start(bf16[64,1024]{1,0:T(8,128)(2,1)S(1)} %advance1_0.1.refs_3_), channel_id=1, source_target_pairs={{16,20},{18,22},{17,21},{19,23}} | collective-permute-start | bytes 393224 | tf_op jit(solution)/shard_map/ppermute | solution.py:422
  15.3 27.8 %collective-permute-start.10 = (bf16[64,2048]{1,0:T(8,128)(2,1)S(1)}, bf16[64,2048]{1,0:T(8,128)(2,1)S(1)}, u32[]{:S(2)}, u32[]{:S(2)}) collective-permute-start(bf16[64,2048]{1,0:T(8,128)(2,1)S(1)} %get-tuple-element.45.refs_0_.refs_3_), channel_id=1, source_target_pairs={{24,26},{26,24},{25,27},{27,25}} | collective-permute-start | bytes 786440 | tf_op jit(solution)/shard_map/ppermute | solution.py:422
  16.1 27.1 %collective-permute-start.9 = (bf16[64,1024]{1,0:T(8,128)(2,1)S(1)}, bf16[64,1024]{1,0:T(8,128)(2,1)S(1)}, u32[]{:S(2)}, u32[]{:S(2)}) collective-permute-start(bf16[64,1024]{1,0:T(8,128)(2,1)S(1)} %advance1_1.1.after_ref), channel_id=1, source_target_pairs={{20,24},{22,26},{21,25},{23,27}} | collective-permute-start | bytes 393224 | tf_op jit(solution)/shard_map/ppermute | solution.py:422
  39.8 9.0 %collective-permute-start.14 = (bf16[64,2048]{1,0:T(8,128)(2,1)S(1)}, bf16[64,2048]{1,0:T(8,128)(2,1)S(1)}, u32[]{:S(2)}, u32[]{:S(2)}) collective-permute-start(bf16[64,2048]{1,0:T(8,128)(2,1)S(1)} %get-tuple-element.50), channel_id=1, source_target_pairs={{28,30},{30,28},{29,31},{31,29}} | collective-permute-start | bytes 786440 | tf_op jit(solution)/shard_map/ppermute | solution.py:422
  43.2 5.7 %collective-permute-start.11 = (bf16[64,1024]{1,0:T(8,128)(2,1)S(1)}, bf16[64,1024]{1,0:T(8,128)(2,1)S(1)}, u32[]{:S(2)}, u32[]{:S(2)}) collective-permute-start(bf16[64,1024]{1,0:T(8,128)(2,1)S(1)} %advance1_2.1.after_ref), channel_id=1, source_target_pairs={{24,28},{26,30},{25,29},{27,31}} | collective-permute-start | bytes 393224 | tf_op jit(solution)/shard_map/ppermute | solution.py:422

commit v13 on v12

--- a/solution.py
+++ b/solution.py
@@ -281,47 +281,40 @@
         out_ref[:, index * PAIR : (index + 1) * PAIR] = state.astype(BF16)
 
 
-def advance(active, place, own_ref, got_ref, state_ref, after_ref, out_ref):
+def advance(active, place, own_ref, got_ref, state_refs, after_ref, out_ref):
     width = out_ref.shape[1]
 
-    def body(refs):
+    def body(state_ref, refs):
         def state_of(start):
             return state_ref[:, start : start + PAIR].astype(F32) if place else pair_state(state_ref, start // PAIR)
 
         put_states(out_ref, moved_states(state_of, refs, width))
 
     here = at_pair([place], active)
-    if got_ref is None:
-        pl.when(here)(lambda: body((own_ref,)))
+    side = lax.rem(lax.axis_index("seq"), 2)
+    orders = [(own_ref,)] * 2 if got_ref is None else [(own_ref, got_ref), (got_ref, own_ref)]
+    if got_ref is None and len(state_refs) == 1:
+        pl.when(here)(lambda: body(state_refs[0], orders[0]))
     else:
-        side = lax.rem(lax.axis_index("seq"), 2)
-        pl.when(here & (side == 0))(lambda: body((own_ref, got_ref)))
-        pl.when(here & (side == 1))(lambda: body((got_ref, own_ref)))
+        pl.when(here & (side == 0))(lambda: body(state_refs[0], orders[0]))
+        pl.when(here & (side == 1))(lambda: body(state_refs[-1], orders[1]))
 
 
 def first_step(own_ref, init_ref, out_ref):
-    width = out_ref.shape[1]
-
     @pl.when((lax.axis_index("section") == 0) & (lax.axis_index("seq") == 0))
     def _():
-        put_states(out_ref, moved_states(lambda start: pair_state(init_ref, start // PAIR), (own_ref,), width))
-
-
-def first_advance(own_ref, got_ref, init_ref, state_ref, after_ref, out_ref):
-    width = out_ref.shape[1]
-    here = at_pair([0], 0)
-    side = lax.rem(lax.axis_index("seq"), 2)
-
-    @pl.when(here & (side == 0))
+        put_states(out_ref, moved_states(lambda start: pair_state(init_ref, start // PAIR), (own_ref,), out_ref.shape[1]))
+
+
+def second_step(own_ref, state_ref, after_ref, out_ref):
+    @pl.when((lax.axis_index("section") == 0) & (lax.axis_index("seq") == 1))
     def _():
-        put_states(out_ref, moved_states(lambda start: pair_state(init_ref, start // PAIR), (own_ref, got_ref), width))
-
-    @pl.when(here & (side == 1))
-    def _():
-        put_states(out_ref, moved_states(lambda start: state_ref[:, start : start + PAIR].astype(F32), (own_ref,), width))
-
-
-def finish(here, begins, state_ref, got_ref, reads_ref, w_out_ref, h_ref, store, followed=None):
+        put_states(
+            out_ref, moved_states(lambda start: state_ref[:, start : start + PAIR].astype(F32), (own_ref,), out_ref.shape[1])
+        )
+
+
+def finish(here, begins, state_refs, got_ref, reads_ref, w_out_ref, h_ref, store, followed=None):
     width = w_out_ref.shape[0]
     model = h_ref.shape[1]
     chunk = model // 4
@@ -329,7 +322,13 @@
     def body():
         follows = lax.rem(lax.axis_index("seq"), 2) == 1
         starts = range(0, width, PAIR)
-        states = [pair_state(state_ref, start // PAIR) if begins else state_ref[:, start : start + PAIR].astype(F32) for start in starts]
+        if begins:
+            states = [pair_state(state_refs[0], start // PAIR) for start in starts]
+        else:
+            states = [state_refs[0][:, start : start + PAIR].astype(F32) for start in starts]
+            for ref in state_refs[1:]:
+                others = [ref[:, start : start + PAIR].astype(F32) for start in starts]
+                states = [jnp.where(follows, other, state) for other, state in zip(others, states)]
         if followed is None:
             moved = [apply_map(state, got_ref, start, width) for state, start in zip(states, starts)]
         else:
@@ -352,14 +351,15 @@
     pl.when(here)(body)
 
 
-def first_finish(place, state_ref, got_ref, reads_ref, w_out_ref, h_ref, after_ref, *rest):
+def first_finish(place, count, *refs):
+    state_refs, (got_ref, reads_ref, w_out_ref, h_ref, after_ref, *rest) = refs[:count], refs[count:]
     out_ref = rest[-1]
 
     def store(start, value):
         out_ref[:, start : start + value.shape[1]] = value
 
     followed = None if place else got_ref
-    finish(at_pair([place], 0), place == 0, state_ref, got_ref, reads_ref, w_out_ref, h_ref, store, followed)
+    finish(at_pair([place], 0), place == 0, state_refs, got_ref, reads_ref, w_out_ref, h_ref, store, followed)
 
 
 def last_finish(count, w_out_ref, *refs):
@@ -377,7 +377,7 @@
         write(start).start()
 
     for place in range(count):
-        finish(at_pair([place], 1), place == 0, states[place], gots[place], reads[place], w_out_ref, hiddens[place], store)
+        finish(at_pair([place], 1), place == 0, [states[place]], gots[place], reads[place], w_out_ref, hiddens[place], store)
 
         @pl.when(at_pair([place], 0))
         def _():
@@ -435,14 +435,17 @@
         )
         return [reads] + [in_vmem(value) for value in w_out_near]
 
-    def hop(active, place, maps_here, state, after):
+    def hop(active, place, maps_here, states, after):
+        count_here = len(maps_here)
+
         def body(*refs):
-            advance(active, place, refs[0], None if len(maps_here) == 1 else refs[1], *refs[len(maps_here) :])
-
-        kinds = [pltpu.VMEM] * (len(maps_here) + 1) + [pl.ANY]
-        (ahead,) = call(body, [shape((HD, width), BF16)], [], maps_here + [state, after], kinds, name=f"advance{active}_{place}")
-        return ahead, permute(ahead, active, [(2 * place + side, 2 * place + 2 + side) for side in range(2)])
-
+            advance(active, place, refs[0], None if count_here == 1 else refs[1], refs[count_here:-2], *refs[-2:])
+
+        kinds = [pltpu.VMEM] * (count_here + len(states)) + [pl.ANY]
+        (ahead,) = call(body, [state_out], [], maps_here + states + [after], kinds, name=f"advance{active}_{place}")
+        return ahead, [permute(ahead, active, [(2 * place + side, 2 * place + 2 + side) for side in range(2)])]
+
+    state_out = shape((HD, width), BF16)
     groups = count // 2
 
     own, *rows_of, wq_near = call(
@@ -455,21 +458,14 @@
         name="first_front",
     )
     wq_near = in_vmem(wq_near)
-    state_out = shape((HD, width), BF16)
-    got_first = permute(own, 0, [(1, 0)])
     (stepped,) = call(first_step, [state_out], [], [own, init_state], name="first_step")
     stepped = permute(stepped, 0, [(0, 1)])
     got_rest = swap(own, 0, range(1, groups))
     read_first = layer_reads(0, [0], 1, rows_of, wq_near, init_state)
     (ahead,) = call(
-        first_advance,
-        [state_out],
-        [],
-        [own, got_first, init_state, stepped, read_first[0]],
-        [pltpu.VMEM] * 4 + [pl.ANY],
-        name="first_advance",
+        second_step, [state_out], [], [own, stepped, read_first[0]], [pltpu.VMEM] * 2 + [pl.ANY], name="second_step"
     )
-    state = permute(ahead, 0, [(side, 2 + side) for side in range(2)])
+    state = [permute(ahead, 0, [(1, 2 + side)]) for side in range(2)]
     read_rest = layer_reads(0, range(1, groups), 1, rows_of, wq_near, ahead)
     (both,) = call(
         functools.partial(compose, 0), [maps], [], [own, got_rest, read_rest[0]], [pltpu.VMEM] * 2 + [pl.ANY], name="compose"
@@ -500,7 +496,7 @@
         )
         return hidden, own, rows_of, [swap(own, 1, [place]) for place in places]
 
-    here, passed = init_state, []
+    here, passed = [init_state], []
     for place in range(groups):
         got, (reads, near) = (got_rest, read_rest) if place else (stepped, read_first)
         if 0 < place < groups - 1:
@@ -508,13 +504,13 @@
         if place + 1 == groups:
             firsts, passed = passed, []
         (first,) = call(
-            functools.partial(first_finish, place),
+            functools.partial(first_finish, place, len(here)),
             [shape((rows, model), BF16)],
             [],
-            [here, got, reads, near, tokens, ahead, *passed],
-            [pltpu.VMEM] * 5 + [pl.ANY] + [pltpu.VMEM] * len(passed),
+            [*here, got, reads, near, tokens, ahead, *passed],
+            [pltpu.VMEM] * (len(here) + 4) + [pl.ANY] + [pltpu.VMEM] * len(passed),
             name=f"first_finish_{place}",
-            aliases={6: 0} if passed else None,
+            aliases={len(here) + 5: 0} if passed else None,
         )
         passed, here = [first], state
     firsts += passed
@@ -528,8 +524,8 @@
             gots += got
             reads = layer_reads(1, range(groups - 1), 0, rows_later, params[1], after)
             after = reads[0]
-        after, state = hop(1, place, [own_later, gots[place]], states[-1], after)
-        states.append(state)
+        after, state = hop(1, place, [own_later, gots[place]], states[-1:], after)
+        states += state
     reads += layer_reads(1, [groups - 1], 0, rows_last, params[1], after)
     (result,) = call(
         functools.partial(last_finish, groups),

time: 51.1 us -> 50.6 us (level)
  the two profiles are of different devices: /device:TPU:31 before, /device:TPU:25 now
where the time goes in v13:
time: 50.6 us; the launch traced here: 50.1 us
  waiting for transfers between devices  23.4 us (46%)
  Pallas kernels  13.2 us (26%)
  starting transfers between devices  12.8 us (25%)
  between operations  0.54 us (1%)
    ppermute x2, waiting for transfers between devices, begin(): lax.ppermute(first, ('section', 'seq'), [(place, count + place) for place...  21 us
    pallas_call x21, Pallas kernels, call(): pl.pallas_call(body, out_shape=outs, in_specs=specs, out_specs=[pl.BlockS...  13.2 us
    ppermute x13, starting transfers between devices, permute(): lax.ppermute(value, ('section', 'seq'), [(base + source, base + target) f...  10.9 us
    ppermute x13, waiting for transfers between devices, permute(): lax.ppermute(value, ('section', 'seq'), [(base + source, base + target) f...  2.35 us
    ppermute x2, starting transfers between devices, begin(): lax.ppermute(first, ('section', 'seq'), [(place, count + place) for place...  1.99 us
  transfers between devices with their start and end apart: 15, of which 2 were waited for; matrix products, arithmetic and copies ran while one was open for 0% of the time, Pallas kernels for 22%

profile of v13, /device:TPU:25, one launch (start us, length us, event | category | flops | bytes accessed | tf_op | source)
XLA Modules:
  0.0 50.1 jit_solution(16587921367506089749)
XLA Ops:
  0.0 0.0 copy-start
  0.0 0.1 first_front.1
  0.1 0.8 %collective-permute-start = (bf16[64,2048]{1,0:T(8,128)(2,1)S(1)}, bf16[64,2048]{1,0:T(8,128)(2,1)S(1)}, u32[]{:S(2)}, u32[]{:S(2)}) collective-permute-start(bf16[64,2048]{1,0:T(8,128)(2,1)S(1)} %get-tuple-element.30.own_ref.after_ref), channel_id=1, source_target_pairs={{4,6},{6,4},{8,10},{10,8},{12,14},{14,12},{5,7},{7,5},{9,11},{11,9... | collective-permute-start | bytes 786440 | tf_op jit(solution)/shard_map/ppermute | solution.py:422
  0.9 0.1 copy-done
  1.0 0.7 %collective-permute-start.1 = (bf16[64,1024]{1,0:T(8,128)(2,1)S(1)}, bf16[64,1024]{1,0:T(8,128)(2,1)S(1)}, u32[]{:S(2)}, u32[]{:S(2)}) collective-permute-start(bf16[64,1024]{1,0:T(8,128)(2,1)S(1)} %first_step.1), channel_id=1, source_target_pairs={{0,2},{1,3}} | collective-permute-start | bytes 393224 | tf_op jit(solution)/shard_map/ppermute | solution.py:422
  1.8 0.0 collective-permute-done.1.state_ref.refs_1_
  1.8 0.0 copy-start.1
  1.8 0.8 %collective-permute-start.3 = (bf16[64,1024]{1,0:T(8,128)(2,1)S(1)}, bf16[64,1024]{1,0:T(8,128)(2,1)S(1)}, u32[]{:S(2)}, u32[]{:S(2)}) collective-permute-start(bf16[64,1024]{1,0:T(8,128)(2,1)S(1)} %second_step.1.after_ref.refs_5_), channel_id=1, source_target_pairs={{2,6},{3,7}} | collective-permute-start | bytes 393224 | tf_op jit(solution)/shard_map/ppermute | solution.py:422
  2.6 0.7 %collective-permute-start.2 = (bf16[64,1024]{1,0:T(8,128)(2,1)S(1)}, bf16[64,1024]{1,0:T(8,128)(2,1)S(1)}, u32[]{:S(2)}, u32[]{:S(2)}) collective-permute-start(bf16[64,1024]{1,0:T(8,128)(2,1)S(1)} %second_step.1.after_ref.refs_5_), channel_id=1, source_target_pairs={{2,4},{3,5}} | collective-permute-start | bytes 393224 | tf_op jit(solution)/shard_map/ppermute | solution.py:422
  3.3 0.0 copy-done.1
  3.4 0.0 collective-permute-done.got_ref.refs_2_.refs_1_
  3.4 0.0 collective-permute-done.3.refs_2_.refs_1_
  3.4 0.0 collective-permute-done.2.refs_1_.refs_0_
  3.5 0.7 %collective-permute-start.4 = (bf16[64,1024]{1,0:T(8,128)(2,1)S(1)}, bf16[64,1024]{1,0:T(8,128)(2,1)S(1)}, u32[]{:S(2)}, u32[]{:S(2)}) collective-permute-start(bf16[64,1024]{1,0:T(8,128)(2,1)S(1)} %advance0_1.1.refs_6_), channel_id=1, source_target_pairs={{4,8},{6,10},{5,9},{7,11}} | collective-permute-start | bytes 393224 | tf_op jit(solution)/shard_map/ppermute | solution.py:422
  4.2 0.0 collective-permute-done.4.refs_1_.refs_0_
  4.3 0.7 %collective-permute-start.5 = (bf16[128,2048]{1,0:T(8,128)(2,1)S(1)}, bf16[128,2048]{1,0:T(8,128)(2,1)S(1)}, u32[]{:S(2)}, u32[]{:S(2)}) collective-permute-start(bf16[128,2048]{1,0:T(8,128)(2,1)S(1)} %first_finish_2.1.refs_12_), channel_id=1, source_target_pairs={{0,16},{2,18},{4,20},{6,22},{8,24},{10,26},{1,17},{3,19},{5,21},{7... | collective-permute-start | bytes 1572872 | tf_op jit(solution)/shard_map/ppermute | solution.py:488
  5.0 0.7 %collective-permute-start.12 = (bf16[64,1024]{1,0:T(8,128)(2,1)S(1)}, bf16[64,1024]{1,0:T(8,128)(2,1)S(1)}, u32[]{:S(2)}, u32[]{:S(2)}) collective-permute-start(bf16[64,1024]{1,0:T(8,128)(2,1)S(1)} %advance0_2.1.refs_5_), channel_id=1, source_target_pairs={{8,12},{10,14},{9,13},{11,15}} | collective-permute-start | bytes 393224 | tf_op jit(solution)/shard_map/ppermute | solution.py:422
  5.7 0.0 collective-permute-done.12.refs_0_
  5.7 1.3 %collective-permute-start.13 = (bf16[128,2048]{1,0:T(8,128)(2,1)S(1)}, bf16[128,2048]{1,0:T(8,128)(2,1)S(1)}, u32[]{:S(2)}, u32[]{:S(2)}) collective-permute-start(bf16[128,2048]{1,0:T(8,128)(2,1)S(1)} %first_finish_3.1.refs_13_), channel_id=1, source_target_pairs={{12,28},{14,30},{13,29},{15,31}} | collective-permute-start | bytes 1572872 | tf_op jit(solution)/shard_map/ppermute | solution.py:488
  7.0 5.9 %load.1 = (f32[1,2048]{1,0:T(1,128)S(1)}, bf16[1,2048,3072]{2,1,0:T(8,128)(2,1)S(1)}, bf16[1,16,2048]{2,1,0:T(8,128)(2,1)S(1)}, f32[1,16]{1,0:T(1,128)S(1)}, bf16[1,1024,2048]{2,1,0:T(8,128)(2,1)S(1)}) custom-call(f32[1,2048]{1,0:T(1,128)} %refs_0_.3, bf16[1,2048,3072]{2,1,0:T(8,128)(2,1)} %w_hbm.7, bf16[1,16,2048]{2,1,0:T(8,128)(2,1)} %bitcast.9, ...), custom_call_target="tpu_custom_call" | custom-call | tf_op jit(solution)/shard_map/load/pallas_call | solution.py:393
  12.9 0.0 collective-permute-done.5.h_ref.refs_10_
  12.9 0.2 later_front_0.1
  13.1 0.7 %collective-permute-start.6 = (bf16[64,2048]{1,0:T(8,128)(2,1)S(1)}, bf16[64,2048]{1,0:T(8,128)(2,1)S(1)}, u32[]{:S(2)}, u32[]{:S(2)}) collective-permute-start(bf16[64,2048]{1,0:T(8,128)(2,1)S(1)} %get-tuple-element.45.refs_0_.refs_3_), channel_id=1, source_target_pairs={{16,18},{18,16},{17,19},{19,17}} | collective-permute-start | bytes 786440 | tf_op jit(solution)/shard_map/ppermute | solution.py:422
  13.8 0.7 %collective-permute-start.8 = (bf16[64,2048]{1,0:T(8,128)(2,1)S(1)}, bf16[64,2048]{1,0:T(8,128)(2,1)S(1)}, u32[]{:S(2)}, u32[]{:S(2)}) collective-permute-start(bf16[64,2048]{1,0:T(8,128)(2,1)S(1)} %get-tuple-element.45.refs_0_.refs_3_), channel_id=1, source_target_pairs={{20,22},{22,20},{21,23},{23,21}} | collective-permute-start | bytes 786440 | tf_op jit(solution)/shard_map/ppermute | solution.py:422
  14.5 0.0 collective-permute-done.6.refs_1_.refs_4_
  14.5 0.7 %collective-permute-start.7 = (bf16[64,1024]{1,0:T(8,128)(2,1)S(1)}, bf16[64,1024]{1,0:T(8,128)(2,1)S(1)}, u32[]{:S(2)}, u32[]{:S(2)}) collective-permute-start(bf16[64,1024]{1,0:T(8,128)(2,1)S(1)} %advance1_0.1.refs_3_), channel_id=1, source_target_pairs={{16,20},{18,22},{17,21},{19,23}} | collective-permute-start | bytes 393224 | tf_op jit(solution)/shard_map/ppermute | solution.py:422
  15.2 0.7 %collective-permute-start.10 = (bf16[64,2048]{1,0:T(8,128)(2,1)S(1)}, bf16[64,2048]{1,0:T(8,128)(2,1)S(1)}, u32[]{:S(2)}, u32[]{:S(2)}) collective-permute-start(bf16[64,2048]{1,0:T(8,128)(2,1)S(1)} %get-tuple-element.45.refs_0_.refs_3_), channel_id=1, source_target_pairs={{24,26},{26,24},{25,27},{27,25}} | collective-permute-start | bytes 786440 | tf_op jit(solution)/shard_map/ppermute | solution.py:422
  15.9 0.0 collective-permute-done.8.refs_1_.refs_5_
  15.9 0.0 collective-permute-done.7.refs_2_.refs_1_
  16.0 0.7 %collective-permute-start.9 = (bf16[64,1024]{1,0:T(8,128)(2,1)S(1)}, bf16[64,1024]{1,0:T(8,128)(2,1)S(1)}, u32[]{:S(2)}, u32[]{:S(2)}) collective-permute-start(bf16[64,1024]{1,0:T(8,128)(2,1)S(1)} %advance1_1.1.after_ref), channel_id=1, source_target_pairs={{20,24},{22,26},{21,25},{23,27}} | collective-permute-start | bytes 393224 | tf_op jit(solution)/shard_map/ppermute | solution.py:422
  16.6 21.0 %collective-permute-done.13.h_ref.refs_11_ = bf16[128,2048]{1,0:T(8,128)(2,1)S(1)} collective-permute-done((bf16[128,2048]{1,0:T(8,128)(2,1)S(1)}, bf16[128,2048]{1,0:T(8,128)(2,1)S(1)}, u32[]{:S(2)}, u32[]{:S(2)}) %collective-permute-start.13) | collective-permute-done | bytes 524320 | tf_op jit(solution)/shard_map/ppermute | solution.py:488
  37.7 2.7 %later_front_3.1 = (bf16[64,2048]{1,0:T(8,128)(2,1)S(1)}, bf16[128,2048]{1,0:T(8,128)(2,1)S(1)}, bf16[128,1024]{1,0:T(8,128)(2,1)S(1)}, bf16[128,1024]{1,0:T(8,128)(2,1)S(1)}, bf16[128,1024]{1,0:T(8,128)(2,1)S(1)}) custom-call(bf16[128,2048]{1,0:T(8,128)(2,1)S(1)} %collective-permute-done.13.h_ref.refs_11_, f32[1,2048]{1,0:T(1,128)S(1)} %get-tuple-element.41.gain, ...), custom_call_target="tpu_custom_call" | custom-call | tf_op jit(solution)/shard_map/later_front_3/pallas_call | solution.py:393
  40.4 1.9 %collective-permute-start.14 = (bf16[64,2048]{1,0:T(8,128)(2,1)S(1)}, bf16[64,2048]{1,0:T(8,128)(2,1)S(1)}, u32[]{:S(2)}, u32[]{:S(2)}) collective-permute-start(bf16[64,2048]{1,0:T(8,128)(2,1)S(1)} %get-tuple-element.50), channel_id=1, source_target_pairs={{28,30},{30,28},{29,31},{31,29}} | collective-permute-start | bytes 786440 | tf_op jit(solution)/shard_map/ppermute | solution.py:422
  42.4 0.0 collective-permute-done.10.refs_1_.refs_6_
  42.4 0.0 collective-permute-done.9.refs_2_
  42.4 1.3 %collective-permute-start.11 = (bf16[64,1024]{1,0:T(8,128)(2,1)S(1)}, bf16[64,1024]{1,0:T(8,128)(2,1)S(1)}, u32[]{:S(2)}, u32[]{:S(2)}) collective-permute-start(bf16[64,1024]{1,0:T(8,128)(2,1)S(1)} %advance1_2.1.after_ref), channel_id=1, source_target_pairs={{24,28},{26,30},{25,29},{27,31}} | collective-permute-start | bytes 393224 | tf_op jit(solution)/shard_map/ppermute | solution.py:422
  43.7 2.1 %reads1_3.1.refs_9_ = bf16[128,2048]{1,0:T(8,128)(2,1)S(1)} custom-call(bf16[128,2048]{1,0:T(8,128)(2,1)S(1)} %get-tuple-element.51.normed_ref, bf16[128,1024]{1,0:T(8,128)(2,1)S(1)} %get-tuple-element.52.keys_ref, bf16[128,1024]{1,0:T(8,128)(2,1)S(1)} %get-tuple-element.53.x_ref, bf16[128,1024]{1,0:T(8,128)(2,1)S(1)} %get-tuple-element.54.y_ref, ...), custom_call_target="tpu_custom_call" | custom-call | tf_op jit(solution)/shard_map/reads1_3/pallas_call | solution.py:393
  45.8 2.3 %collective-permute-done.11.refs_3_ = bf16[64,1024]{1,0:T(8,128)(2,1)S(1)} collective-permute-done((bf16[64,1024]{1,0:T(8,128)(2,1)S(1)}, bf16[64,1024]{1,0:T(8,128)(2,1)S(1)}, u32[]{:S(2)}, u32[]{:S(2)}) %collective-permute-start.11) | collective-permute-done | bytes 131104 | tf_op jit(solution)/shard_map/ppermute | solution.py:422
  48.1 0.0 collective-permute-done.14.refs_7_
  48.1 1.7 %last_finish.1 = bf16[1,128,2048]{2,1,0:T(8,128)(2,1)} custom-call(bf16[1024,2048]{1,0:T(8,128)(2,1)S(1)} %bitcast.7, f32[1,16,64,64]{3,2,1,0:T(8,128)S(1)} %copy-done, bf16[64,1024]{1,0:T(8,128)(2,1)S(1)} %collective-permute-done.7.refs_2_.refs_1_, bf16[64,1024]{1,0:T(8,128)(2,1)S(1)} %collective-permute-done.9.refs_2_, ...), custom_call_target="tpu_custom_call" | custom-call | tf_op jit(solution)/shard_map/last_finish/pallas_call | solution.py:393
  (15 shorter events, 0.4 us)
Async XLA Ops:
  0.0 1.0 %copy-start = (f32[1,16,64,64]{3,2,1,0:T(8,128)S(1)}, f32[1,16,64,64]{3,2,1,0:T(8,128)}, u32[]{:S(2)}) copy-start(f32[1,16,64,64]{3,2,1,0:T(8,128)} %refs_0_.5) | copy-start | bytes 786436
  0.1 3.3 %collective-permute-start = (bf16[64,2048]{1,0:T(8,128)(2,1)S(1)}, bf16[64,2048]{1,0:T(8,128)(2,1)S(1)}, u32[]{:S(2)}, u32[]{:S(2)}) collective-permute-start(bf16[64,2048]{1,0:T(8,128)(2,1)S(1)} %get-tuple-element.30.own_ref.after_ref), channel_id=1, source_target_pairs={{4,6},{6,4},{8,10},{10,8},{12,14},{14,12},{5,7},{7,5},{9,11},{11,9... | collective-permute-start | bytes 786440 | tf_op jit(solution)/shard_map/ppermute | solution.py:422
  1.0 0.7 %collective-permute-start.1 = (bf16[64,1024]{1,0:T(8,128)(2,1)S(1)}, bf16[64,1024]{1,0:T(8,128)(2,1)S(1)}, u32[]{:S(2)}, u32[]{:S(2)}) collective-permute-start(bf16[64,1024]{1,0:T(8,128)(2,1)S(1)} %first_step.1), channel_id=1, source_target_pairs={{0,2},{1,3}} | collective-permute-start | bytes 393224 | tf_op jit(solution)/shard_map/ppermute | solution.py:422
  1.8 1.6 %copy-start.1 = (bf16[128,2048]{1,0:T(8,128)(2,1)S(1)}, bf16[128,2048]{1,0:T(8,128)(2,1)}, u32[]{:S(2)}) copy-start(bf16[128,2048]{1,0:T(8,128)(2,1)} %refs_4_.7) | copy-start | bytes 1572868
  1.8 1.6 %collective-permute-start.3 = (bf16[64,1024]{1,0:T(8,128)(2,1)S(1)}, bf16[64,1024]{1,0:T(8,128)(2,1)S(1)}, u32[]{:S(2)}, u32[]{:S(2)}) collective-permute-start(bf16[64,1024]{1,0:T(8,128)(2,1)S(1)} %second_step.1.after_ref.refs_5_), channel_id=1, source_target_pairs={{2,6},{3,7}} | collective-permute-start | bytes 393224 | tf_op jit(solution)/shard_map/ppermute | solution.py:422
  2.6 0.8 %collective-permute-start.2 = (bf16[64,1024]{1,0:T(8,128)(2,1)S(1)}, bf16[64,1024]{1,0:T(8,128)(2,1)S(1)}, u32[]{:S(2)}, u32[]{:S(2)}) collective-permute-start(bf16[64,1024]{1,0:T(8,128)(2,1)S(1)} %second_step.1.after_ref.refs_5_), channel_id=1, source_target_pairs={{2,4},{3,5}} | collective-permute-start | bytes 393224 | tf_op jit(solution)/shard_map/ppermute | solution.py:422
  3.5 0.7 %collective-permute-start.4 = (bf16[64,1024]{1,0:T(8,128)(2,1)S(1)}, bf16[64,1024]{1,0:T(8,128)(2,1)S(1)}, u32[]{:S(2)}, u32[]{:S(2)}) collective-permute-start(bf16[64,1024]{1,0:T(8,128)(2,1)S(1)} %advance0_1.1.refs_6_), channel_id=1, source_target_pairs={{4,8},{6,10},{5,9},{7,11}} | collective-permute-start | bytes 393224 | tf_op jit(solution)/shard_map/ppermute | solution.py:422
  4.3 8.6 %collective-permute-start.5 = (bf16[128,2048]{1,0:T(8,128)(2,1)S(1)}, bf16[128,2048]{1,0:T(8,128)(2,1)S(1)}, u32[]{:S(2)}, u32[]{:S(2)}) collective-permute-start(bf16[128,2048]{1,0:T(8,128)(2,1)S(1)} %first_finish_2.1.refs_12_), channel_id=1, source_target_pairs={{0,16},{2,18},{4,20},{6,22},{8,24},{10,26},{1,17},{3,19},{5,21},{7... | collective-permute-start | bytes 1572872 | tf_op jit(solution)/shard_map/ppermute | solution.py:488
  5.0 0.7 %collective-permute-start.12 = (bf16[64,1024]{1,0:T(8,128)(2,1)S(1)}, bf16[64,1024]{1,0:T(8,128)(2,1)S(1)}, u32[]{:S(2)}, u32[]{:S(2)}) collective-permute-start(bf16[64,1024]{1,0:T(8,128)(2,1)S(1)} %advance0_2.1.refs_5_), channel_id=1, source_target_pairs={{8,12},{10,14},{9,13},{11,15}} | collective-permute-start | bytes 393224 | tf_op jit(solution)/shard_map/ppermute | solution.py:422
  5.7 32.0 %collective-permute-start.13 = (bf16[128,2048]{1,0:T(8,128)(2,1)S(1)}, bf16[128,2048]{1,0:T(8,128)(2,1)S(1)}, u32[]{:S(2)}, u32[]{:S(2)}) collective-permute-start(bf16[128,2048]{1,0:T(8,128)(2,1)S(1)} %first_finish_3.1.refs_13_), channel_id=1, source_target_pairs={{12,28},{14,30},{13,29},{15,31}} | collective-permute-start | bytes 1572872 | tf_op jit(solution)/shard_map/ppermute | solution.py:488
  13.1 1.4 %collective-permute-start.6 = (bf16[64,2048]{1,0:T(8,128)(2,1)S(1)}, bf16[64,2048]{1,0:T(8,128)(2,1)S(1)}, u32[]{:S(2)}, u32[]{:S(2)}) collective-permute-start(bf16[64,2048]{1,0:T(8,128)(2,1)S(1)} %get-tuple-element.45.refs_0_.refs_3_), channel_id=1, source_target_pairs={{16,18},{18,16},{17,19},{19,17}} | collective-permute-start | bytes 786440 | tf_op jit(solution)/shard_map/ppermute | solution.py:422
  13.8 2.1 %collective-permute-start.8 = (bf16[64,2048]{1,0:T(8,128)(2,1)S(1)}, bf16[64,2048]{1,0:T(8,128)(2,1)S(1)}, u32[]{:S(2)}, u32[]{:S(2)}) collective-permute-start(bf16[64,2048]{1,0:T(8,128)(2,1)S(1)} %get-tuple-element.45.refs_0_.refs_3_), channel_id=1, source_target_pairs={{20,22},{22,20},{21,23},{23,21}} | collective-permute-start | bytes 786440 | tf_op jit(solution)/shard_map/ppermute | solution.py:422
  14.5 1.4 %collective-permute-start.7 = (bf16[64,1024]{1,0:T(8,128)(2,1)S(1)}, bf16[64,1024]{1,0:T(8,128)(2,1)S(1)}, u32[]{:S(2)}, u32[]{:S(2)}) collective-permute-start(bf16[64,1024]{1,0:T(8,128)(2,1)S(1)} %advance1_0.1.refs_3_), channel_id=1, source_target_pairs={{16,20},{18,22},{17,21},{19,23}} | collective-permute-start | bytes 393224 | tf_op jit(solution)/shard_map/ppermute | solution.py:422
  15.2 27.2 %collective-permute-start.10 = (bf16[64,2048]{1,0:T(8,128)(2,1)S(1)}, bf16[64,2048]{1,0:T(8,128)(2,1)S(1)}, u32[]{:S(2)}, u32[]{:S(2)}) collective-permute-start(bf16[64,2048]{1,0:T(8,128)(2,1)S(1)} %get-tuple-element.45.refs_0_.refs_3_), channel_id=1, source_target_pairs={{24,26},{26,24},{25,27},{27,25}} | collective-permute-start | bytes 786440 | tf_op jit(solution)/shard_map/ppermute | solution.py:422
  16.0 26.4 %collective-permute-start.9 = (bf16[64,1024]{1,0:T(8,128)(2,1)S(1)}, bf16[64,1024]{1,0:T(8,128)(2,1)S(1)}, u32[]{:S(2)}, u32[]{:S(2)}) collective-permute-start(bf16[64,1024]{1,0:T(8,128)(2,1)S(1)} %advance1_1.1.after_ref), channel_id=1, source_target_pairs={{20,24},{22,26},{21,25},{23,27}} | collective-permute-start | bytes 393224 | tf_op jit(solution)/shard_map/ppermute | solution.py:422
  40.4 7.8 %collective-permute-start.14 = (bf16[64,2048]{1,0:T(8,128)(2,1)S(1)}, bf16[64,2048]{1,0:T(8,128)(2,1)S(1)}, u32[]{:S(2)}, u32[]{:S(2)}) collective-permute-start(bf16[64,2048]{1,0:T(8,128)(2,1)S(1)} %get-tuple-element.50), channel_id=1, source_target_pairs={{28,30},{30,28},{29,31},{31,29}} | collective-permute-start | bytes 786440 | tf_op jit(solution)/shard_map/ppermute | solution.py:422
  42.4 5.7 %collective-permute-start.11 = (bf16[64,1024]{1,0:T(8,128)(2,1)S(1)}, bf16[64,1024]{1,0:T(8,128)(2,1)S(1)}, u32[]{:S(2)}, u32[]{:S(2)}) collective-permute-start(bf16[64,1024]{1,0:T(8,128)(2,1)S(1)} %advance1_2.1.after_ref), channel_id=1, source_target_pairs={{24,28},{26,30},{25,29},{27,31}} | collective-permute-start | bytes 393224 | tf_op jit(solution)/shard_map/ppermute | solution.py:422

commit v14 on v13

--- a/solution.py
+++ b/solution.py
@@ -352,7 +352,7 @@
 
 
 def first_finish(place, count, *refs):
-    state_refs, (got_ref, reads_ref, w_out_ref, h_ref, after_ref, *rest) = refs[:count], refs[count:]
+    state_refs, (got_ref, reads_ref, w_out_ref, h_ref, after_ref, *rest) = refs[:count][::-1], refs[count:]
     out_ref = rest[-1]
 
     def store(start, value):
@@ -439,10 +439,10 @@
         count_here = len(maps_here)
 
         def body(*refs):
-            advance(active, place, refs[0], None if count_here == 1 else refs[1], refs[count_here:-2], *refs[-2:])
+            advance(active, place, refs[0], None if count_here == 1 else refs[1], refs[count_here:-2][::-1], *refs[-2:])
 
         kinds = [pltpu.VMEM] * (count_here + len(states)) + [pl.ANY]
-        (ahead,) = call(body, [state_out], [], maps_here + states + [after], kinds, name=f"advance{active}_{place}")
+        (ahead,) = call(body, [state_out], [], maps_here + states[::-1] + [after], kinds, name=f"advance{active}_{place}")
         return ahead, [permute(ahead, active, [(2 * place + side, 2 * place + 2 + side) for side in range(2)])]
 
     state_out = shape((HD, width), BF16)
@@ -507,7 +507,7 @@
             functools.partial(first_finish, place, len(here)),
             [shape((rows, model), BF16)],
             [],
-            [*here, got, reads, near, tokens, ahead, *passed],
+            [*here[::-1], got, reads, near, tokens, ahead, *passed],
             [pltpu.VMEM] * (len(here) + 4) + [pl.ANY] + [pltpu.VMEM] * len(passed),
             name=f"first_finish_{place}",
             aliases={len(here) + 5: 0} if passed else None,

time: 50.6 us -> 50.6 us (level)
  starting transfers between devices: 12.8 us -> 14.5 us
  waiting for transfers between devices: 23.4 us -> 22 us
    ppermute x13, starting transfers between devices: 10.9 us -> 12.5 us  [permute(): lax.ppermute(value, ('section', 'seq'), [(base + source, base + target) f...]
    ppermute x2, waiting for transfers between devices: 21 us -> 19.6 us  [begin(): lax.ppermute(first, ('section', 'seq'), [(place, count + place) for place...]
where the time goes in v14:
time: 50.6 us; the launch traced here: 50.3 us
  waiting for transfers between devices  22 us (43%)
  starting transfers between devices  14.5 us (29%)
  Pallas kernels  13.2 us (26%)
  between operations  0.54 us (1%)
    ppermute x2, waiting for transfers between devices, begin(): lax.ppermute(first, ('section', 'seq'), [(place, count + place) for place...  19.6 us
    pallas_call x21, Pallas kernels, call(): pl.pallas_call(body, out_shape=outs, in_specs=specs, out_specs=[pl.BlockS...  13.2 us
    ppermute x13, starting transfers between devices, permute(): lax.ppermute(value, ('section', 'seq'), [(base + source, base + target) f...  12.5 us
    ppermute x13, waiting for transfers between devices, permute(): lax.ppermute(value, ('section', 'seq'), [(base + source, base + target) f...  2.34 us
    ppermute x2, starting transfers between devices, begin(): lax.ppermute(first, ('section', 'seq'), [(place, count + place) for place...  1.99 us
  transfers between devices with their start and end apart: 15, of which 2 were waited for; matrix products, arithmetic and copies ran while one was open for 0% of the time, Pallas kernels for 22%

profile of v14, /device:TPU:25, one launch (start us, length us, event | category | flops | bytes accessed | tf_op | source)
XLA Modules:
  0.0 50.3 jit_solution(13826621356040475482)
XLA Ops:
  0.0 0.0 copy-start
  0.0 0.1 first_front.1
  0.1 0.8 %collective-permute-start = (bf16[64,2048]{1,0:T(8,128)(2,1)S(1)}, bf16[64,2048]{1,0:T(8,128)(2,1)S(1)}, u32[]{:S(2)}, u32[]{:S(2)}) collective-permute-start(bf16[64,2048]{1,0:T(8,128)(2,1)S(1)} %get-tuple-element.30.own_ref.after_ref), channel_id=1, source_target_pairs={{4,6},{6,4},{8,10},{10,8},{12,14},{14,12},{5,7},{7,5},{9,11},{11,9... | collective-permute-start | bytes 786440 | tf_op jit(solution)/shard_map/ppermute | solution.py:422
  0.9 0.1 copy-done
  1.0 0.7 %collective-permute-start.1 = (bf16[64,1024]{1,0:T(8,128)(2,1)S(1)}, bf16[64,1024]{1,0:T(8,128)(2,1)S(1)}, u32[]{:S(2)}, u32[]{:S(2)}) collective-permute-start(bf16[64,1024]{1,0:T(8,128)(2,1)S(1)} %first_step.1), channel_id=1, source_target_pairs={{0,2},{1,3}} | collective-permute-start | bytes 393224 | tf_op jit(solution)/shard_map/ppermute | solution.py:422
  1.8 0.0 collective-permute-done.1.state_ref.refs_1_
  1.8 0.0 copy-start.1
  1.8 0.8 %collective-permute-start.3 = (bf16[64,1024]{1,0:T(8,128)(2,1)S(1)}, bf16[64,1024]{1,0:T(8,128)(2,1)S(1)}, u32[]{:S(2)}, u32[]{:S(2)}) collective-permute-start(bf16[64,1024]{1,0:T(8,128)(2,1)S(1)} %second_step.1.after_ref.refs_5_), channel_id=1, source_target_pairs={{2,4},{3,5}} | collective-permute-start | bytes 393224 | tf_op jit(solution)/shard_map/ppermute | solution.py:422
  2.6 0.7 %collective-permute-start.2 = (bf16[64,1024]{1,0:T(8,128)(2,1)S(1)}, bf16[64,1024]{1,0:T(8,128)(2,1)S(1)}, u32[]{:S(2)}, u32[]{:S(2)}) collective-permute-start(bf16[64,1024]{1,0:T(8,128)(2,1)S(1)} %second_step.1.after_ref.refs_5_), channel_id=1, source_target_pairs={{2,6},{3,7}} | collective-permute-start | bytes 393224 | tf_op jit(solution)/shard_map/ppermute | solution.py:422
  3.3 0.0 copy-done.1
  3.4 0.0 collective-permute-done.got_ref.refs_2_.refs_1_
  3.4 0.0 collective-permute-done.3.refs_2_.refs_1_
  3.4 0.0 collective-permute-done.2.refs_1_.refs_0_
  3.5 0.7 %collective-permute-start.4 = (bf16[64,1024]{1,0:T(8,128)(2,1)S(1)}, bf16[64,1024]{1,0:T(8,128)(2,1)S(1)}, u32[]{:S(2)}, u32[]{:S(2)}) collective-permute-start(bf16[64,1024]{1,0:T(8,128)(2,1)S(1)} %advance0_1.1.refs_6_), channel_id=1, source_target_pairs={{4,8},{6,10},{5,9},{7,11}} | collective-permute-start | bytes 393224 | tf_op jit(solution)/shard_map/ppermute | solution.py:422
  4.2 0.0 collective-permute-done.4.refs_1_.refs_0_
  4.3 0.7 %collective-permute-start.5 = (bf16[128,2048]{1,0:T(8,128)(2,1)S(1)}, bf16[128,2048]{1,0:T(8,128)(2,1)S(1)}, u32[]{:S(2)}, u32[]{:S(2)}) collective-permute-start(bf16[128,2048]{1,0:T(8,128)(2,1)S(1)} %first_finish_2.1.refs_12_), channel_id=1, source_target_pairs={{0,16},{2,18},{4,20},{6,22},{8,24},{10,26},{1,17},{3,19},{5,21},{7... | collective-permute-start | bytes 1572872 | tf_op jit(solution)/shard_map/ppermute | solution.py:488
  5.0 0.7 %collective-permute-start.12 = (bf16[64,1024]{1,0:T(8,128)(2,1)S(1)}, bf16[64,1024]{1,0:T(8,128)(2,1)S(1)}, u32[]{:S(2)}, u32[]{:S(2)}) collective-permute-start(bf16[64,1024]{1,0:T(8,128)(2,1)S(1)} %advance0_2.1.refs_5_), channel_id=1, source_target_pairs={{8,12},{10,14},{9,13},{11,15}} | collective-permute-start | bytes 393224 | tf_op jit(solution)/shard_map/ppermute | solution.py:422
  5.7 0.0 collective-permute-done.12.refs_0_
  5.7 1.3 %collective-permute-start.13 = (bf16[128,2048]{1,0:T(8,128)(2,1)S(1)}, bf16[128,2048]{1,0:T(8,128)(2,1)S(1)}, u32[]{:S(2)}, u32[]{:S(2)}) collective-permute-start(bf16[128,2048]{1,0:T(8,128)(2,1)S(1)} %first_finish_3.1.refs_13_), channel_id=1, source_target_pairs={{12,28},{14,30},{13,29},{15,31}} | collective-permute-start | bytes 1572872 | tf_op jit(solution)/shard_map/ppermute | solution.py:488
  7.0 5.9 %load.1 = (f32[1,2048]{1,0:T(1,128)S(1)}, bf16[1,2048,3072]{2,1,0:T(8,128)(2,1)S(1)}, bf16[1,16,2048]{2,1,0:T(8,128)(2,1)S(1)}, f32[1,16]{1,0:T(1,128)S(1)}, bf16[1,1024,2048]{2,1,0:T(8,128)(2,1)S(1)}) custom-call(f32[1,2048]{1,0:T(1,128)} %refs_0_.3, bf16[1,2048,3072]{2,1,0:T(8,128)(2,1)} %w_hbm.7, bf16[1,16,2048]{2,1,0:T(8,128)(2,1)} %bitcast.9, ...), custom_call_target="tpu_custom_call" | custom-call | tf_op jit(solution)/shard_map/load/pallas_call | solution.py:393
  12.9 0.0 collective-permute-done.5.h_ref.refs_10_
  12.9 0.2 later_front_0.1
  13.1 0.7 %collective-permute-start.6 = (bf16[64,2048]{1,0:T(8,128)(2,1)S(1)}, bf16[64,2048]{1,0:T(8,128)(2,1)S(1)}, u32[]{:S(2)}, u32[]{:S(2)}) collective-permute-start(bf16[64,2048]{1,0:T(8,128)(2,1)S(1)} %get-tuple-element.45.refs_0_.refs_3_), channel_id=1, source_target_pairs={{16,18},{18,16},{17,19},{19,17}} | collective-permute-start | bytes 786440 | tf_op jit(solution)/shard_map/ppermute | solution.py:422
  13.8 0.7 %collective-permute-start.8 = (bf16[64,2048]{1,0:T(8,128)(2,1)S(1)}, bf16[64,2048]{1,0:T(8,128)(2,1)S(1)}, u32[]{:S(2)}, u32[]{:S(2)}) collective-permute-start(bf16[64,2048]{1,0:T(8,128)(2,1)S(1)} %get-tuple-element.45.refs_0_.refs_3_), channel_id=1, source_target_pairs={{20,22},{22,20},{21,23},{23,21}} | collective-permute-start | bytes 786440 | tf_op jit(solution)/shard_map/ppermute | solution.py:422
  14.5 0.0 collective-permute-done.6.refs_1_.refs_4_
  14.5 0.7 %collective-permute-start.7 = (bf16[64,1024]{1,0:T(8,128)(2,1)S(1)}, bf16[64,1024]{1,0:T(8,128)(2,1)S(1)}, u32[]{:S(2)}, u32[]{:S(2)}) collective-permute-start(bf16[64,1024]{1,0:T(8,128)(2,1)S(1)} %advance1_0.1.refs_3_), channel_id=1, source_target_pairs={{16,20},{18,22},{17,21},{19,23}} | collective-permute-start | bytes 393224 | tf_op jit(solution)/shard_map/ppermute | solution.py:422
  15.2 0.7 %collective-permute-start.10 = (bf16[64,2048]{1,0:T(8,128)(2,1)S(1)}, bf16[64,2048]{1,0:T(8,128)(2,1)S(1)}, u32[]{:S(2)}, u32[]{:S(2)}) collective-permute-start(bf16[64,2048]{1,0:T(8,128)(2,1)S(1)} %get-tuple-element.45.refs_0_.refs_3_), channel_id=1, source_target_pairs={{24,26},{26,24},{25,27},{27,25}} | collective-permute-start | bytes 786440 | tf_op jit(solution)/shard_map/ppermute | solution.py:422
  15.9 0.0 collective-permute-done.8.refs_1_.refs_5_
  15.9 0.0 collective-permute-done.7.refs_2_.refs_1_
  16.0 0.7 %collective-permute-start.9 = (bf16[64,1024]{1,0:T(8,128)(2,1)S(1)}, bf16[64,1024]{1,0:T(8,128)(2,1)S(1)}, u32[]{:S(2)}, u32[]{:S(2)}) collective-permute-start(bf16[64,1024]{1,0:T(8,128)(2,1)S(1)} %advance1_1.1.after_ref), channel_id=1, source_target_pairs={{20,24},{22,26},{21,25},{23,27}} | collective-permute-start | bytes 393224 | tf_op jit(solution)/shard_map/ppermute | solution.py:422
  16.6 19.6 %collective-permute-done.13.h_ref.refs_11_ = bf16[128,2048]{1,0:T(8,128)(2,1)S(1)} collective-permute-done((bf16[128,2048]{1,0:T(8,128)(2,1)S(1)}, bf16[128,2048]{1,0:T(8,128)(2,1)S(1)}, u32[]{:S(2)}, u32[]{:S(2)}) %collective-permute-start.13) | collective-permute-done | bytes 524320 | tf_op jit(solution)/shard_map/ppermute | solution.py:488
  36.3 2.7 %later_front_3.1 = (bf16[64,2048]{1,0:T(8,128)(2,1)S(1)}, bf16[128,2048]{1,0:T(8,128)(2,1)S(1)}, bf16[128,1024]{1,0:T(8,128)(2,1)S(1)}, bf16[128,1024]{1,0:T(8,128)(2,1)S(1)}, bf16[128,1024]{1,0:T(8,128)(2,1)S(1)}) custom-call(bf16[128,2048]{1,0:T(8,128)(2,1)S(1)} %collective-permute-done.13.h_ref.refs_11_, f32[1,2048]{1,0:T(1,128)S(1)} %get-tuple-element.41.gain, ...), custom_call_target="tpu_custom_call" | custom-call | tf_op jit(solution)/shard_map/later_front_3/pallas_call | solution.py:393
  39.0 3.6 %collective-permute-start.14 = (bf16[64,2048]{1,0:T(8,128)(2,1)S(1)}, bf16[64,2048]{1,0:T(8,128)(2,1)S(1)}, u32[]{:S(2)}, u32[]{:S(2)}) collective-permute-start(bf16[64,2048]{1,0:T(8,128)(2,1)S(1)} %get-tuple-element.50), channel_id=1, source_target_pairs={{28,30},{30,28},{29,31},{31,29}} | collective-permute-start | bytes 786440 | tf_op jit(solution)/shard_map/ppermute | solution.py:422
  42.6 0.0 collective-permute-done.10.refs_1_.refs_6_
  42.6 0.0 collective-permute-done.9.refs_2_
  42.7 1.3 %collective-permute-start.11 = (bf16[64,1024]{1,0:T(8,128)(2,1)S(1)}, bf16[64,1024]{1,0:T(8,128)(2,1)S(1)}, u32[]{:S(2)}, u32[]{:S(2)}) collective-permute-start(bf16[64,1024]{1,0:T(8,128)(2,1)S(1)} %advance1_2.1.after_ref), channel_id=1, source_target_pairs={{24,28},{26,30},{25,29},{27,31}} | collective-permute-start | bytes 393224 | tf_op jit(solution)/shard_map/ppermute | solution.py:422
  44.0 2.1 %reads1_3.1.refs_9_ = bf16[128,2048]{1,0:T(8,128)(2,1)S(1)} custom-call(bf16[128,2048]{1,0:T(8,128)(2,1)S(1)} %get-tuple-element.51.normed_ref, bf16[128,1024]{1,0:T(8,128)(2,1)S(1)} %get-tuple-element.52.keys_ref, bf16[128,1024]{1,0:T(8,128)(2,1)S(1)} %get-tuple-element.53.x_ref, bf16[128,1024]{1,0:T(8,128)(2,1)S(1)} %get-tuple-element.54.y_ref, ...), custom_call_target="tpu_custom_call" | custom-call | tf_op jit(solution)/shard_map/reads1_3/pallas_call | solution.py:393
  46.1 2.3 %collective-permute-done.11.refs_3_ = bf16[64,1024]{1,0:T(8,128)(2,1)S(1)} collective-permute-done((bf16[64,1024]{1,0:T(8,128)(2,1)S(1)}, bf16[64,1024]{1,0:T(8,128)(2,1)S(1)}, u32[]{:S(2)}, u32[]{:S(2)}) %collective-permute-start.11) | collective-permute-done | bytes 131104 | tf_op jit(solution)/shard_map/ppermute | solution.py:422
  48.4 0.0 collective-permute-done.14.refs_7_
  48.4 1.7 %last_finish.1 = bf16[1,128,2048]{2,1,0:T(8,128)(2,1)} custom-call(bf16[1024,2048]{1,0:T(8,128)(2,1)S(1)} %bitcast.7, f32[1,16,64,64]{3,2,1,0:T(8,128)S(1)} %copy-done, bf16[64,1024]{1,0:T(8,128)(2,1)S(1)} %collective-permute-done.7.refs_2_.refs_1_, bf16[64,1024]{1,0:T(8,128)(2,1)S(1)} %collective-permute-done.9.refs_2_, ...), custom_call_target="tpu_custom_call" | custom-call | tf_op jit(solution)/shard_map/last_finish/pallas_call | solution.py:393
  (15 shorter events, 0.4 us)
Async XLA Ops:
  0.0 1.0 %copy-start = (f32[1,16,64,64]{3,2,1,0:T(8,128)S(1)}, f32[1,16,64,64]{3,2,1,0:T(8,128)}, u32[]{:S(2)}) copy-start(f32[1,16,64,64]{3,2,1,0:T(8,128)} %refs_0_.5) | copy-start | bytes 786436
  0.1 3.3 %collective-permute-start = (bf16[64,2048]{1,0:T(8,128)(2,1)S(1)}, bf16[64,2048]{1,0:T(8,128)(2,1)S(1)}, u32[]{:S(2)}, u32[]{:S(2)}) collective-permute-start(bf16[64,2048]{1,0:T(8,128)(2,1)S(1)} %get-tuple-element.30.own_ref.after_ref), channel_id=1, source_target_pairs={{4,6},{6,4},{8,10},{10,8},{12,14},{14,12},{5,7},{7,5},{9,11},{11,9... | collective-permute-start | bytes 786440 | tf_op jit(solution)/shard_map/ppermute | solution.py:422
  1.0 0.7 %collective-permute-start.1 = (bf16[64,1024]{1,0:T(8,128)(2,1)S(1)}, bf16[64,1024]{1,0:T(8,128)(2,1)S(1)}, u32[]{:S(2)}, u32[]{:S(2)}) collective-permute-start(bf16[64,1024]{1,0:T(8,128)(2,1)S(1)} %first_step.1), channel_id=1, source_target_pairs={{0,2},{1,3}} | collective-permute-start | bytes 393224 | tf_op jit(solution)/shard_map/ppermute | solution.py:422
  1.8 1.6 %copy-start.1 = (bf16[128,2048]{1,0:T(8,128)(2,1)S(1)}, bf16[128,2048]{1,0:T(8,128)(2,1)}, u32[]{:S(2)}) copy-start(bf16[128,2048]{1,0:T(8,128)(2,1)} %refs_4_.7) | copy-start | bytes 1572868
  1.8 1.6 %collective-permute-start.3 = (bf16[64,1024]{1,0:T(8,128)(2,1)S(1)}, bf16[64,1024]{1,0:T(8,128)(2,1)S(1)}, u32[]{:S(2)}, u32[]{:S(2)}) collective-permute-start(bf16[64,1024]{1,0:T(8,128)(2,1)S(1)} %second_step.1.after_ref.refs_5_), channel_id=1, source_target_pairs={{2,4},{3,5}} | collective-permute-start | bytes 393224 | tf_op jit(solution)/shard_map/ppermute | solution.py:422
  2.6 0.8 %collective-permute-start.2 = (bf16[64,1024]{1,0:T(8,128)(2,1)S(1)}, bf16[64,1024]{1,0:T(8,128)(2,1)S(1)}, u32[]{:S(2)}, u32[]{:S(2)}) collective-permute-start(bf16[64,1024]{1,0:T(8,128)(2,1)S(1)} %second_step.1.after_ref.refs_5_), channel_id=1, source_target_pairs={{2,6},{3,7}} | collective-permute-start | bytes 393224 | tf_op jit(solution)/shard_map/ppermute | solution.py:422
  3.5 0.7 %collective-permute-start.4 = (bf16[64,1024]{1,0:T(8,128)(2,1)S(1)}, bf16[64,1024]{1,0:T(8,128)(2,1)S(1)}, u32[]{:S(2)}, u32[]{:S(2)}) collective-permute-start(bf16[64,1024]{1,0:T(8,128)(2,1)S(1)} %advance0_1.1.refs_6_), channel_id=1, source_target_pairs={{4,8},{6,10},{5,9},{7,11}} | collective-permute-start | bytes 393224 | tf_op jit(solution)/shard_map/ppermute | solution.py:422
  4.3 8.6 %collective-permute-start.5 = (bf16[128,2048]{1,0:T(8,128)(2,1)S(1)}, bf16[128,2048]{1,0:T(8,128)(2,1)S(1)}, u32[]{:S(2)}, u32[]{:S(2)}) collective-permute-start(bf16[128,2048]{1,0:T(8,128)(2,1)S(1)} %first_finish_2.1.refs_12_), channel_id=1, source_target_pairs={{0,16},{2,18},{4,20},{6,22},{8,24},{10,26},{1,17},{3,19},{5,21},{7... | collective-permute-start | bytes 1572872 | tf_op jit(solution)/shard_map/ppermute | solution.py:488
  5.0 0.7 %collective-permute-start.12 = (bf16[64,1024]{1,0:T(8,128)(2,1)S(1)}, bf16[64,1024]{1,0:T(8,128)(2,1)S(1)}, u32[]{:S(2)}, u32[]{:S(2)}) collective-permute-start(bf16[64,1024]{1,0:T(8,128)(2,1)S(1)} %advance0_2.1.refs_5_), channel_id=1, source_target_pairs={{8,12},{10,14},{9,13},{11,15}} | collective-permute-start | bytes 393224 | tf_op jit(solution)/shard_map/ppermute | solution.py:422
  5.7 30.6 %collective-permute-start.13 = (bf16[128,2048]{1,0:T(8,128)(2,1)S(1)}, bf16[128,2048]{1,0:T(8,128)(2,1)S(1)}, u32[]{:S(2)}, u32[]{:S(2)}) collective-permute-start(bf16[128,2048]{1,0:T(8,128)(2,1)S(1)} %first_finish_3.1.refs_13_), channel_id=1, source_target_pairs={{12,28},{14,30},{13,29},{15,31}} | collective-permute-start | bytes 1572872 | tf_op jit(solution)/shard_map/ppermute | solution.py:488
  13.1 1.4 %collective-permute-start.6 = (bf16[64,2048]{1,0:T(8,128)(2,1)S(1)}, bf16[64,2048]{1,0:T(8,128)(2,1)S(1)}, u32[]{:S(2)}, u32[]{:S(2)}) collective-permute-start(bf16[64,2048]{1,0:T(8,128)(2,1)S(1)} %get-tuple-element.45.refs_0_.refs_3_), channel_id=1, source_target_pairs={{16,18},{18,16},{17,19},{19,17}} | collective-permute-start | bytes 786440 | tf_op jit(solution)/shard_map/ppermute | solution.py:422
  13.8 2.1 %collective-permute-start.8 = (bf16[64,2048]{1,0:T(8,128)(2,1)S(1)}, bf16[64,2048]{1,0:T(8,128)(2,1)S(1)}, u32[]{:S(2)}, u32[]{:S(2)}) collective-permute-start(bf16[64,2048]{1,0:T(8,128)(2,1)S(1)} %get-tuple-element.45.refs_0_.refs_3_), channel_id=1, source_target_pairs={{20,22},{22,20},{21,23},{23,21}} | collective-permute-start | bytes 786440 | tf_op jit(solution)/shard_map/ppermute | solution.py:422
  14.5 1.4 %collective-permute-start.7 = (bf16[64,1024]{1,0:T(8,128)(2,1)S(1)}, bf16[64,1024]{1,0:T(8,128)(2,1)S(1)}, u32[]{:S(2)}, u32[]{:S(2)}) collective-permute-start(bf16[64,1024]{1,0:T(8,128)(2,1)S(1)} %advance1_0.1.refs_3_), channel_id=1, source_target_pairs={{16,20},{18,22},{17,21},{19,23}} | collective-permute-start | bytes 393224 | tf_op jit(solution)/shard_map/ppermute | solution.py:422
  15.2 27.4 %collective-permute-start.10 = (bf16[64,2048]{1,0:T(8,128)(2,1)S(1)}, bf16[64,2048]{1,0:T(8,128)(2,1)S(1)}, u32[]{:S(2)}, u32[]{:S(2)}) collective-permute-start(bf16[64,2048]{1,0:T(8,128)(2,1)S(1)} %get-tuple-element.45.refs_0_.refs_3_), channel_id=1, source_target_pairs={{24,26},{26,24},{25,27},{27,25}} | collective-permute-start | bytes 786440 | tf_op jit(solution)/shard_map/ppermute | solution.py:422
  16.0 26.7 %collective-permute-start.9 = (bf16[64,1024]{1,0:T(8,128)(2,1)S(1)}, bf16[64,1024]{1,0:T(8,128)(2,1)S(1)}, u32[]{:S(2)}, u32[]{:S(2)}) collective-permute-start(bf16[64,1024]{1,0:T(8,128)(2,1)S(1)} %advance1_1.1.after_ref), channel_id=1, source_target_pairs={{20,24},{22,26},{21,25},{23,27}} | collective-permute-start | bytes 393224 | tf_op jit(solution)/shard_map/ppermute | solution.py:422
  39.0 9.4 %collective-permute-start.14 = (bf16[64,2048]{1,0:T(8,128)(2,1)S(1)}, bf16[64,2048]{1,0:T(8,128)(2,1)S(1)}, u32[]{:S(2)}, u32[]{:S(2)}) collective-permute-start(bf16[64,2048]{1,0:T(8,128)(2,1)S(1)} %get-tuple-element.50), channel_id=1, source_target_pairs={{28,30},{30,28},{29,31},{31,29}} | collective-permute-start | bytes 786440 | tf_op jit(solution)/shard_map/ppermute | solution.py:422
  42.7 5.7 %collective-permute-start.11 = (bf16[64,1024]{1,0:T(8,128)(2,1)S(1)}, bf16[64,1024]{1,0:T(8,128)(2,1)S(1)}, u32[]{:S(2)}, u32[]{:S(2)}) collective-permute-start(bf16[64,1024]{1,0:T(8,128)(2,1)S(1)} %advance1_2.1.after_ref), channel_id=1, source_target_pairs={{24,28},{26,30},{25,29},{27,31}} | collective-permute-start | bytes 393224 | tf_op jit(solution)/shard_map/ppermute | solution.py:422

commit v15 on v14

--- a/solution.py
+++ b/solution.py
@@ -102,57 +102,54 @@
 
     def body():
         if near is None:
-            groups, last = [], []
+            copies = None
             h_in, gain, w_rate, base, weights, base_lane = h_ref, gain_ref, w_rate_ref, base_ref, w_ref, width
         else:
-            wq, h_in, gain, w_rate, base, weights, small_sems, sems = near
+            h_in, gain, w_rate, base, weights, small_sems, sems = near
             base_lane = 0
             pairs = [(gain_ref, gain), (w_rate_ref, w_rate), (base_ref, base), (h_ref, h_in)]
             small = [pltpu.make_async_copy(source, target, small_sems.at[index]) for index, (source, target) in enumerate(pairs)]
-            half = wq.shape[1]
-            last = [pltpu.make_async_copy(w_ref.at[0, :, pl.ds(0, half)], wq, small_sems.at[len(pairs)])]
-            groups = [
+            copies = [
                 [
                     pltpu.make_async_copy(
                         w_ref.at[0, :, pl.ds((side + 1) * width + quad * QUAD, QUAD)],
                         weights.at[:, pl.ds(side * width + quad * QUAD, QUAD)],
                         sems.at[quad, side],
                     )
-                    for side in range(2)
+                    for quad in range(quads)
                 ]
-                for quad in range(quads)
+                for side in range(2)
             ]
             start_all(small)
-            start_all(groups[0])
+            start_all(copies[0][:1])
             wait_all(small)
-            for group in groups[1:]:
-                start_all(group)
+            start_all(copies[0][1:])
         normed = norm_rows(h_in[...], gain[...])
         normed_out[...] = normed
         rates = spread_rates(normed, w_rate[0], base[...])
         ones = head_ones()
 
-        def project(quad):
-            if groups:
-                wait_all(groups[quad])
-                if quad + 1 == quads:
-                    start_all(last)
-            key_lane = base_lane + quad * QUAD
-            return [mm(normed, weights[:, lane : lane + QUAD]) for lane in (key_lane, key_lane + width)]
-
-        def unit(quad, keys, values):
+        def project(side, quad):
+            if copies is not None:
+                wait_all([copies[side][quad]])
+                if side == 0:
+                    start_all([copies[1][quad]])
+            lane = base_lane + side * width + quad * QUAD
+            return mm(normed, weights[:, lane : lane + QUAD])
+
+        def unit(quad, keys):
             lanes = slice(quad * QUAD, (quad + 1) * QUAD)
             keys = unit_heads(keys, ones)
             keys_bf = keys.astype(BF16)
             keys_out[:, lanes] = keys_bf
-            rate = rates[:, lanes]
-            return keys_bf, rate * keys, rate * values
-
-        def crossed(quad, keys_bf, x_all, y_all):
+            return keys_bf, rates[:, lanes] * keys
+
+        def crossed(quad, keys_bf, x_all):
             return mm_nt(keys_bf[HD:], spread(keys_bf[:HD])).astype(BF16)
 
-        def fixed(quad, cross, keys_bf, x_all, y_all):
+        def fixed(quad, cross, values, keys_bf, x_all):
             lanes = slice(quad * QUAD, (quad + 1) * QUAD)
+            y_all = rates[:, lanes] * values
             rate = rates[HD:, lanes]
             x_first, y_first = x_all[:HD].astype(BF16), y_all[:HD].astype(BF16)
             fix = mm(cross, spread_two(x_first, y_first))
@@ -173,12 +170,12 @@
                 maps[:, width + start : width + start + PAIR] = diagonal(both[:, PAIR:]).astype(BF16)
 
         picked = range(quads)
-        units = [unit(quad, *value) for quad, value in zip(picked, [project(quad) for quad in picked])]
+        units = [unit(quad, keys) for quad, keys in zip(picked, [project(0, quad) for quad in picked])]
         crosses = [crossed(quad, *value) for quad, value in zip(picked, units)]
-        fixes = [fixed(quad, cross, *value) for quad, cross, value in zip(picked, crosses, units)]
+        values = [project(1, quad) for quad in picked]
+        fixes = [fixed(quad, cross, value, *pair) for quad, cross, value, pair in zip(picked, crosses, values, units)]
         for quad, value, fix in zip(picked, units, fixes):
             mapped(quad, value[0], *fix)
-        wait_all(last)
 
     pl.when(here)(body)
 
@@ -204,24 +201,25 @@
     on_section(1, body)
 
 
-def read_out(active, places, fetches, normed_ref, keys_ref, x_ref, y_ref, weights, w_hbm, w_out_hbm, after_ref, reads_out, *rest):
+def read_out(active, places, fetches, normed_ref, keys_ref, x_ref, y_ref, weights, w_out_hbm, after_ref, reads_out, *rest):
     rows, width = keys_ref.shape
     *w_out, wq, sems = rest
     half = width // 2
 
     def body():
-        late = [pltpu.make_async_copy(w_hbm.at[0, :, pl.ds(half, half)], wq, sems.at[0])] * fetches
-        fetch = [pltpu.make_async_copy(w_out_hbm.at[0], target, sems.at[1]) for target in w_out]
-        start_all(late + fetch)
+        fetch = [pltpu.make_async_copy(w_out_hbm.at[0], target, sems.at[2]) for target in w_out]
+        halves = [pl.ds(index * half, half) for index in range(2)] if fetches else []
+        late = [pltpu.make_async_copy(weights.at[0, :, lanes], wq.at[:, lanes], sems.at[index]) for index, lanes in enumerate(halves)]
+        start_all(late)
         normed = normed_ref[...]
         ones = head_ones()
         row = lax.broadcasted_iota(jnp.int32, (rows, 2 * rows), 0)
         lane = lax.rem(lax.broadcasted_iota(jnp.int32, (rows, 2 * rows), 1), rows)
         causal = row >= lane
 
-        def stages(start, stop, source, base):
+        def stages(start, stop, source):
             quads = range(start, stop, QUAD)
-            queries = [unit_heads(mm(normed, source[:, lane - base : lane - base + QUAD]), ones) for lane in quads]
+            queries = [unit_heads(mm(normed, source[:, lane : lane + QUAD]), ones) for lane in quads]
             parts = [value[:, own : own + PAIR] for value in queries for own in range(0, QUAD, PAIR)]
             places = [slice(lane, lane + PAIR) for lane in range(start, stop, PAIR)]
             scores = [mm_nt(part.astype(BF16), spread(keys_ref[:, place])) for part, place in zip(parts, places)]
@@ -232,12 +230,14 @@
                 reads_out[:, width + place.start : width + place.stop] = value[:, PAIR:].astype(BF16)
 
         if fetches:
-            stages(0, half, weights, 0)
-            wait_all(late)
-            stages(half, width, wq, half)
+            wait_all(late[:1])
+            start_all(fetch)
+            stages(0, half, wq)
+            wait_all(late[1:])
+            stages(half, width, wq)
             wait_all(fetch)
         else:
-            stages(0, width, weights, 0)
+            stages(0, width, weights)
 
     pl.when(at_pair(places, active))(body)
 
@@ -428,9 +428,9 @@
         reads, *w_out_near = call(
             functools.partial(read_out, active, places, fetches),
             [shape((rows, 2 * width), BF16)] + [pltpu.VMEM(w_out.shape[1:], BF16)] * fetches,
-            [pltpu.VMEM((depth, width // 2), BF16) if fetches else pltpu.VMEM((16, 128), BF16), pltpu.SemaphoreType.DMA((2,))],
-            [*rows_of, weights, w_qkv, w_out, after],
-            [pltpu.VMEM] * 5 + [pltpu.HBM, pltpu.HBM, pl.ANY],
+            [pltpu.VMEM((depth, width) if fetches else (16, 128), BF16), pltpu.SemaphoreType.DMA((3,))],
+            [*rows_of, weights, w_out, after],
+            [pltpu.VMEM] * 4 + [pltpu.HBM if fetches else pltpu.VMEM, pltpu.HBM, pl.ANY],
             name=f"reads{active}_{places[0]}",
         )
         return [reads] + [in_vmem(value) for value in w_out_near]
@@ -448,25 +448,24 @@
     state_out = shape((HD, width), BF16)
     groups = count // 2
 
-    own, *rows_of, wq_near = call(
+    own, *rows_of = call(
         first_front,
-        [maps] + rows_out + [pltpu.VMEM((depth, width // 2), BF16)],
+        [maps] + rows_out,
         [pltpu.VMEM(value.shape, value.dtype) for value in (tokens, norm_gain, w_rate, rate_base)]
-        + [pltpu.VMEM((depth, 2 * width), BF16), pltpu.SemaphoreType.DMA((5,)), pltpu.SemaphoreType.DMA((quads, 2))],
+        + [pltpu.VMEM((depth, 2 * width), BF16), pltpu.SemaphoreType.DMA((4,)), pltpu.SemaphoreType.DMA((quads, 2))],
         [in_hbm(tokens), norm_gain, w_qkv, w_rate, rate_base],
         [pltpu.HBM] * 5,
         name="first_front",
     )
-    wq_near = in_vmem(wq_near)
     (stepped,) = call(first_step, [state_out], [], [own, init_state], name="first_step")
     stepped = permute(stepped, 0, [(0, 1)])
     got_rest = swap(own, 0, range(1, groups))
-    read_first = layer_reads(0, [0], 1, rows_of, wq_near, init_state)
+    read_first = layer_reads(0, [0], 1, rows_of, w_qkv, init_state)
     (ahead,) = call(
         second_step, [state_out], [], [own, stepped, read_first[0]], [pltpu.VMEM] * 2 + [pl.ANY], name="second_step"
     )
     state = [permute(ahead, 0, [(1, 2 + side)]) for side in range(2)]
-    read_rest = layer_reads(0, range(1, groups), 1, rows_of, wq_near, ahead)
+    read_rest = layer_reads(0, range(1, groups), 1, rows_of, w_qkv, ahead)
     (both,) = call(
         functools.partial(compose, 0), [maps], [], [own, got_rest, read_rest[0]], [pltpu.VMEM] * 2 + [pl.ANY], name="compose"
     )

time: 50.6 us -> 50.8 us (level)
  no operation moved by 1% of the time
where the time goes in v15:
time: 50.8 us; the launch traced here: 50.5 us
  waiting for transfers between devices  22.1 us (44%)
  starting transfers between devices  14.5 us (29%)
  Pallas kernels  13.3 us (26%)
  between operations  0.54 us (1%)
    ppermute x2, waiting for transfers between devices, begin(): lax.ppermute(first, ('section', 'seq'), [(place, count + place) for place...  19.7 us
    pallas_call x21, Pallas kernels, call(): pl.pallas_call(body, out_shape=outs, in_specs=specs, out_specs=[pl.BlockS...  13.3 us
    ppermute x13, starting transfers between devices, permute(): lax.ppermute(value, ('section', 'seq'), [(base + source, base + target) f...  12.5 us
    ppermute x13, waiting for transfers between devices, permute(): lax.ppermute(value, ('section', 'seq'), [(base + source, base + target) f...  2.36 us
    ppermute x2, starting transfers between devices, begin(): lax.ppermute(first, ('section', 'seq'), [(place, count + place) for place...  1.99 us
  transfers between devices with their start and end apart: 15, of which 2 were waited for; matrix products, arithmetic and copies ran while one was open for 0% of the time, Pallas kernels for 22%

profile of v15, /device:TPU:25, one launch (start us, length us, event | category | flops | bytes accessed | tf_op | source)
XLA Modules:
  0.0 50.5 jit_solution(6778375011757483010)
XLA Ops:
  0.0 0.0 copy-start
  0.0 0.1 first_front.1
  0.1 0.8 %collective-permute-start = (bf16[64,2048]{1,0:T(8,128)(2,1)S(1)}, bf16[64,2048]{1,0:T(8,128)(2,1)S(1)}, u32[]{:S(2)}, u32[]{:S(2)}) collective-permute-start(bf16[64,2048]{1,0:T(8,128)(2,1)S(1)} %get-tuple-element.29.own_ref.after_ref), channel_id=1, source_target_pairs={{4,6},{6,4},{8,10},{10,8},{12,14},{14,12},{5,7},{7,5},{9,11},{11,9... | collective-permute-start | bytes 786440 | tf_op jit(solution)/shard_map/ppermute | solution.py:422
  0.9 0.1 copy-done
  1.0 0.7 %collective-permute-start.1 = (bf16[64,1024]{1,0:T(8,128)(2,1)S(1)}, bf16[64,1024]{1,0:T(8,128)(2,1)S(1)}, u32[]{:S(2)}, u32[]{:S(2)}) collective-permute-start(bf16[64,1024]{1,0:T(8,128)(2,1)S(1)} %first_step.1), channel_id=1, source_target_pairs={{0,2},{1,3}} | collective-permute-start | bytes 393224 | tf_op jit(solution)/shard_map/ppermute | solution.py:422
  1.7 0.1 reads0_0.1
  1.8 0.0 collective-permute-done.1.state_ref.refs_1_
  1.8 0.0 copy-start.1
  1.8 0.8 %collective-permute-start.3 = (bf16[64,1024]{1,0:T(8,128)(2,1)S(1)}, bf16[64,1024]{1,0:T(8,128)(2,1)S(1)}, u32[]{:S(2)}, u32[]{:S(2)}) collective-permute-start(bf16[64,1024]{1,0:T(8,128)(2,1)S(1)} %second_step.1.after_ref.refs_5_), channel_id=1, source_target_pairs={{2,4},{3,5}} | collective-permute-start | bytes 393224 | tf_op jit(solution)/shard_map/ppermute | solution.py:422
  2.6 0.7 %collective-permute-start.2 = (bf16[64,1024]{1,0:T(8,128)(2,1)S(1)}, bf16[64,1024]{1,0:T(8,128)(2,1)S(1)}, u32[]{:S(2)}, u32[]{:S(2)}) collective-permute-start(bf16[64,1024]{1,0:T(8,128)(2,1)S(1)} %second_step.1.after_ref.refs_5_), channel_id=1, source_target_pairs={{2,6},{3,7}} | collective-permute-start | bytes 393224 | tf_op jit(solution)/shard_map/ppermute | solution.py:422
  3.3 0.1 reads0_1.1
  3.4 0.0 copy-done.1
  3.4 0.0 collective-permute-done.got_ref.refs_2_.refs_1_
  3.4 0.0 collective-permute-done.3.refs_2_.refs_1_
  3.5 0.0 collective-permute-done.2.refs_1_.refs_0_
  3.5 0.7 %collective-permute-start.4 = (bf16[64,1024]{1,0:T(8,128)(2,1)S(1)}, bf16[64,1024]{1,0:T(8,128)(2,1)S(1)}, u32[]{:S(2)}, u32[]{:S(2)}) collective-permute-start(bf16[64,1024]{1,0:T(8,128)(2,1)S(1)} %advance0_1.1.refs_6_), channel_id=1, source_target_pairs={{4,8},{6,10},{5,9},{7,11}} | collective-permute-start | bytes 393224 | tf_op jit(solution)/shard_map/ppermute | solution.py:422
  4.2 0.0 collective-permute-done.4.refs_1_.refs_0_
  4.3 0.7 %collective-permute-start.5 = (bf16[128,2048]{1,0:T(8,128)(2,1)S(1)}, bf16[128,2048]{1,0:T(8,128)(2,1)S(1)}, u32[]{:S(2)}, u32[]{:S(2)}) collective-permute-start(bf16[128,2048]{1,0:T(8,128)(2,1)S(1)} %first_finish_2.1.refs_12_), channel_id=1, source_target_pairs={{0,16},{2,18},{4,20},{6,22},{8,24},{10,26},{1,17},{3,19},{5,21},{7... | collective-permute-start | bytes 1572872 | tf_op jit(solution)/shard_map/ppermute | solution.py:487
  5.0 0.7 %collective-permute-start.12 = (bf16[64,1024]{1,0:T(8,128)(2,1)S(1)}, bf16[64,1024]{1,0:T(8,128)(2,1)S(1)}, u32[]{:S(2)}, u32[]{:S(2)}) collective-permute-start(bf16[64,1024]{1,0:T(8,128)(2,1)S(1)} %advance0_2.1.refs_5_), channel_id=1, source_target_pairs={{8,12},{10,14},{9,13},{11,15}} | collective-permute-start | bytes 393224 | tf_op jit(solution)/shard_map/ppermute | solution.py:422
  5.7 0.0 collective-permute-done.12.refs_0_
  5.7 1.3 %collective-permute-start.13 = (bf16[128,2048]{1,0:T(8,128)(2,1)S(1)}, bf16[128,2048]{1,0:T(8,128)(2,1)S(1)}, u32[]{:S(2)}, u32[]{:S(2)}) collective-permute-start(bf16[128,2048]{1,0:T(8,128)(2,1)S(1)} %first_finish_3.1.refs_13_), channel_id=1, source_target_pairs={{12,28},{14,30},{13,29},{15,31}} | collective-permute-start | bytes 1572872 | tf_op jit(solution)/shard_map/ppermute | solution.py:487
  7.0 5.9 %load.1 = (f32[1,2048]{1,0:T(1,128)S(1)}, bf16[1,2048,3072]{2,1,0:T(8,128)(2,1)S(1)}, bf16[1,16,2048]{2,1,0:T(8,128)(2,1)S(1)}, f32[1,16]{1,0:T(1,128)S(1)}, bf16[1,1024,2048]{2,1,0:T(8,128)(2,1)S(1)}) custom-call(f32[1,2048]{1,0:T(1,128)} %refs_0_.3, bf16[1,2048,3072]{2,1,0:T(8,128)(2,1)} %refs_1_.1, bf16[1,16,2048]{2,1,0:T(8,128)(2,1)} %bitcast.9, ...), custom_call_target="tpu_custom_call" | custom-call | tf_op jit(solution)/shard_map/load/pallas_call | solution.py:393
  12.9 0.0 collective-permute-done.5.h_ref.refs_10_
  12.9 0.2 later_front_0.1
  13.1 0.7 %collective-permute-start.6 = (bf16[64,2048]{1,0:T(8,128)(2,1)S(1)}, bf16[64,2048]{1,0:T(8,128)(2,1)S(1)}, u32[]{:S(2)}, u32[]{:S(2)}) collective-permute-start(bf16[64,2048]{1,0:T(8,128)(2,1)S(1)} %get-tuple-element.43.refs_0_.refs_3_), channel_id=1, source_target_pairs={{16,18},{18,16},{17,19},{19,17}} | collective-permute-start | bytes 786440 | tf_op jit(solution)/shard_map/ppermute | solution.py:422
  13.8 0.7 %collective-permute-start.8 = (bf16[64,2048]{1,0:T(8,128)(2,1)S(1)}, bf16[64,2048]{1,0:T(8,128)(2,1)S(1)}, u32[]{:S(2)}, u32[]{:S(2)}) collective-permute-start(bf16[64,2048]{1,0:T(8,128)(2,1)S(1)} %get-tuple-element.43.refs_0_.refs_3_), channel_id=1, source_target_pairs={{20,22},{22,20},{21,23},{23,21}} | collective-permute-start | bytes 786440 | tf_op jit(solution)/shard_map/ppermute | solution.py:422
  14.5 0.0 collective-permute-done.6.refs_1_.refs_4_
  14.5 0.7 %collective-permute-start.7 = (bf16[64,1024]{1,0:T(8,128)(2,1)S(1)}, bf16[64,1024]{1,0:T(8,128)(2,1)S(1)}, u32[]{:S(2)}, u32[]{:S(2)}) collective-permute-start(bf16[64,1024]{1,0:T(8,128)(2,1)S(1)} %advance1_0.1.refs_3_), channel_id=1, source_target_pairs={{16,20},{18,22},{17,21},{19,23}} | collective-permute-start | bytes 393224 | tf_op jit(solution)/shard_map/ppermute | solution.py:422
  15.2 0.7 %collective-permute-start.10 = (bf16[64,2048]{1,0:T(8,128)(2,1)S(1)}, bf16[64,2048]{1,0:T(8,128)(2,1)S(1)}, u32[]{:S(2)}, u32[]{:S(2)}) collective-permute-start(bf16[64,2048]{1,0:T(8,128)(2,1)S(1)} %get-tuple-element.43.refs_0_.refs_3_), channel_id=1, source_target_pairs={{24,26},{26,24},{25,27},{27,25}} | collective-permute-start | bytes 786440 | tf_op jit(solution)/shard_map/ppermute | solution.py:422
  15.9 0.0 collective-permute-done.8.refs_1_.refs_5_
  15.9 0.0 collective-permute-done.7.refs_2_.refs_1_
  16.0 0.7 %collective-permute-start.9 = (bf16[64,1024]{1,0:T(8,128)(2,1)S(1)}, bf16[64,1024]{1,0:T(8,128)(2,1)S(1)}, u32[]{:S(2)}, u32[]{:S(2)}) collective-permute-start(bf16[64,1024]{1,0:T(8,128)(2,1)S(1)} %advance1_1.1.after_ref), channel_id=1, source_target_pairs={{20,24},{22,26},{21,25},{23,27}} | collective-permute-start | bytes 393224 | tf_op jit(solution)/shard_map/ppermute | solution.py:422
  16.6 19.7 %collective-permute-done.13.h_ref.refs_11_ = bf16[128,2048]{1,0:T(8,128)(2,1)S(1)} collective-permute-done((bf16[128,2048]{1,0:T(8,128)(2,1)S(1)}, bf16[128,2048]{1,0:T(8,128)(2,1)S(1)}, u32[]{:S(2)}, u32[]{:S(2)}) %collective-permute-start.13) | collective-permute-done | bytes 524320 | tf_op jit(solution)/shard_map/ppermute | solution.py:487
  36.4 2.8 %later_front_3.1 = (bf16[64,2048]{1,0:T(8,128)(2,1)S(1)}, bf16[128,2048]{1,0:T(8,128)(2,1)S(1)}, bf16[128,1024]{1,0:T(8,128)(2,1)S(1)}, bf16[128,1024]{1,0:T(8,128)(2,1)S(1)}, bf16[128,1024]{1,0:T(8,128)(2,1)S(1)}) custom-call(bf16[128,2048]{1,0:T(8,128)(2,1)S(1)} %collective-permute-done.13.h_ref.refs_11_, f32[1,2048]{1,0:T(1,128)S(1)} %get-tuple-element.39.gain, ...), custom_call_target="tpu_custom_call" | custom-call | tf_op jit(solution)/shard_map/later_front_3/pallas_call | solution.py:393
  39.2 3.6 %collective-permute-start.14 = (bf16[64,2048]{1,0:T(8,128)(2,1)S(1)}, bf16[64,2048]{1,0:T(8,128)(2,1)S(1)}, u32[]{:S(2)}, u32[]{:S(2)}) collective-permute-start(bf16[64,2048]{1,0:T(8,128)(2,1)S(1)} %get-tuple-element.48), channel_id=1, source_target_pairs={{28,30},{30,28},{29,31},{31,29}} | collective-permute-start | bytes 786440 | tf_op jit(solution)/shard_map/ppermute | solution.py:422
  42.8 0.1 reads1_0.1.refs_3_.refs_8_
  42.8 0.0 collective-permute-done.10.refs_1_.refs_6_
  42.8 0.0 collective-permute-done.9.refs_2_
  42.9 1.3 %collective-permute-start.11 = (bf16[64,1024]{1,0:T(8,128)(2,1)S(1)}, bf16[64,1024]{1,0:T(8,128)(2,1)S(1)}, u32[]{:S(2)}, u32[]{:S(2)}) collective-permute-start(bf16[64,1024]{1,0:T(8,128)(2,1)S(1)} %advance1_2.1.after_ref), channel_id=1, source_target_pairs={{24,28},{26,30},{25,29},{27,31}} | collective-permute-start | bytes 393224 | tf_op jit(solution)/shard_map/ppermute | solution.py:422
  44.2 2.1 %reads1_3.1.refs_9_ = bf16[128,2048]{1,0:T(8,128)(2,1)S(1)} custom-call(bf16[128,2048]{1,0:T(8,128)(2,1)S(1)} %get-tuple-element.49.normed_ref, bf16[128,1024]{1,0:T(8,128)(2,1)S(1)} %get-tuple-element.50.keys_ref, bf16[128,1024]{1,0:T(8,128)(2,1)S(1)} %get-tuple-element.51.x_ref, bf16[128,1024]{1,0:T(8,128)(2,1)S(1)} %get-tuple-element.52.y_ref, ...), custom_call_target="tpu_custom_call" | custom-call | tf_op jit(solution)/shard_map/reads1_3/pallas_call | solution.py:393
  46.3 2.3 %collective-permute-done.11.refs_3_ = bf16[64,1024]{1,0:T(8,128)(2,1)S(1)} collective-permute-done((bf16[64,1024]{1,0:T(8,128)(2,1)S(1)}, bf16[64,1024]{1,0:T(8,128)(2,1)S(1)}, u32[]{:S(2)}, u32[]{:S(2)}) %collective-permute-start.11) | collective-permute-done | bytes 131104 | tf_op jit(solution)/shard_map/ppermute | solution.py:422
  48.6 0.0 collective-permute-done.14.refs_7_
  48.6 1.7 %last_finish.1 = bf16[1,128,2048]{2,1,0:T(8,128)(2,1)} custom-call(bf16[1024,2048]{1,0:T(8,128)(2,1)S(1)} %bitcast.7, f32[1,16,64,64]{3,2,1,0:T(8,128)S(1)} %copy-done, bf16[64,1024]{1,0:T(8,128)(2,1)S(1)} %collective-permute-done.7.refs_2_.refs_1_, bf16[64,1024]{1,0:T(8,128)(2,1)S(1)} %collective-permute-done.9.refs_2_, ...), custom_call_target="tpu_custom_call" | custom-call | tf_op jit(solution)/shard_map/last_finish/pallas_call | solution.py:393
  (12 shorter events, 0.3 us)
Async XLA Ops:
  0.0 1.0 %copy-start = (f32[1,16,64,64]{3,2,1,0:T(8,128)S(1)}, f32[1,16,64,64]{3,2,1,0:T(8,128)}, u32[]{:S(2)}) copy-start(f32[1,16,64,64]{3,2,1,0:T(8,128)} %refs_0_.5) | copy-start | bytes 786436
  0.1 3.3 %collective-permute-start = (bf16[64,2048]{1,0:T(8,128)(2,1)S(1)}, bf16[64,2048]{1,0:T(8,128)(2,1)S(1)}, u32[]{:S(2)}, u32[]{:S(2)}) collective-permute-start(bf16[64,2048]{1,0:T(8,128)(2,1)S(1)} %get-tuple-element.29.own_ref.after_ref), channel_id=1, source_target_pairs={{4,6},{6,4},{8,10},{10,8},{12,14},{14,12},{5,7},{7,5},{9,11},{11,9... | collective-permute-start | bytes 786440 | tf_op jit(solution)/shard_map/ppermute | solution.py:422
  1.0 0.7 %collective-permute-start.1 = (bf16[64,1024]{1,0:T(8,128)(2,1)S(1)}, bf16[64,1024]{1,0:T(8,128)(2,1)S(1)}, u32[]{:S(2)}, u32[]{:S(2)}) collective-permute-start(bf16[64,1024]{1,0:T(8,128)(2,1)S(1)} %first_step.1), channel_id=1, source_target_pairs={{0,2},{1,3}} | collective-permute-start | bytes 393224 | tf_op jit(solution)/shard_map/ppermute | solution.py:422
  1.8 1.6 %copy-start.1 = (bf16[128,2048]{1,0:T(8,128)(2,1)S(1)}, bf16[128,2048]{1,0:T(8,128)(2,1)}, u32[]{:S(2)}) copy-start(bf16[128,2048]{1,0:T(8,128)(2,1)} %refs_4_.7) | copy-start | bytes 1572868
  1.8 1.6 %collective-permute-start.3 = (bf16[64,1024]{1,0:T(8,128)(2,1)S(1)}, bf16[64,1024]{1,0:T(8,128)(2,1)S(1)}, u32[]{:S(2)}, u32[]{:S(2)}) collective-permute-start(bf16[64,1024]{1,0:T(8,128)(2,1)S(1)} %second_step.1.after_ref.refs_5_), channel_id=1, source_target_pairs={{2,4},{3,5}} | collective-permute-start | bytes 393224 | tf_op jit(solution)/shard_map/ppermute | solution.py:422
  2.6 0.8 %collective-permute-start.2 = (bf16[64,1024]{1,0:T(8,128)(2,1)S(1)}, bf16[64,1024]{1,0:T(8,128)(2,1)S(1)}, u32[]{:S(2)}, u32[]{:S(2)}) collective-permute-start(bf16[64,1024]{1,0:T(8,128)(2,1)S(1)} %second_step.1.after_ref.refs_5_), channel_id=1, source_target_pairs={{2,6},{3,7}} | collective-permute-start | bytes 393224 | tf_op jit(solution)/shard_map/ppermute | solution.py:422
  3.5 0.7 %collective-permute-start.4 = (bf16[64,1024]{1,0:T(8,128)(2,1)S(1)}, bf16[64,1024]{1,0:T(8,128)(2,1)S(1)}, u32[]{:S(2)}, u32[]{:S(2)}) collective-permute-start(bf16[64,1024]{1,0:T(8,128)(2,1)S(1)} %advance0_1.1.refs_6_), channel_id=1, source_target_pairs={{4,8},{6,10},{5,9},{7,11}} | collective-permute-start | bytes 393224 | tf_op jit(solution)/shard_map/ppermute | solution.py:422
  4.3 8.6 %collective-permute-start.5 = (bf16[128,2048]{1,0:T(8,128)(2,1)S(1)}, bf16[128,2048]{1,0:T(8,128)(2,1)S(1)}, u32[]{:S(2)}, u32[]{:S(2)}) collective-permute-start(bf16[128,2048]{1,0:T(8,128)(2,1)S(1)} %first_finish_2.1.refs_12_), channel_id=1, source_target_pairs={{0,16},{2,18},{4,20},{6,22},{8,24},{10,26},{1,17},{3,19},{5,21},{7... | collective-permute-start | bytes 1572872 | tf_op jit(solution)/shard_map/ppermute | solution.py:487
  5.0 0.7 %collective-permute-start.12 = (bf16[64,1024]{1,0:T(8,128)(2,1)S(1)}, bf16[64,1024]{1,0:T(8,128)(2,1)S(1)}, u32[]{:S(2)}, u32[]{:S(2)}) collective-permute-start(bf16[64,1024]{1,0:T(8,128)(2,1)S(1)} %advance0_2.1.refs_5_), channel_id=1, source_target_pairs={{8,12},{10,14},{9,13},{11,15}} | collective-permute-start | bytes 393224 | tf_op jit(solution)/shard_map/ppermute | solution.py:422
  5.7 30.7 %collective-permute-start.13 = (bf16[128,2048]{1,0:T(8,128)(2,1)S(1)}, bf16[128,2048]{1,0:T(8,128)(2,1)S(1)}, u32[]{:S(2)}, u32[]{:S(2)}) collective-permute-start(bf16[128,2048]{1,0:T(8,128)(2,1)S(1)} %first_finish_3.1.refs_13_), channel_id=1, source_target_pairs={{12,28},{14,30},{13,29},{15,31}} | collective-permute-start | bytes 1572872 | tf_op jit(solution)/shard_map/ppermute | solution.py:487
  13.1 1.4 %collective-permute-start.6 = (bf16[64,2048]{1,0:T(8,128)(2,1)S(1)}, bf16[64,2048]{1,0:T(8,128)(2,1)S(1)}, u32[]{:S(2)}, u32[]{:S(2)}) collective-permute-start(bf16[64,2048]{1,0:T(8,128)(2,1)S(1)} %get-tuple-element.43.refs_0_.refs_3_), channel_id=1, source_target_pairs={{16,18},{18,16},{17,19},{19,17}} | collective-permute-start | bytes 786440 | tf_op jit(solution)/shard_map/ppermute | solution.py:422
  13.8 2.1 %collective-permute-start.8 = (bf16[64,2048]{1,0:T(8,128)(2,1)S(1)}, bf16[64,2048]{1,0:T(8,128)(2,1)S(1)}, u32[]{:S(2)}, u32[]{:S(2)}) collective-permute-start(bf16[64,2048]{1,0:T(8,128)(2,1)S(1)} %get-tuple-element.43.refs_0_.refs_3_), channel_id=1, source_target_pairs={{20,22},{22,20},{21,23},{23,21}} | collective-permute-start | bytes 786440 | tf_op jit(solution)/shard_map/ppermute | solution.py:422
  14.5 1.4 %collective-permute-start.7 = (bf16[64,1024]{1,0:T(8,128)(2,1)S(1)}, bf16[64,1024]{1,0:T(8,128)(2,1)S(1)}, u32[]{:S(2)}, u32[]{:S(2)}) collective-permute-start(bf16[64,1024]{1,0:T(8,128)(2,1)S(1)} %advance1_0.1.refs_3_), channel_id=1, source_target_pairs={{16,20},{18,22},{17,21},{19,23}} | collective-permute-start | bytes 393224 | tf_op jit(solution)/shard_map/ppermute | solution.py:422
  15.2 27.6 %collective-permute-start.10 = (bf16[64,2048]{1,0:T(8,128)(2,1)S(1)}, bf16[64,2048]{1,0:T(8,128)(2,1)S(1)}, u32[]{:S(2)}, u32[]{:S(2)}) collective-permute-start(bf16[64,2048]{1,0:T(8,128)(2,1)S(1)} %get-tuple-element.43.refs_0_.refs_3_), channel_id=1, source_target_pairs={{24,26},{26,24},{25,27},{27,25}} | collective-permute-start | bytes 786440 | tf_op jit(solution)/shard_map/ppermute | solution.py:422
  16.0 26.9 %collective-permute-start.9 = (bf16[64,1024]{1,0:T(8,128)(2,1)S(1)}, bf16[64,1024]{1,0:T(8,128)(2,1)S(1)}, u32[]{:S(2)}, u32[]{:S(2)}) collective-permute-start(bf16[64,1024]{1,0:T(8,128)(2,1)S(1)} %advance1_1.1.after_ref), channel_id=1, source_target_pairs={{20,24},{22,26},{21,25},{23,27}} | collective-permute-start | bytes 393224 | tf_op jit(solution)/shard_map/ppermute | solution.py:422
  39.2 9.4 %collective-permute-start.14 = (bf16[64,2048]{1,0:T(8,128)(2,1)S(1)}, bf16[64,2048]{1,0:T(8,128)(2,1)S(1)}, u32[]{:S(2)}, u32[]{:S(2)}) collective-permute-start(bf16[64,2048]{1,0:T(8,128)(2,1)S(1)} %get-tuple-element.48), channel_id=1, source_target_pairs={{28,30},{30,28},{29,31},{31,29}} | collective-permute-start | bytes 786440 | tf_op jit(solution)/shard_map/ppermute | solution.py:422
  42.9 5.7 %collective-permute-start.11 = (bf16[64,1024]{1,0:T(8,128)(2,1)S(1)}, bf16[64,1024]{1,0:T(8,128)(2,1)S(1)}, u32[]{:S(2)}, u32[]{:S(2)}) collective-permute-start(bf16[64,1024]{1,0:T(8,128)(2,1)S(1)} %advance1_2.1.after_ref), channel_id=1, source_target_pairs={{24,28},{26,30},{25,29},{27,31}} | collective-permute-start | bytes 393224 | tf_op jit(solution)/shard_map/ppermute | solution.py:422

commit v16 on v15

--- a/solution.py
+++ b/solution.py
@@ -121,19 +121,21 @@
                 for side in range(2)
             ]
             start_all(small)
-            start_all(copies[0][:1])
+            start_all(copies[0][:2])
             wait_all(small)
-            start_all(copies[0][1:])
+            start_all(copies[0][2:])
         normed = norm_rows(h_in[...], gain[...])
         normed_out[...] = normed
+        if copies is not None:
+            start_all(copies[1][:2])
         rates = spread_rates(normed, w_rate[0], base[...])
         ones = head_ones()
 
         def project(side, quad):
             if copies is not None:
                 wait_all([copies[side][quad]])
-                if side == 0:
-                    start_all([copies[1][quad]])
+                if (side, quad) == (0, 1):
+                    start_all(copies[1][2:])
             lane = base_lane + side * width + quad * QUAD
             return mm(normed, weights[:, lane : lane + QUAD])
 

time: 50.8 us -> 51.1 us (level)
  no operation moved by 1% of the time
where the time goes in v16:
time: 51.1 us; the launch traced here: 50.8 us
  waiting for transfers between devices  22.4 us (44%)
  starting transfers between devices  14.5 us (28%)
  Pallas kernels  13.3 us (26%)
  between operations  0.54 us (1%)
    ppermute x2, waiting for transfers between devices, begin(): lax.ppermute(first, ('section', 'seq'), [(place, count + place) for place...  20.1 us
    pallas_call x21, Pallas kernels, call(): pl.pallas_call(body, out_shape=outs, in_specs=specs, out_specs=[pl.BlockS...  13.3 us
    ppermute x13, starting transfers between devices, permute(): lax.ppermute(value, ('section', 'seq'), [(base + source, base + target) f...  12.5 us
    ppermute x13, waiting for transfers between devices, permute(): lax.ppermute(value, ('section', 'seq'), [(base + source, base + target) f...  2.36 us
    ppermute x2, starting transfers between devices, begin(): lax.ppermute(first, ('section', 'seq'), [(place, count + place) for place...  1.99 us
  transfers between devices with their start and end apart: 15, of which 2 were waited for; matrix products, arithmetic and copies ran while one was open for 0% of the time, Pallas kernels for 22%

profile of v16, /device:TPU:25, one launch (start us, length us, event | category | flops | bytes accessed | tf_op | source)
XLA Modules:
  0.0 50.8 jit_solution(11093408835216937525)
XLA Ops:
  0.0 0.0 copy-start
  0.0 0.1 first_front.1
  0.1 0.8 %collective-permute-start = (bf16[64,2048]{1,0:T(8,128)(2,1)S(1)}, bf16[64,2048]{1,0:T(8,128)(2,1)S(1)}, u32[]{:S(2)}, u32[]{:S(2)}) collective-permute-start(bf16[64,2048]{1,0:T(8,128)(2,1)S(1)} %get-tuple-element.29.own_ref.after_ref), channel_id=1, source_target_pairs={{4,6},{6,4},{8,10},{10,8},{12,14},{14,12},{5,7},{7,5},{9,11},{11,9... | collective-permute-start | bytes 786440 | tf_op jit(solution)/shard_map/ppermute | solution.py:424
  0.9 0.1 copy-done
  1.0 0.7 %collective-permute-start.1 = (bf16[64,1024]{1,0:T(8,128)(2,1)S(1)}, bf16[64,1024]{1,0:T(8,128)(2,1)S(1)}, u32[]{:S(2)}, u32[]{:S(2)}) collective-permute-start(bf16[64,1024]{1,0:T(8,128)(2,1)S(1)} %first_step.1), channel_id=1, source_target_pairs={{0,2},{1,3}} | collective-permute-start | bytes 393224 | tf_op jit(solution)/shard_map/ppermute | solution.py:424
  1.7 0.1 reads0_0.1
  1.8 0.0 collective-permute-done.1.state_ref.refs_1_
  1.8 0.0 copy-start.1
  1.8 0.8 %collective-permute-start.3 = (bf16[64,1024]{1,0:T(8,128)(2,1)S(1)}, bf16[64,1024]{1,0:T(8,128)(2,1)S(1)}, u32[]{:S(2)}, u32[]{:S(2)}) collective-permute-start(bf16[64,1024]{1,0:T(8,128)(2,1)S(1)} %second_step.1.after_ref.refs_5_), channel_id=1, source_target_pairs={{2,4},{3,5}} | collective-permute-start | bytes 393224 | tf_op jit(solution)/shard_map/ppermute | solution.py:424
  2.6 0.7 %collective-permute-start.2 = (bf16[64,1024]{1,0:T(8,128)(2,1)S(1)}, bf16[64,1024]{1,0:T(8,128)(2,1)S(1)}, u32[]{:S(2)}, u32[]{:S(2)}) collective-permute-start(bf16[64,1024]{1,0:T(8,128)(2,1)S(1)} %second_step.1.after_ref.refs_5_), channel_id=1, source_target_pairs={{2,6},{3,7}} | collective-permute-start | bytes 393224 | tf_op jit(solution)/shard_map/ppermute | solution.py:424
  3.3 0.1 reads0_1.1
  3.4 0.0 copy-done.1
  3.4 0.0 collective-permute-done.got_ref.refs_2_.refs_1_
  3.4 0.0 collective-permute-done.3.refs_2_.refs_1_
  3.5 0.0 collective-permute-done.2.refs_1_.refs_0_
  3.5 0.7 %collective-permute-start.4 = (bf16[64,1024]{1,0:T(8,128)(2,1)S(1)}, bf16[64,1024]{1,0:T(8,128)(2,1)S(1)}, u32[]{:S(2)}, u32[]{:S(2)}) collective-permute-start(bf16[64,1024]{1,0:T(8,128)(2,1)S(1)} %advance0_1.1.refs_6_), channel_id=1, source_target_pairs={{4,8},{6,10},{5,9},{7,11}} | collective-permute-start | bytes 393224 | tf_op jit(solution)/shard_map/ppermute | solution.py:424
  4.2 0.0 collective-permute-done.4.refs_1_.refs_0_
  4.3 0.7 %collective-permute-start.5 = (bf16[128,2048]{1,0:T(8,128)(2,1)S(1)}, bf16[128,2048]{1,0:T(8,128)(2,1)S(1)}, u32[]{:S(2)}, u32[]{:S(2)}) collective-permute-start(bf16[128,2048]{1,0:T(8,128)(2,1)S(1)} %first_finish_2.1.refs_12_), channel_id=1, source_target_pairs={{0,16},{2,18},{4,20},{6,22},{8,24},{10,26},{1,17},{3,19},{5,21},{7... | collective-permute-start | bytes 1572872 | tf_op jit(solution)/shard_map/ppermute | solution.py:489
  5.0 0.7 %collective-permute-start.12 = (bf16[64,1024]{1,0:T(8,128)(2,1)S(1)}, bf16[64,1024]{1,0:T(8,128)(2,1)S(1)}, u32[]{:S(2)}, u32[]{:S(2)}) collective-permute-start(bf16[64,1024]{1,0:T(8,128)(2,1)S(1)} %advance0_2.1.refs_5_), channel_id=1, source_target_pairs={{8,12},{10,14},{9,13},{11,15}} | collective-permute-start | bytes 393224 | tf_op jit(solution)/shard_map/ppermute | solution.py:424
  5.7 0.0 collective-permute-done.12.refs_0_
  5.7 1.3 %collective-permute-start.13 = (bf16[128,2048]{1,0:T(8,128)(2,1)S(1)}, bf16[128,2048]{1,0:T(8,128)(2,1)S(1)}, u32[]{:S(2)}, u32[]{:S(2)}) collective-permute-start(bf16[128,2048]{1,0:T(8,128)(2,1)S(1)} %first_finish_3.1.refs_13_), channel_id=1, source_target_pairs={{12,28},{14,30},{13,29},{15,31}} | collective-permute-start | bytes 1572872 | tf_op jit(solution)/shard_map/ppermute | solution.py:489
  7.0 5.9 %load.1 = (f32[1,2048]{1,0:T(1,128)S(1)}, bf16[1,2048,3072]{2,1,0:T(8,128)(2,1)S(1)}, bf16[1,16,2048]{2,1,0:T(8,128)(2,1)S(1)}, f32[1,16]{1,0:T(1,128)S(1)}, bf16[1,1024,2048]{2,1,0:T(8,128)(2,1)S(1)}) custom-call(f32[1,2048]{1,0:T(1,128)} %refs_0_.3, bf16[1,2048,3072]{2,1,0:T(8,128)(2,1)} %refs_1_.1, bf16[1,16,2048]{2,1,0:T(8,128)(2,1)} %bitcast.9, ...), custom_call_target="tpu_custom_call" | custom-call | tf_op jit(solution)/shard_map/load/pallas_call | solution.py:395
  12.9 0.0 collective-permute-done.5.h_ref.refs_10_
  12.9 0.2 later_front_0.1
  13.1 0.7 %collective-permute-start.6 = (bf16[64,2048]{1,0:T(8,128)(2,1)S(1)}, bf16[64,2048]{1,0:T(8,128)(2,1)S(1)}, u32[]{:S(2)}, u32[]{:S(2)}) collective-permute-start(bf16[64,2048]{1,0:T(8,128)(2,1)S(1)} %get-tuple-element.43.refs_0_.refs_3_), channel_id=1, source_target_pairs={{16,18},{18,16},{17,19},{19,17}} | collective-permute-start | bytes 786440 | tf_op jit(solution)/shard_map/ppermute | solution.py:424
  13.8 0.7 %collective-permute-start.8 = (bf16[64,2048]{1,0:T(8,128)(2,1)S(1)}, bf16[64,2048]{1,0:T(8,128)(2,1)S(1)}, u32[]{:S(2)}, u32[]{:S(2)}) collective-permute-start(bf16[64,2048]{1,0:T(8,128)(2,1)S(1)} %get-tuple-element.43.refs_0_.refs_3_), channel_id=1, source_target_pairs={{20,22},{22,20},{21,23},{23,21}} | collective-permute-start | bytes 786440 | tf_op jit(solution)/shard_map/ppermute | solution.py:424
  14.5 0.0 collective-permute-done.6.refs_1_.refs_4_
  14.5 0.7 %collective-permute-start.7 = (bf16[64,1024]{1,0:T(8,128)(2,1)S(1)}, bf16[64,1024]{1,0:T(8,128)(2,1)S(1)}, u32[]{:S(2)}, u32[]{:S(2)}) collective-permute-start(bf16[64,1024]{1,0:T(8,128)(2,1)S(1)} %advance1_0.1.refs_3_), channel_id=1, source_target_pairs={{16,20},{18,22},{17,21},{19,23}} | collective-permute-start | bytes 393224 | tf_op jit(solution)/shard_map/ppermute | solution.py:424
  15.2 0.7 %collective-permute-start.10 = (bf16[64,2048]{1,0:T(8,128)(2,1)S(1)}, bf16[64,2048]{1,0:T(8,128)(2,1)S(1)}, u32[]{:S(2)}, u32[]{:S(2)}) collective-permute-start(bf16[64,2048]{1,0:T(8,128)(2,1)S(1)} %get-tuple-element.43.refs_0_.refs_3_), channel_id=1, source_target_pairs={{24,26},{26,24},{25,27},{27,25}} | collective-permute-start | bytes 786440 | tf_op jit(solution)/shard_map/ppermute | solution.py:424
  15.9 0.0 collective-permute-done.8.refs_1_.refs_5_
  15.9 0.0 collective-permute-done.7.refs_2_.refs_1_
  16.0 0.7 %collective-permute-start.9 = (bf16[64,1024]{1,0:T(8,128)(2,1)S(1)}, bf16[64,1024]{1,0:T(8,128)(2,1)S(1)}, u32[]{:S(2)}, u32[]{:S(2)}) collective-permute-start(bf16[64,1024]{1,0:T(8,128)(2,1)S(1)} %advance1_1.1.after_ref), channel_id=1, source_target_pairs={{20,24},{22,26},{21,25},{23,27}} | collective-permute-start | bytes 393224 | tf_op jit(solution)/shard_map/ppermute | solution.py:424
  16.6 20.1 %collective-permute-done.13.h_ref.refs_11_ = bf16[128,2048]{1,0:T(8,128)(2,1)S(1)} collective-permute-done((bf16[128,2048]{1,0:T(8,128)(2,1)S(1)}, bf16[128,2048]{1,0:T(8,128)(2,1)S(1)}, u32[]{:S(2)}, u32[]{:S(2)}) %collective-permute-start.13) | collective-permute-done | bytes 524320 | tf_op jit(solution)/shard_map/ppermute | solution.py:489
  36.7 2.8 %later_front_3.1 = (bf16[64,2048]{1,0:T(8,128)(2,1)S(1)}, bf16[128,2048]{1,0:T(8,128)(2,1)S(1)}, bf16[128,1024]{1,0:T(8,128)(2,1)S(1)}, bf16[128,1024]{1,0:T(8,128)(2,1)S(1)}, bf16[128,1024]{1,0:T(8,128)(2,1)S(1)}) custom-call(bf16[128,2048]{1,0:T(8,128)(2,1)S(1)} %collective-permute-done.13.h_ref.refs_11_, f32[1,2048]{1,0:T(1,128)S(1)} %get-tuple-element.39.gain, ...), custom_call_target="tpu_custom_call" | custom-call | tf_op jit(solution)/shard_map/later_front_3/pallas_call | solution.py:395
  39.5 3.6 %collective-permute-start.14 = (bf16[64,2048]{1,0:T(8,128)(2,1)S(1)}, bf16[64,2048]{1,0:T(8,128)(2,1)S(1)}, u32[]{:S(2)}, u32[]{:S(2)}) collective-permute-start(bf16[64,2048]{1,0:T(8,128)(2,1)S(1)} %get-tuple-element.48), channel_id=1, source_target_pairs={{28,30},{30,28},{29,31},{31,29}} | collective-permute-start | bytes 786440 | tf_op jit(solution)/shard_map/ppermute | solution.py:424
  43.1 0.1 reads1_0.1.refs_3_.refs_8_
  43.2 0.0 collective-permute-done.10.refs_1_.refs_6_
  43.2 0.0 collective-permute-done.9.refs_2_
  43.2 1.3 %collective-permute-start.11 = (bf16[64,1024]{1,0:T(8,128)(2,1)S(1)}, bf16[64,1024]{1,0:T(8,128)(2,1)S(1)}, u32[]{:S(2)}, u32[]{:S(2)}) collective-permute-start(bf16[64,1024]{1,0:T(8,128)(2,1)S(1)} %advance1_2.1.after_ref), channel_id=1, source_target_pairs={{24,28},{26,30},{25,29},{27,31}} | collective-permute-start | bytes 393224 | tf_op jit(solution)/shard_map/ppermute | solution.py:424
  44.5 2.1 %reads1_3.1.refs_9_ = bf16[128,2048]{1,0:T(8,128)(2,1)S(1)} custom-call(bf16[128,2048]{1,0:T(8,128)(2,1)S(1)} %get-tuple-element.49.normed_ref, bf16[128,1024]{1,0:T(8,128)(2,1)S(1)} %get-tuple-element.50.keys_ref, bf16[128,1024]{1,0:T(8,128)(2,1)S(1)} %get-tuple-element.51.x_ref, bf16[128,1024]{1,0:T(8,128)(2,1)S(1)} %get-tuple-element.52.y_ref, ...), custom_call_target="tpu_custom_call" | custom-call | tf_op jit(solution)/shard_map/reads1_3/pallas_call | solution.py:395
  46.6 2.3 %collective-permute-done.11.refs_3_ = bf16[64,1024]{1,0:T(8,128)(2,1)S(1)} collective-permute-done((bf16[64,1024]{1,0:T(8,128)(2,1)S(1)}, bf16[64,1024]{1,0:T(8,128)(2,1)S(1)}, u32[]{:S(2)}, u32[]{:S(2)}) %collective-permute-start.11) | collective-permute-done | bytes 131104 | tf_op jit(solution)/shard_map/ppermute | solution.py:424
  48.9 0.0 collective-permute-done.14.refs_7_
  48.9 1.7 %last_finish.1 = bf16[1,128,2048]{2,1,0:T(8,128)(2,1)} custom-call(bf16[1024,2048]{1,0:T(8,128)(2,1)S(1)} %bitcast.7, f32[1,16,64,64]{3,2,1,0:T(8,128)S(1)} %copy-done, bf16[64,1024]{1,0:T(8,128)(2,1)S(1)} %collective-permute-done.7.refs_2_.refs_1_, bf16[64,1024]{1,0:T(8,128)(2,1)S(1)} %collective-permute-done.9.refs_2_, ...), custom_call_target="tpu_custom_call" | custom-call | tf_op jit(solution)/shard_map/last_finish/pallas_call | solution.py:395
  (12 shorter events, 0.3 us)
Async XLA Ops:
  0.0 1.0 %copy-start = (f32[1,16,64,64]{3,2,1,0:T(8,128)S(1)}, f32[1,16,64,64]{3,2,1,0:T(8,128)}, u32[]{:S(2)}) copy-start(f32[1,16,64,64]{3,2,1,0:T(8,128)} %refs_0_.5) | copy-start | bytes 786436
  0.1 3.3 %collective-permute-start = (bf16[64,2048]{1,0:T(8,128)(2,1)S(1)}, bf16[64,2048]{1,0:T(8,128)(2,1)S(1)}, u32[]{:S(2)}, u32[]{:S(2)}) collective-permute-start(bf16[64,2048]{1,0:T(8,128)(2,1)S(1)} %get-tuple-element.29.own_ref.after_ref), channel_id=1, source_target_pairs={{4,6},{6,4},{8,10},{10,8},{12,14},{14,12},{5,7},{7,5},{9,11},{11,9... | collective-permute-start | bytes 786440 | tf_op jit(solution)/shard_map/ppermute | solution.py:424
  1.0 0.7 %collective-permute-start.1 = (bf16[64,1024]{1,0:T(8,128)(2,1)S(1)}, bf16[64,1024]{1,0:T(8,128)(2,1)S(1)}, u32[]{:S(2)}, u32[]{:S(2)}) collective-permute-start(bf16[64,1024]{1,0:T(8,128)(2,1)S(1)} %first_step.1), channel_id=1, source_target_pairs={{0,2},{1,3}} | collective-permute-start | bytes 393224 | tf_op jit(solution)/shard_map/ppermute | solution.py:424
  1.8 1.6 %copy-start.1 = (bf16[128,2048]{1,0:T(8,128)(2,1)S(1)}, bf16[128,2048]{1,0:T(8,128)(2,1)}, u32[]{:S(2)}) copy-start(bf16[128,2048]{1,0:T(8,128)(2,1)} %refs_4_.7) | copy-start | bytes 1572868
  1.8 1.6 %collective-permute-start.3 = (bf16[64,1024]{1,0:T(8,128)(2,1)S(1)}, bf16[64,1024]{1,0:T(8,128)(2,1)S(1)}, u32[]{:S(2)}, u32[]{:S(2)}) collective-permute-start(bf16[64,1024]{1,0:T(8,128)(2,1)S(1)} %second_step.1.after_ref.refs_5_), channel_id=1, source_target_pairs={{2,4},{3,5}} | collective-permute-start | bytes 393224 | tf_op jit(solution)/shard_map/ppermute | solution.py:424
  2.6 0.8 %collective-permute-start.2 = (bf16[64,1024]{1,0:T(8,128)(2,1)S(1)}, bf16[64,1024]{1,0:T(8,128)(2,1)S(1)}, u32[]{:S(2)}, u32[]{:S(2)}) collective-permute-start(bf16[64,1024]{1,0:T(8,128)(2,1)S(1)} %second_step.1.after_ref.refs_5_), channel_id=1, source_target_pairs={{2,6},{3,7}} | collective-permute-start | bytes 393224 | tf_op jit(solution)/shard_map/ppermute | solution.py:424
  3.5 0.7 %collective-permute-start.4 = (bf16[64,1024]{1,0:T(8,128)(2,1)S(1)}, bf16[64,1024]{1,0:T(8,128)(2,1)S(1)}, u32[]{:S(2)}, u32[]{:S(2)}) collective-permute-start(bf16[64,1024]{1,0:T(8,128)(2,1)S(1)} %advance0_1.1.refs_6_), channel_id=1, source_target_pairs={{4,8},{6,10},{5,9},{7,11}} | collective-permute-start | bytes 393224 | tf_op jit(solution)/shard_map/ppermute | solution.py:424
  4.3 8.6 %collective-permute-start.5 = (bf16[128,2048]{1,0:T(8,128)(2,1)S(1)}, bf16[128,2048]{1,0:T(8,128)(2,1)S(1)}, u32[]{:S(2)}, u32[]{:S(2)}) collective-permute-start(bf16[128,2048]{1,0:T(8,128)(2,1)S(1)} %first_finish_2.1.refs_12_), channel_id=1, source_target_pairs={{0,16},{2,18},{4,20},{6,22},{8,24},{10,26},{1,17},{3,19},{5,21},{7... | collective-permute-start | bytes 1572872 | tf_op jit(solution)/shard_map/ppermute | solution.py:489
  5.0 0.7 %collective-permute-start.12 = (bf16[64,1024]{1,0:T(8,128)(2,1)S(1)}, bf16[64,1024]{1,0:T(8,128)(2,1)S(1)}, u32[]{:S(2)}, u32[]{:S(2)}) collective-permute-start(bf16[64,1024]{1,0:T(8,128)(2,1)S(1)} %advance0_2.1.refs_5_), channel_id=1, source_target_pairs={{8,12},{10,14},{9,13},{11,15}} | collective-permute-start | bytes 393224 | tf_op jit(solution)/shard_map/ppermute | solution.py:424
  5.7 31.0 %collective-permute-start.13 = (bf16[128,2048]{1,0:T(8,128)(2,1)S(1)}, bf16[128,2048]{1,0:T(8,128)(2,1)S(1)}, u32[]{:S(2)}, u32[]{:S(2)}) collective-permute-start(bf16[128,2048]{1,0:T(8,128)(2,1)S(1)} %first_finish_3.1.refs_13_), channel_id=1, source_target_pairs={{12,28},{14,30},{13,29},{15,31}} | collective-permute-start | bytes 1572872 | tf_op jit(solution)/shard_map/ppermute | solution.py:489
  13.1 1.4 %collective-permute-start.6 = (bf16[64,2048]{1,0:T(8,128)(2,1)S(1)}, bf16[64,2048]{1,0:T(8,128)(2,1)S(1)}, u32[]{:S(2)}, u32[]{:S(2)}) collective-permute-start(bf16[64,2048]{1,0:T(8,128)(2,1)S(1)} %get-tuple-element.43.refs_0_.refs_3_), channel_id=1, source_target_pairs={{16,18},{18,16},{17,19},{19,17}} | collective-permute-start | bytes 786440 | tf_op jit(solution)/shard_map/ppermute | solution.py:424
  13.8 2.1 %collective-permute-start.8 = (bf16[64,2048]{1,0:T(8,128)(2,1)S(1)}, bf16[64,2048]{1,0:T(8,128)(2,1)S(1)}, u32[]{:S(2)}, u32[]{:S(2)}) collective-permute-start(bf16[64,2048]{1,0:T(8,128)(2,1)S(1)} %get-tuple-element.43.refs_0_.refs_3_), channel_id=1, source_target_pairs={{20,22},{22,20},{21,23},{23,21}} | collective-permute-start | bytes 786440 | tf_op jit(solution)/shard_map/ppermute | solution.py:424
  14.5 1.4 %collective-permute-start.7 = (bf16[64,1024]{1,0:T(8,128)(2,1)S(1)}, bf16[64,1024]{1,0:T(8,128)(2,1)S(1)}, u32[]{:S(2)}, u32[]{:S(2)}) collective-permute-start(bf16[64,1024]{1,0:T(8,128)(2,1)S(1)} %advance1_0.1.refs_3_), channel_id=1, source_target_pairs={{16,20},{18,22},{17,21},{19,23}} | collective-permute-start | bytes 393224 | tf_op jit(solution)/shard_map/ppermute | solution.py:424
  15.2 27.9 %collective-permute-start.10 = (bf16[64,2048]{1,0:T(8,128)(2,1)S(1)}, bf16[64,2048]{1,0:T(8,128)(2,1)S(1)}, u32[]{:S(2)}, u32[]{:S(2)}) collective-permute-start(bf16[64,2048]{1,0:T(8,128)(2,1)S(1)} %get-tuple-element.43.refs_0_.refs_3_), channel_id=1, source_target_pairs={{24,26},{26,24},{25,27},{27,25}} | collective-permute-start | bytes 786440 | tf_op jit(solution)/shard_map/ppermute | solution.py:424
  16.0 27.2 %collective-permute-start.9 = (bf16[64,1024]{1,0:T(8,128)(2,1)S(1)}, bf16[64,1024]{1,0:T(8,128)(2,1)S(1)}, u32[]{:S(2)}, u32[]{:S(2)}) collective-permute-start(bf16[64,1024]{1,0:T(8,128)(2,1)S(1)} %advance1_1.1.after_ref), channel_id=1, source_target_pairs={{20,24},{22,26},{21,25},{23,27}} | collective-permute-start | bytes 393224 | tf_op jit(solution)/shard_map/ppermute | solution.py:424
  39.5 9.4 %collective-permute-start.14 = (bf16[64,2048]{1,0:T(8,128)(2,1)S(1)}, bf16[64,2048]{1,0:T(8,128)(2,1)S(1)}, u32[]{:S(2)}, u32[]{:S(2)}) collective-permute-start(bf16[64,2048]{1,0:T(8,128)(2,1)S(1)} %get-tuple-element.48), channel_id=1, source_target_pairs={{28,30},{30,28},{29,31},{31,29}} | collective-permute-start | bytes 786440 | tf_op jit(solution)/shard_map/ppermute | solution.py:424
  43.2 5.7 %collective-permute-start.11 = (bf16[64,1024]{1,0:T(8,128)(2,1)S(1)}, bf16[64,1024]{1,0:T(8,128)(2,1)S(1)}, u32[]{:S(2)}, u32[]{:S(2)}) collective-permute-start(bf16[64,1024]{1,0:T(8,128)(2,1)S(1)} %advance1_2.1.after_ref), channel_id=1, source_target_pairs={{24,28},{26,30},{25,29},{27,31}} | collective-permute-start | bytes 393224 | tf_op jit(solution)/shard_map/ppermute | solution.py:424

commit v17 on v15

--- a/solution.py
+++ b/solution.py
@@ -110,30 +110,23 @@
             pairs = [(gain_ref, gain), (w_rate_ref, w_rate), (base_ref, base), (h_ref, h_in)]
             small = [pltpu.make_async_copy(source, target, small_sems.at[index]) for index, (source, target) in enumerate(pairs)]
             copies = [
-                [
-                    pltpu.make_async_copy(
-                        w_ref.at[0, :, pl.ds((side + 1) * width + quad * QUAD, QUAD)],
-                        weights.at[:, pl.ds(side * width + quad * QUAD, QUAD)],
-                        sems.at[quad, side],
-                    )
-                    for quad in range(quads)
-                ]
+                pltpu.make_async_copy(
+                    w_ref.at[0, :, pl.ds((side + 1) * width, width)], weights.at[:, pl.ds(side * width, width)], sems.at[side]
+                )
                 for side in range(2)
             ]
             start_all(small)
-            start_all(copies[0][:1])
+            start_all(copies[:1])
             wait_all(small)
-            start_all(copies[0][1:])
+            start_all(copies[1:])
         normed = norm_rows(h_in[...], gain[...])
         normed_out[...] = normed
         rates = spread_rates(normed, w_rate[0], base[...])
         ones = head_ones()
 
         def project(side, quad):
-            if copies is not None:
-                wait_all([copies[side][quad]])
-                if side == 0:
-                    start_all([copies[1][quad]])
+            if copies is not None and quad == 0:
+                wait_all([copies[side]])
             lane = base_lane + side * width + quad * QUAD
             return mm(normed, weights[:, lane : lane + QUAD])
 
@@ -204,12 +197,10 @@
 def read_out(active, places, fetches, normed_ref, keys_ref, x_ref, y_ref, weights, w_out_hbm, after_ref, reads_out, *rest):
     rows, width = keys_ref.shape
     *w_out, wq, sems = rest
-    half = width // 2
 
     def body():
-        fetch = [pltpu.make_async_copy(w_out_hbm.at[0], target, sems.at[2]) for target in w_out]
-        halves = [pl.ds(index * half, half) for index in range(2)] if fetches else []
-        late = [pltpu.make_async_copy(weights.at[0, :, lanes], wq.at[:, lanes], sems.at[index]) for index, lanes in enumerate(halves)]
+        fetch = [pltpu.make_async_copy(w_out_hbm.at[0], target, sems.at[1]) for target in w_out]
+        late = [pltpu.make_async_copy(weights.at[0, :, pl.ds(0, width)], wq, sems.at[0])] if fetches else []
         start_all(late)
         normed = normed_ref[...]
         ones = head_ones()
@@ -230,11 +221,9 @@
                 reads_out[:, width + place.start : width + place.stop] = value[:, PAIR:].astype(BF16)
 
         if fetches:
-            wait_all(late[:1])
             start_all(fetch)
-            stages(0, half, wq)
-            wait_all(late[1:])
-            stages(half, width, wq)
+            wait_all(late)
+            stages(0, width, wq)
             wait_all(fetch)
         else:
             stages(0, width, weights)
@@ -428,7 +417,7 @@
         reads, *w_out_near = call(
             functools.partial(read_out, active, places, fetches),
             [shape((rows, 2 * width), BF16)] + [pltpu.VMEM(w_out.shape[1:], BF16)] * fetches,
-            [pltpu.VMEM((depth, width) if fetches else (16, 128), BF16), pltpu.SemaphoreType.DMA((3,))],
+            [pltpu.VMEM((depth, width) if fetches else (16, 128), BF16), pltpu.SemaphoreType.DMA((2,))],
             [*rows_of, weights, w_out, after],
             [pltpu.VMEM] * 4 + [pltpu.HBM if fetches else pltpu.VMEM, pltpu.HBM, pl.ANY],
             name=f"reads{active}_{places[0]}",
@@ -452,7 +441,7 @@
         first_front,
         [maps] + rows_out,
         [pltpu.VMEM(value.shape, value.dtype) for value in (tokens, norm_gain, w_rate, rate_base)]
-        + [pltpu.VMEM((depth, 2 * width), BF16), pltpu.SemaphoreType.DMA((4,)), pltpu.SemaphoreType.DMA((quads, 2))],
+        + [pltpu.VMEM((depth, 2 * width), BF16), pltpu.SemaphoreType.DMA((4,)), pltpu.SemaphoreType.DMA((2,))],
         [in_hbm(tokens), norm_gain, w_qkv, w_rate, rate_base],
         [pltpu.HBM] * 5,
         name="first_front",

time: 50.8 us -> 49.7 us (0.978)
  waiting for transfers between devices: 22.1 us -> 21 us
    ppermute x2, waiting for transfers between devices: 19.7 us -> 18.6 us  [begin(): lax.ppermute(first, ('section', 'seq'), [(place, count + place) for place...]
  transfers between devices with their start and end apart: 15 -> 15, of which waited for: 2 -> 2; matrix products, arithmetic and copies ran while one was open for 0% -> 0% of each run, Pallas kernels for 22% -> 23%
where the time goes in v17:
time: 49.7 us; the launch traced here: 49.4 us
  waiting for transfers between devices  21 us (42%)
  starting transfers between devices  14.5 us (29%)
  Pallas kernels  13.2 us (27%)
  between operations  0.54 us (1%)
    ppermute x2, waiting for transfers between devices, begin(): lax.ppermute(first, ('section', 'seq'), [(place, count + place) for place...  18.6 us
    pallas_call x21, Pallas kernels, call(): pl.pallas_call(body, out_shape=outs, in_specs=specs, out_specs=[pl.BlockS...  13.2 us
    ppermute x13, starting transfers between devices, permute(): lax.ppermute(value, ('section', 'seq'), [(base + source, base + target) f...  12.5 us
    ppermute x13, waiting for transfers between devices, permute(): lax.ppermute(value, ('section', 'seq'), [(base + source, base + target) f...  2.36 us
    ppermute x2, starting transfers between devices, begin(): lax.ppermute(first, ('section', 'seq'), [(place, count + place) for place...  1.99 us
  transfers between devices with their start and end apart: 15, of which 2 were waited for; matrix products, arithmetic and copies ran while one was open for 0% of the time, Pallas kernels for 23%

profile of v17, /device:TPU:25, one launch (start us, length us, event | category | flops | bytes accessed | tf_op | source)
XLA Modules:
  0.0 49.4 jit_solution(13825450047447885340)
XLA Ops:
  0.0 0.0 copy-start
  0.0 0.1 first_front.1
  0.1 0.8 %collective-permute-start = (bf16[64,2048]{1,0:T(8,128)(2,1)S(1)}, bf16[64,2048]{1,0:T(8,128)(2,1)S(1)}, u32[]{:S(2)}, u32[]{:S(2)}) collective-permute-start(bf16[64,2048]{1,0:T(8,128)(2,1)S(1)} %get-tuple-element.29.own_ref.after_ref), channel_id=1, source_target_pairs={{4,6},{6,4},{8,10},{10,8},{12,14},{14,12},{5,7},{7,5},{9,11},{11,9... | collective-permute-start | bytes 786440 | tf_op jit(solution)/shard_map/ppermute | solution.py:411
  0.9 0.2 copy-done
  1.0 0.7 %collective-permute-start.1 = (bf16[64,1024]{1,0:T(8,128)(2,1)S(1)}, bf16[64,1024]{1,0:T(8,128)(2,1)S(1)}, u32[]{:S(2)}, u32[]{:S(2)}) collective-permute-start(bf16[64,1024]{1,0:T(8,128)(2,1)S(1)} %first_step.1), channel_id=1, source_target_pairs={{0,2},{1,3}} | collective-permute-start | bytes 393224 | tf_op jit(solution)/shard_map/ppermute | solution.py:411
  1.8 0.0 collective-permute-done.1.state_ref.refs_1_
  1.8 0.0 copy-start.1
  1.8 0.8 %collective-permute-start.3 = (bf16[64,1024]{1,0:T(8,128)(2,1)S(1)}, bf16[64,1024]{1,0:T(8,128)(2,1)S(1)}, u32[]{:S(2)}, u32[]{:S(2)}) collective-permute-start(bf16[64,1024]{1,0:T(8,128)(2,1)S(1)} %second_step.1.after_ref.refs_5_), channel_id=1, source_target_pairs={{2,4},{3,5}} | collective-permute-start | bytes 393224 | tf_op jit(solution)/shard_map/ppermute | solution.py:411
  2.6 0.7 %collective-permute-start.2 = (bf16[64,1024]{1,0:T(8,128)(2,1)S(1)}, bf16[64,1024]{1,0:T(8,128)(2,1)S(1)}, u32[]{:S(2)}, u32[]{:S(2)}) collective-permute-start(bf16[64,1024]{1,0:T(8,128)(2,1)S(1)} %second_step.1.after_ref.refs_5_), channel_id=1, source_target_pairs={{2,6},{3,7}} | collective-permute-start | bytes 393224 | tf_op jit(solution)/shard_map/ppermute | solution.py:411
  3.3 0.0 copy-done.1
  3.4 0.0 collective-permute-done.got_ref.refs_2_.refs_1_
  3.4 0.0 collective-permute-done.3.refs_2_.refs_1_
  3.4 0.0 collective-permute-done.2.refs_1_.refs_0_
  3.5 0.7 %collective-permute-start.4 = (bf16[64,1024]{1,0:T(8,128)(2,1)S(1)}, bf16[64,1024]{1,0:T(8,128)(2,1)S(1)}, u32[]{:S(2)}, u32[]{:S(2)}) collective-permute-start(bf16[64,1024]{1,0:T(8,128)(2,1)S(1)} %advance0_1.1.refs_6_), channel_id=1, source_target_pairs={{4,8},{6,10},{5,9},{7,11}} | collective-permute-start | bytes 393224 | tf_op jit(solution)/shard_map/ppermute | solution.py:411
  4.2 0.0 collective-permute-done.4.refs_1_.refs_0_
  4.3 0.7 %collective-permute-start.5 = (bf16[128,2048]{1,0:T(8,128)(2,1)S(1)}, bf16[128,2048]{1,0:T(8,128)(2,1)S(1)}, u32[]{:S(2)}, u32[]{:S(2)}) collective-permute-start(bf16[128,2048]{1,0:T(8,128)(2,1)S(1)} %first_finish_2.1.refs_12_), channel_id=1, source_target_pairs={{0,16},{2,18},{4,20},{6,22},{8,24},{10,26},{1,17},{3,19},{5,21},{7... | collective-permute-start | bytes 1572872 | tf_op jit(solution)/shard_map/ppermute | solution.py:476
  5.0 0.7 %collective-permute-start.12 = (bf16[64,1024]{1,0:T(8,128)(2,1)S(1)}, bf16[64,1024]{1,0:T(8,128)(2,1)S(1)}, u32[]{:S(2)}, u32[]{:S(2)}) collective-permute-start(bf16[64,1024]{1,0:T(8,128)(2,1)S(1)} %advance0_2.1.refs_5_), channel_id=1, source_target_pairs={{8,12},{10,14},{9,13},{11,15}} | collective-permute-start | bytes 393224 | tf_op jit(solution)/shard_map/ppermute | solution.py:411
  5.7 0.0 collective-permute-done.12.refs_0_
  5.7 1.3 %collective-permute-start.13 = (bf16[128,2048]{1,0:T(8,128)(2,1)S(1)}, bf16[128,2048]{1,0:T(8,128)(2,1)S(1)}, u32[]{:S(2)}, u32[]{:S(2)}) collective-permute-start(bf16[128,2048]{1,0:T(8,128)(2,1)S(1)} %first_finish_3.1.refs_13_), channel_id=1, source_target_pairs={{12,28},{14,30},{13,29},{15,31}} | collective-permute-start | bytes 1572872 | tf_op jit(solution)/shard_map/ppermute | solution.py:476
  7.0 5.9 %load.1 = (f32[1,2048]{1,0:T(1,128)S(1)}, bf16[1,2048,3072]{2,1,0:T(8,128)(2,1)S(1)}, bf16[1,16,2048]{2,1,0:T(8,128)(2,1)S(1)}, f32[1,16]{1,0:T(1,128)S(1)}, bf16[1,1024,2048]{2,1,0:T(8,128)(2,1)S(1)}) custom-call(f32[1,2048]{1,0:T(1,128)} %refs_0_.3, bf16[1,2048,3072]{2,1,0:T(8,128)(2,1)} %refs_1_.1, bf16[1,16,2048]{2,1,0:T(8,128)(2,1)} %bitcast.9, ...), custom_call_target="tpu_custom_call" | custom-call | tf_op jit(solution)/shard_map/load/pallas_call | solution.py:382
  12.9 0.0 collective-permute-done.5.h_ref.refs_10_
  12.9 0.2 later_front_0.1
  13.1 0.7 %collective-permute-start.6 = (bf16[64,2048]{1,0:T(8,128)(2,1)S(1)}, bf16[64,2048]{1,0:T(8,128)(2,1)S(1)}, u32[]{:S(2)}, u32[]{:S(2)}) collective-permute-start(bf16[64,2048]{1,0:T(8,128)(2,1)S(1)} %get-tuple-element.43.refs_0_.refs_3_), channel_id=1, source_target_pairs={{16,18},{18,16},{17,19},{19,17}} | collective-permute-start | bytes 786440 | tf_op jit(solution)/shard_map/ppermute | solution.py:411
  13.8 0.7 %collective-permute-start.8 = (bf16[64,2048]{1,0:T(8,128)(2,1)S(1)}, bf16[64,2048]{1,0:T(8,128)(2,1)S(1)}, u32[]{:S(2)}, u32[]{:S(2)}) collective-permute-start(bf16[64,2048]{1,0:T(8,128)(2,1)S(1)} %get-tuple-element.43.refs_0_.refs_3_), channel_id=1, source_target_pairs={{20,22},{22,20},{21,23},{23,21}} | collective-permute-start | bytes 786440 | tf_op jit(solution)/shard_map/ppermute | solution.py:411
  14.5 0.0 collective-permute-done.6.refs_1_.refs_4_
  14.5 0.7 %collective-permute-start.7 = (bf16[64,1024]{1,0:T(8,128)(2,1)S(1)}, bf16[64,1024]{1,0:T(8,128)(2,1)S(1)}, u32[]{:S(2)}, u32[]{:S(2)}) collective-permute-start(bf16[64,1024]{1,0:T(8,128)(2,1)S(1)} %advance1_0.1.refs_3_), channel_id=1, source_target_pairs={{16,20},{18,22},{17,21},{19,23}} | collective-permute-start | bytes 393224 | tf_op jit(solution)/shard_map/ppermute | solution.py:411
  15.2 0.7 %collective-permute-start.10 = (bf16[64,2048]{1,0:T(8,128)(2,1)S(1)}, bf16[64,2048]{1,0:T(8,128)(2,1)S(1)}, u32[]{:S(2)}, u32[]{:S(2)}) collective-permute-start(bf16[64,2048]{1,0:T(8,128)(2,1)S(1)} %get-tuple-element.43.refs_0_.refs_3_), channel_id=1, source_target_pairs={{24,26},{26,24},{25,27},{27,25}} | collective-permute-start | bytes 786440 | tf_op jit(solution)/shard_map/ppermute | solution.py:411
  15.9 0.0 collective-permute-done.8.refs_1_.refs_5_
  15.9 0.0 collective-permute-done.7.refs_2_.refs_1_
  16.0 0.7 %collective-permute-start.9 = (bf16[64,1024]{1,0:T(8,128)(2,1)S(1)}, bf16[64,1024]{1,0:T(8,128)(2,1)S(1)}, u32[]{:S(2)}, u32[]{:S(2)}) collective-permute-start(bf16[64,1024]{1,0:T(8,128)(2,1)S(1)} %advance1_1.1.after_ref), channel_id=1, source_target_pairs={{20,24},{22,26},{21,25},{23,27}} | collective-permute-start | bytes 393224 | tf_op jit(solution)/shard_map/ppermute | solution.py:411
  16.6 18.6 %collective-permute-done.13.h_ref.refs_11_ = bf16[128,2048]{1,0:T(8,128)(2,1)S(1)} collective-permute-done((bf16[128,2048]{1,0:T(8,128)(2,1)S(1)}, bf16[128,2048]{1,0:T(8,128)(2,1)S(1)}, u32[]{:S(2)}, u32[]{:S(2)}) %collective-permute-start.13) | collective-permute-done | bytes 524320 | tf_op jit(solution)/shard_map/ppermute | solution.py:476
  35.3 2.8 %later_front_3.1 = (bf16[64,2048]{1,0:T(8,128)(2,1)S(1)}, bf16[128,2048]{1,0:T(8,128)(2,1)S(1)}, bf16[128,1024]{1,0:T(8,128)(2,1)S(1)}, bf16[128,1024]{1,0:T(8,128)(2,1)S(1)}, bf16[128,1024]{1,0:T(8,128)(2,1)S(1)}) custom-call(bf16[128,2048]{1,0:T(8,128)(2,1)S(1)} %collective-permute-done.13.h_ref.refs_11_, f32[1,2048]{1,0:T(1,128)S(1)} %get-tuple-element.39.gain, ...), custom_call_target="tpu_custom_call" | custom-call | tf_op jit(solution)/shard_map/later_front_3/pallas_call | solution.py:382
  38.1 3.6 %collective-permute-start.14 = (bf16[64,2048]{1,0:T(8,128)(2,1)S(1)}, bf16[64,2048]{1,0:T(8,128)(2,1)S(1)}, u32[]{:S(2)}, u32[]{:S(2)}) collective-permute-start(bf16[64,2048]{1,0:T(8,128)(2,1)S(1)} %get-tuple-element.48), channel_id=1, source_target_pairs={{28,30},{30,28},{29,31},{31,29}} | collective-permute-start | bytes 786440 | tf_op jit(solution)/shard_map/ppermute | solution.py:411
  41.7 0.0 collective-permute-done.10.refs_1_.refs_6_
  41.7 0.0 collective-permute-done.9.refs_2_
  41.8 1.3 %collective-permute-start.11 = (bf16[64,1024]{1,0:T(8,128)(2,1)S(1)}, bf16[64,1024]{1,0:T(8,128)(2,1)S(1)}, u32[]{:S(2)}, u32[]{:S(2)}) collective-permute-start(bf16[64,1024]{1,0:T(8,128)(2,1)S(1)} %advance1_2.1.after_ref), channel_id=1, source_target_pairs={{24,28},{26,30},{25,29},{27,31}} | collective-permute-start | bytes 393224 | tf_op jit(solution)/shard_map/ppermute | solution.py:411
  43.1 2.1 %reads1_3.1.refs_9_ = bf16[128,2048]{1,0:T(8,128)(2,1)S(1)} custom-call(bf16[128,2048]{1,0:T(8,128)(2,1)S(1)} %get-tuple-element.49.normed_ref, bf16[128,1024]{1,0:T(8,128)(2,1)S(1)} %get-tuple-element.50.keys_ref, bf16[128,1024]{1,0:T(8,128)(2,1)S(1)} %get-tuple-element.51.x_ref, bf16[128,1024]{1,0:T(8,128)(2,1)S(1)} %get-tuple-element.52.y_ref, ...), custom_call_target="tpu_custom_call" | custom-call | tf_op jit(solution)/shard_map/reads1_3/pallas_call | solution.py:382
  45.1 2.3 %collective-permute-done.11.refs_3_ = bf16[64,1024]{1,0:T(8,128)(2,1)S(1)} collective-permute-done((bf16[64,1024]{1,0:T(8,128)(2,1)S(1)}, bf16[64,1024]{1,0:T(8,128)(2,1)S(1)}, u32[]{:S(2)}, u32[]{:S(2)}) %collective-permute-start.11) | collective-permute-done | bytes 131104 | tf_op jit(solution)/shard_map/ppermute | solution.py:411
  47.5 0.0 collective-permute-done.14.refs_7_
  47.5 1.7 %last_finish.1 = bf16[1,128,2048]{2,1,0:T(8,128)(2,1)} custom-call(bf16[1024,2048]{1,0:T(8,128)(2,1)S(1)} %bitcast.7, f32[1,16,64,64]{3,2,1,0:T(8,128)S(1)} %copy-done, bf16[64,1024]{1,0:T(8,128)(2,1)S(1)} %collective-permute-done.7.refs_2_.refs_1_, bf16[64,1024]{1,0:T(8,128)(2,1)S(1)} %collective-permute-done.9.refs_2_, ...), custom_call_target="tpu_custom_call" | custom-call | tf_op jit(solution)/shard_map/last_finish/pallas_call | solution.py:382
  (15 shorter events, 0.4 us)
Async XLA Ops:
  0.0 1.0 %copy-start = (f32[1,16,64,64]{3,2,1,0:T(8,128)S(1)}, f32[1,16,64,64]{3,2,1,0:T(8,128)}, u32[]{:S(2)}) copy-start(f32[1,16,64,64]{3,2,1,0:T(8,128)} %refs_0_.5) | copy-start | bytes 786436
  0.1 3.3 %collective-permute-start = (bf16[64,2048]{1,0:T(8,128)(2,1)S(1)}, bf16[64,2048]{1,0:T(8,128)(2,1)S(1)}, u32[]{:S(2)}, u32[]{:S(2)}) collective-permute-start(bf16[64,2048]{1,0:T(8,128)(2,1)S(1)} %get-tuple-element.29.own_ref.after_ref), channel_id=1, source_target_pairs={{4,6},{6,4},{8,10},{10,8},{12,14},{14,12},{5,7},{7,5},{9,11},{11,9... | collective-permute-start | bytes 786440 | tf_op jit(solution)/shard_map/ppermute | solution.py:411
  1.0 0.7 %collective-permute-start.1 = (bf16[64,1024]{1,0:T(8,128)(2,1)S(1)}, bf16[64,1024]{1,0:T(8,128)(2,1)S(1)}, u32[]{:S(2)}, u32[]{:S(2)}) collective-permute-start(bf16[64,1024]{1,0:T(8,128)(2,1)S(1)} %first_step.1), channel_id=1, source_target_pairs={{0,2},{1,3}} | collective-permute-start | bytes 393224 | tf_op jit(solution)/shard_map/ppermute | solution.py:411
  1.8 1.6 %copy-start.1 = (bf16[128,2048]{1,0:T(8,128)(2,1)S(1)}, bf16[128,2048]{1,0:T(8,128)(2,1)}, u32[]{:S(2)}) copy-start(bf16[128,2048]{1,0:T(8,128)(2,1)} %refs_4_.7) | copy-start | bytes 1572868
  1.8 1.6 %collective-permute-start.3 = (bf16[64,1024]{1,0:T(8,128)(2,1)S(1)}, bf16[64,1024]{1,0:T(8,128)(2,1)S(1)}, u32[]{:S(2)}, u32[]{:S(2)}) collective-permute-start(bf16[64,1024]{1,0:T(8,128)(2,1)S(1)} %second_step.1.after_ref.refs_5_), channel_id=1, source_target_pairs={{2,4},{3,5}} | collective-permute-start | bytes 393224 | tf_op jit(solution)/shard_map/ppermute | solution.py:411
  2.6 0.8 %collective-permute-start.2 = (bf16[64,1024]{1,0:T(8,128)(2,1)S(1)}, bf16[64,1024]{1,0:T(8,128)(2,1)S(1)}, u32[]{:S(2)}, u32[]{:S(2)}) collective-permute-start(bf16[64,1024]{1,0:T(8,128)(2,1)S(1)} %second_step.1.after_ref.refs_5_), channel_id=1, source_target_pairs={{2,6},{3,7}} | collective-permute-start | bytes 393224 | tf_op jit(solution)/shard_map/ppermute | solution.py:411
  3.5 0.7 %collective-permute-start.4 = (bf16[64,1024]{1,0:T(8,128)(2,1)S(1)}, bf16[64,1024]{1,0:T(8,128)(2,1)S(1)}, u32[]{:S(2)}, u32[]{:S(2)}) collective-permute-start(bf16[64,1024]{1,0:T(8,128)(2,1)S(1)} %advance0_1.1.refs_6_), channel_id=1, source_target_pairs={{4,8},{6,10},{5,9},{7,11}} | collective-permute-start | bytes 393224 | tf_op jit(solution)/shard_map/ppermute | solution.py:411
  4.3 8.6 %collective-permute-start.5 = (bf16[128,2048]{1,0:T(8,128)(2,1)S(1)}, bf16[128,2048]{1,0:T(8,128)(2,1)S(1)}, u32[]{:S(2)}, u32[]{:S(2)}) collective-permute-start(bf16[128,2048]{1,0:T(8,128)(2,1)S(1)} %first_finish_2.1.refs_12_), channel_id=1, source_target_pairs={{0,16},{2,18},{4,20},{6,22},{8,24},{10,26},{1,17},{3,19},{5,21},{7... | collective-permute-start | bytes 1572872 | tf_op jit(solution)/shard_map/ppermute | solution.py:476
  5.0 0.7 %collective-permute-start.12 = (bf16[64,1024]{1,0:T(8,128)(2,1)S(1)}, bf16[64,1024]{1,0:T(8,128)(2,1)S(1)}, u32[]{:S(2)}, u32[]{:S(2)}) collective-permute-start(bf16[64,1024]{1,0:T(8,128)(2,1)S(1)} %advance0_2.1.refs_5_), channel_id=1, source_target_pairs={{8,12},{10,14},{9,13},{11,15}} | collective-permute-start | bytes 393224 | tf_op jit(solution)/shard_map/ppermute | solution.py:411
  5.7 29.6 %collective-permute-start.13 = (bf16[128,2048]{1,0:T(8,128)(2,1)S(1)}, bf16[128,2048]{1,0:T(8,128)(2,1)S(1)}, u32[]{:S(2)}, u32[]{:S(2)}) collective-permute-start(bf16[128,2048]{1,0:T(8,128)(2,1)S(1)} %first_finish_3.1.refs_13_), channel_id=1, source_target_pairs={{12,28},{14,30},{13,29},{15,31}} | collective-permute-start | bytes 1572872 | tf_op jit(solution)/shard_map/ppermute | solution.py:476
  13.1 1.4 %collective-permute-start.6 = (bf16[64,2048]{1,0:T(8,128)(2,1)S(1)}, bf16[64,2048]{1,0:T(8,128)(2,1)S(1)}, u32[]{:S(2)}, u32[]{:S(2)}) collective-permute-start(bf16[64,2048]{1,0:T(8,128)(2,1)S(1)} %get-tuple-element.43.refs_0_.refs_3_), channel_id=1, source_target_pairs={{16,18},{18,16},{17,19},{19,17}} | collective-permute-start | bytes 786440 | tf_op jit(solution)/shard_map/ppermute | solution.py:411
  13.8 2.1 %collective-permute-start.8 = (bf16[64,2048]{1,0:T(8,128)(2,1)S(1)}, bf16[64,2048]{1,0:T(8,128)(2,1)S(1)}, u32[]{:S(2)}, u32[]{:S(2)}) collective-permute-start(bf16[64,2048]{1,0:T(8,128)(2,1)S(1)} %get-tuple-element.43.refs_0_.refs_3_), channel_id=1, source_target_pairs={{20,22},{22,20},{21,23},{23,21}} | collective-permute-start | bytes 786440 | tf_op jit(solution)/shard_map/ppermute | solution.py:411
  14.5 1.4 %collective-permute-start.7 = (bf16[64,1024]{1,0:T(8,128)(2,1)S(1)}, bf16[64,1024]{1,0:T(8,128)(2,1)S(1)}, u32[]{:S(2)}, u32[]{:S(2)}) collective-permute-start(bf16[64,1024]{1,0:T(8,128)(2,1)S(1)} %advance1_0.1.refs_3_), channel_id=1, source_target_pairs={{16,20},{18,22},{17,21},{19,23}} | collective-permute-start | bytes 393224 | tf_op jit(solution)/shard_map/ppermute | solution.py:411
  15.2 26.5 %collective-permute-start.10 = (bf16[64,2048]{1,0:T(8,128)(2,1)S(1)}, bf16[64,2048]{1,0:T(8,128)(2,1)S(1)}, u32[]{:S(2)}, u32[]{:S(2)}) collective-permute-start(bf16[64,2048]{1,0:T(8,128)(2,1)S(1)} %get-tuple-element.43.refs_0_.refs_3_), channel_id=1, source_target_pairs={{24,26},{26,24},{25,27},{27,25}} | collective-permute-start | bytes 786440 | tf_op jit(solution)/shard_map/ppermute | solution.py:411
  16.0 25.8 %collective-permute-start.9 = (bf16[64,1024]{1,0:T(8,128)(2,1)S(1)}, bf16[64,1024]{1,0:T(8,128)(2,1)S(1)}, u32[]{:S(2)}, u32[]{:S(2)}) collective-permute-start(bf16[64,1024]{1,0:T(8,128)(2,1)S(1)} %advance1_1.1.after_ref), channel_id=1, source_target_pairs={{20,24},{22,26},{21,25},{23,27}} | collective-permute-start | bytes 393224 | tf_op jit(solution)/shard_map/ppermute | solution.py:411
  38.1 9.4 %collective-permute-start.14 = (bf16[64,2048]{1,0:T(8,128)(2,1)S(1)}, bf16[64,2048]{1,0:T(8,128)(2,1)S(1)}, u32[]{:S(2)}, u32[]{:S(2)}) collective-permute-start(bf16[64,2048]{1,0:T(8,128)(2,1)S(1)} %get-tuple-element.48), channel_id=1, source_target_pairs={{28,30},{30,28},{29,31},{31,29}} | collective-permute-start | bytes 786440 | tf_op jit(solution)/shard_map/ppermute | solution.py:411
  41.8 5.7 %collective-permute-start.11 = (bf16[64,1024]{1,0:T(8,128)(2,1)S(1)}, bf16[64,1024]{1,0:T(8,128)(2,1)S(1)}, u32[]{:S(2)}, u32[]{:S(2)}) collective-permute-start(bf16[64,1024]{1,0:T(8,128)(2,1)S(1)} %advance1_2.1.after_ref), channel_id=1, source_target_pairs={{24,28},{26,30},{25,29},{27,31}} | collective-permute-start | bytes 393224 | tf_op jit(solution)/shard_map/ppermute | solution.py:411

commit v18 on v17

--- a/solution.py
+++ b/solution.py
@@ -231,7 +231,7 @@
     pl.when(at_pair(places, active))(body)
 
 
-def compose(active, own_ref, got_ref, after_ref, out_ref):
+def compose(active, places, own_ref, got_ref, after_ref, out_ref):
     width = own_ref.shape[1] // 2
 
     def body(first_ref, second_ref):
@@ -242,7 +242,7 @@
             out_ref[:, s_lanes] = (s_second.astype(F32) + s_first.astype(F32) - step[:, :PAIR]).astype(BF16)
             out_ref[:, b_lanes] = (second_ref[:, b_lanes].astype(F32) + b_first.astype(F32) - step[:, PAIR:]).astype(BF16)
 
-    here = lax.axis_index("section") == active
+    here = at_pair(places, active)
     side = lax.rem(lax.axis_index("seq"), 2)
     pl.when(here & (side == 0))(lambda: body(own_ref, got_ref))
     pl.when(here & (side == 1))(lambda: body(got_ref, own_ref))
@@ -308,21 +308,18 @@
     model = h_ref.shape[1]
     chunk = model // 4
 
-    def body():
-        follows = lax.rem(lax.axis_index("seq"), 2) == 1
+    def body(follows):
+        state_ref = state_refs[-1] if follows else state_refs[0]
         starts = range(0, width, PAIR)
-        if begins:
-            states = [pair_state(state_refs[0], start // PAIR) for start in starts]
+        if follows and followed is not None:
+            states = [followed[:, start : start + PAIR].astype(F32) for start in starts]
+        elif begins:
+            states = [pair_state(state_ref, start // PAIR) for start in starts]
         else:
-            states = [state_refs[0][:, start : start + PAIR].astype(F32) for start in starts]
-            for ref in state_refs[1:]:
-                others = [ref[:, start : start + PAIR].astype(F32) for start in starts]
-                states = [jnp.where(follows, other, state) for other, state in zip(others, states)]
-        if followed is None:
-            moved = [apply_map(state, got_ref, start, width) for state, start in zip(states, starts)]
-        else:
-            moved = [followed[:, start : start + PAIR].astype(F32) for start in starts]
-        states = [jnp.where(follows, after, state).astype(BF16) for after, state in zip(moved, states)]
+            states = [state_ref[:, start : start + PAIR].astype(F32) for start in starts]
+        if follows and followed is None:
+            states = [apply_map(state, got_ref, start, width) for state, start in zip(states, starts)]
+        states = [state.astype(BF16) for state in states]
         quads = range(0, width, QUAD)
         spreads = [spread(jnp.concatenate(states[start // PAIR : (start + QUAD) // PAIR], axis=1)) for start in quads]
         reads = [mm(reads_ref[:, start : start + QUAD], value) for start, value in zip(quads, spreads)]
@@ -337,7 +334,9 @@
             lanes = slice(start, start + chunk)
             store(start, (h_ref[:, lanes].astype(F32) + mm(inner_bf, w_out_ref[:, lanes])).astype(BF16))
 
-    pl.when(here)(body)
+    side = lax.rem(lax.axis_index("seq"), 2)
+    pl.when(here & (side == 0))(lambda: body(False))
+    pl.when(here & (side == 1))(lambda: body(True))
 
 
 def first_finish(place, count, *refs):
@@ -455,9 +454,18 @@
     )
     state = [permute(ahead, 0, [(1, 2 + side)]) for side in range(2)]
     read_rest = layer_reads(0, range(1, groups), 1, rows_of, w_qkv, ahead)
-    (both,) = call(
-        functools.partial(compose, 0), [maps], [], [own, got_rest, read_rest[0]], [pltpu.VMEM] * 2 + [pl.ANY], name="compose"
-    )
+    def composed(active, places, own, got, after):
+        (both,) = call(
+            functools.partial(compose, active, places),
+            [maps],
+            [],
+            [own, got, after],
+            [pltpu.VMEM] * 2 + [pl.ANY],
+            name=f"compose{active}_{places[0]}",
+        )
+        return both
+
+    both = composed(0, range(1, groups), own, got_rest, read_rest[0])
 
     params = [norm_gain, w_qkv, w_rate, rate_base, w_out]
     gain_near, w_near, rate_near, base_near, w_out_near = call(
@@ -512,7 +520,8 @@
             gots += got
             reads = layer_reads(1, range(groups - 1), 0, rows_later, params[1], after)
             after = reads[0]
-        after, state = hop(1, place, [own_later, gots[place]], states[-1:], after)
+        own_maps = [composed(1, [place], own_later, gots[place], after)] if place else [own_later, gots[place]]
+        after, state = hop(1, place, own_maps, states[-1:], after)
         states += state
     reads += layer_reads(1, [groups - 1], 0, rows_last, params[1], after)
     (result,) = call(

time: 49.7 us -> 49.5 us (level)
    pallas_call x21 -> x23, Pallas kernels: 13.2 us -> 13.1 us  [call(): pl.pallas_call(body, out_shape=outs, in_specs=specs, out_specs=[pl.BlockS...]
where the time goes in v18:
time: 49.5 us; the launch traced here: 49.2 us
  waiting for transfers between devices  20.6 us (42%)
  starting transfers between devices  14.8 us (30%)
  Pallas kernels  13.1 us (26%)
  between operations  0.58 us (1%)
    ppermute x2, waiting for transfers between devices, begin(): lax.ppermute(first, ('section', 'seq'), [(place, count + place) for place...  18.3 us
    pallas_call x23, Pallas kernels, call(): pl.pallas_call(body, out_shape=outs, in_specs=specs, out_specs=[pl.BlockS...  13.1 us
    ppermute x13, starting transfers between devices, permute(): lax.ppermute(value, ('section', 'seq'), [(base + source, base + target) f...  12.8 us
    ppermute x13, waiting for transfers between devices, permute(): lax.ppermute(value, ('section', 'seq'), [(base + source, base + target) f...  2.34 us
    ppermute x2, starting transfers between devices, begin(): lax.ppermute(first, ('section', 'seq'), [(place, count + place) for place...  1.99 us
  transfers between devices with their start and end apart: 15, of which 2 were waited for; matrix products, arithmetic and copies ran while one was open for 0% of the time, Pallas kernels for 23%

profile of v18, /device:TPU:25, one launch (start us, length us, event | category | flops | bytes accessed | tf_op | source)
XLA Modules:
  0.0 49.2 jit_solution(8438702663412855869)
XLA Ops:
  0.0 0.0 copy-start
  0.0 0.1 first_front.1
  0.1 0.8 %collective-permute-start = (bf16[64,2048]{1,0:T(8,128)(2,1)S(1)}, bf16[64,2048]{1,0:T(8,128)(2,1)S(1)}, u32[]{:S(2)}, u32[]{:S(2)}) collective-permute-start(bf16[64,2048]{1,0:T(8,128)(2,1)S(1)} %get-tuple-element.29.own_ref.after_ref), channel_id=1, source_target_pairs={{4,6},{6,4},{8,10},{10,8},{12,14},{14,12},{5,7},{7,5},{9,11},{11,9... | collective-permute-start | bytes 786440 | tf_op jit(solution)/shard_map/ppermute | solution.py:410
  0.9 0.2 copy-done
  1.0 0.7 %collective-permute-start.1 = (bf16[64,1024]{1,0:T(8,128)(2,1)S(1)}, bf16[64,1024]{1,0:T(8,128)(2,1)S(1)}, u32[]{:S(2)}, u32[]{:S(2)}) collective-permute-start(bf16[64,1024]{1,0:T(8,128)(2,1)S(1)} %first_step.1), channel_id=1, source_target_pairs={{0,2},{1,3}} | collective-permute-start | bytes 393224 | tf_op jit(solution)/shard_map/ppermute | solution.py:410
  1.8 0.0 collective-permute-done.1.state_ref.refs_1_
  1.8 0.0 copy-start.1
  1.8 0.8 %collective-permute-start.3 = (bf16[64,1024]{1,0:T(8,128)(2,1)S(1)}, bf16[64,1024]{1,0:T(8,128)(2,1)S(1)}, u32[]{:S(2)}, u32[]{:S(2)}) collective-permute-start(bf16[64,1024]{1,0:T(8,128)(2,1)S(1)} %second_step.1.after_ref.refs_5_), channel_id=1, source_target_pairs={{2,4},{3,5}} | collective-permute-start | bytes 393224 | tf_op jit(solution)/shard_map/ppermute | solution.py:410
  2.6 0.7 %collective-permute-start.2 = (bf16[64,1024]{1,0:T(8,128)(2,1)S(1)}, bf16[64,1024]{1,0:T(8,128)(2,1)S(1)}, u32[]{:S(2)}, u32[]{:S(2)}) collective-permute-start(bf16[64,1024]{1,0:T(8,128)(2,1)S(1)} %second_step.1.after_ref.refs_5_), channel_id=1, source_target_pairs={{2,6},{3,7}} | collective-permute-start | bytes 393224 | tf_op jit(solution)/shard_map/ppermute | solution.py:410
  3.3 0.0 copy-done.1
  3.4 0.0 collective-permute-done.got_ref.refs_2_.refs_1_
  3.4 0.0 collective-permute-done.3.refs_2_.refs_1_
  3.5 0.0 collective-permute-done.2.refs_1_.refs_0_
  3.5 0.7 %collective-permute-start.4 = (bf16[64,1024]{1,0:T(8,128)(2,1)S(1)}, bf16[64,1024]{1,0:T(8,128)(2,1)S(1)}, u32[]{:S(2)}, u32[]{:S(2)}) collective-permute-start(bf16[64,1024]{1,0:T(8,128)(2,1)S(1)} %advance0_1.1.refs_6_), channel_id=1, source_target_pairs={{4,8},{6,10},{5,9},{7,11}} | collective-permute-start | bytes 393224 | tf_op jit(solution)/shard_map/ppermute | solution.py:410
  4.2 0.0 collective-permute-done.4.refs_1_.refs_0_
  4.3 0.7 %collective-permute-start.5 = (bf16[128,2048]{1,0:T(8,128)(2,1)S(1)}, bf16[128,2048]{1,0:T(8,128)(2,1)S(1)}, u32[]{:S(2)}, u32[]{:S(2)}) collective-permute-start(bf16[128,2048]{1,0:T(8,128)(2,1)S(1)} %first_finish_2.1.refs_12_), channel_id=1, source_target_pairs={{0,16},{2,18},{4,20},{6,22},{8,24},{10,26},{1,17},{3,19},{5,21},{7... | collective-permute-start | bytes 1572872 | tf_op jit(solution)/shard_map/ppermute | solution.py:484
  5.0 0.7 %collective-permute-start.12 = (bf16[64,1024]{1,0:T(8,128)(2,1)S(1)}, bf16[64,1024]{1,0:T(8,128)(2,1)S(1)}, u32[]{:S(2)}, u32[]{:S(2)}) collective-permute-start(bf16[64,1024]{1,0:T(8,128)(2,1)S(1)} %advance0_2.1.refs_5_), channel_id=1, source_target_pairs={{8,12},{10,14},{9,13},{11,15}} | collective-permute-start | bytes 393224 | tf_op jit(solution)/shard_map/ppermute | solution.py:410
  5.7 0.0 collective-permute-done.12.refs_0_
  5.7 0.2 first_finish_3.1.refs_13_
  5.9 1.3 %collective-permute-start.13 = (bf16[128,2048]{1,0:T(8,128)(2,1)S(1)}, bf16[128,2048]{1,0:T(8,128)(2,1)S(1)}, u32[]{:S(2)}, u32[]{:S(2)}) collective-permute-start(bf16[128,2048]{1,0:T(8,128)(2,1)S(1)} %first_finish_3.1.refs_13_), channel_id=1, source_target_pairs={{12,28},{14,30},{13,29},{15,31}} | collective-permute-start | bytes 1572872 | tf_op jit(solution)/shard_map/ppermute | solution.py:484
  7.2 5.9 %load.1 = (f32[1,2048]{1,0:T(1,128)S(1)}, bf16[1,2048,3072]{2,1,0:T(8,128)(2,1)S(1)}, bf16[1,16,2048]{2,1,0:T(8,128)(2,1)S(1)}, f32[1,16]{1,0:T(1,128)S(1)}, bf16[1,1024,2048]{2,1,0:T(8,128)(2,1)S(1)}) custom-call(f32[1,2048]{1,0:T(1,128)} %refs_0_.3, bf16[1,2048,3072]{2,1,0:T(8,128)(2,1)} %refs_1_.1, bf16[1,16,2048]{2,1,0:T(8,128)(2,1)} %bitcast.9, ...), custom_call_target="tpu_custom_call" | custom-call | tf_op jit(solution)/shard_map/load/pallas_call | solution.py:381
  13.1 0.0 collective-permute-done.5.h_ref.refs_10_
  13.1 0.7 %collective-permute-start.6 = (bf16[64,2048]{1,0:T(8,128)(2,1)S(1)}, bf16[64,2048]{1,0:T(8,128)(2,1)S(1)}, u32[]{:S(2)}, u32[]{:S(2)}) collective-permute-start(bf16[64,2048]{1,0:T(8,128)(2,1)S(1)} %get-tuple-element.43.refs_0_.refs_3_.own_ref), channel_id=1, source_target_pairs={{16,18},{18,16},{17,19},{19,17}} | collective-permute-start | bytes 786440 | tf_op jit(solution)/shard_map/ppermute | solution.py:410
  13.8 0.7 %collective-permute-start.8 = (bf16[64,2048]{1,0:T(8,128)(2,1)S(1)}, bf16[64,2048]{1,0:T(8,128)(2,1)S(1)}, u32[]{:S(2)}, u32[]{:S(2)}) collective-permute-start(bf16[64,2048]{1,0:T(8,128)(2,1)S(1)} %get-tuple-element.43.refs_0_.refs_3_.own_ref), channel_id=1, source_target_pairs={{20,22},{22,20},{21,23},{23,21}} | collective-permute-start | bytes 786440 | tf_op jit(solution)/shard_map/ppermute | solution.py:410
  14.5 0.0 collective-permute-done.6.refs_1_.refs_4_
  14.6 0.7 %collective-permute-start.7 = (bf16[64,1024]{1,0:T(8,128)(2,1)S(1)}, bf16[64,1024]{1,0:T(8,128)(2,1)S(1)}, u32[]{:S(2)}, u32[]{:S(2)}) collective-permute-start(bf16[64,1024]{1,0:T(8,128)(2,1)S(1)} %advance1_0.1.after_ref.refs_2_), channel_id=1, source_target_pairs={{16,20},{18,22},{17,21},{19,23}} | collective-permute-start | bytes 393224 | tf_op jit(solution)/shard_map/ppermute | solution.py:410
  15.2 0.7 %collective-permute-start.10 = (bf16[64,2048]{1,0:T(8,128)(2,1)S(1)}, bf16[64,2048]{1,0:T(8,128)(2,1)S(1)}, u32[]{:S(2)}, u32[]{:S(2)}) collective-permute-start(bf16[64,2048]{1,0:T(8,128)(2,1)S(1)} %get-tuple-element.43.refs_0_.refs_3_.own_ref), channel_id=1, source_target_pairs={{24,26},{26,24},{25,27},{27,25}} | collective-permute-start | bytes 786440 | tf_op jit(solution)/shard_map/ppermute | solution.py:410
  15.9 0.0 collective-permute-done.8.got_ref.refs_5_
  16.0 0.0 collective-permute-done.7.refs_1_
  16.0 0.7 %collective-permute-start.9 = (bf16[64,1024]{1,0:T(8,128)(2,1)S(1)}, bf16[64,1024]{1,0:T(8,128)(2,1)S(1)}, u32[]{:S(2)}, u32[]{:S(2)}) collective-permute-start(bf16[64,1024]{1,0:T(8,128)(2,1)S(1)} %advance1_1.1.after_ref), channel_id=1, source_target_pairs={{20,24},{22,26},{21,25},{23,27}} | collective-permute-start | bytes 393224 | tf_op jit(solution)/shard_map/ppermute | solution.py:410
  16.7 18.2 %collective-permute-done.13.h_ref.refs_11_ = bf16[128,2048]{1,0:T(8,128)(2,1)S(1)} collective-permute-done((bf16[128,2048]{1,0:T(8,128)(2,1)S(1)}, bf16[128,2048]{1,0:T(8,128)(2,1)S(1)}, u32[]{:S(2)}, u32[]{:S(2)}) %collective-permute-start.13) | collective-permute-done | bytes 524320 | tf_op jit(solution)/shard_map/ppermute | solution.py:484
  34.9 2.8 %later_front_3.1 = (bf16[64,2048]{1,0:T(8,128)(2,1)S(1)}, bf16[128,2048]{1,0:T(8,128)(2,1)S(1)}, bf16[128,1024]{1,0:T(8,128)(2,1)S(1)}, bf16[128,1024]{1,0:T(8,128)(2,1)S(1)}, bf16[128,1024]{1,0:T(8,128)(2,1)S(1)}) custom-call(bf16[128,2048]{1,0:T(8,128)(2,1)S(1)} %collective-permute-done.13.h_ref.refs_11_, f32[1,2048]{1,0:T(1,128)S(1)} %get-tuple-element.39.gain, ...), custom_call_target="tpu_custom_call" | custom-call | tf_op jit(solution)/shard_map/later_front_3/pallas_call | solution.py:381
  37.7 3.9 %collective-permute-start.14 = (bf16[64,2048]{1,0:T(8,128)(2,1)S(1)}, bf16[64,2048]{1,0:T(8,128)(2,1)S(1)}, u32[]{:S(2)}, u32[]{:S(2)}) collective-permute-start(bf16[64,2048]{1,0:T(8,128)(2,1)S(1)} %get-tuple-element.48), channel_id=1, source_target_pairs={{28,30},{30,28},{29,31},{31,29}} | collective-permute-start | bytes 786440 | tf_op jit(solution)/shard_map/ppermute | solution.py:410
  41.7 0.0 collective-permute-done.10.got_ref.refs_6_
  41.7 0.0 collective-permute-done.9.refs_1_.refs_2_
  41.8 1.3 %collective-permute-start.11 = (bf16[64,1024]{1,0:T(8,128)(2,1)S(1)}, bf16[64,1024]{1,0:T(8,128)(2,1)S(1)}, u32[]{:S(2)}, u32[]{:S(2)}) collective-permute-start(bf16[64,1024]{1,0:T(8,128)(2,1)S(1)} %advance1_2.1.after_ref), channel_id=1, source_target_pairs={{24,28},{26,30},{25,29},{27,31}} | collective-permute-start | bytes 393224 | tf_op jit(solution)/shard_map/ppermute | solution.py:410
  43.1 2.1 %reads1_3.1.refs_9_ = bf16[128,2048]{1,0:T(8,128)(2,1)S(1)} custom-call(bf16[128,2048]{1,0:T(8,128)(2,1)S(1)} %get-tuple-element.49.normed_ref, bf16[128,1024]{1,0:T(8,128)(2,1)S(1)} %get-tuple-element.50.keys_ref, bf16[128,1024]{1,0:T(8,128)(2,1)S(1)} %get-tuple-element.51.x_ref, bf16[128,1024]{1,0:T(8,128)(2,1)S(1)} %get-tuple-element.52.y_ref, ...), custom_call_target="tpu_custom_call" | custom-call | tf_op jit(solution)/shard_map/reads1_3/pallas_call | solution.py:381
  45.2 2.3 %collective-permute-done.11.refs_3_ = bf16[64,1024]{1,0:T(8,128)(2,1)S(1)} collective-permute-done((bf16[64,1024]{1,0:T(8,128)(2,1)S(1)}, bf16[64,1024]{1,0:T(8,128)(2,1)S(1)}, u32[]{:S(2)}, u32[]{:S(2)}) %collective-permute-start.11) | collective-permute-done | bytes 131104 | tf_op jit(solution)/shard_map/ppermute | solution.py:410
  47.5 0.0 collective-permute-done.14.refs_7_
  47.5 1.6 %last_finish.1 = bf16[1,128,2048]{2,1,0:T(8,128)(2,1)} custom-call(bf16[1024,2048]{1,0:T(8,128)(2,1)S(1)} %bitcast.7, f32[1,16,64,64]{3,2,1,0:T(8,128)S(1)} %copy-done, bf16[64,1024]{1,0:T(8,128)(2,1)S(1)} %collective-permute-done.7.refs_1_, bf16[64,1024]{1,0:T(8,128)(2,1)S(1)} %collective-permute-done.9.refs_1_.refs_2_, ...), custom_call_target="tpu_custom_call" | custom-call | tf_op jit(solution)/shard_map/last_finish/pallas_call | solution.py:381
  (17 shorter events, 0.5 us)
Async XLA Ops:
  0.0 1.0 %copy-start = (f32[1,16,64,64]{3,2,1,0:T(8,128)S(1)}, f32[1,16,64,64]{3,2,1,0:T(8,128)}, u32[]{:S(2)}) copy-start(f32[1,16,64,64]{3,2,1,0:T(8,128)} %refs_0_.5) | copy-start | bytes 786436
  0.1 3.3 %collective-permute-start = (bf16[64,2048]{1,0:T(8,128)(2,1)S(1)}, bf16[64,2048]{1,0:T(8,128)(2,1)S(1)}, u32[]{:S(2)}, u32[]{:S(2)}) collective-permute-start(bf16[64,2048]{1,0:T(8,128)(2,1)S(1)} %get-tuple-element.29.own_ref.after_ref), channel_id=1, source_target_pairs={{4,6},{6,4},{8,10},{10,8},{12,14},{14,12},{5,7},{7,5},{9,11},{11,9... | collective-permute-start | bytes 786440 | tf_op jit(solution)/shard_map/ppermute | solution.py:410
  1.0 0.7 %collective-permute-start.1 = (bf16[64,1024]{1,0:T(8,128)(2,1)S(1)}, bf16[64,1024]{1,0:T(8,128)(2,1)S(1)}, u32[]{:S(2)}, u32[]{:S(2)}) collective-permute-start(bf16[64,1024]{1,0:T(8,128)(2,1)S(1)} %first_step.1), channel_id=1, source_target_pairs={{0,2},{1,3}} | collective-permute-start | bytes 393224 | tf_op jit(solution)/shard_map/ppermute | solution.py:410
  1.8 1.6 %copy-start.1 = (bf16[128,2048]{1,0:T(8,128)(2,1)S(1)}, bf16[128,2048]{1,0:T(8,128)(2,1)}, u32[]{:S(2)}) copy-start(bf16[128,2048]{1,0:T(8,128)(2,1)} %refs_4_.7) | copy-start | bytes 1572868
  1.8 1.6 %collective-permute-start.3 = (bf16[64,1024]{1,0:T(8,128)(2,1)S(1)}, bf16[64,1024]{1,0:T(8,128)(2,1)S(1)}, u32[]{:S(2)}, u32[]{:S(2)}) collective-permute-start(bf16[64,1024]{1,0:T(8,128)(2,1)S(1)} %second_step.1.after_ref.refs_5_), channel_id=1, source_target_pairs={{2,4},{3,5}} | collective-permute-start | bytes 393224 | tf_op jit(solution)/shard_map/ppermute | solution.py:410
  2.6 0.8 %collective-permute-start.2 = (bf16[64,1024]{1,0:T(8,128)(2,1)S(1)}, bf16[64,1024]{1,0:T(8,128)(2,1)S(1)}, u32[]{:S(2)}, u32[]{:S(2)}) collective-permute-start(bf16[64,1024]{1,0:T(8,128)(2,1)S(1)} %second_step.1.after_ref.refs_5_), channel_id=1, source_target_pairs={{2,6},{3,7}} | collective-permute-start | bytes 393224 | tf_op jit(solution)/shard_map/ppermute | solution.py:410
  3.5 0.7 %collective-permute-start.4 = (bf16[64,1024]{1,0:T(8,128)(2,1)S(1)}, bf16[64,1024]{1,0:T(8,128)(2,1)S(1)}, u32[]{:S(2)}, u32[]{:S(2)}) collective-permute-start(bf16[64,1024]{1,0:T(8,128)(2,1)S(1)} %advance0_1.1.refs_6_), channel_id=1, source_target_pairs={{4,8},{6,10},{5,9},{7,11}} | collective-permute-start | bytes 393224 | tf_op jit(solution)/shard_map/ppermute | solution.py:410
  4.3 8.8 %collective-permute-start.5 = (bf16[128,2048]{1,0:T(8,128)(2,1)S(1)}, bf16[128,2048]{1,0:T(8,128)(2,1)S(1)}, u32[]{:S(2)}, u32[]{:S(2)}) collective-permute-start(bf16[128,2048]{1,0:T(8,128)(2,1)S(1)} %first_finish_2.1.refs_12_), channel_id=1, source_target_pairs={{0,16},{2,18},{4,20},{6,22},{8,24},{10,26},{1,17},{3,19},{5,21},{7... | collective-permute-start | bytes 1572872 | tf_op jit(solution)/shard_map/ppermute | solution.py:484
  5.0 0.7 %collective-permute-start.12 = (bf16[64,1024]{1,0:T(8,128)(2,1)S(1)}, bf16[64,1024]{1,0:T(8,128)(2,1)S(1)}, u32[]{:S(2)}, u32[]{:S(2)}) collective-permute-start(bf16[64,1024]{1,0:T(8,128)(2,1)S(1)} %advance0_2.1.refs_5_), channel_id=1, source_target_pairs={{8,12},{10,14},{9,13},{11,15}} | collective-permute-start | bytes 393224 | tf_op jit(solution)/shard_map/ppermute | solution.py:410
  5.9 29.0 %collective-permute-start.13 = (bf16[128,2048]{1,0:T(8,128)(2,1)S(1)}, bf16[128,2048]{1,0:T(8,128)(2,1)S(1)}, u32[]{:S(2)}, u32[]{:S(2)}) collective-permute-start(bf16[128,2048]{1,0:T(8,128)(2,1)S(1)} %first_finish_3.1.refs_13_), channel_id=1, source_target_pairs={{12,28},{14,30},{13,29},{15,31}} | collective-permute-start | bytes 1572872 | tf_op jit(solution)/shard_map/ppermute | solution.py:484
  13.1 1.4 %collective-permute-start.6 = (bf16[64,2048]{1,0:T(8,128)(2,1)S(1)}, bf16[64,2048]{1,0:T(8,128)(2,1)S(1)}, u32[]{:S(2)}, u32[]{:S(2)}) collective-permute-start(bf16[64,2048]{1,0:T(8,128)(2,1)S(1)} %get-tuple-element.43.refs_0_.refs_3_.own_ref), channel_id=1, source_target_pairs={{16,18},{18,16},{17,19},{19,17}} | collective-permute-start | bytes 786440 | tf_op jit(solution)/shard_map/ppermute | solution.py:410
  13.8 2.1 %collective-permute-start.8 = (bf16[64,2048]{1,0:T(8,128)(2,1)S(1)}, bf16[64,2048]{1,0:T(8,128)(2,1)S(1)}, u32[]{:S(2)}, u32[]{:S(2)}) collective-permute-start(bf16[64,2048]{1,0:T(8,128)(2,1)S(1)} %get-tuple-element.43.refs_0_.refs_3_.own_ref), channel_id=1, source_target_pairs={{20,22},{22,20},{21,23},{23,21}} | collective-permute-start | bytes 786440 | tf_op jit(solution)/shard_map/ppermute | solution.py:410
  14.6 1.4 %collective-permute-start.7 = (bf16[64,1024]{1,0:T(8,128)(2,1)S(1)}, bf16[64,1024]{1,0:T(8,128)(2,1)S(1)}, u32[]{:S(2)}, u32[]{:S(2)}) collective-permute-start(bf16[64,1024]{1,0:T(8,128)(2,1)S(1)} %advance1_0.1.after_ref.refs_2_), channel_id=1, source_target_pairs={{16,20},{18,22},{17,21},{19,23}} | collective-permute-start | bytes 393224 | tf_op jit(solution)/shard_map/ppermute | solution.py:410
  15.2 26.4 %collective-permute-start.10 = (bf16[64,2048]{1,0:T(8,128)(2,1)S(1)}, bf16[64,2048]{1,0:T(8,128)(2,1)S(1)}, u32[]{:S(2)}, u32[]{:S(2)}) collective-permute-start(bf16[64,2048]{1,0:T(8,128)(2,1)S(1)} %get-tuple-element.43.refs_0_.refs_3_.own_ref), channel_id=1, source_target_pairs={{24,26},{26,24},{25,27},{27,25}} | collective-permute-start | bytes 786440 | tf_op jit(solution)/shard_map/ppermute | solution.py:410
  16.0 25.7 %collective-permute-start.9 = (bf16[64,1024]{1,0:T(8,128)(2,1)S(1)}, bf16[64,1024]{1,0:T(8,128)(2,1)S(1)}, u32[]{:S(2)}, u32[]{:S(2)}) collective-permute-start(bf16[64,1024]{1,0:T(8,128)(2,1)S(1)} %advance1_1.1.after_ref), channel_id=1, source_target_pairs={{20,24},{22,26},{21,25},{23,27}} | collective-permute-start | bytes 393224 | tf_op jit(solution)/shard_map/ppermute | solution.py:410
  37.7 9.7 %collective-permute-start.14 = (bf16[64,2048]{1,0:T(8,128)(2,1)S(1)}, bf16[64,2048]{1,0:T(8,128)(2,1)S(1)}, u32[]{:S(2)}, u32[]{:S(2)}) collective-permute-start(bf16[64,2048]{1,0:T(8,128)(2,1)S(1)} %get-tuple-element.48), channel_id=1, source_target_pairs={{28,30},{30,28},{29,31},{31,29}} | collective-permute-start | bytes 786440 | tf_op jit(solution)/shard_map/ppermute | solution.py:410
  41.8 5.7 %collective-permute-start.11 = (bf16[64,1024]{1,0:T(8,128)(2,1)S(1)}, bf16[64,1024]{1,0:T(8,128)(2,1)S(1)}, u32[]{:S(2)}, u32[]{:S(2)}) collective-permute-start(bf16[64,1024]{1,0:T(8,128)(2,1)S(1)} %advance1_2.1.after_ref), channel_id=1, source_target_pairs={{24,28},{26,30},{25,29},{27,31}} | collective-permute-start | bytes 393224 | tf_op jit(solution)/shard_map/ppermute | solution.py:410

commit v19 on v18

--- a/solution.py
+++ b/solution.py
@@ -109,24 +109,28 @@
             base_lane = 0
             pairs = [(gain_ref, gain), (w_rate_ref, w_rate), (base_ref, base), (h_ref, h_in)]
             small = [pltpu.make_async_copy(source, target, small_sems.at[index]) for index, (source, target) in enumerate(pairs)]
+            half = width // 2
+            cuts = [(0, width), (width, half), (width + half, half)]
             copies = [
                 pltpu.make_async_copy(
-                    w_ref.at[0, :, pl.ds((side + 1) * width, width)], weights.at[:, pl.ds(side * width, width)], sems.at[side]
+                    w_ref.at[0, :, pl.ds(width + start, size)], weights.at[:, pl.ds(start, size)], sems.at[index]
                 )
-                for side in range(2)
+                for index, (start, size) in enumerate(cuts)
             ]
             start_all(small)
             start_all(copies[:1])
             wait_all(small)
-            start_all(copies[1:])
+            start_all(copies[1:2])
         normed = norm_rows(h_in[...], gain[...])
         normed_out[...] = normed
+        if copies is not None:
+            start_all(copies[2:])
         rates = spread_rates(normed, w_rate[0], base[...])
         ones = head_ones()
 
         def project(side, quad):
-            if copies is not None and quad == 0:
-                wait_all([copies[side]])
+            if copies is not None and quad % (quads // 2) == 0 and (side or quad == 0):
+                wait_all([copies[side + (2 * quad) // quads]])
             lane = base_lane + side * width + quad * QUAD
             return mm(normed, weights[:, lane : lane + QUAD])
 
@@ -440,7 +444,7 @@
         first_front,
         [maps] + rows_out,
         [pltpu.VMEM(value.shape, value.dtype) for value in (tokens, norm_gain, w_rate, rate_base)]
-        + [pltpu.VMEM((depth, 2 * width), BF16), pltpu.SemaphoreType.DMA((4,)), pltpu.SemaphoreType.DMA((2,))],
+        + [pltpu.VMEM((depth, 2 * width), BF16), pltpu.SemaphoreType.DMA((4,)), pltpu.SemaphoreType.DMA((3,))],
         [in_hbm(tokens), norm_gain, w_qkv, w_rate, rate_base],
         [pltpu.HBM] * 5,
         name="first_front",

time: 49.5 us -> 49.3 us (level)
  no operation moved by 1% of the time
where the time goes in v19:
time: 49.3 us; the launch traced here: 49 us
  waiting for transfers between devices  20.4 us (41%)
  starting transfers between devices  14.8 us (30%)
  Pallas kernels  13.1 us (27%)
  between operations  0.58 us (1%)
    ppermute x2, waiting for transfers between devices, begin(): lax.ppermute(first, ('section', 'seq'), [(place, count + place) for place...  18 us
    pallas_call x23, Pallas kernels, call(): pl.pallas_call(body, out_shape=outs, in_specs=specs, out_specs=[pl.BlockS...  13.1 us
    ppermute x13, starting transfers between devices, permute(): lax.ppermute(value, ('section', 'seq'), [(base + source, base + target) f...  12.8 us
    ppermute x13, waiting for transfers between devices, permute(): lax.ppermute(value, ('section', 'seq'), [(base + source, base + target) f...  2.34 us
    ppermute x2, starting transfers between devices, begin(): lax.ppermute(first, ('section', 'seq'), [(place, count + place) for place...  1.99 us
  transfers between devices with their start and end apart: 15, of which 2 were waited for; matrix products, arithmetic and copies ran while one was open for 0% of the time, Pallas kernels for 23%

profile of v19, /device:TPU:25, one launch (start us, length us, event | category | flops | bytes accessed | tf_op | source)
XLA Modules:
  0.0 49.0 jit_solution(17698906109992065610)
XLA Ops:
  0.0 0.0 copy-start
  0.0 0.1 first_front.1
  0.1 0.8 %collective-permute-start = (bf16[64,2048]{1,0:T(8,128)(2,1)S(1)}, bf16[64,2048]{1,0:T(8,128)(2,1)S(1)}, u32[]{:S(2)}, u32[]{:S(2)}) collective-permute-start(bf16[64,2048]{1,0:T(8,128)(2,1)S(1)} %get-tuple-element.29.own_ref.after_ref), channel_id=1, source_target_pairs={{4,6},{6,4},{8,10},{10,8},{12,14},{14,12},{5,7},{7,5},{9,11},{11,9... | collective-permute-start | bytes 786440 | tf_op jit(solution)/shard_map/ppermute | solution.py:414
  0.9 0.2 copy-done
  1.0 0.7 %collective-permute-start.1 = (bf16[64,1024]{1,0:T(8,128)(2,1)S(1)}, bf16[64,1024]{1,0:T(8,128)(2,1)S(1)}, u32[]{:S(2)}, u32[]{:S(2)}) collective-permute-start(bf16[64,1024]{1,0:T(8,128)(2,1)S(1)} %first_step.1), channel_id=1, source_target_pairs={{0,2},{1,3}} | collective-permute-start | bytes 393224 | tf_op jit(solution)/shard_map/ppermute | solution.py:414
  1.8 0.0 collective-permute-done.1.state_ref.refs_1_
  1.8 0.0 copy-start.1
  1.8 0.8 %collective-permute-start.3 = (bf16[64,1024]{1,0:T(8,128)(2,1)S(1)}, bf16[64,1024]{1,0:T(8,128)(2,1)S(1)}, u32[]{:S(2)}, u32[]{:S(2)}) collective-permute-start(bf16[64,1024]{1,0:T(8,128)(2,1)S(1)} %second_step.1.after_ref.refs_5_), channel_id=1, source_target_pairs={{2,4},{3,5}} | collective-permute-start | bytes 393224 | tf_op jit(solution)/shard_map/ppermute | solution.py:414
  2.6 0.7 %collective-permute-start.2 = (bf16[64,1024]{1,0:T(8,128)(2,1)S(1)}, bf16[64,1024]{1,0:T(8,128)(2,1)S(1)}, u32[]{:S(2)}, u32[]{:S(2)}) collective-permute-start(bf16[64,1024]{1,0:T(8,128)(2,1)S(1)} %second_step.1.after_ref.refs_5_), channel_id=1, source_target_pairs={{2,6},{3,7}} | collective-permute-start | bytes 393224 | tf_op jit(solution)/shard_map/ppermute | solution.py:414
  3.3 0.0 copy-done.1
  3.4 0.0 collective-permute-done.got_ref.refs_2_.refs_1_
  3.4 0.0 collective-permute-done.3.refs_2_.refs_1_
  3.5 0.0 collective-permute-done.2.refs_1_.refs_0_
  3.5 0.7 %collective-permute-start.4 = (bf16[64,1024]{1,0:T(8,128)(2,1)S(1)}, bf16[64,1024]{1,0:T(8,128)(2,1)S(1)}, u32[]{:S(2)}, u32[]{:S(2)}) collective-permute-start(bf16[64,1024]{1,0:T(8,128)(2,1)S(1)} %advance0_1.1.refs_6_), channel_id=1, source_target_pairs={{4,8},{6,10},{5,9},{7,11}} | collective-permute-start | bytes 393224 | tf_op jit(solution)/shard_map/ppermute | solution.py:414
  4.2 0.0 collective-permute-done.4.refs_1_.refs_0_
  4.3 0.7 %collective-permute-start.5 = (bf16[128,2048]{1,0:T(8,128)(2,1)S(1)}, bf16[128,2048]{1,0:T(8,128)(2,1)S(1)}, u32[]{:S(2)}, u32[]{:S(2)}) collective-permute-start(bf16[128,2048]{1,0:T(8,128)(2,1)S(1)} %first_finish_2.1.refs_12_), channel_id=1, source_target_pairs={{0,16},{2,18},{4,20},{6,22},{8,24},{10,26},{1,17},{3,19},{5,21},{7... | collective-permute-start | bytes 1572872 | tf_op jit(solution)/shard_map/ppermute | solution.py:488
  5.0 0.7 %collective-permute-start.12 = (bf16[64,1024]{1,0:T(8,128)(2,1)S(1)}, bf16[64,1024]{1,0:T(8,128)(2,1)S(1)}, u32[]{:S(2)}, u32[]{:S(2)}) collective-permute-start(bf16[64,1024]{1,0:T(8,128)(2,1)S(1)} %advance0_2.1.refs_5_), channel_id=1, source_target_pairs={{8,12},{10,14},{9,13},{11,15}} | collective-permute-start | bytes 393224 | tf_op jit(solution)/shard_map/ppermute | solution.py:414
  5.7 0.0 collective-permute-done.12.refs_0_
  5.7 0.2 first_finish_3.1.refs_13_
  5.9 1.3 %collective-permute-start.13 = (bf16[128,2048]{1,0:T(8,128)(2,1)S(1)}, bf16[128,2048]{1,0:T(8,128)(2,1)S(1)}, u32[]{:S(2)}, u32[]{:S(2)}) collective-permute-start(bf16[128,2048]{1,0:T(8,128)(2,1)S(1)} %first_finish_3.1.refs_13_), channel_id=1, source_target_pairs={{12,28},{14,30},{13,29},{15,31}} | collective-permute-start | bytes 1572872 | tf_op jit(solution)/shard_map/ppermute | solution.py:488
  7.2 5.9 %load.1 = (f32[1,2048]{1,0:T(1,128)S(1)}, bf16[1,2048,3072]{2,1,0:T(8,128)(2,1)S(1)}, bf16[1,16,2048]{2,1,0:T(8,128)(2,1)S(1)}, f32[1,16]{1,0:T(1,128)S(1)}, bf16[1,1024,2048]{2,1,0:T(8,128)(2,1)S(1)}) custom-call(f32[1,2048]{1,0:T(1,128)} %refs_0_.3, bf16[1,2048,3072]{2,1,0:T(8,128)(2,1)} %refs_1_.1, bf16[1,16,2048]{2,1,0:T(8,128)(2,1)} %bitcast.9, ...), custom_call_target="tpu_custom_call" | custom-call | tf_op jit(solution)/shard_map/load/pallas_call | solution.py:385
  13.1 0.0 collective-permute-done.5.h_ref.refs_10_
  13.1 0.7 %collective-permute-start.6 = (bf16[64,2048]{1,0:T(8,128)(2,1)S(1)}, bf16[64,2048]{1,0:T(8,128)(2,1)S(1)}, u32[]{:S(2)}, u32[]{:S(2)}) collective-permute-start(bf16[64,2048]{1,0:T(8,128)(2,1)S(1)} %get-tuple-element.43.refs_0_.refs_3_.own_ref), channel_id=1, source_target_pairs={{16,18},{18,16},{17,19},{19,17}} | collective-permute-start | bytes 786440 | tf_op jit(solution)/shard_map/ppermute | solution.py:414
  13.8 0.7 %collective-permute-start.8 = (bf16[64,2048]{1,0:T(8,128)(2,1)S(1)}, bf16[64,2048]{1,0:T(8,128)(2,1)S(1)}, u32[]{:S(2)}, u32[]{:S(2)}) collective-permute-start(bf16[64,2048]{1,0:T(8,128)(2,1)S(1)} %get-tuple-element.43.refs_0_.refs_3_.own_ref), channel_id=1, source_target_pairs={{20,22},{22,20},{21,23},{23,21}} | collective-permute-start | bytes 786440 | tf_op jit(solution)/shard_map/ppermute | solution.py:414
  14.5 0.0 collective-permute-done.6.refs_1_.refs_4_
  14.6 0.7 %collective-permute-start.7 = (bf16[64,1024]{1,0:T(8,128)(2,1)S(1)}, bf16[64,1024]{1,0:T(8,128)(2,1)S(1)}, u32[]{:S(2)}, u32[]{:S(2)}) collective-permute-start(bf16[64,1024]{1,0:T(8,128)(2,1)S(1)} %advance1_0.1.after_ref.refs_2_), channel_id=1, source_target_pairs={{16,20},{18,22},{17,21},{19,23}} | collective-permute-start | bytes 393224 | tf_op jit(solution)/shard_map/ppermute | solution.py:414
  15.2 0.7 %collective-permute-start.10 = (bf16[64,2048]{1,0:T(8,128)(2,1)S(1)}, bf16[64,2048]{1,0:T(8,128)(2,1)S(1)}, u32[]{:S(2)}, u32[]{:S(2)}) collective-permute-start(bf16[64,2048]{1,0:T(8,128)(2,1)S(1)} %get-tuple-element.43.refs_0_.refs_3_.own_ref), channel_id=1, source_target_pairs={{24,26},{26,24},{25,27},{27,25}} | collective-permute-start | bytes 786440 | tf_op jit(solution)/shard_map/ppermute | solution.py:414
  15.9 0.0 collective-permute-done.8.got_ref.refs_5_
  16.0 0.0 collective-permute-done.7.refs_1_
  16.0 0.7 %collective-permute-start.9 = (bf16[64,1024]{1,0:T(8,128)(2,1)S(1)}, bf16[64,1024]{1,0:T(8,128)(2,1)S(1)}, u32[]{:S(2)}, u32[]{:S(2)}) collective-permute-start(bf16[64,1024]{1,0:T(8,128)(2,1)S(1)} %advance1_1.1.after_ref), channel_id=1, source_target_pairs={{20,24},{22,26},{21,25},{23,27}} | collective-permute-start | bytes 393224 | tf_op jit(solution)/shard_map/ppermute | solution.py:414
  16.7 18.0 %collective-permute-done.13.h_ref.refs_11_ = bf16[128,2048]{1,0:T(8,128)(2,1)S(1)} collective-permute-done((bf16[128,2048]{1,0:T(8,128)(2,1)S(1)}, bf16[128,2048]{1,0:T(8,128)(2,1)S(1)}, u32[]{:S(2)}, u32[]{:S(2)}) %collective-permute-start.13) | collective-permute-done | bytes 524320 | tf_op jit(solution)/shard_map/ppermute | solution.py:488
  34.7 2.8 %later_front_3.1 = (bf16[64,2048]{1,0:T(8,128)(2,1)S(1)}, bf16[128,2048]{1,0:T(8,128)(2,1)S(1)}, bf16[128,1024]{1,0:T(8,128)(2,1)S(1)}, bf16[128,1024]{1,0:T(8,128)(2,1)S(1)}, bf16[128,1024]{1,0:T(8,128)(2,1)S(1)}) custom-call(bf16[128,2048]{1,0:T(8,128)(2,1)S(1)} %collective-permute-done.13.h_ref.refs_11_, f32[1,2048]{1,0:T(1,128)S(1)} %get-tuple-element.39.gain, ...), custom_call_target="tpu_custom_call" | custom-call | tf_op jit(solution)/shard_map/later_front_3/pallas_call | solution.py:385
  37.5 3.9 %collective-permute-start.14 = (bf16[64,2048]{1,0:T(8,128)(2,1)S(1)}, bf16[64,2048]{1,0:T(8,128)(2,1)S(1)}, u32[]{:S(2)}, u32[]{:S(2)}) collective-permute-start(bf16[64,2048]{1,0:T(8,128)(2,1)S(1)} %get-tuple-element.48), channel_id=1, source_target_pairs={{28,30},{30,28},{29,31},{31,29}} | collective-permute-start | bytes 786440 | tf_op jit(solution)/shard_map/ppermute | solution.py:414
  41.5 0.0 collective-permute-done.10.got_ref.refs_6_
  41.5 0.0 collective-permute-done.9.refs_1_.refs_2_
  41.5 1.3 %collective-permute-start.11 = (bf16[64,1024]{1,0:T(8,128)(2,1)S(1)}, bf16[64,1024]{1,0:T(8,128)(2,1)S(1)}, u32[]{:S(2)}, u32[]{:S(2)}) collective-permute-start(bf16[64,1024]{1,0:T(8,128)(2,1)S(1)} %advance1_2.1.after_ref), channel_id=1, source_target_pairs={{24,28},{26,30},{25,29},{27,31}} | collective-permute-start | bytes 393224 | tf_op jit(solution)/shard_map/ppermute | solution.py:414
  42.8 2.1 %reads1_3.1.refs_9_ = bf16[128,2048]{1,0:T(8,128)(2,1)S(1)} custom-call(bf16[128,2048]{1,0:T(8,128)(2,1)S(1)} %get-tuple-element.49.normed_ref, bf16[128,1024]{1,0:T(8,128)(2,1)S(1)} %get-tuple-element.50.keys_ref, bf16[128,1024]{1,0:T(8,128)(2,1)S(1)} %get-tuple-element.51.x_ref, bf16[128,1024]{1,0:T(8,128)(2,1)S(1)} %get-tuple-element.52.y_ref, ...), custom_call_target="tpu_custom_call" | custom-call | tf_op jit(solution)/shard_map/reads1_3/pallas_call | solution.py:385
  44.9 2.3 %collective-permute-done.11.refs_3_ = bf16[64,1024]{1,0:T(8,128)(2,1)S(1)} collective-permute-done((bf16[64,1024]{1,0:T(8,128)(2,1)S(1)}, bf16[64,1024]{1,0:T(8,128)(2,1)S(1)}, u32[]{:S(2)}, u32[]{:S(2)}) %collective-permute-start.11) | collective-permute-done | bytes 131104 | tf_op jit(solution)/shard_map/ppermute | solution.py:414
  47.3 0.0 collective-permute-done.14.refs_7_
  47.3 1.6 %last_finish.1 = bf16[1,128,2048]{2,1,0:T(8,128)(2,1)} custom-call(bf16[1024,2048]{1,0:T(8,128)(2,1)S(1)} %bitcast.7, f32[1,16,64,64]{3,2,1,0:T(8,128)S(1)} %copy-done, bf16[64,1024]{1,0:T(8,128)(2,1)S(1)} %collective-permute-done.7.refs_1_, bf16[64,1024]{1,0:T(8,128)(2,1)S(1)} %collective-permute-done.9.refs_1_.refs_2_, ...), custom_call_target="tpu_custom_call" | custom-call | tf_op jit(solution)/shard_map/last_finish/pallas_call | solution.py:385
  (17 shorter events, 0.5 us)
Async XLA Ops:
  0.0 1.0 %copy-start = (f32[1,16,64,64]{3,2,1,0:T(8,128)S(1)}, f32[1,16,64,64]{3,2,1,0:T(8,128)}, u32[]{:S(2)}) copy-start(f32[1,16,64,64]{3,2,1,0:T(8,128)} %refs_0_.5) | copy-start | bytes 786436
  0.1 3.3 %collective-permute-start = (bf16[64,2048]{1,0:T(8,128)(2,1)S(1)}, bf16[64,2048]{1,0:T(8,128)(2,1)S(1)}, u32[]{:S(2)}, u32[]{:S(2)}) collective-permute-start(bf16[64,2048]{1,0:T(8,128)(2,1)S(1)} %get-tuple-element.29.own_ref.after_ref), channel_id=1, source_target_pairs={{4,6},{6,4},{8,10},{10,8},{12,14},{14,12},{5,7},{7,5},{9,11},{11,9... | collective-permute-start | bytes 786440 | tf_op jit(solution)/shard_map/ppermute | solution.py:414
  1.0 0.7 %collective-permute-start.1 = (bf16[64,1024]{1,0:T(8,128)(2,1)S(1)}, bf16[64,1024]{1,0:T(8,128)(2,1)S(1)}, u32[]{:S(2)}, u32[]{:S(2)}) collective-permute-start(bf16[64,1024]{1,0:T(8,128)(2,1)S(1)} %first_step.1), channel_id=1, source_target_pairs={{0,2},{1,3}} | collective-permute-start | bytes 393224 | tf_op jit(solution)/shard_map/ppermute | solution.py:414
  1.8 1.6 %copy-start.1 = (bf16[128,2048]{1,0:T(8,128)(2,1)S(1)}, bf16[128,2048]{1,0:T(8,128)(2,1)}, u32[]{:S(2)}) copy-start(bf16[128,2048]{1,0:T(8,128)(2,1)} %refs_4_.7) | copy-start | bytes 1572868
  1.8 1.6 %collective-permute-start.3 = (bf16[64,1024]{1,0:T(8,128)(2,1)S(1)}, bf16[64,1024]{1,0:T(8,128)(2,1)S(1)}, u32[]{:S(2)}, u32[]{:S(2)}) collective-permute-start(bf16[64,1024]{1,0:T(8,128)(2,1)S(1)} %second_step.1.after_ref.refs_5_), channel_id=1, source_target_pairs={{2,4},{3,5}} | collective-permute-start | bytes 393224 | tf_op jit(solution)/shard_map/ppermute | solution.py:414
  2.6 0.8 %collective-permute-start.2 = (bf16[64,1024]{1,0:T(8,128)(2,1)S(1)}, bf16[64,1024]{1,0:T(8,128)(2,1)S(1)}, u32[]{:S(2)}, u32[]{:S(2)}) collective-permute-start(bf16[64,1024]{1,0:T(8,128)(2,1)S(1)} %second_step.1.after_ref.refs_5_), channel_id=1, source_target_pairs={{2,6},{3,7}} | collective-permute-start | bytes 393224 | tf_op jit(solution)/shard_map/ppermute | solution.py:414
  3.5 0.7 %collective-permute-start.4 = (bf16[64,1024]{1,0:T(8,128)(2,1)S(1)}, bf16[64,1024]{1,0:T(8,128)(2,1)S(1)}, u32[]{:S(2)}, u32[]{:S(2)}) collective-permute-start(bf16[64,1024]{1,0:T(8,128)(2,1)S(1)} %advance0_1.1.refs_6_), channel_id=1, source_target_pairs={{4,8},{6,10},{5,9},{7,11}} | collective-permute-start | bytes 393224 | tf_op jit(solution)/shard_map/ppermute | solution.py:414
  4.3 8.8 %collective-permute-start.5 = (bf16[128,2048]{1,0:T(8,128)(2,1)S(1)}, bf16[128,2048]{1,0:T(8,128)(2,1)S(1)}, u32[]{:S(2)}, u32[]{:S(2)}) collective-permute-start(bf16[128,2048]{1,0:T(8,128)(2,1)S(1)} %first_finish_2.1.refs_12_), channel_id=1, source_target_pairs={{0,16},{2,18},{4,20},{6,22},{8,24},{10,26},{1,17},{3,19},{5,21},{7... | collective-permute-start | bytes 1572872 | tf_op jit(solution)/shard_map/ppermute | solution.py:488
  5.0 0.7 %collective-permute-start.12 = (bf16[64,1024]{1,0:T(8,128)(2,1)S(1)}, bf16[64,1024]{1,0:T(8,128)(2,1)S(1)}, u32[]{:S(2)}, u32[]{:S(2)}) collective-permute-start(bf16[64,1024]{1,0:T(8,128)(2,1)S(1)} %advance0_2.1.refs_5_), channel_id=1, source_target_pairs={{8,12},{10,14},{9,13},{11,15}} | collective-permute-start | bytes 393224 | tf_op jit(solution)/shard_map/ppermute | solution.py:414
  5.9 28.8 %collective-permute-start.13 = (bf16[128,2048]{1,0:T(8,128)(2,1)S(1)}, bf16[128,2048]{1,0:T(8,128)(2,1)S(1)}, u32[]{:S(2)}, u32[]{:S(2)}) collective-permute-start(bf16[128,2048]{1,0:T(8,128)(2,1)S(1)} %first_finish_3.1.refs_13_), channel_id=1, source_target_pairs={{12,28},{14,30},{13,29},{15,31}} | collective-permute-start | bytes 1572872 | tf_op jit(solution)/shard_map/ppermute | solution.py:488
  13.1 1.4 %collective-permute-start.6 = (bf16[64,2048]{1,0:T(8,128)(2,1)S(1)}, bf16[64,2048]{1,0:T(8,128)(2,1)S(1)}, u32[]{:S(2)}, u32[]{:S(2)}) collective-permute-start(bf16[64,2048]{1,0:T(8,128)(2,1)S(1)} %get-tuple-element.43.refs_0_.refs_3_.own_ref), channel_id=1, source_target_pairs={{16,18},{18,16},{17,19},{19,17}} | collective-permute-start | bytes 786440 | tf_op jit(solution)/shard_map/ppermute | solution.py:414
  13.8 2.1 %collective-permute-start.8 = (bf16[64,2048]{1,0:T(8,128)(2,1)S(1)}, bf16[64,2048]{1,0:T(8,128)(2,1)S(1)}, u32[]{:S(2)}, u32[]{:S(2)}) collective-permute-start(bf16[64,2048]{1,0:T(8,128)(2,1)S(1)} %get-tuple-element.43.refs_0_.refs_3_.own_ref), channel_id=1, source_target_pairs={{20,22},{22,20},{21,23},{23,21}} | collective-permute-start | bytes 786440 | tf_op jit(solution)/shard_map/ppermute | solution.py:414
  14.6 1.4 %collective-permute-start.7 = (bf16[64,1024]{1,0:T(8,128)(2,1)S(1)}, bf16[64,1024]{1,0:T(8,128)(2,1)S(1)}, u32[]{:S(2)}, u32[]{:S(2)}) collective-permute-start(bf16[64,1024]{1,0:T(8,128)(2,1)S(1)} %advance1_0.1.after_ref.refs_2_), channel_id=1, source_target_pairs={{16,20},{18,22},{17,21},{19,23}} | collective-permute-start | bytes 393224 | tf_op jit(solution)/shard_map/ppermute | solution.py:414
  15.2 26.2 %collective-permute-start.10 = (bf16[64,2048]{1,0:T(8,128)(2,1)S(1)}, bf16[64,2048]{1,0:T(8,128)(2,1)S(1)}, u32[]{:S(2)}, u32[]{:S(2)}) collective-permute-start(bf16[64,2048]{1,0:T(8,128)(2,1)S(1)} %get-tuple-element.43.refs_0_.refs_3_.own_ref), channel_id=1, source_target_pairs={{24,26},{26,24},{25,27},{27,25}} | collective-permute-start | bytes 786440 | tf_op jit(solution)/shard_map/ppermute | solution.py:414
  16.0 25.5 %collective-permute-start.9 = (bf16[64,1024]{1,0:T(8,128)(2,1)S(1)}, bf16[64,1024]{1,0:T(8,128)(2,1)S(1)}, u32[]{:S(2)}, u32[]{:S(2)}) collective-permute-start(bf16[64,1024]{1,0:T(8,128)(2,1)S(1)} %advance1_1.1.after_ref), channel_id=1, source_target_pairs={{20,24},{22,26},{21,25},{23,27}} | collective-permute-start | bytes 393224 | tf_op jit(solution)/shard_map/ppermute | solution.py:414
  37.5 9.7 %collective-permute-start.14 = (bf16[64,2048]{1,0:T(8,128)(2,1)S(1)}, bf16[64,2048]{1,0:T(8,128)(2,1)S(1)}, u32[]{:S(2)}, u32[]{:S(2)}) collective-permute-start(bf16[64,2048]{1,0:T(8,128)(2,1)S(1)} %get-tuple-element.48), channel_id=1, source_target_pairs={{28,30},{30,28},{29,31},{31,29}} | collective-permute-start | bytes 786440 | tf_op jit(solution)/shard_map/ppermute | solution.py:414
  41.5 5.7 %collective-permute-start.11 = (bf16[64,1024]{1,0:T(8,128)(2,1)S(1)}, bf16[64,1024]{1,0:T(8,128)(2,1)S(1)}, u32[]{:S(2)}, u32[]{:S(2)}) collective-permute-start(bf16[64,1024]{1,0:T(8,128)(2,1)S(1)} %advance1_2.1.after_ref), channel_id=1, source_target_pairs={{24,28},{26,30},{25,29},{27,31}} | collective-permute-start | bytes 393224 | tf_op jit(solution)/shard_map/ppermute | solution.py:414

commit v20 on v19

--- a/solution.py
+++ b/solution.py
@@ -110,7 +110,7 @@
             pairs = [(gain_ref, gain), (w_rate_ref, w_rate), (base_ref, base), (h_ref, h_in)]
             small = [pltpu.make_async_copy(source, target, small_sems.at[index]) for index, (source, target) in enumerate(pairs)]
             half = width // 2
-            cuts = [(0, width), (width, half), (width + half, half)]
+            cuts = [(index * half, half) for index in range(4)]
             copies = [
                 pltpu.make_async_copy(
                     w_ref.at[0, :, pl.ds(width + start, size)], weights.at[:, pl.ds(start, size)], sems.at[index]
@@ -120,17 +120,17 @@
             start_all(small)
             start_all(copies[:1])
             wait_all(small)
-            start_all(copies[1:2])
+            start_all(copies[1:3])
         normed = norm_rows(h_in[...], gain[...])
         normed_out[...] = normed
         if copies is not None:
-            start_all(copies[2:])
+            start_all(copies[3:])
         rates = spread_rates(normed, w_rate[0], base[...])
         ones = head_ones()
 
         def project(side, quad):
-            if copies is not None and quad % (quads // 2) == 0 and (side or quad == 0):
-                wait_all([copies[side + (2 * quad) // quads]])
+            if copies is not None and quad % (quads // 2) == 0:
+                wait_all([copies[2 * side + (2 * quad) // quads]])
             lane = base_lane + side * width + quad * QUAD
             return mm(normed, weights[:, lane : lane + QUAD])
 
@@ -444,7 +444,7 @@
         first_front,
         [maps] + rows_out,
         [pltpu.VMEM(value.shape, value.dtype) for value in (tokens, norm_gain, w_rate, rate_base)]
-        + [pltpu.VMEM((depth, 2 * width), BF16), pltpu.SemaphoreType.DMA((4,)), pltpu.SemaphoreType.DMA((3,))],
+        + [pltpu.VMEM((depth, 2 * width), BF16), pltpu.SemaphoreType.DMA((4,)), pltpu.SemaphoreType.DMA((4,))],
         [in_hbm(tokens), norm_gain, w_qkv, w_rate, rate_base],
         [pltpu.HBM] * 5,
         name="first_front",

time: 49.3 us -> 49.5 us (level)
  no operation moved by 1% of the time
where the time goes in v20:
time: 49.5 us; the launch traced here: 49.2 us
  waiting for transfers between devices  20.5 us (41%)
  starting transfers between devices  14.8 us (30%)
  Pallas kernels  13.1 us (26%)
  between operations  0.58 us (1%)
    ppermute x2, waiting for transfers between devices, begin(): lax.ppermute(first, ('section', 'seq'), [(place, count + place) for place...  18.2 us
    pallas_call x23, Pallas kernels, call(): pl.pallas_call(body, out_shape=outs, in_specs=specs, out_specs=[pl.BlockS...  13.1 us
    ppermute x13, starting transfers between devices, permute(): lax.ppermute(value, ('section', 'seq'), [(base + source, base + target) f...  12.8 us
    ppermute x13, waiting for transfers between devices, permute(): lax.ppermute(value, ('section', 'seq'), [(base + source, base + target) f...  2.34 us
    ppermute x2, starting transfers between devices, begin(): lax.ppermute(first, ('section', 'seq'), [(place, count + place) for place...  1.99 us
  transfers between devices with their start and end apart: 15, of which 2 were waited for; matrix products, arithmetic and copies ran while one was open for 0% of the time, Pallas kernels for 23%

profile of v20, /device:TPU:25, one launch (start us, length us, event | category | flops | bytes accessed | tf_op | source)
XLA Modules:
  0.0 49.2 jit_solution(12063042951346399234)
XLA Ops:
  0.0 0.0 copy-start
  0.0 0.1 first_front.1
  0.1 0.8 %collective-permute-start = (bf16[64,2048]{1,0:T(8,128)(2,1)S(1)}, bf16[64,2048]{1,0:T(8,128)(2,1)S(1)}, u32[]{:S(2)}, u32[]{:S(2)}) collective-permute-start(bf16[64,2048]{1,0:T(8,128)(2,1)S(1)} %get-tuple-element.29.own_ref.after_ref), channel_id=1, source_target_pairs={{4,6},{6,4},{8,10},{10,8},{12,14},{14,12},{5,7},{7,5},{9,11},{11,9... | collective-permute-start | bytes 786440 | tf_op jit(solution)/shard_map/ppermute | solution.py:414
  0.9 0.1 copy-done
  1.0 0.7 %collective-permute-start.1 = (bf16[64,1024]{1,0:T(8,128)(2,1)S(1)}, bf16[64,1024]{1,0:T(8,128)(2,1)S(1)}, u32[]{:S(2)}, u32[]{:S(2)}) collective-permute-start(bf16[64,1024]{1,0:T(8,128)(2,1)S(1)} %first_step.1), channel_id=1, source_target_pairs={{0,2},{1,3}} | collective-permute-start | bytes 393224 | tf_op jit(solution)/shard_map/ppermute | solution.py:414
  1.8 0.0 collective-permute-done.1.state_ref.refs_1_
  1.8 0.0 copy-start.1
  1.8 0.8 %collective-permute-start.3 = (bf16[64,1024]{1,0:T(8,128)(2,1)S(1)}, bf16[64,1024]{1,0:T(8,128)(2,1)S(1)}, u32[]{:S(2)}, u32[]{:S(2)}) collective-permute-start(bf16[64,1024]{1,0:T(8,128)(2,1)S(1)} %second_step.1.after_ref.refs_5_), channel_id=1, source_target_pairs={{2,4},{3,5}} | collective-permute-start | bytes 393224 | tf_op jit(solution)/shard_map/ppermute | solution.py:414
  2.6 0.7 %collective-permute-start.2 = (bf16[64,1024]{1,0:T(8,128)(2,1)S(1)}, bf16[64,1024]{1,0:T(8,128)(2,1)S(1)}, u32[]{:S(2)}, u32[]{:S(2)}) collective-permute-start(bf16[64,1024]{1,0:T(8,128)(2,1)S(1)} %second_step.1.after_ref.refs_5_), channel_id=1, source_target_pairs={{2,6},{3,7}} | collective-permute-start | bytes 393224 | tf_op jit(solution)/shard_map/ppermute | solution.py:414
  3.3 0.0 copy-done.1
  3.4 0.0 collective-permute-done.got_ref.refs_2_.refs_1_
  3.4 0.0 collective-permute-done.3.refs_2_.refs_1_
  3.5 0.0 collective-permute-done.2.refs_1_.refs_0_
  3.5 0.7 %collective-permute-start.4 = (bf16[64,1024]{1,0:T(8,128)(2,1)S(1)}, bf16[64,1024]{1,0:T(8,128)(2,1)S(1)}, u32[]{:S(2)}, u32[]{:S(2)}) collective-permute-start(bf16[64,1024]{1,0:T(8,128)(2,1)S(1)} %advance0_1.1.refs_6_), channel_id=1, source_target_pairs={{4,8},{6,10},{5,9},{7,11}} | collective-permute-start | bytes 393224 | tf_op jit(solution)/shard_map/ppermute | solution.py:414
  4.2 0.0 collective-permute-done.4.refs_1_.refs_0_
  4.3 0.7 %collective-permute-start.5 = (bf16[128,2048]{1,0:T(8,128)(2,1)S(1)}, bf16[128,2048]{1,0:T(8,128)(2,1)S(1)}, u32[]{:S(2)}, u32[]{:S(2)}) collective-permute-start(bf16[128,2048]{1,0:T(8,128)(2,1)S(1)} %first_finish_2.1.refs_12_), channel_id=1, source_target_pairs={{0,16},{2,18},{4,20},{6,22},{8,24},{10,26},{1,17},{3,19},{5,21},{7... | collective-permute-start | bytes 1572872 | tf_op jit(solution)/shard_map/ppermute | solution.py:488
  5.0 0.7 %collective-permute-start.12 = (bf16[64,1024]{1,0:T(8,128)(2,1)S(1)}, bf16[64,1024]{1,0:T(8,128)(2,1)S(1)}, u32[]{:S(2)}, u32[]{:S(2)}) collective-permute-start(bf16[64,1024]{1,0:T(8,128)(2,1)S(1)} %advance0_2.1.refs_5_), channel_id=1, source_target_pairs={{8,12},{10,14},{9,13},{11,15}} | collective-permute-start | bytes 393224 | tf_op jit(solution)/shard_map/ppermute | solution.py:414
  5.7 0.0 collective-permute-done.12.refs_0_
  5.7 0.2 first_finish_3.1.refs_13_
  5.9 1.3 %collective-permute-start.13 = (bf16[128,2048]{1,0:T(8,128)(2,1)S(1)}, bf16[128,2048]{1,0:T(8,128)(2,1)S(1)}, u32[]{:S(2)}, u32[]{:S(2)}) collective-permute-start(bf16[128,2048]{1,0:T(8,128)(2,1)S(1)} %first_finish_3.1.refs_13_), channel_id=1, source_target_pairs={{12,28},{14,30},{13,29},{15,31}} | collective-permute-start | bytes 1572872 | tf_op jit(solution)/shard_map/ppermute | solution.py:488
  7.2 5.9 %load.1 = (f32[1,2048]{1,0:T(1,128)S(1)}, bf16[1,2048,3072]{2,1,0:T(8,128)(2,1)S(1)}, bf16[1,16,2048]{2,1,0:T(8,128)(2,1)S(1)}, f32[1,16]{1,0:T(1,128)S(1)}, bf16[1,1024,2048]{2,1,0:T(8,128)(2,1)S(1)}) custom-call(f32[1,2048]{1,0:T(1,128)} %refs_0_.3, bf16[1,2048,3072]{2,1,0:T(8,128)(2,1)} %refs_1_.1, bf16[1,16,2048]{2,1,0:T(8,128)(2,1)} %bitcast.9, ...), custom_call_target="tpu_custom_call" | custom-call | tf_op jit(solution)/shard_map/load/pallas_call | solution.py:385
  13.1 0.0 collective-permute-done.5.h_ref.refs_10_
  13.1 0.7 %collective-permute-start.6 = (bf16[64,2048]{1,0:T(8,128)(2,1)S(1)}, bf16[64,2048]{1,0:T(8,128)(2,1)S(1)}, u32[]{:S(2)}, u32[]{:S(2)}) collective-permute-start(bf16[64,2048]{1,0:T(8,128)(2,1)S(1)} %get-tuple-element.43.refs_0_.refs_3_.own_ref), channel_id=1, source_target_pairs={{16,18},{18,16},{17,19},{19,17}} | collective-permute-start | bytes 786440 | tf_op jit(solution)/shard_map/ppermute | solution.py:414
  13.8 0.7 %collective-permute-start.8 = (bf16[64,2048]{1,0:T(8,128)(2,1)S(1)}, bf16[64,2048]{1,0:T(8,128)(2,1)S(1)}, u32[]{:S(2)}, u32[]{:S(2)}) collective-permute-start(bf16[64,2048]{1,0:T(8,128)(2,1)S(1)} %get-tuple-element.43.refs_0_.refs_3_.own_ref), channel_id=1, source_target_pairs={{20,22},{22,20},{21,23},{23,21}} | collective-permute-start | bytes 786440 | tf_op jit(solution)/shard_map/ppermute | solution.py:414
  14.5 0.0 collective-permute-done.6.refs_1_.refs_4_
  14.6 0.7 %collective-permute-start.7 = (bf16[64,1024]{1,0:T(8,128)(2,1)S(1)}, bf16[64,1024]{1,0:T(8,128)(2,1)S(1)}, u32[]{:S(2)}, u32[]{:S(2)}) collective-permute-start(bf16[64,1024]{1,0:T(8,128)(2,1)S(1)} %advance1_0.1.after_ref.refs_2_), channel_id=1, source_target_pairs={{16,20},{18,22},{17,21},{19,23}} | collective-permute-start | bytes 393224 | tf_op jit(solution)/shard_map/ppermute | solution.py:414
  15.2 0.7 %collective-permute-start.10 = (bf16[64,2048]{1,0:T(8,128)(2,1)S(1)}, bf16[64,2048]{1,0:T(8,128)(2,1)S(1)}, u32[]{:S(2)}, u32[]{:S(2)}) collective-permute-start(bf16[64,2048]{1,0:T(8,128)(2,1)S(1)} %get-tuple-element.43.refs_0_.refs_3_.own_ref), channel_id=1, source_target_pairs={{24,26},{26,24},{25,27},{27,25}} | collective-permute-start | bytes 786440 | tf_op jit(solution)/shard_map/ppermute | solution.py:414
  15.9 0.0 collective-permute-done.8.got_ref.refs_5_
  16.0 0.0 collective-permute-done.7.refs_1_
  16.0 0.7 %collective-permute-start.9 = (bf16[64,1024]{1,0:T(8,128)(2,1)S(1)}, bf16[64,1024]{1,0:T(8,128)(2,1)S(1)}, u32[]{:S(2)}, u32[]{:S(2)}) collective-permute-start(bf16[64,1024]{1,0:T(8,128)(2,1)S(1)} %advance1_1.1.after_ref), channel_id=1, source_target_pairs={{20,24},{22,26},{21,25},{23,27}} | collective-permute-start | bytes 393224 | tf_op jit(solution)/shard_map/ppermute | solution.py:414
  16.7 18.2 %collective-permute-done.13.h_ref.refs_11_ = bf16[128,2048]{1,0:T(8,128)(2,1)S(1)} collective-permute-done((bf16[128,2048]{1,0:T(8,128)(2,1)S(1)}, bf16[128,2048]{1,0:T(8,128)(2,1)S(1)}, u32[]{:S(2)}, u32[]{:S(2)}) %collective-permute-start.13) | collective-permute-done | bytes 524320 | tf_op jit(solution)/shard_map/ppermute | solution.py:488
  34.9 2.8 %later_front_3.1 = (bf16[64,2048]{1,0:T(8,128)(2,1)S(1)}, bf16[128,2048]{1,0:T(8,128)(2,1)S(1)}, bf16[128,1024]{1,0:T(8,128)(2,1)S(1)}, bf16[128,1024]{1,0:T(8,128)(2,1)S(1)}, bf16[128,1024]{1,0:T(8,128)(2,1)S(1)}) custom-call(bf16[128,2048]{1,0:T(8,128)(2,1)S(1)} %collective-permute-done.13.h_ref.refs_11_, f32[1,2048]{1,0:T(1,128)S(1)} %get-tuple-element.39.gain, ...), custom_call_target="tpu_custom_call" | custom-call | tf_op jit(solution)/shard_map/later_front_3/pallas_call | solution.py:385
  37.7 3.9 %collective-permute-start.14 = (bf16[64,2048]{1,0:T(8,128)(2,1)S(1)}, bf16[64,2048]{1,0:T(8,128)(2,1)S(1)}, u32[]{:S(2)}, u32[]{:S(2)}) collective-permute-start(bf16[64,2048]{1,0:T(8,128)(2,1)S(1)} %get-tuple-element.48), channel_id=1, source_target_pairs={{28,30},{30,28},{29,31},{31,29}} | collective-permute-start | bytes 786440 | tf_op jit(solution)/shard_map/ppermute | solution.py:414
  41.6 0.0 collective-permute-done.10.got_ref.refs_6_
  41.7 0.0 collective-permute-done.9.refs_1_.refs_2_
  41.7 1.3 %collective-permute-start.11 = (bf16[64,1024]{1,0:T(8,128)(2,1)S(1)}, bf16[64,1024]{1,0:T(8,128)(2,1)S(1)}, u32[]{:S(2)}, u32[]{:S(2)}) collective-permute-start(bf16[64,1024]{1,0:T(8,128)(2,1)S(1)} %advance1_2.1.after_ref), channel_id=1, source_target_pairs={{24,28},{26,30},{25,29},{27,31}} | collective-permute-start | bytes 393224 | tf_op jit(solution)/shard_map/ppermute | solution.py:414
  43.0 2.1 %reads1_3.1.refs_9_ = bf16[128,2048]{1,0:T(8,128)(2,1)S(1)} custom-call(bf16[128,2048]{1,0:T(8,128)(2,1)S(1)} %get-tuple-element.49.normed_ref, bf16[128,1024]{1,0:T(8,128)(2,1)S(1)} %get-tuple-element.50.keys_ref, bf16[128,1024]{1,0:T(8,128)(2,1)S(1)} %get-tuple-element.51.x_ref, bf16[128,1024]{1,0:T(8,128)(2,1)S(1)} %get-tuple-element.52.y_ref, ...), custom_call_target="tpu_custom_call" | custom-call | tf_op jit(solution)/shard_map/reads1_3/pallas_call | solution.py:385
  45.1 2.3 %collective-permute-done.11.refs_3_ = bf16[64,1024]{1,0:T(8,128)(2,1)S(1)} collective-permute-done((bf16[64,1024]{1,0:T(8,128)(2,1)S(1)}, bf16[64,1024]{1,0:T(8,128)(2,1)S(1)}, u32[]{:S(2)}, u32[]{:S(2)}) %collective-permute-start.11) | collective-permute-done | bytes 131104 | tf_op jit(solution)/shard_map/ppermute | solution.py:414
  47.4 0.0 collective-permute-done.14.refs_7_
  47.4 1.6 %last_finish.1 = bf16[1,128,2048]{2,1,0:T(8,128)(2,1)} custom-call(bf16[1024,2048]{1,0:T(8,128)(2,1)S(1)} %bitcast.7, f32[1,16,64,64]{3,2,1,0:T(8,128)S(1)} %copy-done, bf16[64,1024]{1,0:T(8,128)(2,1)S(1)} %collective-permute-done.7.refs_1_, bf16[64,1024]{1,0:T(8,128)(2,1)S(1)} %collective-permute-done.9.refs_1_.refs_2_, ...), custom_call_target="tpu_custom_call" | custom-call | tf_op jit(solution)/shard_map/last_finish/pallas_call | solution.py:385
  (17 shorter events, 0.5 us)
Async XLA Ops:
  0.0 1.0 %copy-start = (f32[1,16,64,64]{3,2,1,0:T(8,128)S(1)}, f32[1,16,64,64]{3,2,1,0:T(8,128)}, u32[]{:S(2)}) copy-start(f32[1,16,64,64]{3,2,1,0:T(8,128)} %refs_0_.5) | copy-start | bytes 786436
  0.1 3.3 %collective-permute-start = (bf16[64,2048]{1,0:T(8,128)(2,1)S(1)}, bf16[64,2048]{1,0:T(8,128)(2,1)S(1)}, u32[]{:S(2)}, u32[]{:S(2)}) collective-permute-start(bf16[64,2048]{1,0:T(8,128)(2,1)S(1)} %get-tuple-element.29.own_ref.after_ref), channel_id=1, source_target_pairs={{4,6},{6,4},{8,10},{10,8},{12,14},{14,12},{5,7},{7,5},{9,11},{11,9... | collective-permute-start | bytes 786440 | tf_op jit(solution)/shard_map/ppermute | solution.py:414
  1.0 0.7 %collective-permute-start.1 = (bf16[64,1024]{1,0:T(8,128)(2,1)S(1)}, bf16[64,1024]{1,0:T(8,128)(2,1)S(1)}, u32[]{:S(2)}, u32[]{:S(2)}) collective-permute-start(bf16[64,1024]{1,0:T(8,128)(2,1)S(1)} %first_step.1), channel_id=1, source_target_pairs={{0,2},{1,3}} | collective-permute-start | bytes 393224 | tf_op jit(solution)/shard_map/ppermute | solution.py:414
  1.8 1.6 %copy-start.1 = (bf16[128,2048]{1,0:T(8,128)(2,1)S(1)}, bf16[128,2048]{1,0:T(8,128)(2,1)}, u32[]{:S(2)}) copy-start(bf16[128,2048]{1,0:T(8,128)(2,1)} %refs_4_.7) | copy-start | bytes 1572868
  1.8 1.6 %collective-permute-start.3 = (bf16[64,1024]{1,0:T(8,128)(2,1)S(1)}, bf16[64,1024]{1,0:T(8,128)(2,1)S(1)}, u32[]{:S(2)}, u32[]{:S(2)}) collective-permute-start(bf16[64,1024]{1,0:T(8,128)(2,1)S(1)} %second_step.1.after_ref.refs_5_), channel_id=1, source_target_pairs={{2,4},{3,5}} | collective-permute-start | bytes 393224 | tf_op jit(solution)/shard_map/ppermute | solution.py:414
  2.6 0.8 %collective-permute-start.2 = (bf16[64,1024]{1,0:T(8,128)(2,1)S(1)}, bf16[64,1024]{1,0:T(8,128)(2,1)S(1)}, u32[]{:S(2)}, u32[]{:S(2)}) collective-permute-start(bf16[64,1024]{1,0:T(8,128)(2,1)S(1)} %second_step.1.after_ref.refs_5_), channel_id=1, source_target_pairs={{2,6},{3,7}} | collective-permute-start | bytes 393224 | tf_op jit(solution)/shard_map/ppermute | solution.py:414
  3.5 0.7 %collective-permute-start.4 = (bf16[64,1024]{1,0:T(8,128)(2,1)S(1)}, bf16[64,1024]{1,0:T(8,128)(2,1)S(1)}, u32[]{:S(2)}, u32[]{:S(2)}) collective-permute-start(bf16[64,1024]{1,0:T(8,128)(2,1)S(1)} %advance0_1.1.refs_6_), channel_id=1, source_target_pairs={{4,8},{6,10},{5,9},{7,11}} | collective-permute-start | bytes 393224 | tf_op jit(solution)/shard_map/ppermute | solution.py:414
  4.3 8.8 %collective-permute-start.5 = (bf16[128,2048]{1,0:T(8,128)(2,1)S(1)}, bf16[128,2048]{1,0:T(8,128)(2,1)S(1)}, u32[]{:S(2)}, u32[]{:S(2)}) collective-permute-start(bf16[128,2048]{1,0:T(8,128)(2,1)S(1)} %first_finish_2.1.refs_12_), channel_id=1, source_target_pairs={{0,16},{2,18},{4,20},{6,22},{8,24},{10,26},{1,17},{3,19},{5,21},{7... | collective-permute-start | bytes 1572872 | tf_op jit(solution)/shard_map/ppermute | solution.py:488
  5.0 0.7 %collective-permute-start.12 = (bf16[64,1024]{1,0:T(8,128)(2,1)S(1)}, bf16[64,1024]{1,0:T(8,128)(2,1)S(1)}, u32[]{:S(2)}, u32[]{:S(2)}) collective-permute-start(bf16[64,1024]{1,0:T(8,128)(2,1)S(1)} %advance0_2.1.refs_5_), channel_id=1, source_target_pairs={{8,12},{10,14},{9,13},{11,15}} | collective-permute-start | bytes 393224 | tf_op jit(solution)/shard_map/ppermute | solution.py:414
  5.9 29.0 %collective-permute-start.13 = (bf16[128,2048]{1,0:T(8,128)(2,1)S(1)}, bf16[128,2048]{1,0:T(8,128)(2,1)S(1)}, u32[]{:S(2)}, u32[]{:S(2)}) collective-permute-start(bf16[128,2048]{1,0:T(8,128)(2,1)S(1)} %first_finish_3.1.refs_13_), channel_id=1, source_target_pairs={{12,28},{14,30},{13,29},{15,31}} | collective-permute-start | bytes 1572872 | tf_op jit(solution)/shard_map/ppermute | solution.py:488
  13.1 1.4 %collective-permute-start.6 = (bf16[64,2048]{1,0:T(8,128)(2,1)S(1)}, bf16[64,2048]{1,0:T(8,128)(2,1)S(1)}, u32[]{:S(2)}, u32[]{:S(2)}) collective-permute-start(bf16[64,2048]{1,0:T(8,128)(2,1)S(1)} %get-tuple-element.43.refs_0_.refs_3_.own_ref), channel_id=1, source_target_pairs={{16,18},{18,16},{17,19},{19,17}} | collective-permute-start | bytes 786440 | tf_op jit(solution)/shard_map/ppermute | solution.py:414
  13.8 2.1 %collective-permute-start.8 = (bf16[64,2048]{1,0:T(8,128)(2,1)S(1)}, bf16[64,2048]{1,0:T(8,128)(2,1)S(1)}, u32[]{:S(2)}, u32[]{:S(2)}) collective-permute-start(bf16[64,2048]{1,0:T(8,128)(2,1)S(1)} %get-tuple-element.43.refs_0_.refs_3_.own_ref), channel_id=1, source_target_pairs={{20,22},{22,20},{21,23},{23,21}} | collective-permute-start | bytes 786440 | tf_op jit(solution)/shard_map/ppermute | solution.py:414
  14.6 1.4 %collective-permute-start.7 = (bf16[64,1024]{1,0:T(8,128)(2,1)S(1)}, bf16[64,1024]{1,0:T(8,128)(2,1)S(1)}, u32[]{:S(2)}, u32[]{:S(2)}) collective-permute-start(bf16[64,1024]{1,0:T(8,128)(2,1)S(1)} %advance1_0.1.after_ref.refs_2_), channel_id=1, source_target_pairs={{16,20},{18,22},{17,21},{19,23}} | collective-permute-start | bytes 393224 | tf_op jit(solution)/shard_map/ppermute | solution.py:414
  15.2 26.4 %collective-permute-start.10 = (bf16[64,2048]{1,0:T(8,128)(2,1)S(1)}, bf16[64,2048]{1,0:T(8,128)(2,1)S(1)}, u32[]{:S(2)}, u32[]{:S(2)}) collective-permute-start(bf16[64,2048]{1,0:T(8,128)(2,1)S(1)} %get-tuple-element.43.refs_0_.refs_3_.own_ref), channel_id=1, source_target_pairs={{24,26},{26,24},{25,27},{27,25}} | collective-permute-start | bytes 786440 | tf_op jit(solution)/shard_map/ppermute | solution.py:414
  16.0 25.7 %collective-permute-start.9 = (bf16[64,1024]{1,0:T(8,128)(2,1)S(1)}, bf16[64,1024]{1,0:T(8,128)(2,1)S(1)}, u32[]{:S(2)}, u32[]{:S(2)}) collective-permute-start(bf16[64,1024]{1,0:T(8,128)(2,1)S(1)} %advance1_1.1.after_ref), channel_id=1, source_target_pairs={{20,24},{22,26},{21,25},{23,27}} | collective-permute-start | bytes 393224 | tf_op jit(solution)/shard_map/ppermute | solution.py:414
  37.7 9.8 %collective-permute-start.14 = (bf16[64,2048]{1,0:T(8,128)(2,1)S(1)}, bf16[64,2048]{1,0:T(8,128)(2,1)S(1)}, u32[]{:S(2)}, u32[]{:S(2)}) collective-permute-start(bf16[64,2048]{1,0:T(8,128)(2,1)S(1)} %get-tuple-element.48), channel_id=1, source_target_pairs={{28,30},{30,28},{29,31},{31,29}} | collective-permute-start | bytes 786440 | tf_op jit(solution)/shard_map/ppermute | solution.py:414
  41.7 5.7 %collective-permute-start.11 = (bf16[64,1024]{1,0:T(8,128)(2,1)S(1)}, bf16[64,1024]{1,0:T(8,128)(2,1)S(1)}, u32[]{:S(2)}, u32[]{:S(2)}) collective-permute-start(bf16[64,1024]{1,0:T(8,128)(2,1)S(1)} %advance1_2.1.after_ref), channel_id=1, source_target_pairs={{24,28},{26,30},{25,29},{27,31}} | collective-permute-start | bytes 393224 | tf_op jit(solution)/shard_map/ppermute | solution.py:414
